TPU v7x, 32 devices: a whole 2x2x4 slice. The times are simulated.
32 devices in a mesh: parts: 2 (over x), cuts: 16 (over z, y, core).
Axes of the slice: x: 2, y: 2, z: 4, core: 2. Of those that a mesh axis runs over, the one named last changes fastest.
Arguments:
- objects: bfloat16 [32, 2, 384, 384], P(('parts', 'cuts')), parts along dimension 0, may hold values from -0.14941406 to 0.14941406
- propagators: bfloat16 [4, 2, 192, 192], replicated, may hold values from -1 to 1
- prop_index: int32 [32], P(('parts', 'cuts')), parts along dimension 0, may hold values from 0 to 3
- probes: bfloat16 [8, 2, 192, 192], replicated, may hold values from -6 to 6
- probe_group: int32 [6], replicated, may hold values from 0 to 7, as said below
- offsets: int32 [12, 2], P('parts'), parts along dimension 0, may hold values from 0 to 192
- measured: float32 [12, 192, 192], P('parts', 'cuts'), parts along dimension 0, may hold values from 0.3 to 4
Outputs:
- object_grad: float32 [32, 2, 384, 384], P(('parts', 'cuts')), parts along dimension 0
There are 2 independent parts, one for each index of `parts`. A program takes and returns all parts, laid end to end along the dimension named above; an argument that names none is the same for every part. Nothing has to cross between parts.
Inputs may be any that keep to these rules, and one draw needn't show every extreme that they name: `probe_group`: within each run of 8 consecutive positions every group appears once.
All inputs are finite; a program needn't handle non-finite values.
Results may differ from a plain program's by a relative error of at most 0.035.
Values may be sent and summed in bfloat16 or wider, within the bound.
No kernel may reach another device: no remote copies, remote signals or barrier semaphores. Data moves between devices by JAX's collectives and lax.ppermute only.
A program may use at most 64 MiB of HBM per device.

v0:
```python
import math

import jax
import jax.numpy as jnp
from jax import lax
from jax.sharding import PartitionSpec as P

TRANSMIT = 0.985


def passed_along(block, axis, distance):
    devices = range(lax.axis_size(axis))
    route = [(i - distance, i) for i in devices if i - distance in devices]
    return lax.ppermute(block, axis, route)


def plain_product(former, latter):
    return jnp.dot(
        former.astype(jnp.float32),
        latter.astype(jnp.float32),
        precision=lax.Precision.HIGHEST,
        preferred_element_type=jnp.float32,
    )


def product_transposed(former, latter):
    return jnp.dot(
        former.astype(jnp.float32),
        latter.astype(jnp.float32).T,
        precision=lax.Precision.HIGHEST,
        preferred_element_type=jnp.float32,
    )


def transposed_product(former, latter):
    return jnp.dot(
        former.astype(jnp.float32).T,
        latter.astype(jnp.float32),
        precision=lax.Precision.HIGHEST,
        preferred_element_type=jnp.float32,
    )


def precise_product(former, latter):
    return jnp.dot(
        former, latter, precision=lax.Precision.HIGHEST, preferred_element_type=jnp.float32
    )


def dft_tables(wave_width):
    counter = jnp.arange(wave_width, dtype=jnp.int32)
    phase = counter[:, None] * counter[None, :] % wave_width
    angle = phase.astype(jnp.float32) * (2.0 * math.pi / wave_width)
    factor = 1.0 / math.sqrt(wave_width)
    return (jnp.cos(angle) * factor, -jnp.sin(angle) * factor)


def window_of(object_field, corner, wave_width):
    anchor = (jnp.zeros((), jnp.int32), corner[0], corner[1])
    window = lax.dynamic_slice(object_field, anchor, (2, wave_width, wave_width)).astype(
        jnp.float32
    )
    return (TRANSMIT + window[0], window[1])


def forward_slice(object_field, prop_pair, entering, corner):
    wave_width = entering.shape[-1]
    trans_real, trans_imag = window_of(object_field, corner, wave_width)
    wave_real = entering[0].astype(jnp.float32)
    wave_imag = entering[1].astype(jnp.float32)
    mixed_real = (trans_real * wave_real - trans_imag * wave_imag).astype(jnp.bfloat16)
    mixed_imag = (trans_real * wave_imag + trans_imag * wave_real).astype(jnp.bfloat16)
    prop_real = prop_pair[0]
    prop_imag = prop_pair[1]
    half_real = (
        plain_product(prop_real, mixed_real) - plain_product(prop_imag, mixed_imag)
    ).astype(jnp.bfloat16)
    half_imag = (
        plain_product(prop_real, mixed_imag) + plain_product(prop_imag, mixed_real)
    ).astype(jnp.bfloat16)
    out_real = product_transposed(half_real, prop_real) - product_transposed(half_imag, prop_imag)
    out_imag = product_transposed(half_real, prop_imag) + product_transposed(half_imag, prop_real)
    return jnp.stack([out_real, out_imag]).astype(jnp.bfloat16)


def detector(leaving, measured_here):
    wave_width = leaving.shape[-1]
    dft_real, dft_imag = dft_tables(wave_width)
    wave_real = leaving[0].astype(jnp.float32)
    wave_imag = leaving[1].astype(jnp.float32)
    near_real = precise_product(dft_real, wave_real) - precise_product(dft_imag, wave_imag)
    near_imag = precise_product(dft_real, wave_imag) + precise_product(dft_imag, wave_real)
    far_real = precise_product(near_real, dft_real) - precise_product(near_imag, dft_imag)
    far_imag = precise_product(near_real, dft_imag) + precise_product(near_imag, dft_real)
    misfit = far_real * far_real + far_imag * far_imag - measured_here
    push_real = misfit * far_real
    push_imag = misfit * far_imag
    back_real = precise_product(dft_real, push_real) + precise_product(dft_imag, push_imag)
    back_imag = precise_product(dft_real, push_imag) - precise_product(dft_imag, push_real)
    exit_real = precise_product(back_real, dft_real) + precise_product(back_imag, dft_imag)
    exit_imag = precise_product(back_imag, dft_real) - precise_product(back_real, dft_imag)
    return jnp.stack([exit_real, exit_imag]).astype(jnp.bfloat16)


def backward_slice(object_field, prop_pair, arriving, before, corner):
    wave_width = arriving.shape[-1]
    trans_real, trans_imag = window_of(object_field, corner, wave_width)
    prop_real = prop_pair[0]
    prop_imag = prop_pair[1]
    grad_real = arriving[0]
    grad_imag = arriving[1]
    back_real = (
        transposed_product(prop_real, grad_real) + transposed_product(prop_imag, grad_imag)
    ).astype(jnp.bfloat16)
    back_imag = (
        transposed_product(prop_real, grad_imag) - transposed_product(prop_imag, grad_real)
    ).astype(jnp.bfloat16)
    inner_real = plain_product(back_real, prop_real) + plain_product(back_imag, prop_imag)
    inner_imag = plain_product(back_imag, prop_real) - plain_product(back_real, prop_imag)
    before_real = before[0].astype(jnp.float32)
    before_imag = before[1].astype(jnp.float32)
    window_grad = jnp.stack(
        [
            inner_real * before_real + inner_imag * before_imag,
            inner_imag * before_real - inner_real * before_imag,
        ]
    )
    passed = jnp.stack(
        [
            trans_real * inner_real + trans_imag * inner_imag,
            trans_real * inner_imag - trans_imag * inner_real,
        ]
    ).astype(jnp.bfloat16)
    return (window_grad, passed)


def pick_table(propagators, which):
    chosen_mask = jnp.arange(propagators.shape[0], dtype=jnp.int32) == which
    return jnp.sum(
        jnp.where(chosen_mask[:, None, None, None], propagators, jnp.zeros_like(propagators)),
        axis=0,
    )


def shards(objects, propagators, prop_index, probes, probe_group, offsets, measured):
    sections = lax.axis_size("cuts")
    rank_here = lax.axis_index("cuts")
    last_section = sections - 1
    positions = probe_group.shape[0]
    wave_width = probes.shape[-1]
    object_field = objects[0]
    observed = lax.all_gather(measured, "cuts", axis=1, tiled=True)
    zero_wave = jnp.zeros((2, wave_width, wave_width), jnp.bfloat16)
    prop_pair = pick_table(propagators, prop_index[0])

    def one_tick(tick_index, states, forward, backward, return_base):
        incoming, stored_waves, exit_grads, returning, accumulated = states
        if forward:
            slot_raw = tick_index - rank_here
            active = (slot_raw >= 0) & (slot_raw < positions)
            position_slot = jnp.clip(slot_raw, 0, positions - 1)
            corner = lax.dynamic_index_in_dim(offsets, position_slot, 0, False)
            group_here = lax.dynamic_index_in_dim(probe_group, position_slot, 0, False)
            start_wave = lax.dynamic_index_in_dim(probes, group_here, 0, False)
            entering = jnp.where(rank_here == 0, start_wave, incoming)

            def advance(buffers):
                kept_waves = lax.dynamic_update_index_in_dim(buffers[0], entering, position_slot, 0)
                leaving = forward_slice(object_field, prop_pair, entering, corner)
                measured_here = lax.dynamic_index_in_dim(observed, position_slot, 0, False)
                exit_here = lax.cond(
                    rank_here == last_section,
                    lambda: detector(leaving, measured_here),
                    lambda: zero_wave,
                )
                kept_exits = lax.dynamic_update_index_in_dim(
                    buffers[1], exit_here, position_slot, 0
                )
                return (leaving, kept_waves, kept_exits)

            def resting(buffers):
                return (zero_wave, buffers[0], buffers[1])

            leaving, stored_waves, exit_grads = lax.cond(
                active, advance, resting, (stored_waves, exit_grads)
            )
            incoming = passed_along(leaving, "cuts", 1)
        if backward:
            slot_raw = tick_index - return_base - (last_section - rank_here)
            active = (slot_raw >= 0) & (slot_raw < positions)
            position_slot = jnp.clip(slot_raw, 0, positions - 1)
            corner = lax.dynamic_index_in_dim(offsets, position_slot, 0, False)
            exit_here = lax.dynamic_index_in_dim(exit_grads, position_slot, 0, False)
            arriving = jnp.where(rank_here == last_section, exit_here, returning)
            before = lax.dynamic_index_in_dim(stored_waves, position_slot, 0, False)

            def retreat(summed):
                window_grad, passed = backward_slice(
                    object_field, prop_pair, arriving, before, corner
                )
                anchor = (jnp.zeros((), jnp.int32), corner[0], corner[1])
                current = lax.dynamic_slice(summed, anchor, window_grad.shape)
                return (passed, lax.dynamic_update_slice(summed, current + window_grad, anchor))

            def holding(summed):
                return (zero_wave, summed)

            passed, accumulated = lax.cond(active, retreat, holding, accumulated)
            returning = passed_along(passed, "cuts", -1)
        return (incoming, stored_waves, exit_grads, returning, accumulated)

    states = (
        zero_wave,
        jnp.zeros((positions, 2, wave_width, wave_width), jnp.bfloat16),
        jnp.zeros((positions, 2, wave_width, wave_width), jnp.bfloat16),
        zero_wave,
        jnp.zeros(object_field.shape, jnp.float32),
    )
    forward_ticks = sections + positions - 1
    states = lax.fori_loop(
        0,
        forward_ticks,
        lambda tick_index, carried: one_tick(tick_index, carried, True, False, forward_ticks),
        states,
    )
    states = lax.fori_loop(
        forward_ticks,
        2 * forward_ticks,
        lambda tick_index, carried: one_tick(tick_index, carried, False, True, forward_ticks),
        states,
    )
    return states[4][None]


def solution(mesh):
    in_specs = (
        P(("parts", "cuts"), None, None, None),
        P(),
        P(("parts", "cuts")),
        P(),
        P(),
        P("parts", None),
        P("parts", "cuts", None),
    )
    out_specs = P(("parts", "cuts"), None, None, None)
    return jax.shard_map(shards, mesh=mesh, in_specs=in_specs, out_specs=out_specs, check_vma=False)
```

profile of v0, /device:TPU:0, one launch (start us, length us, event | category | flops | bytes accessed | tf_op | source)
XLA Modules:
  0.0 869.2 jit_solution(3121019229716739674)
XLA Ops:
  2.9 27.5 %all_gather.3 = f32[6,192,192]{2,0,1:T(8,128)S(1)} all-gather(f32[6,12,192]{2,0,1:T(8,128)S(1)} %copy.8), channel_id=1, replica_groups=mesh['parts'=2,'cuts'=16] {'cuts'}, dimensions={1}, use_global_device_ids=true | all-gather | bytes 940032 | tf_op jit(solution)/shard_map/all_gather | solution.py:152
  33.1 277.7 %while.40 = (s32[]{:T(128)}, bf16[2,192,192]{2,1,0:T(8,128)(2,1)S(1)}, bf16[6,2,192,192]{3,2,1,0:T(8,128)(2,1)}, bf16[6,2,192,192]{3,2,1,0:T(8,128)(2,1)S(1)}, s...) while((s32[]{:T(128)}, ...), condition=%wide.region_6.7_spmd, body=%wide.region_1.6_spmd.sunk | while | flops 1479979008 | bytes 12535379 | solution.py:220
  33.1 11.2 %conditional.5 = (bf16[2,192,192]{2,1,0:T(8,128)(2,1)}, bf16[6,2,192,192]{3,2,1,0:T(8,128)(2,1)}, bf16[6,2,192,192]{3,2,1,0:T(8,128)(2,1)S(1)}) conditional(s32[]{:T(128)} %convert_element_type.275, (bf16[6,2,192,192]{3,2,1,0:T(8,128)(2,1)}, bf16[6,2,192,192]{3,2,1,0:T(8,128)(2,1)S(1)}) %tuple.146, (s32[]{:T(128)}, s32[6,2]{0,1:T(2,128)S(1)}, ...), branch_computations={%region_2.2_spmd, %region_3.5_spmd} | conditional | flops 1479979008 | bytes 11945224 | solution.py:184
  46.9 11.1 %conditional.5 = (bf16[2,192,192]{2,1,0:T(8,128)(2,1)}, bf16[6,2,192,192]{3,2,1,0:T(8,128)(2,1)}, bf16[6,2,192,192]{3,2,1,0:T(8,128)(2,1)S(1)}) conditional(s32[]{:T(128)} %convert_element_type.275, (bf16[6,2,192,192]{3,2,1,0:T(8,128)(2,1)}, bf16[6,2,192,192]{3,2,1,0:T(8,128)(2,1)S(1)}) %tuple.146, (s32[]{:T(128)}, s32[6,2]{0,1:T(2,128)S(1)}, ...), branch_computations={%region_2.2_spmd, %region_3.5_spmd} | conditional | flops 1479979008 | bytes 11945224 | solution.py:184
  61.6 11.1 %conditional.5 = (bf16[2,192,192]{2,1,0:T(8,128)(2,1)}, bf16[6,2,192,192]{3,2,1,0:T(8,128)(2,1)}, bf16[6,2,192,192]{3,2,1,0:T(8,128)(2,1)S(1)}) conditional(s32[]{:T(128)} %convert_element_type.275, (bf16[6,2,192,192]{3,2,1,0:T(8,128)(2,1)}, bf16[6,2,192,192]{3,2,1,0:T(8,128)(2,1)S(1)}) %tuple.146, (s32[]{:T(128)}, s32[6,2]{0,1:T(2,128)S(1)}, ...), branch_computations={%region_2.2_spmd, %region_3.5_spmd} | conditional | flops 1479979008 | bytes 11945224 | solution.py:184
  77.6 11.1 %conditional.5 = (bf16[2,192,192]{2,1,0:T(8,128)(2,1)}, bf16[6,2,192,192]{3,2,1,0:T(8,128)(2,1)}, bf16[6,2,192,192]{3,2,1,0:T(8,128)(2,1)S(1)}) conditional(s32[]{:T(128)} %convert_element_type.275, (bf16[6,2,192,192]{3,2,1,0:T(8,128)(2,1)}, bf16[6,2,192,192]{3,2,1,0:T(8,128)(2,1)S(1)}) %tuple.146, (s32[]{:T(128)}, s32[6,2]{0,1:T(2,128)S(1)}, ...), branch_computations={%region_2.2_spmd, %region_3.5_spmd} | conditional | flops 1479979008 | bytes 11945224 | solution.py:184
  95.9 11.1 %conditional.5 = (bf16[2,192,192]{2,1,0:T(8,128)(2,1)}, bf16[6,2,192,192]{3,2,1,0:T(8,128)(2,1)}, bf16[6,2,192,192]{3,2,1,0:T(8,128)(2,1)S(1)}) conditional(s32[]{:T(128)} %convert_element_type.275, (bf16[6,2,192,192]{3,2,1,0:T(8,128)(2,1)}, bf16[6,2,192,192]{3,2,1,0:T(8,128)(2,1)S(1)}) %tuple.146, (s32[]{:T(128)}, s32[6,2]{0,1:T(2,128)S(1)}, ...), branch_computations={%region_2.2_spmd, %region_3.5_spmd} | conditional | flops 1479979008 | bytes 11945224 | solution.py:184
  107.1 5.9 collective-permute-start
  114.3 11.1 %conditional.5 = (bf16[2,192,192]{2,1,0:T(8,128)(2,1)}, bf16[6,2,192,192]{3,2,1,0:T(8,128)(2,1)}, bf16[6,2,192,192]{3,2,1,0:T(8,128)(2,1)S(1)}) conditional(s32[]{:T(128)} %convert_element_type.275, (bf16[6,2,192,192]{3,2,1,0:T(8,128)(2,1)}, bf16[6,2,192,192]{3,2,1,0:T(8,128)(2,1)S(1)}) %tuple.146, (s32[]{:T(128)}, s32[6,2]{0,1:T(2,128)S(1)}, ...), branch_computations={%region_2.2_spmd, %region_3.5_spmd} | conditional | flops 1479979008 | bytes 11945224 | solution.py:184
  125.4 5.9 collective-permute-start
  133.3 16.4 %collective-permute-start = (bf16[2,192,192]{2,1,0:T(8,128)(2,1)}, bf16[2,192,192]{2,1,0:T(8,128)(2,1)S(1)}, u32[]{:S(2)}, u32[]{:S(2)}) collective-permute-start(bf16[2,192,192]{2,1,0:T(8,128)(2,1)} %get-tuple-element.1050), channel_id=1, source_target_pairs={{0,1},{1,2},{2,3},{3,4},{4,5},{5,6},{6,7},{7,8},{8,9},{9,10},{10,1... | collective-permute-start | bytes 442376 | tf_op jit(solution)/shard_map/while/body/eval_jaxpr/ppermute | solution.py:14
  159.6 16.4 %collective-permute-start = (bf16[2,192,192]{2,1,0:T(8,128)(2,1)}, bf16[2,192,192]{2,1,0:T(8,128)(2,1)S(1)}, u32[]{:S(2)}, u32[]{:S(2)}) collective-permute-start(bf16[2,192,192]{2,1,0:T(8,128)(2,1)} %get-tuple-element.1050), channel_id=1, source_target_pairs={{0,1},{1,2},{2,3},{3,4},{4,5},{5,6},{6,7},{7,8},{8,9},{9,10},{10,1... | collective-permute-start | bytes 442376 | tf_op jit(solution)/shard_map/while/body/eval_jaxpr/ppermute | solution.py:14
  185.8 10.0 %collective-permute-start = (bf16[2,192,192]{2,1,0:T(8,128)(2,1)}, bf16[2,192,192]{2,1,0:T(8,128)(2,1)S(1)}, u32[]{:S(2)}, u32[]{:S(2)}) collective-permute-start(bf16[2,192,192]{2,1,0:T(8,128)(2,1)} %get-tuple-element.1050), channel_id=1, source_target_pairs={{0,1},{1,2},{2,3},{3,4},{4,5},{5,6},{6,7},{7,8},{8,9},{9,10},{10,1... | collective-permute-start | bytes 442376 | tf_op jit(solution)/shard_map/while/body/eval_jaxpr/ppermute | solution.py:14
  197.7 6.8 collective-permute-start
  206.5 17.3 %collective-permute-start = (bf16[2,192,192]{2,1,0:T(8,128)(2,1)}, bf16[2,192,192]{2,1,0:T(8,128)(2,1)S(1)}, u32[]{:S(2)}, u32[]{:S(2)}) collective-permute-start(bf16[2,192,192]{2,1,0:T(8,128)(2,1)} %get-tuple-element.1050), channel_id=1, source_target_pairs={{0,1},{1,2},{2,3},{3,4},{4,5},{5,6},{6,7},{7,8},{8,9},{9,10},{10,1... | collective-permute-start | bytes 442376 | tf_op jit(solution)/shard_map/while/body/eval_jaxpr/ppermute | solution.py:14
  225.7 6.8 collective-permute-start
  234.5 7.8 collective-permute-start
  244.3 6.8 collective-permute-start
  253.1 13.2 %collective-permute-start = (bf16[2,192,192]{2,1,0:T(8,128)(2,1)}, bf16[2,192,192]{2,1,0:T(8,128)(2,1)S(1)}, u32[]{:S(2)}, u32[]{:S(2)}) collective-permute-start(bf16[2,192,192]{2,1,0:T(8,128)(2,1)} %get-tuple-element.1050), channel_id=1, source_target_pairs={{0,1},{1,2},{2,3},{3,4},{4,5},{5,6},{6,7},{7,8},{8,9},{9,10},{10,1... | collective-permute-start | bytes 442376 | tf_op jit(solution)/shard_map/while/body/eval_jaxpr/ppermute | solution.py:14
  268.2 6.8 collective-permute-start
  276.9 7.8 collective-permute-start
  286.7 6.8 collective-permute-start
  295.5 14.0 %collective-permute-start = (bf16[2,192,192]{2,1,0:T(8,128)(2,1)}, bf16[2,192,192]{2,1,0:T(8,128)(2,1)S(1)}, u32[]{:S(2)}, u32[]{:S(2)}) collective-permute-start(bf16[2,192,192]{2,1,0:T(8,128)(2,1)} %get-tuple-element.1050), channel_id=1, source_target_pairs={{0,1},{1,2},{2,3},{3,4},{4,5},{5,6},{6,7},{7,8},{8,9},{9,10},{10,1... | collective-permute-start | bytes 442376 | tf_op jit(solution)/shard_map/while/body/eval_jaxpr/ppermute | solution.py:14
  311.9 556.2 %while.41 = (s32[]{:T(128)}, bf16[2,192,192]{2,1,0:T(8,128)(2,1)S(1)}, f32[2,384,384]{2,1,0:T(8,128)S(1)}, s32[]{:T(128)}, s32[6,2]{0,1:T(2,128)S(1)}, /*index=5...) while((s32[]{:T(128)}, ...), condition=%wide.region_10.11_spmd, body=%wide.region_7.10_spmd.sunk | while | flops 114462736 | bytes 7668176 | solution.py:226
  313.3 6.5 collective-permute-done.1
  321.1 8.2 collective-permute-done.1
  330.7 6.5 collective-permute-done.1
  338.5 13.5 %collective-permute-done.1 = bf16[2,192,192]{2,1,0:T(8,128)(2,1)S(1)} collective-permute-done((bf16[2,192,192]{2,1,0:T(8,128)(2,1)S(1)}, bf16[2,192,192]{2,1,0:T(8,128)(2,1)S(1)}, u32[]{:S(2)}, u32[]{:S(2)}) %collective-permute-start.1) | collective-permute-done | bytes 147488 | tf_op jit(solution)/shard_map/while/body/eval_jaxpr/ppermute | solution.py:14
  353.4 6.6 collective-permute-done.1
  361.3 8.1 collective-permute-done.1
  370.8 6.6 collective-permute-done.1
  378.7 14.3 %collective-permute-done.1 = bf16[2,192,192]{2,1,0:T(8,128)(2,1)S(1)} collective-permute-done((bf16[2,192,192]{2,1,0:T(8,128)(2,1)S(1)}, bf16[2,192,192]{2,1,0:T(8,128)(2,1)S(1)}, u32[]{:S(2)}, u32[]{:S(2)}) %collective-permute-start.1) | collective-permute-done | bytes 147488 | tf_op jit(solution)/shard_map/while/body/eval_jaxpr/ppermute | solution.py:14
  394.3 6.6 collective-permute-done.1
  402.3 33.4 %collective-permute-done.1 = bf16[2,192,192]{2,1,0:T(8,128)(2,1)S(1)} collective-permute-done((bf16[2,192,192]{2,1,0:T(8,128)(2,1)S(1)}, bf16[2,192,192]{2,1,0:T(8,128)(2,1)S(1)}, u32[]{:S(2)}, u32[]{:S(2)}) %collective-permute-start.1) | collective-permute-done | bytes 147488 | tf_op jit(solution)/shard_map/while/body/eval_jaxpr/ppermute | solution.py:14
  437.0 23.6 %collective-permute-done.1 = bf16[2,192,192]{2,1,0:T(8,128)(2,1)S(1)} collective-permute-done((bf16[2,192,192]{2,1,0:T(8,128)(2,1)S(1)}, bf16[2,192,192]{2,1,0:T(8,128)(2,1)S(1)}, u32[]{:S(2)}, u32[]{:S(2)}) %collective-permute-start.1) | collective-permute-done | bytes 147488 | tf_op jit(solution)/shard_map/while/body/eval_jaxpr/ppermute | solution.py:14
  461.9 34.9 %collective-permute-done.1 = bf16[2,192,192]{2,1,0:T(8,128)(2,1)S(1)} collective-permute-done((bf16[2,192,192]{2,1,0:T(8,128)(2,1)S(1)}, bf16[2,192,192]{2,1,0:T(8,128)(2,1)S(1)}, u32[]{:S(2)}, u32[]{:S(2)}) %collective-permute-start.1) | collective-permute-done | bytes 147488 | tf_op jit(solution)/shard_map/while/body/eval_jaxpr/ppermute | solution.py:14
  498.1 23.6 %collective-permute-done.1 = bf16[2,192,192]{2,1,0:T(8,128)(2,1)S(1)} collective-permute-done((bf16[2,192,192]{2,1,0:T(8,128)(2,1)S(1)}, bf16[2,192,192]{2,1,0:T(8,128)(2,1)S(1)}, u32[]{:S(2)}, u32[]{:S(2)}) %collective-permute-start.1) | collective-permute-done | bytes 147488 | tf_op jit(solution)/shard_map/while/body/eval_jaxpr/ppermute | solution.py:14
  523.1 34.9 %collective-permute-done.1 = bf16[2,192,192]{2,1,0:T(8,128)(2,1)S(1)} collective-permute-done((bf16[2,192,192]{2,1,0:T(8,128)(2,1)S(1)}, bf16[2,192,192]{2,1,0:T(8,128)(2,1)S(1)}, u32[]{:S(2)}, u32[]{:S(2)}) %collective-permute-start.1) | collective-permute-done | bytes 147488 | tf_op jit(solution)/shard_map/while/body/eval_jaxpr/ppermute | solution.py:14
  559.3 190.1 %collective-permute-done.1 = bf16[2,192,192]{2,1,0:T(8,128)(2,1)S(1)} collective-permute-done((bf16[2,192,192]{2,1,0:T(8,128)(2,1)S(1)}, bf16[2,192,192]{2,1,0:T(8,128)(2,1)S(1)}, u32[]{:S(2)}, u32[]{:S(2)}) %collective-permute-start.1) | collective-permute-done | bytes 147488 | tf_op jit(solution)/shard_map/while/body/eval_jaxpr/ppermute | solution.py:14
  749.5 12.6 %conditional.6 = (bf16[2,192,192]{2,1,0:T(8,128)(2,1)S(1)}, f32[2,384,384]{2,1,0:T(8,128)S(1)}) conditional(s32[]{:T(128)} %convert_element_type.276, f32[2,384,384]{2,1,0:T(8,128)S(1)} %get-tuple-element.1135, (s32[]{:T(128)}, s32[6,2]{0,1:T(2,128)S(1)}, bf16[2,384,384]{2,1,0:T(8,128)(2,1)S(1)}, pred[]{:T(512)}, bf16[6,2,192,192]{3,2,1,0:T(8,128)(2,1)}, ...), branch_computations={%region_8.8_spmd, %region_9.9_spmd} | conditional | flops 114462728 | bytes 7078077 | solution.py:208
  768.7 12.2 %conditional.6 = (bf16[2,192,192]{2,1,0:T(8,128)(2,1)S(1)}, f32[2,384,384]{2,1,0:T(8,128)S(1)}) conditional(s32[]{:T(128)} %convert_element_type.276, f32[2,384,384]{2,1,0:T(8,128)S(1)} %get-tuple-element.1135, (s32[]{:T(128)}, s32[6,2]{0,1:T(2,128)S(1)}, bf16[2,384,384]{2,1,0:T(8,128)(2,1)S(1)}, pred[]{:T(512)}, bf16[6,2,192,192]{3,2,1,0:T(8,128)(2,1)}, ...), branch_computations={%region_8.8_spmd, %region_9.9_spmd} | conditional | flops 114462728 | bytes 7078077 | solution.py:208
  787.2 11.5 %conditional.6 = (bf16[2,192,192]{2,1,0:T(8,128)(2,1)S(1)}, f32[2,384,384]{2,1,0:T(8,128)S(1)}) conditional(s32[]{:T(128)} %convert_element_type.276, f32[2,384,384]{2,1,0:T(8,128)S(1)} %get-tuple-element.1135, (s32[]{:T(128)}, s32[6,2]{0,1:T(2,128)S(1)}, bf16[2,384,384]{2,1,0:T(8,128)(2,1)S(1)}, pred[]{:T(512)}, bf16[6,2,192,192]{3,2,1,0:T(8,128)(2,1)}, ...), branch_computations={%region_8.8_spmd, %region_9.9_spmd} | conditional | flops 114462728 | bytes 7078077 | solution.py:208
  800.0 7.0 collective-permute-done.1
  807.0 11.8 %conditional.6 = (bf16[2,192,192]{2,1,0:T(8,128)(2,1)S(1)}, f32[2,384,384]{2,1,0:T(8,128)S(1)}) conditional(s32[]{:T(128)} %convert_element_type.276, f32[2,384,384]{2,1,0:T(8,128)S(1)} %get-tuple-element.1135, (s32[]{:T(128)}, s32[6,2]{0,1:T(2,128)S(1)}, bf16[2,384,384]{2,1,0:T(8,128)(2,1)S(1)}, pred[]{:T(512)}, bf16[6,2,192,192]{3,2,1,0:T(8,128)(2,1)}, ...), branch_computations={%region_8.8_spmd, %region_9.9_spmd} | conditional | flops 114462728 | bytes 7078077 | solution.py:208
  820.1 11.3 %collective-permute-done.1 = bf16[2,192,192]{2,1,0:T(8,128)(2,1)S(1)} collective-permute-done((bf16[2,192,192]{2,1,0:T(8,128)(2,1)S(1)}, bf16[2,192,192]{2,1,0:T(8,128)(2,1)S(1)}, u32[]{:S(2)}, u32[]{:S(2)}) %collective-permute-start.1) | collective-permute-done | bytes 147488 | tf_op jit(solution)/shard_map/while/body/eval_jaxpr/ppermute | solution.py:14
  831.5 12.8 %conditional.6 = (bf16[2,192,192]{2,1,0:T(8,128)(2,1)S(1)}, f32[2,384,384]{2,1,0:T(8,128)S(1)}) conditional(s32[]{:T(128)} %convert_element_type.276, f32[2,384,384]{2,1,0:T(8,128)S(1)} %get-tuple-element.1135, (s32[]{:T(128)}, s32[6,2]{0,1:T(2,128)S(1)}, bf16[2,384,384]{2,1,0:T(8,128)(2,1)S(1)}, pred[]{:T(512)}, bf16[6,2,192,192]{3,2,1,0:T(8,128)(2,1)}, ...), branch_computations={%region_8.8_spmd, %region_9.9_spmd} | conditional | flops 114462728 | bytes 7078077 | solution.py:208
  845.6 6.4 collective-permute-done.1
  852.0 12.8 %conditional.6 = (bf16[2,192,192]{2,1,0:T(8,128)(2,1)S(1)}, f32[2,384,384]{2,1,0:T(8,128)S(1)}) conditional(s32[]{:T(128)} %convert_element_type.276, f32[2,384,384]{2,1,0:T(8,128)S(1)} %get-tuple-element.1135, (s32[]{:T(128)}, s32[6,2]{0,1:T(2,128)S(1)}, bf16[2,384,384]{2,1,0:T(8,128)(2,1)S(1)}, pred[]{:T(512)}, bf16[6,2,192,192]{3,2,1,0:T(8,128)(2,1)}, ...), branch_computations={%region_8.8_spmd, %region_9.9_spmd} | conditional | flops 114462728 | bytes 7078077 | solution.py:208
  (322 shorter events, 203.1 us)
Async XLA Ops:
  31.8 1.3 copy-start.1
  31.8 1.3 copy-start.3
  31.8 1.3 copy-start.4
  44.3 2.6 collective-permute-start
  58.0 3.5 collective-permute-start
  72.7 4.8 collective-permute-start
  88.7 7.2 collective-permute-start
  107.1 7.2 collective-permute-start
  125.4 7.2 collective-permute-start
  133.3 17.7 %collective-permute-start = (bf16[2,192,192]{2,1,0:T(8,128)(2,1)}, bf16[2,192,192]{2,1,0:T(8,128)(2,1)S(1)}, u32[]{:S(2)}, u32[]{:S(2)}) collective-permute-start(bf16[2,192,192]{2,1,0:T(8,128)(2,1)} %get-tuple-element.1050), channel_id=1, source_target_pairs={{0,1},{1,2},{2,3},{3,4},{4,5},{5,6},{6,7},{7,8},{8,9},{9,10},{10,1... | collective-permute-start | bytes 442376 | tf_op jit(solution)/shard_map/while/body/eval_jaxpr/ppermute | solution.py:14
  151.7 7.2 collective-permute-start
  159.6 17.7 %collective-permute-start = (bf16[2,192,192]{2,1,0:T(8,128)(2,1)}, bf16[2,192,192]{2,1,0:T(8,128)(2,1)S(1)}, u32[]{:S(2)}, u32[]{:S(2)}) collective-permute-start(bf16[2,192,192]{2,1,0:T(8,128)(2,1)} %get-tuple-element.1050), channel_id=1, source_target_pairs={{0,1},{1,2},{2,3},{3,4},{4,5},{5,6},{6,7},{7,8},{8,9},{9,10},{10,1... | collective-permute-start | bytes 442376 | tf_op jit(solution)/shard_map/while/body/eval_jaxpr/ppermute | solution.py:14
  177.9 7.2 collective-permute-start
  185.8 11.2 %collective-permute-start = (bf16[2,192,192]{2,1,0:T(8,128)(2,1)}, bf16[2,192,192]{2,1,0:T(8,128)(2,1)S(1)}, u32[]{:S(2)}, u32[]{:S(2)}) collective-permute-start(bf16[2,192,192]{2,1,0:T(8,128)(2,1)} %get-tuple-element.1050), channel_id=1, source_target_pairs={{0,1},{1,2},{2,3},{3,4},{4,5},{5,6},{6,7},{7,8},{8,9},{9,10},{10,1... | collective-permute-start | bytes 442376 | tf_op jit(solution)/shard_map/while/body/eval_jaxpr/ppermute | solution.py:14
  197.7 8.1 collective-permute-start
  206.5 18.6 %collective-permute-start = (bf16[2,192,192]{2,1,0:T(8,128)(2,1)}, bf16[2,192,192]{2,1,0:T(8,128)(2,1)S(1)}, u32[]{:S(2)}, u32[]{:S(2)}) collective-permute-start(bf16[2,192,192]{2,1,0:T(8,128)(2,1)} %get-tuple-element.1050), channel_id=1, source_target_pairs={{0,1},{1,2},{2,3},{3,4},{4,5},{5,6},{6,7},{7,8},{8,9},{9,10},{10,1... | collective-permute-start | bytes 442376 | tf_op jit(solution)/shard_map/while/body/eval_jaxpr/ppermute | solution.py:14
  225.7 8.1 collective-permute-start
  234.5 9.1 %collective-permute-start = (bf16[2,192,192]{2,1,0:T(8,128)(2,1)}, bf16[2,192,192]{2,1,0:T(8,128)(2,1)S(1)}, u32[]{:S(2)}, u32[]{:S(2)}) collective-permute-start(bf16[2,192,192]{2,1,0:T(8,128)(2,1)} %get-tuple-element.1050), channel_id=1, source_target_pairs={{0,1},{1,2},{2,3},{3,4},{4,5},{5,6},{6,7},{7,8},{8,9},{9,10},{10,1... | collective-permute-start | bytes 442376 | tf_op jit(solution)/shard_map/while/body/eval_jaxpr/ppermute | solution.py:14
  244.3 8.1 collective-permute-start
  253.1 14.4 %collective-permute-start = (bf16[2,192,192]{2,1,0:T(8,128)(2,1)}, bf16[2,192,192]{2,1,0:T(8,128)(2,1)S(1)}, u32[]{:S(2)}, u32[]{:S(2)}) collective-permute-start(bf16[2,192,192]{2,1,0:T(8,128)(2,1)} %get-tuple-element.1050), channel_id=1, source_target_pairs={{0,1},{1,2},{2,3},{3,4},{4,5},{5,6},{6,7},{7,8},{8,9},{9,10},{10,1... | collective-permute-start | bytes 442376 | tf_op jit(solution)/shard_map/while/body/eval_jaxpr/ppermute | solution.py:14
  268.2 8.1 collective-permute-start
  276.9 9.1 %collective-permute-start = (bf16[2,192,192]{2,1,0:T(8,128)(2,1)}, bf16[2,192,192]{2,1,0:T(8,128)(2,1)S(1)}, u32[]{:S(2)}, u32[]{:S(2)}) collective-permute-start(bf16[2,192,192]{2,1,0:T(8,128)(2,1)} %get-tuple-element.1050), channel_id=1, source_target_pairs={{0,1},{1,2},{2,3},{3,4},{4,5},{5,6},{6,7},{7,8},{8,9},{9,10},{10,1... | collective-permute-start | bytes 442376 | tf_op jit(solution)/shard_map/while/body/eval_jaxpr/ppermute | solution.py:14
  286.7 8.1 collective-permute-start
  295.5 15.3 %collective-permute-start = (bf16[2,192,192]{2,1,0:T(8,128)(2,1)}, bf16[2,192,192]{2,1,0:T(8,128)(2,1)S(1)}, u32[]{:S(2)}, u32[]{:S(2)}) collective-permute-start(bf16[2,192,192]{2,1,0:T(8,128)(2,1)} %get-tuple-element.1050), channel_id=1, source_target_pairs={{0,1},{1,2},{2,3},{3,4},{4,5},{5,6},{6,7},{7,8},{8,9},{9,10},{10,1... | collective-permute-start | bytes 442376 | tf_op jit(solution)/shard_map/while/body/eval_jaxpr/ppermute | solution.py:14
  310.8 1.0 copy-start.2
  312.0 7.8 collective-permute-start.1
  319.8 9.6 %collective-permute-start.1 = (bf16[2,192,192]{2,1,0:T(8,128)(2,1)S(1)}, bf16[2,192,192]{2,1,0:T(8,128)(2,1)S(1)}, u32[]{:S(2)}, u32[]{:S(2)}) collective-permute-start(bf16[2,192,192]{2,1,0:T(8,128)(2,1)S(1)} %get-tuple-element.1063), channel_id=1, source_target_pairs={{1,0},{2,1},{3,2},{4,3},{5,4},{6,5},{7,6},{8,7},{9,8},{10,9},{11,1... | collective-permute-start | bytes 442376 | tf_op jit(solution)/shard_map/while/body/eval_jaxpr/ppermute | solution.py:14
  329.4 7.8 collective-permute-start.1
  337.2 14.9 %collective-permute-start.1 = (bf16[2,192,192]{2,1,0:T(8,128)(2,1)S(1)}, bf16[2,192,192]{2,1,0:T(8,128)(2,1)S(1)}, u32[]{:S(2)}, u32[]{:S(2)}) collective-permute-start(bf16[2,192,192]{2,1,0:T(8,128)(2,1)S(1)} %get-tuple-element.1063), channel_id=1, source_target_pairs={{1,0},{2,1},{3,2},{4,3},{5,4},{6,5},{7,6},{8,7},{9,8},{10,9},{11,1... | collective-permute-start | bytes 442376 | tf_op jit(solution)/shard_map/while/body/eval_jaxpr/ppermute | solution.py:14
  352.1 7.9 collective-permute-start.1
  360.0 9.4 %collective-permute-start.1 = (bf16[2,192,192]{2,1,0:T(8,128)(2,1)S(1)}, bf16[2,192,192]{2,1,0:T(8,128)(2,1)S(1)}, u32[]{:S(2)}, u32[]{:S(2)}) collective-permute-start(bf16[2,192,192]{2,1,0:T(8,128)(2,1)S(1)} %get-tuple-element.1063), channel_id=1, source_target_pairs={{1,0},{2,1},{3,2},{4,3},{5,4},{6,5},{7,6},{8,7},{9,8},{10,9},{11,1... | collective-permute-start | bytes 442376 | tf_op jit(solution)/shard_map/while/body/eval_jaxpr/ppermute | solution.py:14
  369.5 7.9 collective-permute-start.1
  377.4 15.6 %collective-permute-start.1 = (bf16[2,192,192]{2,1,0:T(8,128)(2,1)S(1)}, bf16[2,192,192]{2,1,0:T(8,128)(2,1)S(1)}, u32[]{:S(2)}, u32[]{:S(2)}) collective-permute-start(bf16[2,192,192]{2,1,0:T(8,128)(2,1)S(1)} %get-tuple-element.1063), channel_id=1, source_target_pairs={{1,0},{2,1},{3,2},{4,3},{5,4},{6,5},{7,6},{8,7},{9,8},{10,9},{11,1... | collective-permute-start | bytes 442376 | tf_op jit(solution)/shard_map/while/body/eval_jaxpr/ppermute | solution.py:14
  393.0 7.9 collective-permute-start.1
  401.0 34.7 %collective-permute-start.1 = (bf16[2,192,192]{2,1,0:T(8,128)(2,1)S(1)}, bf16[2,192,192]{2,1,0:T(8,128)(2,1)S(1)}, u32[]{:S(2)}, u32[]{:S(2)}) collective-permute-start(bf16[2,192,192]{2,1,0:T(8,128)(2,1)S(1)} %get-tuple-element.1063), channel_id=1, source_target_pairs={{1,0},{2,1},{3,2},{4,3},{5,4},{6,5},{7,6},{8,7},{9,8},{10,9},{11,1... | collective-permute-start | bytes 442376 | tf_op jit(solution)/shard_map/while/body/eval_jaxpr/ppermute | solution.py:14
  435.7 24.9 %collective-permute-start.1 = (bf16[2,192,192]{2,1,0:T(8,128)(2,1)S(1)}, bf16[2,192,192]{2,1,0:T(8,128)(2,1)S(1)}, u32[]{:S(2)}, u32[]{:S(2)}) collective-permute-start(bf16[2,192,192]{2,1,0:T(8,128)(2,1)S(1)} %get-tuple-element.1063), channel_id=1, source_target_pairs={{1,0},{2,1},{3,2},{4,3},{5,4},{6,5},{7,6},{8,7},{9,8},{10,9},{11,1... | collective-permute-start | bytes 442376 | tf_op jit(solution)/shard_map/while/body/eval_jaxpr/ppermute | solution.py:14
  460.6 36.2 %collective-permute-start.1 = (bf16[2,192,192]{2,1,0:T(8,128)(2,1)S(1)}, bf16[2,192,192]{2,1,0:T(8,128)(2,1)S(1)}, u32[]{:S(2)}, u32[]{:S(2)}) collective-permute-start(bf16[2,192,192]{2,1,0:T(8,128)(2,1)S(1)} %get-tuple-element.1063), channel_id=1, source_target_pairs={{1,0},{2,1},{3,2},{4,3},{5,4},{6,5},{7,6},{8,7},{9,8},{10,9},{11,1... | collective-permute-start | bytes 442376 | tf_op jit(solution)/shard_map/while/body/eval_jaxpr/ppermute | solution.py:14
  496.8 24.9 %collective-permute-start.1 = (bf16[2,192,192]{2,1,0:T(8,128)(2,1)S(1)}, bf16[2,192,192]{2,1,0:T(8,128)(2,1)S(1)}, u32[]{:S(2)}, u32[]{:S(2)}) collective-permute-start(bf16[2,192,192]{2,1,0:T(8,128)(2,1)S(1)} %get-tuple-element.1063), channel_id=1, source_target_pairs={{1,0},{2,1},{3,2},{4,3},{5,4},{6,5},{7,6},{8,7},{9,8},{10,9},{11,1... | collective-permute-start | bytes 442376 | tf_op jit(solution)/shard_map/while/body/eval_jaxpr/ppermute | solution.py:14
  521.8 36.2 %collective-permute-start.1 = (bf16[2,192,192]{2,1,0:T(8,128)(2,1)S(1)}, bf16[2,192,192]{2,1,0:T(8,128)(2,1)S(1)}, u32[]{:S(2)}, u32[]{:S(2)}) collective-permute-start(bf16[2,192,192]{2,1,0:T(8,128)(2,1)S(1)} %get-tuple-element.1063), channel_id=1, source_target_pairs={{1,0},{2,1},{3,2},{4,3},{5,4},{6,5},{7,6},{8,7},{9,8},{10,9},{11,1... | collective-permute-start | bytes 442376 | tf_op jit(solution)/shard_map/while/body/eval_jaxpr/ppermute | solution.py:14
  558.0 191.4 %collective-permute-start.1 = (bf16[2,192,192]{2,1,0:T(8,128)(2,1)S(1)}, bf16[2,192,192]{2,1,0:T(8,128)(2,1)S(1)}, u32[]{:S(2)}, u32[]{:S(2)}) collective-permute-start(bf16[2,192,192]{2,1,0:T(8,128)(2,1)S(1)} %get-tuple-element.1063), channel_id=1, source_target_pairs={{1,0},{2,1},{3,2},{4,3},{5,4},{6,5},{7,6},{8,7},{9,8},{10,9},{11,1... | collective-permute-start | bytes 442376 | tf_op jit(solution)/shard_map/while/body/eval_jaxpr/ppermute | solution.py:14
  762.1 6.6 collective-permute-start.1
  780.9 6.3 collective-permute-start.1
  798.7 8.3 collective-permute-start.1
  818.8 12.6 %collective-permute-start.1 = (bf16[2,192,192]{2,1,0:T(8,128)(2,1)S(1)}, bf16[2,192,192]{2,1,0:T(8,128)(2,1)S(1)}, u32[]{:S(2)}, u32[]{:S(2)}) collective-permute-start(bf16[2,192,192]{2,1,0:T(8,128)(2,1)S(1)} %get-tuple-element.1063), channel_id=1, source_target_pairs={{1,0},{2,1},{3,2},{4,3},{5,4},{6,5},{7,6},{8,7},{9,8},{10,9},{11,1... | collective-permute-start | bytes 442376 | tf_op jit(solution)/shard_map/while/body/eval_jaxpr/ppermute | solution.py:14
  844.3 7.7 collective-permute-start.1
  864.8 3.3 collective-permute-start.1
  868.2 1.0 copy-start
where the time goes:
time: 872 us; the launch traced here: 869 us
  waiting for transfers between devices  481 us (55%)
  starting transfers between devices  201 us (23%)
  loops' own time  57.4 us (7%)
  local copies, waits for them, and re-layouts  50.8 us (6%)
  blocking collectives  27.5 us (3%)
  matrix products  26.1 us (3%)
  other arithmetic  24.8 us (3%)
    ppermute x42, waiting for transfers between devices, passed_along(): return lax.ppermute(block, axis, route)  481 us
    ppermute x42, starting transfers between devices, passed_along(): return lax.ppermute(block, axis, route)  201 us
    another operation x21, loops' own time, one_tick(): lax.cond(active, advance, resting, (stored_waves, exit_grads))  33.6 us
    all_gather x1, blocking collectives, shards(): observed = lax.all_gather(measured, 'cuts', axis=1, tiled=True)  27.5 us
    another operation x21, loops' own time, one_tick(): passed, accumulated = lax.cond(active, retreat, holding, accumulated)  23 us
    dynamic_update_slice x6, local copies, waits for them, and re-layouts, retreat(): lax.dynamic_update_slice(summed, current + window_grad, anchor)  23 us
  transfers between devices with their start and end apart: 42, of which 42 were waited for; matrix products, arithmetic and copies ran while one was open for 0% of the time, Pallas kernels for 0%

commit v1 on v0

v1 whole, which is shorter than its diff:
```python
import math

import jax
import jax.numpy as jnp
import ml_dtypes
import numpy as np
from jax import lax
from jax.experimental import pallas as pl
from jax.experimental.pallas import tpu as pltpu
from jax.sharding import PartitionSpec as P

TRANSMIT = 0.985
GROUP = 16
LANES = 128
ROWS = 16
F32 = jnp.float32
BF16 = jnp.bfloat16


def dot(former, latter):
    return jnp.dot(former, latter, preferred_element_type=F32)


def halves(x):
    return x[:, :LANES], x[:, LANES : 2 * LANES], x[:, 2 * LANES :]


def swapped(tail):
    return pltpu.roll(tail, LANES // 2, 1)


def low_half(rows):
    return lax.broadcasted_iota(jnp.int32, (rows, LANES), 1) < LANES // 2


def spread(tail):
    other = swapped(tail)
    low = low_half(tail.shape[0])
    return jnp.where(low, tail, other), jnp.where(low, other, tail)


def signed(tail, minus_low):
    low = low_half(tail.shape[0])
    return jnp.where(low == minus_low, -tail, tail)


def times(a, b):
    a0, a1, at = halves(a)
    b0, b1, bt = halves(b)
    b_real, b_imag = spread(bt)
    tail = at * b_real + signed(swapped(at), True) * b_imag
    return jnp.concatenate([a0 * b0 - a1 * b1, a1 * b0 + a0 * b1, tail], axis=1)


def times_conj(a, *others):
    a0, a1, at = halves(a)
    turned = signed(swapped(at), False)
    results = []
    for b in others:
        b0, b1, bt = halves(b)
        b_real, b_imag = spread(bt)
        tail = at * b_real + turned * b_imag
        results.append(jnp.concatenate([a0 * b0 + a1 * b1, a1 * b0 - a0 * b1, tail], axis=1))
    return results


def joined(both, conj):
    width = both.shape[0] // 2
    u0, u1, ut = halves(both[:width])
    v0, v1, vt = halves(both[width:])
    turned = signed(swapped(vt), not conj)
    if conj:
        return jnp.concatenate([u0 + v1, u1 - v0, ut + turned], axis=1)
    return jnp.concatenate([u0 - v1, u1 + v0, ut + turned], axis=1)


def with_mean(window):
    x = window.astype(F32)
    x0, x1, xt = halves(x)
    mean = jnp.where(low_half(xt.shape[0]), TRANSMIT, 0.0)
    return jnp.concatenate([TRANSMIT + x0, x1, mean + xt], axis=1)


def split2(x):
    high = x.astype(BF16)
    return high, (x - high.astype(F32)).astype(BF16)


def picker(columns, start, high_tail, transposed=False):
    shape = (2 * LANES, columns) if transposed else (columns, 2 * LANES)
    a = lax.broadcasted_iota(jnp.int32, shape, 1 if transposed else 0) - start
    q = lax.broadcasted_iota(jnp.int32, shape, 0 if transposed else 1)
    if high_tail:
        half = LANES // 2
        wanted = jnp.where(q < LANES, q, jnp.where(q < LANES + half, -columns, q - half))
    else:
        wanted = jnp.where(q < LANES + LANES // 2, q, -columns)
    return jnp.where(a == wanted, 1.0, 0.0).astype(BF16)


def row_picker(shape, distance):
    taken = lax.broadcasted_iota(jnp.int32, shape, 1)
    wanted = lax.broadcasted_iota(jnp.int32, shape, 0) + distance
    return jnp.where(taken == wanted, 1.0, 0.0).astype(BF16)


def packed(real, imag, columns, start):
    left = dot(real, picker(columns, start, False))
    right = dot(imag, picker(columns, start, True))
    return jnp.concatenate(
        [left[:, :LANES], right[:, :LANES], left[:, LANES:] + right[:, LANES:]], axis=1
    )


def dft_constants(width):
    counter = np.arange(width)
    angle = (counter[:, None] * counter[None, :] % width) * (2.0 * math.pi / width)
    real = np.cos(angle) / math.sqrt(width)
    imag = -np.sin(angle) / math.sqrt(width)
    order = np.concatenate(
        [
            np.arange(LANES),
            width + np.arange(LANES),
            np.arange(LANES, width),
            width + np.arange(LANES, width),
        ]
    )

    def right(mr, mi):
        full = np.block([[mr, mi], [-mi, mr]])
        return full[order][:, order]

    tables = []
    for table in (np.concatenate([real, imag]), right(real, imag), right(real, -imag)):
        high = table.astype(np.float32).astype(ml_dtypes.bfloat16)
        low = (table - high.astype(np.float64)).astype(np.float32).astype(ml_dtypes.bfloat16)
        tables += [high, low]
    return tables


def window_kernel(
    offsets_ref, index_ref, objects_ref, measured_ref, props_ref, blocks_ref, lb_ref, rf_ref, rb_ref
):
    positions, near_rows, width = measured_ref.shape
    extent = objects_ref.shape[-1]
    tag = jnp.full((ROWS, LANES), index_ref[0], jnp.int32).astype(F32).astype(BF16)
    lane = lax.broadcasted_iota(jnp.int32, (width, 2 * LANES), 0)
    spot = lax.broadcasted_iota(jnp.int32, (width, 2 * LANES), 1)
    doubled = jnp.where(lane == jnp.where(spot < LANES + LANES // 2, spot, spot - LANES // 2), 1.0, 0.0).astype(BF16)
    blank = jnp.zeros((ROWS - near_rows, width), F32)
    starts = [offsets_ref[p, 0] for p in range(positions)]
    rows = jnp.concatenate([row_picker((width, extent), start) for start in starts], axis=0)
    real, imag = (dot(rows, objects_ref[0, c]).astype(BF16) for c in range(2))
    for p in range(positions):
        here = slice(p * width, (p + 1) * width)
        window = packed(real[here], imag[here], extent, offsets_ref[p, 1])
        blocks_ref[p, :width, :] = window.astype(BF16)
        high, low = split2(jnp.concatenate([measured_ref[p], blank], axis=0))
        for place, part in ((width, high), (width + ROWS, low)):
            blocks_ref[p, place : place + ROWS, : 2 * LANES] = dot(part, doubled).astype(BF16)
            blocks_ref[p, place : place + ROWS, 2 * LANES :] = tag
    for k in range(props_ref.shape[0]):
        real, imag = props_ref[k, 0], props_ref[k, 1]
        lb_ref[k, :width, :] = real.astype(F32).T.astype(BF16)
        lb_ref[k, width:, :] = imag.astype(F32).T.astype(BF16)
        upper = packed(real, -imag, width, 0)
        lower = packed(imag, real, width, 0)
        table = jnp.concatenate(
            [upper[:LANES], lower[:LANES], upper[LANES:], lower[LANES:]], axis=0
        )
        rb_ref[k] = table.astype(BF16)
        rf_ref[k] = table.T.astype(BF16)


def forward_steps(blocks, waves, indices, lf, rf, first, last_out):
    width = blocks.shape[2] // 2
    sections = blocks.shape[0]

    def step(k, carried):
        which = indices[k]
        z = times(waves[k].astype(F32), with_mean(blocks[k, :width, :])).astype(BF16)
        left = lf[which].reshape(2 * width, width)
        h = joined(dot(left, z), False).astype(BF16)
        waves[k + 1] = dot(h, rf[which]).astype(BF16)
        return carried

    lax.fori_loop(0, sections, step, 0)


def backward_steps(blocks, waves, indices, lb, rb, grads, g):
    width = blocks.shape[2] // 2
    sections = blocks.shape[0]

    def step(n, carried):
        k = sections - 1 - n
        which = indices[k]
        c = joined(dot(lb[which], g[...]), True).astype(BF16)
        y = dot(c, rb[which])
        grad, passed = times_conj(y, waves[k].astype(F32), with_mean(blocks[k, :width, :]))
        grads[k] = grad.astype(BF16)
        g[...] = passed.astype(BF16)
        return carried

    lax.fori_loop(0, sections, step, 0)


def detector(psi, observed, lh, ll, rh, rl, ch, cl):
    def product(ah, al, bh, bl):
        return dot(ah, bh) + (dot(ah, bl) + dot(al, bh))

    near = joined(dot(lh, psi) + dot(ll, psi), False)
    nh, nl = split2(near)
    far = product(nh, nl, rh, rl)
    f0, f1, ft = halves(far)
    other = swapped(ft)
    main = f0 * f0 + f1 * f1 - observed[:, :LANES]
    tail = ft * ft + other * other - observed[:, LANES:]
    push = jnp.concatenate([main * f0, main * f1, tail * ft], axis=1)
    ph, pl_ = split2(push)
    back = joined(product(lh, ll, ph, pl_), True)
    bh, bl = split2(back)
    return product(bh, bl, ch, cl).astype(BF16)


def read_indices(blocks, indices, count):
    width = blocks.shape[2] // 2
    for k in range(blocks.shape[0]):
        tag = jnp.max(blocks[k, width : width + ROWS, 2 * LANES :].astype(F32))
        indices[k] = jnp.clip(tag.astype(jnp.int32), 0, count - 1)


def chain_kernel(near_rows):
    def kernel(
        who, group_ref, probes, blocks, lf, rf, lb, rb, lh, ll, rh, rl, ch, cl,
        grads, waves, g, observed, indices,
    ):
        width = blocks.shape[2] // 2
        sections = blocks.shape[0]
        probe = group_ref[who[0]]
        real, imag = probes[probe, 0], probes[probe, 1]
        waves[0] = packed(real, imag, width, 0).astype(BF16)
        read_indices(blocks, indices, lf.shape[0])
        for k in range(sections):
            high = blocks[k, width : width + ROWS, : 2 * LANES].astype(F32)
            low = blocks[k, width + ROWS : width + 2 * ROWS, : 2 * LANES].astype(F32)
            observed[k * near_rows : (k + 1) * near_rows, :] = (high + low)[:near_rows]
        forward_steps(blocks, waves, indices, lf, rf, None, None)
        g[...] = detector(
            waves[sections], observed[...], lh[...], ll[...], rh[...], rl[...], ch[...], cl[...]
        )
        backward_steps(blocks, waves, indices, lb, rb, grads, g)

    return kernel


def gather_kernel(offsets_ref, grads_ref, out_ref):
    positions = offsets_ref.shape[0]
    width = grads_ref.shape[1]
    extent = out_ref.shape[-1]
    spread_out = [[], []]
    for p in range(positions):
        x0, x1, xt = halves(grads_ref[p])
        for c, main in ((0, x0), (1, x1)):
            wide = jnp.concatenate([main, xt], axis=1)
            columns = picker(extent, offsets_ref[p, 1], c == 1, transposed=True)
            spread_out[c].append(dot(wide, columns).astype(BF16))
    rows = jnp.concatenate(
        [row_picker((extent, width), -offsets_ref[p, 0]) for p in range(positions)], axis=1
    )
    for c in range(2):
        out_ref[0, c] = dot(rows, jnp.concatenate(spread_out[c], axis=0))


VMEM = pl.BlockSpec(memory_space=pltpu.VMEM)
SMEM = pl.BlockSpec(memory_space=pltpu.SMEM)
PARAMS = pltpu.CompilerParams(vmem_limit_bytes=48 * 1024 * 1024)


def shards(objects, propagators, prop_index, probes, probe_group, offsets, measured):
    sections = lax.axis_size("cuts")
    rank = lax.axis_index("cuts")
    positions = probe_group.shape[0]
    width = probes.shape[-1]
    kinds = propagators.shape[0]
    near_rows = measured.shape[1]
    size = sections
    rows = width + 2 * ROWS

    blocks, lb, rf, rb = pl.pallas_call(
        window_kernel,
        out_shape=[
            jax.ShapeDtypeStruct((size, rows, 2 * width), BF16),
            jax.ShapeDtypeStruct((kinds, 2 * width, width), BF16),
            jax.ShapeDtypeStruct((kinds, 2 * width, 2 * width), BF16),
            jax.ShapeDtypeStruct((kinds, 2 * width, 2 * width), BF16),
        ],
        in_specs=[SMEM, SMEM, VMEM, VMEM, VMEM],
        out_specs=[VMEM] * 4,
        compiler_params=PARAMS,
        name="windows",
    )(offsets, prop_index, objects, measured, propagators)

    blocks = lax.all_to_all(blocks, "cuts", 0, 0, tiled=True)

    slot = jnp.minimum(rank, positions - 1).astype(jnp.int32)[None]
    constants = [jnp.asarray(table) for table in dft_constants(width)]
    grads = pl.pallas_call(
        chain_kernel(near_rows),
        out_shape=jax.ShapeDtypeStruct((size, width, 2 * width), BF16),
        in_specs=[SMEM, SMEM] + [VMEM] * 12,
        out_specs=VMEM,
        scratch_shapes=[
            pltpu.VMEM((size + 1, width, 2 * width), BF16),
            pltpu.VMEM((width, 2 * width), BF16),
            pltpu.VMEM((width, 2 * LANES), F32),
            pltpu.SMEM((size,), jnp.int32),
        ],
        compiler_params=PARAMS,
        name="chain",
    )(slot, probe_group, probes, blocks, propagators, rf, lb, rb, *constants)

    grads = lax.all_to_all(grads, "cuts", 0, 0, tiled=True)

    return pl.pallas_call(
        gather_kernel,
        out_shape=jax.ShapeDtypeStruct(objects.shape, F32),
        in_specs=[SMEM, VMEM],
        out_specs=VMEM,
        compiler_params=PARAMS,
        name="sum_windows",
    )(offsets, grads)


def solution(mesh):
    in_specs = (
        P(("parts", "cuts"), None, None, None),
        P(),
        P(("parts", "cuts")),
        P(),
        P(),
        P("parts", None),
        P("parts", "cuts", None),
    )
    out_specs = P(("parts", "cuts"), None, None, None)
    return jax.shard_map(shards, mesh=mesh, in_specs=in_specs, out_specs=out_specs, check_vma=False)
```

time: 872 us -> 172 us (0.20)
  waiting for transfers between devices: 481 us -> 52.6 us
  starting transfers between devices: 201 us -> 7.55 us
  loops' own time: 57.4 us -> 0 us
  blocking collectives: 27.5 us -> 67.8 us
  local copies, waits for them, and re-layouts: 50.8 us -> 10.6 us
  Pallas kernels: 0 us -> 31.9 us
  matrix products: 26.1 us -> 0 us
  other arithmetic: 24.8 us -> 0 us
    ppermute x42 -> x0, waiting for transfers between devices: 481 us -> none  [passed_along(): return lax.ppermute(block, axis, route)]
    ppermute x42 -> x0, starting transfers between devices: 201 us -> none  [passed_along(): return lax.ppermute(block, axis, route)]
    all_to_all x0 -> x1, blocking collectives: none -> 67.8 us  [shards(): grads = lax.all_to_all(grads, 'cuts', 0, 0, tiled=True)]
    another operation x50 -> x0, loops' own time: 57.4 us -> none  [the longest x21 33.6 us: one_tick(): lax.cond(active, advance, resting, (stored_waves, exit_grads))]
    all_to_all x0 -> x1, waiting for transfers between devices: none -> 52.6 us  [shards(): blocks = lax.all_to_all(blocks, 'cuts', 0, 0, tiled=True)]
    pallas_call x0 -> x3, Pallas kernels: none -> 31.9 us  [the longest x1 23.6 us: shards(): pl.pallas_call(chain_kernel(near_rows), out_shape=jax.ShapeDtypeStruct((s...]
    all_gather x1 -> x0, blocking collectives: 27.5 us -> none  [shards(): observed = lax.all_gather(measured, 'cuts', axis=1, tiled=True)]
    dot_general x96 -> x0, matrix products: 26.1 us -> none  [the longest x48 16 us: plain_product(): jnp.dot(former.astype(jnp.float32), latter.astype(jnp.float32), precision...]
  transfers between devices with their start and end apart: 42 -> 1, of which waited for: 42 -> 1; matrix products, arithmetic and copies ran while one was open for 0% -> 0% of each run, Pallas kernels for 0% -> 0%
where the time goes in v1:
time: 172 us; the launch traced here: 171 us
  blocking collectives  67.8 us (39%)
  waiting for transfers between devices  52.6 us (31%)
  Pallas kernels  31.9 us (19%)
  local copies, waits for them, and re-layouts  10.6 us (6%)
  starting transfers between devices  7.55 us (4%)
    all_to_all x1, blocking collectives, shards(): grads = lax.all_to_all(grads, 'cuts', 0, 0, tiled=True)  67.8 us
    all_to_all x1, waiting for transfers between devices, shards(): blocks = lax.all_to_all(blocks, 'cuts', 0, 0, tiled=True)  52.6 us
    pallas_call x1, Pallas kernels, shards(): pl.pallas_call(chain_kernel(near_rows), out_shape=jax.ShapeDtypeStruct((s...  23.6 us
    unnamed x27, local copies, waits for them, and re-layouts  10.6 us
    all_to_all x1, starting transfers between devices, shards(): blocks = lax.all_to_all(blocks, 'cuts', 0, 0, tiled=True)  7.55 us
    pallas_call x1, Pallas kernels, shards(): pl.pallas_call(window_kernel, out_shape=[jax.ShapeDtypeStruct((size, rows...  4.89 us
  transfers between devices with their start and end apart: 1, of which 1 were waited for; matrix products, arithmetic and copies ran while one was open for 0% of the time, Pallas kernels for 0%

profile of v1, /device:TPU:0, one launch (start us, length us, event | category | flops | bytes accessed | tf_op | source)
XLA Modules:
  0.0 171.1 jit_solution(4110466683884225862)
XLA Ops:
  0.0 0.8 copy.15.offsets_ref
  1.4 0.0 copy-start
  1.4 1.1 copy-done
  2.6 0.0 copy-start.4
  2.6 1.1 copy-done.4
  3.6 0.0 copy-start.11
  3.6 0.9 copy-done.11
  4.5 4.9 %windows.1 = (bf16[16,224,384]{2,1,0:T(8,128)(2,1)}, bf16[4,384,192]{2,1,0:T(8,128)(2,1)S(1)}, bf16[4,384,384]{2,1,0:T(8,128)(2,1)S(1)}, bf16[4,384,384]{2,1,0:T(8,128)(2,1)S(1)}) custom-call(s32[6,2]{1,0:T(8,128)S(1)} %copy.15.offsets_ref, s32[1]{0:T(128)S(6)} %copy.16.index_ref, bf16[1,2,384,384]{3,2,1,0:T(8,128)(2,1)S(1)} %copy-done.4, ...), custom_call_target="tpu_custom_call" | custom-call | tf_op jit(solution)/shard_map/windows/pallas_call | solution.py:289
  9.4 0.0 copy-start.2
  9.4 0.9 copy-done.2
  10.3 0.0 copy-start.1
  10.3 0.0 copy-start.5
  10.3 0.0 copy-start.12
  10.3 7.5 %all-to-all-start = ((bf16[16,224,384]{2,1,0:T(8,128)(2,1)}), bf16[16,224,384]{2,1,0:T(8,128)(2,1)}, u32[]{:S(2)}, u32[]{:S(2)}) async-start(bf16[16,224,384]{2,1,0:T(8,128)(2,1)} %get-tuple-element.9), calls=%async_computation | async-start | bytes 5505024 | tf_op jit(solution)/shard_map/all_to_all | solution.py:303
  17.9 52.6 %all-to-all-done.blocks = bf16[16,224,384]{2,1,0:T(8,128)(2,1)} async-done(((bf16[16,224,384]{2,1,0:T(8,128)(2,1)}), bf16[16,224,384]{2,1,0:T(8,128)(2,1)}, u32[]{:S(2)}, u32[]{:S(2)}) %all-to-all-start) | async-done | bytes 2752544 | tf_op jit(solution)/shard_map/all_to_all | solution.py:303
  70.4 0.0 copy-done.1
  70.4 0.0 copy-done.5
  70.4 0.0 copy-done.12
  70.4 0.0 copy-start.3
  70.4 1.1 copy-done.3
  71.6 0.0 copy-start.6
  71.6 1.0 copy-done.6
  72.5 0.0 copy-start.7
  72.5 1.0 copy-done.7
  73.5 0.0 copy-start.8
  73.5 1.0 copy-done.8
  74.5 0.0 copy-start.9
  74.5 0.9 copy-done.9
  75.4 0.0 copy-start.10
  75.4 0.9 copy-done.10
  76.3 23.6 %chain.1 = bf16[16,192,384]{2,1,0:T(8,128)(2,1)} custom-call(s32[1]{0:T(128)} %bitcast.who, s32[6]{0:T(128)S(1)} %copy-done.12, bf16[8,2,192,192]{3,2,1,0:T(8,128)(2,1)} %probes.1, bf16[16,224,384]{2,1,0:T(8,128)(2,1)} %all-to-all-done.blocks, bf16[4,2,192,192]{3,2,1,0:T(8,128)(2,1)S(1)} %copy-done.1, bf16[4,384,384]{2,1,0:T(8,128)(2,1)S(1)} %get-tuple-element.10.rf, ...), custom_call_target="tpu_custom_call" | custom-call | tf_op jit(solution)/shard_map/chain/pallas_call | solution.py:307
  99.9 67.8 %all_to_all.10.grads_ref = bf16[16,192,384]{2,1,0:T(8,128)(2,1)S(1)} all-to-all(bf16[16,192,384]{2,1,0:T(8,128)(2,1)} %chain.1), channel_id=1, replica_groups=mesh['parts'=2,'cuts'=16] {'cuts'}, dimensions={0} | all-to-all | bytes 4718592 | tf_op jit(solution)/shard_map/all_to_all | solution.py:322
  167.7 3.4 %sum_windows.1 = f32[1,2,384,384]{3,2,1,0:T(8,128)} custom-call(s32[6,2]{1,0:T(8,128)S(1)} %copy.15.offsets_ref, bf16[16,192,384]{2,1,0:T(8,128)(2,1)S(1)} %all_to_all.10.grads_ref), custom_call_target="tpu_custom_call" | custom-call | tf_op jit(solution)/shard_map/sum_windows/pallas_call | solution.py:324
Async XLA Ops:
  1.4 1.1 copy-start
  2.6 1.1 copy-start.4
  3.6 0.9 copy-start.11
  9.4 0.9 copy-start.2
  10.3 60.1 %copy-start.1 = (bf16[4,2,192,192]{3,2,1,0:T(8,128)(2,1)S(1)}, bf16[4,2,192,192]{3,2,1,0:T(8,128)(2,1)}, u32[]{:S(2)}) copy-start(bf16[4,2,192,192]{3,2,1,0:T(8,128)(2,1)} %lf.1) | copy-start | bytes 1769476
  10.3 60.1 %copy-start.5 = (bf16[384,384]{1,0:T(8,128)(2,1)S(1)}, bf16[384,384]{1,0:T(8,128)(2,1)}, u32[]{:S(2)}) copy-start(bf16[384,384]{1,0:T(8,128)(2,1)} %constant.20.clone.rh) | copy-start | bytes 884740
  10.3 60.1 %copy-start.12 = (s32[6]{0:T(128)S(1)}, s32[6]{0:T(128)}, u32[]{:S(2)}) copy-start(s32[6]{0:T(128)} %group_ref.1) | copy-start | bytes 76
  10.3 60.1 %all-to-all-start = ((bf16[16,224,384]{2,1,0:T(8,128)(2,1)}), bf16[16,224,384]{2,1,0:T(8,128)(2,1)}, u32[]{:S(2)}, u32[]{:S(2)}) async-start(bf16[16,224,384]{2,1,0:T(8,128)(2,1)} %get-tuple-element.9), calls=%async_computation | async-start | bytes 5505024 | tf_op jit(solution)/shard_map/all_to_all | solution.py:303
  70.4 1.1 copy-start.3
  71.6 1.0 copy-start.6
  72.5 1.0 copy-start.7
  73.5 1.0 copy-start.8
  74.5 0.9 copy-start.9
  75.4 0.9 copy-start.10

commit v2 on v1

--- a/solution.py
+++ b/solution.py
@@ -10,7 +10,7 @@
 from jax.sharding import PartitionSpec as P
 
 TRANSMIT = 0.985
-GROUP = 16
+GROUP = 8
 LANES = 128
 ROWS = 16
 F32 = jnp.float32
@@ -138,27 +138,28 @@
     return tables
 
 
-def window_kernel(
-    offsets_ref, index_ref, objects_ref, measured_ref, props_ref, blocks_ref, lb_ref, rf_ref, rb_ref
-):
-    positions, near_rows, width = measured_ref.shape
+def window_kernel(offsets_ref, index_ref, targets_ref, objects_ref, *blocks):
     extent = objects_ref.shape[-1]
-    tag = jnp.full((ROWS, LANES), index_ref[0], jnp.int32).astype(F32).astype(BF16)
-    lane = lax.broadcasted_iota(jnp.int32, (width, 2 * LANES), 0)
-    spot = lax.broadcasted_iota(jnp.int32, (width, 2 * LANES), 1)
-    doubled = jnp.where(lane == jnp.where(spot < LANES + LANES // 2, spot, spot - LANES // 2), 1.0, 0.0).astype(BF16)
-    blank = jnp.zeros((ROWS - near_rows, width), F32)
-    starts = [offsets_ref[p, 0] for p in range(positions)]
-    rows = jnp.concatenate([row_picker((width, extent), start) for start in starts], axis=0)
-    real, imag = (dot(rows, objects_ref[0, c]).astype(BF16) for c in range(2))
-    for p in range(positions):
-        here = slice(p * width, (p + 1) * width)
-        window = packed(real[here], imag[here], extent, offsets_ref[p, 1])
-        blocks_ref[p, :width, :] = window.astype(BF16)
-        high, low = split2(jnp.concatenate([measured_ref[p], blank], axis=0))
-        for place, part in ((width, high), (width + ROWS, low)):
-            blocks_ref[p, place : place + ROWS, : 2 * LANES] = dot(part, doubled).astype(BF16)
-            blocks_ref[p, place : place + ROWS, 2 * LANES :] = tag
+    width = blocks[0].shape[1] // 2
+    tag = jnp.full((ROWS, 2 * width), index_ref[0], jnp.int32).astype(F32).astype(BF16)
+    for r, block in enumerate(blocks):
+        p = targets_ref[r]
+
+        @pl.when(p >= 0)
+        def _(block=block, p=p):
+            rows = row_picker((width, extent), offsets_ref[p, 0])
+            real, imag = (dot(rows, objects_ref[0, c]).astype(BF16) for c in range(2))
+            block[:width, :] = packed(real, imag, extent, offsets_ref[p, 1]).astype(BF16)
+            block[width:, :] = tag
+
+
+def doubled(rows):
+    tail = jnp.concatenate([rows[:, LANES:]] * 2, axis=1)
+    return jnp.concatenate([rows[:, :LANES], tail], axis=1)
+
+
+def table_kernel(props_ref, lb_ref, rf_ref, rb_ref):
+    width = props_ref.shape[-1]
     for k in range(props_ref.shape[0]):
         real, imag = props_ref[k, 0], props_ref[k, 1]
         lb_ref[k, :width, :] = real.astype(F32).T.astype(BF16)
@@ -172,15 +173,15 @@
         rf_ref[k] = table.T.astype(BF16)
 
 
-def forward_steps(blocks, waves, indices, lf, rf, first, last_out):
-    width = blocks.shape[2] // 2
-    sections = blocks.shape[0]
+def forward_steps(blocks, waves, indices, lf, rf, arrived):
+    sections, _, columns = blocks.shape
+    width = columns // 2
 
     def step(k, carried):
+        arrived(k)
         which = indices[k]
         z = times(waves[k].astype(F32), with_mean(blocks[k, :width, :])).astype(BF16)
-        left = lf[which].reshape(2 * width, width)
-        h = joined(dot(left, z), False).astype(BF16)
+        h = joined(dot(lf[which].reshape(columns, width), z), False).astype(BF16)
         waves[k + 1] = dot(h, rf[which]).astype(BF16)
         return carried
 
@@ -188,8 +189,8 @@
 
 
 def backward_steps(blocks, waves, indices, lb, rb, grads, g):
-    width = blocks.shape[2] // 2
-    sections = blocks.shape[0]
+    sections, _, columns = blocks.shape
+    width = columns // 2
 
     def step(n, carried):
         k = sections - 1 - n
@@ -222,113 +223,342 @@
     return product(bh, bl, ch, cl).astype(BF16)
 
 
-def read_indices(blocks, indices, count):
+def read_index(blocks, indices, k, count):
     width = blocks.shape[2] // 2
-    for k in range(blocks.shape[0]):
-        tag = jnp.max(blocks[k, width : width + ROWS, 2 * LANES :].astype(F32))
-        indices[k] = jnp.clip(tag.astype(jnp.int32), 0, count - 1)
-
-
-def chain_kernel(near_rows):
-    def kernel(
-        who, group_ref, probes, blocks, lf, rf, lb, rb, lh, ll, rh, rl, ch, cl,
-        grads, waves, g, observed, indices,
-    ):
-        width = blocks.shape[2] // 2
-        sections = blocks.shape[0]
-        probe = group_ref[who[0]]
-        real, imag = probes[probe, 0], probes[probe, 1]
-        waves[0] = packed(real, imag, width, 0).astype(BF16)
-        read_indices(blocks, indices, lf.shape[0])
-        for k in range(sections):
-            high = blocks[k, width : width + ROWS, : 2 * LANES].astype(F32)
-            low = blocks[k, width + ROWS : width + 2 * ROWS, : 2 * LANES].astype(F32)
-            observed[k * near_rows : (k + 1) * near_rows, :] = (high + low)[:near_rows]
-        forward_steps(blocks, waves, indices, lf, rf, None, None)
-        g[...] = detector(
-            waves[sections], observed[...], lh[...], ll[...], rh[...], rl[...], ch[...], cl[...]
-        )
-        backward_steps(blocks, waves, indices, lb, rb, grads, g)
+    tag = jnp.max(blocks[k, width:, :LANES].astype(F32))
+    indices[k] = jnp.clip(tag.astype(jnp.int32), 0, count - 1)
+
+
+def block_copies(blocks_in, order, blocks, sems):
+    return [
+        pltpu.make_async_copy(block, blocks.at[order[r]], sems.at[order[r]])
+        for r, block in enumerate(blocks_in)
+    ]
+
+
+def forward_kernel(size, kept):
+    def kernel(who, group_ref, order, probes, entering, lf_in, rf_in, *rest):
+        blocks_in, rest = rest[:size], rest[size:]
+        if kept:
+            rest = rest[1:]
+        leaving, waves_out, blocks, waves, lf, rf, probe, indices, block_sems, sems = rest
+        columns = blocks.shape[2]
+
+        @pl.when(who[2] > 0)
+        def _():
+            copies = block_copies(blocks_in, order, blocks, block_sems)
+            tables = [
+                pltpu.make_async_copy(lf_in, lf, sems.at[0]),
+                pltpu.make_async_copy(rf_in, rf, sems.at[1]),
+            ]
+            for copy in tables + copies:
+                copy.start()
+            start_wave(who, group_ref, probes, entering, waves, probe, sems.at[2])
+            for copy in tables:
+                copy.wait()
+
+            def arrived(k):
+                pltpu.make_async_copy(blocks_in[0], blocks.at[k], block_sems.at[k]).wait()
+                read_index(blocks, indices, k, lf.shape[0])
+
+            forward_steps(blocks, waves, indices, lf, rf, arrived)
+            leaving[...] = waves[size]
+            keep = pltpu.make_async_copy(waves.at[pl.ds(0, size)], waves_out, sems.at[3])
+            keep.start()
+            keep.wait()
 
     return kernel
 
 
-def gather_kernel(offsets_ref, grads_ref, out_ref):
+def start_wave(who, group_ref, probes, entering, waves, probe, sem):
+    width = waves.shape[1]
+
+    @pl.when(who[1] > 0)
+    def _():
+        copy = pltpu.make_async_copy(probes.at[group_ref[who[0]]], probe, sem)
+        copy.start()
+        copy.wait()
+        waves[0] = packed(probe[0], probe[1], width, 0).astype(BF16)
+
+    @pl.when(who[1] == 0)
+    def _():
+        copy = pltpu.make_async_copy(entering, waves.at[0], sem)
+        copy.start()
+        copy.wait()
+
+
+def send_out(grads, order, grads_out, sems):
+    copies = [
+        pltpu.make_async_copy(grads.at[order[r]], out, sems.at[r]) for r, out in enumerate(grads_out)
+    ]
+    for copy in copies:
+        copy.start()
+    for copy in copies:
+        copy.wait()
+
+
+def middle_kernel(size, near_rows):
+    def kernel(who, group_ref, order, out_order, probes, entering, lf_in, rf_in, lb_in, rb_in, *rest):
+        constants_in, rest = rest[:6], rest[6:]
+        measured, rest = rest[0], rest[1:]
+        blocks_in, rest = rest[:size], rest[size:]
+        leaving, grads_out, rest = rest[0], rest[1 : 1 + size], rest[1 + size :]
+        blocks, waves, grads, lf, rf, lb, rb, probe, g, gathered, observed, indices = rest[:12]
+        constants, block_sems, sems = rest[12:18], rest[18], rest[19]
+        width, columns = waves.shape[1:]
+
+        @pl.when(who[2] > 0)
+        def _():
+            copies = block_copies(blocks_in, order, blocks, block_sems)
+            tables = [
+                pltpu.make_async_copy(source, target, sems.at[n])
+                for n, (source, target) in enumerate(
+                    [(lf_in, lf), (rf_in, rf), (lb_in, lb), (rb_in, rb)]
+                    + list(zip(constants_in, constants))
+                )
+            ]
+            seen = pltpu.make_async_copy(measured.at[who[0]], gathered, sems.at[10])
+            for copy in tables[:2] + copies + [seen] + tables[2:]:
+                copy.start()
+            start_wave(who, group_ref, probes, entering, waves, probe, sems.at[11])
+            for copy in tables[:2]:
+                copy.wait()
+
+            def arrived(k):
+                pltpu.make_async_copy(blocks_in[0], blocks.at[k], block_sems.at[k]).wait()
+                read_index(blocks, indices, k, lf.shape[0])
+
+            forward_steps(blocks, waves, indices, lf, rf, arrived)
+            for copy in [seen] + tables[2:]:
+                copy.wait()
+            for n in range(gathered.shape[0]):
+                observed[n * near_rows : (n + 1) * near_rows, :] = gathered[n]
+            g[...] = detector(waves[size], doubled(observed[...]), *[table[...] for table in constants])
+            backward_steps(blocks, waves, indices, lb, rb, grads, g)
+            leaving[...] = g[...]
+            send_out(grads, out_order, grads_out, block_sems)
+
+    return kernel
+
+
+def backward_kernel(size):
+    def kernel(who, order, out_order, arriving, waves_in, lb_in, rb_in, *rest):
+        blocks_in, rest = rest[:size], rest[2 * size :]
+        leaving, grads_out, rest = rest[0], rest[1 : 1 + size], rest[1 + size :]
+        blocks, waves, grads, lb, rb, g, indices, block_sems, sems = rest
+
+        @pl.when(who[2] > 0)
+        def _():
+            copies = block_copies(blocks_in, order, blocks, block_sems)
+            copies += [
+                pltpu.make_async_copy(source, target, sems.at[n])
+                for n, (source, target) in enumerate(
+                    [(arriving, g), (waves_in, waves), (lb_in, lb), (rb_in, rb)]
+                )
+            ]
+            for copy in copies:
+                copy.start()
+            for copy in copies:
+                copy.wait()
+            for k in range(size):
+                read_index(blocks, indices, k, lb.shape[0])
+            backward_steps(blocks, waves, indices, lb, rb, grads, g)
+            leaving[...] = g[...]
+            send_out(grads, out_order, grads_out, block_sems)
+
+    return kernel
+
+
+def gather_kernel(offsets_ref, sources_ref, *rest):
+    grads_in, (out_ref, grads, sems) = rest[:-3], rest[-3:]
     positions = offsets_ref.shape[0]
-    width = grads_ref.shape[1]
+    width = grads.shape[1]
     extent = out_ref.shape[-1]
+    for r, block in enumerate(grads_in):
+        p = sources_ref[r]
+
+        @pl.when(p >= 0)
+        def _(block=block, p=p, r=r):
+            pltpu.make_async_copy(block, grads.at[p], sems.at[p]).start()
+
+    rows = jnp.concatenate(
+        [row_picker((extent, width), -offsets_ref[p, 0]) for p in range(positions)], axis=1
+    )
     spread_out = [[], []]
     for p in range(positions):
-        x0, x1, xt = halves(grads_ref[p])
+        pltpu.make_async_copy(grads_in[0], grads.at[p], sems.at[p]).wait()
+        x0, x1, xt = halves(grads[p])
         for c, main in ((0, x0), (1, x1)):
             wide = jnp.concatenate([main, xt], axis=1)
             columns = picker(extent, offsets_ref[p, 1], c == 1, transposed=True)
             spread_out[c].append(dot(wide, columns).astype(BF16))
-    rows = jnp.concatenate(
-        [row_picker((extent, width), -offsets_ref[p, 0]) for p in range(positions)], axis=1
-    )
     for c in range(2):
         out_ref[0, c] = dot(rows, jnp.concatenate(spread_out[c], axis=0))
 
 
 VMEM = pl.BlockSpec(memory_space=pltpu.VMEM)
 SMEM = pl.BlockSpec(memory_space=pltpu.SMEM)
-PARAMS = pltpu.CompilerParams(vmem_limit_bytes=48 * 1024 * 1024)
+HBM = pl.BlockSpec(memory_space=pl.ANY)
+PARAMS = pltpu.CompilerParams(vmem_limit_bytes=56 * 1024 * 1024)
+
+
+def positions_of_slots(size, positions):
+    chips = size // 2
+    inward = sorted(range(chips), key=lambda chip: bin(chip).count("1") % 2)
+    slots = [2 * chip for chip in inward] + [2 * chip + 1 for chip in inward]
+    held = [-1] * size
+    for position, slot in enumerate(sorted(slots[:positions])):
+        held[slot] = position
+    return held
 
 
 def shards(objects, propagators, prop_index, probes, probe_group, offsets, measured):
     sections = lax.axis_size("cuts")
-    rank = lax.axis_index("cuts")
+    rank = lax.axis_index("cuts").astype(jnp.int32)
     positions = probe_group.shape[0]
     width = probes.shape[-1]
     kinds = propagators.shape[0]
     near_rows = measured.shape[1]
-    size = sections
-    rows = width + 2 * ROWS
-
-    blocks, lb, rf, rb = pl.pallas_call(
+    size = GROUP
+    groups = sections // size
+    rows = width + ROWS
+    held = positions_of_slots(size, positions)
+    slot, group = rank % size, rank // size
+    rounds = np.arange(size)
+    held_here = jnp.asarray(np.array(held, np.int32))
+    ahead = (slot + rounds) % size
+    behind = (slot - rounds) % size
+    targets = held_here[ahead]
+    sources = held_here[behind]
+    place = jnp.maximum(held_here[slot], 0)
+
+    def who(stage):
+        return jnp.stack([place, (group == 0).astype(jnp.int32), (group == stage).astype(jnp.int32)])
+
+    def struct(*dims, kind=BF16):
+        return jax.ShapeDtypeStruct(dims, kind)
+
+    def across(block, r, inward):
+        pairs = []
+        for first in range(0, sections, size):
+            for l in range(size):
+                other = (l + r) % size
+                if held[other if inward else l] >= 0:
+                    pairs.append((first + l, first + other))
+        return lax.ppermute(block, "cuts", pairs)
+
+    def between(block, stage, distance):
+        return lax.ppermute(
+            block,
+            "cuts",
+            [(stage * size + l, (stage + distance) * size + l) for l in range(size) if held[l] >= 0],
+        )
+
+    gathered = lax.all_gather(measured, "cuts", axis=1, tiled=False)
+
+    cut = pl.pallas_call(
         window_kernel,
-        out_shape=[
-            jax.ShapeDtypeStruct((size, rows, 2 * width), BF16),
-            jax.ShapeDtypeStruct((kinds, 2 * width, width), BF16),
-            jax.ShapeDtypeStruct((kinds, 2 * width, 2 * width), BF16),
-            jax.ShapeDtypeStruct((kinds, 2 * width, 2 * width), BF16),
-        ],
-        in_specs=[SMEM, SMEM, VMEM, VMEM, VMEM],
-        out_specs=[VMEM] * 4,
+        out_shape=[struct(rows, 2 * width)] * size,
+        in_specs=[SMEM, SMEM, SMEM, VMEM],
+        out_specs=[VMEM] * size,
         compiler_params=PARAMS,
         name="windows",
-    )(offsets, prop_index, objects, measured, propagators)
-
-    blocks = lax.all_to_all(blocks, "cuts", 0, 0, tiled=True)
-
-    slot = jnp.minimum(rank, positions - 1).astype(jnp.int32)[None]
+    )(offsets, prop_index, targets, objects)
+    blocks = [cut[0]] + [across(cut[r], r, True) for r in range(1, size)]
+
+    lb, rf, rb = pl.pallas_call(
+        table_kernel,
+        out_shape=[
+            struct(kinds, 2 * width, width),
+            struct(kinds, 2 * width, 2 * width),
+            struct(kinds, 2 * width, 2 * width),
+        ],
+        in_specs=[VMEM],
+        out_specs=[VMEM] * 3,
+        compiler_params=PARAMS,
+        cost_estimate=pl.CostEstimate(flops=10**9, bytes_accessed=4 * 10**6, transcendentals=0),
+        name="tables",
+    )(propagators)
+    lf = propagators
+
+    wave = (width, 2 * width)
+    block_scratch = pltpu.VMEM((size, rows, 2 * width), BF16)
+    waves_scratch = pltpu.VMEM((size + 1,) + wave, BF16)
+    grads_scratch = pltpu.VMEM((size,) + wave, BF16)
+    probe_scratch = pltpu.VMEM(probes.shape[1:], BF16)
+    indices = pltpu.SMEM((size,), jnp.int32)
+
+    def like(*arrays):
+        return [pltpu.VMEM(array.shape, array.dtype) for array in arrays]
+
+    entering, waves = jnp.zeros(wave, BF16), None
+    for stage in range(groups - 1):
+        kept = waves is not None
+        leaving, waves = pl.pallas_call(
+            forward_kernel(size, kept),
+            out_shape=[struct(*wave), struct(size, *wave)],
+            in_specs=[SMEM] * 3 + [HBM] * (4 + size + kept),
+            out_specs=[VMEM, HBM],
+            scratch_shapes=[block_scratch, waves_scratch]
+            + like(lf, rf)
+            + [probe_scratch, indices, pltpu.SemaphoreType.DMA((size,)), pltpu.SemaphoreType.DMA((4,))],
+            input_output_aliases={7 + size: 1} if kept else {},
+            compiler_params=PARAMS,
+            name="forward",
+        )(who(stage), probe_group, behind, probes, entering, lf, rf, *blocks, *([waves] if kept else []))
+        entering = between(leaving, stage, 1)
+
     constants = [jnp.asarray(table) for table in dft_constants(width)]
-    grads = pl.pallas_call(
-        chain_kernel(near_rows),
-        out_shape=jax.ShapeDtypeStruct((size, width, 2 * width), BF16),
-        in_specs=[SMEM, SMEM] + [VMEM] * 12,
-        out_specs=VMEM,
-        scratch_shapes=[
-            pltpu.VMEM((size + 1, width, 2 * width), BF16),
-            pltpu.VMEM((width, 2 * width), BF16),
-            pltpu.VMEM((width, 2 * LANES), F32),
-            pltpu.SMEM((size,), jnp.int32),
-        ],
+    results = pl.pallas_call(
+        middle_kernel(size, near_rows),
+        out_shape=[struct(*wave)] * (1 + size),
+        in_specs=[SMEM] * 4 + [HBM] * (13 + size),
+        out_specs=[VMEM] + [HBM] * size,
+        scratch_shapes=[block_scratch, waves_scratch, grads_scratch]
+        + like(lf, rf, lb, rb)
+        + [
+            probe_scratch,
+            pltpu.VMEM(wave, BF16),
+            pltpu.VMEM(gathered.shape[1:], F32),
+            pltpu.VMEM((width, width), F32),
+            indices,
+        ]
+        + like(*constants)
+        + [pltpu.SemaphoreType.DMA((size,)), pltpu.SemaphoreType.DMA((12,))],
         compiler_params=PARAMS,
-        name="chain",
-    )(slot, probe_group, probes, blocks, propagators, rf, lb, rb, *constants)
-
-    grads = lax.all_to_all(grads, "cuts", 0, 0, tiled=True)
+        name="middle",
+    )(
+        who(groups - 1), probe_group, behind, ahead, probes, entering, lf, rf, lb, rb, *constants, gathered, *blocks
+    )
+    leaving, grads = results[0], results[1:]
+
+    for stage in range(groups - 2, -1, -1):
+        arriving = between(leaving, stage + 1, -1)
+        results = pl.pallas_call(
+            backward_kernel(size),
+            out_shape=[struct(*wave)] * (1 + size),
+            in_specs=[SMEM] * 3 + [HBM] * (4 + 2 * size),
+            out_specs=[VMEM] + [HBM] * size,
+            scratch_shapes=[block_scratch, pltpu.VMEM((size,) + wave, BF16), grads_scratch]
+            + like(lb, rb)
+            + [pltpu.VMEM(wave, BF16), indices, pltpu.SemaphoreType.DMA((size,)), pltpu.SemaphoreType.DMA((4,))],
+            input_output_aliases={7 + size + r: 1 + r for r in range(size)},
+            compiler_params=PARAMS,
+            name="backward",
+        )(who(stage), behind, ahead, arriving, waves, lb, rb, *blocks, *grads)
+        leaving, grads = results[0], results[1:]
+
+    grads = [grads[0]] + [across(grads[r], r, False) for r in range(1, size)]
 
     return pl.pallas_call(
         gather_kernel,
         out_shape=jax.ShapeDtypeStruct(objects.shape, F32),
-        in_specs=[SMEM, VMEM],
+        in_specs=[SMEM, SMEM] + [HBM] * size,
         out_specs=VMEM,
+        scratch_shapes=[pltpu.VMEM((positions,) + wave, BF16), pltpu.SemaphoreType.DMA((positions,))],
         compiler_params=PARAMS,
         name="sum_windows",
-    )(offsets, grads)
+    )(offsets, sources, *grads)
 
 
 def solution(mesh):

time: 172 us -> 146 us (0.85)
  blocking collectives: 67.8 us -> 27.9 us
  starting transfers between devices: 7.55 us -> 41.9 us
  waiting for transfers between devices: 52.6 us -> 27 us
  Pallas kernels: 31.9 us -> 34.3 us
  other arithmetic: 0 us -> 2.18 us
    all_to_all x1 -> x0, blocking collectives: 67.8 us -> none  [shards(): grads = lax.all_to_all(grads, 'cuts', 0, 0, tiled=True)]
    all_to_all x1 -> x0, waiting for transfers between devices: 52.6 us -> none  [shards(): blocks = lax.all_to_all(blocks, 'cuts', 0, 0, tiled=True)]
    ppermute x0 -> x16, starting transfers between devices: none -> 41.9 us  [the longest x14 39.3 us: across(): return lax.ppermute(block, 'cuts', pairs)]
    all_gather x0 -> x1, blocking collectives: none -> 27.9 us  [shards(): gathered = lax.all_gather(measured, 'cuts', axis=1, tiled=False)]
    ppermute x0 -> x16, waiting for transfers between devices: none -> 27 us  [the longest x2 24.2 us: between(): lax.ppermute(block, 'cuts', [(stage * size + l, (stage + distance) * size...]
    all_to_all x1 -> x0, starting transfers between devices: 7.55 us -> none  [shards(): blocks = lax.all_to_all(blocks, 'cuts', 0, 0, tiled=True)]
    unnamed x27 -> x42, local copies, waits for them, and re-layouts: 10.6 us -> 3.42 us
    gather x0 -> x2, local copies, waits for them, and re-layouts: none -> 2.99 us  [the longest x1 1.87 us: shards(): targets = held_here[ahead]]
  transfers between devices with their start and end apart: 1 -> 16, of which waited for: 1 -> 5; matrix products, arithmetic and copies ran while one was open for 0% -> 4% of each run, Pallas kernels for 0% -> 2%
where the time goes in v2:
time: 146 us; the launch traced here: 145 us
  starting transfers between devices  41.9 us (29%)
  Pallas kernels  34.3 us (23%)
  blocking collectives  27.9 us (19%)
  waiting for transfers between devices  27 us (18%)
  local copies, waits for them, and re-layouts  9.37 us (6%)
  other arithmetic  2.18 us (1%)
  between operations  1.89 us (1%)
    ppermute x14, starting transfers between devices, across(): return lax.ppermute(block, 'cuts', pairs)  39.3 us
    all_gather x1, blocking collectives, shards(): gathered = lax.all_gather(measured, 'cuts', axis=1, tiled=False)  27.9 us
    ppermute x2, waiting for transfers between devices, between(): lax.ppermute(block, 'cuts', [(stage * size + l, (stage + distance) * size...  24.2 us
    pallas_call x1, Pallas kernels, shards(): pl.pallas_call(backward_kernel(size), out_shape=[struct(*wave)] * (1 + si...  9.51 us
    pallas_call x1, Pallas kernels, shards(): pl.pallas_call(forward_kernel(size, kept), out_shape=[struct(*wave), stru...  9.29 us
    pallas_call x1, Pallas kernels, shards(): pl.pallas_call(gather_kernel, out_shape=jax.ShapeDtypeStruct(objects.shap...  5.44 us
    pallas_call x1, Pallas kernels, shards(): pl.pallas_call(window_kernel, out_shape=[struct(rows, 2 * width)] * size,...  5.08 us
    pallas_call x1, Pallas kernels, shards(): pl.pallas_call(table_kernel, out_shape=[struct(kinds, 2 * width, width),...  3.48 us
  transfers between devices with their start and end apart: 16, of which 5 were waited for; matrix products, arithmetic and copies ran while one was open for 4% of the time, Pallas kernels for 2%

profile of v2, /device:TPU:0, one launch (start us, length us, event | category | flops | bytes accessed | tf_op | source)
XLA Modules:
  0.0 144.6 jit_solution(773113290174570440)
XLA Ops:
  0.7 1.4 copy.31.offsets_ref
  2.1 1.9 %gather_fusion.1 = s32[8]{0:T(128)} fusion(s32[8]{0:T(128)} %constant.67.clone, s32[1024]{0:T(1024)S(1)} %pad_clamp_fusion), kind=kCustom, calls=%fused_computation.1 | custom fusion | bytes 96 | tf_op jit(solution)/shard_map/gather | solution.py:431
  4.0 5.1 %windows.1 = (bf16[208,384]{1,0:T(8,128)(2,1)}, bf16[208,384]{1,0:T(8,128)(2,1)}, bf16[208,384]{1,0:T(8,128)(2,1)}, bf16[208,384]{1,0:T(8,128)(2,1)}, bf16[208,3...) custom-call(s32[6,2]{1,0:T(8,128)} %copy.31.offsets_ref, ...), custom_call_target="tpu_custom_call" | custom-call | tf_op jit(solution)/shard_map/windows/pallas_call | solution.py:459
  9.0 2.5 %collective-permute-start = (bf16[208,384]{1,0:T(8,128)(2,1)}, bf16[208,384]{1,0:T(8,128)(2,1)S(1)}, u32[]{:S(2)}, u32[]{:S(2)}) collective-permute-start(bf16[208,384]{1,0:T(8,128)(2,1)} %get-tuple-element.37), channel_id=1, source_target_pairs={{0,1},{1,2},{3,4},{5,6},{6,7},{7,0},{8,9},{9,10},{11,12},{13,14},{... | collective-permute-start | bytes 479240 | tf_op jit(solution)/shard_map/ppermute | solution.py:448
  11.5 3.8 %collective-permute-start.1 = (bf16[208,384]{1,0:T(8,128)(2,1)}, bf16[208,384]{1,0:T(8,128)(2,1)S(1)}, u32[]{:S(2)}, u32[]{:S(2)}) collective-permute-start(bf16[208,384]{1,0:T(8,128)(2,1)} %get-tuple-element.38), channel_id=1, source_target_pairs={{0,2},{2,4},{4,6},{5,7},{6,0},{7,1},{8,10},{10,12},{12,14},{13,15}... | collective-permute-start | bytes 479240 | tf_op jit(solution)/shard_map/ppermute | solution.py:448
  15.3 1.3 collective-permute-start.2
  16.6 6.1 %collective-permute-start.3 = (bf16[208,384]{1,0:T(8,128)(2,1)}, bf16[208,384]{1,0:T(8,128)(2,1)S(1)}, u32[]{:S(2)}, u32[]{:S(2)}) collective-permute-start(bf16[208,384]{1,0:T(8,128)(2,1)} %get-tuple-element.40), channel_id=1, source_target_pairs={{0,4},{2,6},{3,7},{4,0},{5,1},{6,2},{8,12},{10,14},{11,15},{12,8},... | collective-permute-start | bytes 479240 | tf_op jit(solution)/shard_map/ppermute | solution.py:448
  22.7 1.3 collective-permute-start.4
  24.1 27.9 %all-gather = f32[6,192,192]{2,0,1:T(8,128)S(1)} all-gather(f32[6,12,192]{2,0,1:T(8,128)S(1)} %copy.29), channel_id=2, replica_groups=mesh['parts'=2,'cuts'=16] {'cuts'}, dimensions={1}, use_global_device_ids=true | all-gather | bytes 940032 | tf_op jit(solution)/shard_map/all_gather | solution.py:457
  52.0 0.6 dynamic_slice.3
  53.3 0.5 and_select_fusion.1.order
  53.8 0.0 collective-permute-done.rest_1_.rest_8_
  53.8 1.9 %collective-permute-start.5 = (bf16[208,384]{1,0:T(8,128)(2,1)S(1)}, bf16[208,384]{1,0:T(8,128)(2,1)S(1)}, u32[]{:S(2)}, u32[]{:S(2)}) collective-permute-start(bf16[208,384]{1,0:T(8,128)(2,1)S(1)} %copy-done.19), channel_id=1, source_target_pairs={{0,6},{1,7},{2,0},{3,1},{4,2},{6,4},{8,14},{9,15},{10,8},{11,9},{1... | collective-permute-start | bytes 479240 | tf_op jit(solution)/shard_map/ppermute | solution.py:448
  55.7 0.0 collective-permute-done.1.rest_2_.rest_9_
  55.8 1.9 %collective-permute-start.6 = (bf16[208,384]{1,0:T(8,128)(2,1)S(1)}, bf16[208,384]{1,0:T(8,128)(2,1)S(1)}, u32[]{:S(2)}, u32[]{:S(2)}) collective-permute-start(bf16[208,384]{1,0:T(8,128)(2,1)S(1)} %copy-done.18), channel_id=1, source_target_pairs={{0,7},{1,0},{2,1},{3,2},{5,4},{7,6},{8,15},{9,8},{10,9},{11,10},{1... | collective-permute-start | bytes 479240 | tf_op jit(solution)/shard_map/ppermute | solution.py:448
  57.7 3.5 %tables.1 = (bf16[4,384,192]{2,1,0:T(8,128)(2,1)}, bf16[4,384,384]{2,1,0:T(8,128)(2,1)}, bf16[4,384,384]{2,1,0:T(8,128)(2,1)}) custom-call(bf16[4,2,192,192]{3,2,1,0:T(8,128)(2,1)} %lf_in.3), custom_call_target="tpu_custom_call" | custom-call | flops 1000000000 | bytes 4000000 | tf_op jit(solution)/shard_map/tables/pallas_call | solution.py:469
  61.2 0.6 pad_add_fusion.who
  61.8 0.0 collective-permute-done.2.rest_3_.rest_10_
  61.8 0.0 collective-permute-done.3.rest_4_.rest_11_
  61.8 0.3 collective-permute-done.5.rest_6_.rest_13_
  62.1 0.0 collective-permute-done.6.rest_7_.rest_14_
  62.1 0.7 broadcast_in_dim.10.entering
  62.8 0.0 copy-done.7
  62.9 9.3 %forward.1 = (bf16[192,384]{1,0:T(8,128)(2,1)}, bf16[8,192,384]{2,1,0:T(8,128)(2,1)}) custom-call(s32[3]{0:T(128)} %pad_add_fusion.who, s32[6]{0:T(128)} %group_ref.3, s32[8]{0:T(128)} %and_select_fusion.1.order, bf16[8,2,192,192]{3,2,1,0:T(8,128)(2,1)} %probes.3, bf16[192,384]{1,0:T(8,128)(2,1)} %broadcast_in_dim.10.entering, ...), custom_call_target="tpu_custom_call" | custom-call | tf_op jit(solution)/shard_map/forward/pallas_call | solution.py:497
  72.2 1.3 collective-permute-start.7
  73.5 0.5 and_select_fusion.out_order
  74.0 1.6 %copy.32.rest_6_ = f32[6,16,12,192]{3,2,1,0:T(8,128)} copy(f32[6,16,12,192]{3,0,2,1:T(8,128)S(1)} %bitcast.3) | data formatting | bytes 1769472 | tf_op jit(solution)/shard_map/all_gather | solution.py:457
  75.5 0.6 pad_add_fusion.2.who
  76.1 1.1 collective-permute-done.7.entering
  77.2 0.7 copy-done.16
  77.9 1.5 %middle.1 = (bf16[192,384]{1,0:T(8,128)(2,1)}, bf16[192,384]{1,0:T(8,128)(2,1)}, bf16[192,384]{1,0:T(8,128)(2,1)}, bf16[192,384]{1,0:T(8,128)(2,1)}, bf16[192,38...) custom-call(s32[3]{0:T(128)} %pad_add_fusion.2.who, ...), custom_call_target="tpu_custom_call" | custom-call | tf_op jit(solution)/shard_map/middle/pallas_call | solution.py:512
  79.4 1.3 collective-permute-start.8
  80.7 23.1 %collective-permute-done.8.arriving = bf16[192,384]{1,0:T(8,128)(2,1)S(1)} collective-permute-done((bf16[192,384]{1,0:T(8,128)(2,1)}, bf16[192,384]{1,0:T(8,128)(2,1)S(1)}, u32[]{:S(2)}, u32[]{:S(2)}) %collective-permute-start.8) | collective-permute-done | bytes 147488 | tf_op jit(solution)/shard_map/ppermute | solution.py:451
  103.9 0.7 copy-done.8
  104.5 9.5 %backward.1 = (bf16[192,384]{1,0:T(8,128)(2,1)}, bf16[192,384]{1,0:T(8,128)(2,1)}, bf16[192,384]{1,0:T(8,128)(2,1)}, bf16[192,384]{1,0:T(8,128)(2,1)}, bf16[192,...) custom-call(s32[3]{0:T(128)} %pad_add_fusion.who, ...), custom_call_target="tpu_custom_call", output_to_operand_aliasing={{1}: (15, {}), {2}: (16, {}), {3}: (17, {}), {4}: (18, {}),... | custom-call | tf_op jit(solution)/shard_map/backward/pallas_call | solution.py:537
  114.0 2.0 %collective-permute-start.9 = (bf16[192,384]{1,0:T(8,128)(2,1)}, bf16[192,384]{1,0:T(8,128)(2,1)S(1)}, u32[]{:S(2)}, u32[]{:S(2)}) collective-permute-start(bf16[192,384]{1,0:T(8,128)(2,1)} %get-tuple-element.58), channel_id=1, source_target_pairs={{0,1},{1,2},{2,3},{4,5},{6,7},{7,0},{8,9},{9,10},{10,11},{12,13},{... | collective-permute-start | bytes 442376 | tf_op jit(solution)/shard_map/ppermute | solution.py:448
  116.0 4.7 %collective-permute-start.10 = (bf16[192,384]{1,0:T(8,128)(2,1)}, bf16[192,384]{1,0:T(8,128)(2,1)S(1)}, u32[]{:S(2)}, u32[]{:S(2)}) collective-permute-start(bf16[192,384]{1,0:T(8,128)(2,1)} %get-tuple-element.59), channel_id=1, source_target_pairs={{0,2},{1,3},{2,4},{4,6},{6,0},{7,1},{8,10},{9,11},{10,12},{12,14},... | collective-permute-start | bytes 442376 | tf_op jit(solution)/shard_map/ppermute | solution.py:448
  120.7 1.3 collective-permute-start.11
  122.0 5.4 %collective-permute-start.12 = (bf16[192,384]{1,0:T(8,128)(2,1)}, bf16[192,384]{1,0:T(8,128)(2,1)S(1)}, u32[]{:S(2)}, u32[]{:S(2)}) collective-permute-start(bf16[192,384]{1,0:T(8,128)(2,1)} %get-tuple-element.61), channel_id=1, source_target_pairs={{0,4},{1,5},{2,6},{4,0},{6,2},{7,3},{8,12},{9,13},{10,14},{12,8},{... | collective-permute-start | bytes 442376 | tf_op jit(solution)/shard_map/ppermute | solution.py:448
  127.5 1.3 collective-permute-start.13
  128.8 2.3 %collective-permute-start.14 = (bf16[192,384]{1,0:T(8,128)(2,1)}, bf16[192,384]{1,0:T(8,128)(2,1)S(1)}, u32[]{:S(2)}, u32[]{:S(2)}) collective-permute-start(bf16[192,384]{1,0:T(8,128)(2,1)} %get-tuple-element.63), channel_id=1, source_target_pairs={{0,6},{1,7},{2,0},{4,2},{6,4},{7,5},{8,14},{9,15},{10,8},{12,10},{... | collective-permute-start | bytes 442376 | tf_op jit(solution)/shard_map/ppermute | solution.py:448
  131.1 3.5 %collective-permute-start.15 = (bf16[192,384]{1,0:T(8,128)(2,1)}, bf16[192,384]{1,0:T(8,128)(2,1)S(1)}, u32[]{:S(2)}, u32[]{:S(2)}) collective-permute-start(bf16[192,384]{1,0:T(8,128)(2,1)} %get-tuple-element.64), channel_id=1, source_target_pairs={{0,7},{1,0},{2,1},{4,3},{6,5},{7,6},{8,15},{9,8},{10,9},{12,11},{1... | collective-permute-start | bytes 442376 | tf_op jit(solution)/shard_map/ppermute | solution.py:448
  134.7 1.1 gather_fusion
  135.8 0.0 collective-permute-done.13.rest_5_
  135.8 0.9 collective-permute-done.14.rest_6_
  136.7 1.6 %collective-permute-done.15.rest_7_ = bf16[192,384]{1,0:T(8,128)(2,1)S(1)} collective-permute-done((bf16[192,384]{1,0:T(8,128)(2,1)}, bf16[192,384]{1,0:T(8,128)(2,1)S(1)}, u32[]{:S(2)}, u32[]{:S(2)}) %collective-permute-start.15) | collective-permute-done | bytes 147488 | tf_op jit(solution)/shard_map/ppermute | solution.py:448
  138.4 0.6 copy-done.15
  139.0 5.4 %sum_windows.1 = f32[1,2,384,384]{3,2,1,0:T(8,128)} custom-call(s32[6,2]{1,0:T(8,128)} %copy.31.offsets_ref, s32[8]{0:T(128)} %gather_fusion, bf16[192,384]{1,0:T(8,128)(2,1)} %get-tuple-element.57.rest_0_, bf16[192,384]{1,0:T(8,128)(2,1)} %copy-done.9, bf16[192,384]{1,0:T(8,128)(2,1)} %copy-done.10, bf16[192,384]{1,0:T(8,128)(2,1)} %copy-done.11, ...), custom_call_target="tpu_custom_call" | custom-call | tf_op jit(solution)/shard_map/sum_windows/pallas_call | solution.py:553
  (45 shorter events, 0.2 us)
Async XLA Ops:
  0.0 24.0 %copy-start.17 = (f32[6,12,192]{2,1,0:T(8,128)S(1)}, f32[6,12,192]{2,1,0:T(8,128)}, u32[]{:S(2)}) copy-start(f32[6,12,192]{2,1,0:T(8,128)} %param.21) | copy-start | bytes 165892
  4.0 48.0 %copy-start = (s32[8]{0:T(128)S(1)}, s32[8]{0:T(128)}, u32[]{:S(2)}) copy-start(s32[8]{0:T(128)} %constant.67.clone) | copy-start | bytes 100
  9.0 44.8 %copy-start.19 = (bf16[208,384]{1,0:T(8,128)(2,1)S(1)}, bf16[208,384]{1,0:T(8,128)(2,1)}, u32[]{:S(2)}) copy-start(bf16[208,384]{1,0:T(8,128)(2,1)} %get-tuple-element.42) | copy-start | bytes 479236
  9.0 46.7 %copy-start.18 = (bf16[208,384]{1,0:T(8,128)(2,1)S(1)}, bf16[208,384]{1,0:T(8,128)(2,1)}, u32[]{:S(2)}) copy-start(bf16[208,384]{1,0:T(8,128)(2,1)} %get-tuple-element.43) | copy-start | bytes 479236
  9.0 44.8 %collective-permute-start = (bf16[208,384]{1,0:T(8,128)(2,1)}, bf16[208,384]{1,0:T(8,128)(2,1)S(1)}, u32[]{:S(2)}, u32[]{:S(2)}) collective-permute-start(bf16[208,384]{1,0:T(8,128)(2,1)} %get-tuple-element.37), channel_id=1, source_target_pairs={{0,1},{1,2},{3,4},{5,6},{6,7},{7,0},{8,9},{9,10},{11,12},{13,14},{... | collective-permute-start | bytes 479240 | tf_op jit(solution)/shard_map/ppermute | solution.py:448
  11.5 44.2 %collective-permute-start.1 = (bf16[208,384]{1,0:T(8,128)(2,1)}, bf16[208,384]{1,0:T(8,128)(2,1)S(1)}, u32[]{:S(2)}, u32[]{:S(2)}) collective-permute-start(bf16[208,384]{1,0:T(8,128)(2,1)} %get-tuple-element.38), channel_id=1, source_target_pairs={{0,2},{2,4},{4,6},{5,7},{6,0},{7,1},{8,10},{10,12},{12,14},{13,15}... | collective-permute-start | bytes 479240 | tf_op jit(solution)/shard_map/ppermute | solution.py:448
  15.3 46.4 %collective-permute-start.2 = (bf16[208,384]{1,0:T(8,128)(2,1)}, bf16[208,384]{1,0:T(8,128)(2,1)S(1)}, u32[]{:S(2)}, u32[]{:S(2)}) collective-permute-start(bf16[208,384]{1,0:T(8,128)(2,1)} %get-tuple-element.39), channel_id=1, source_target_pairs={{1,4},{3,6},{4,7},{5,0},{6,1},{7,2},{9,12},{11,14},{12,15},{13,8},... | collective-permute-start | bytes 479240 | tf_op jit(solution)/shard_map/ppermute | solution.py:448
  16.6 45.2 %collective-permute-start.3 = (bf16[208,384]{1,0:T(8,128)(2,1)}, bf16[208,384]{1,0:T(8,128)(2,1)S(1)}, u32[]{:S(2)}, u32[]{:S(2)}) collective-permute-start(bf16[208,384]{1,0:T(8,128)(2,1)} %get-tuple-element.40), channel_id=1, source_target_pairs={{0,4},{2,6},{3,7},{4,0},{5,1},{6,2},{8,12},{10,14},{11,15},{12,8},... | collective-permute-start | bytes 479240 | tf_op jit(solution)/shard_map/ppermute | solution.py:448
  22.7 39.1 %collective-permute-start.4 = (bf16[208,384]{1,0:T(8,128)(2,1)}, bf16[208,384]{1,0:T(8,128)(2,1)S(1)}, u32[]{:S(2)}, u32[]{:S(2)}) collective-permute-start(bf16[208,384]{1,0:T(8,128)(2,1)} %get-tuple-element.41), channel_id=1, source_target_pairs={{1,6},{2,7},{3,0},{4,1},{5,2},{7,4},{9,14},{10,15},{11,8},{12,9},{... | collective-permute-start | bytes 479240 | tf_op jit(solution)/shard_map/ppermute | solution.py:448
  53.8 7.4 %copy-start.1 = (bf16[208,384]{1,0:T(8,128)(2,1)}, bf16[208,384]{1,0:T(8,128)(2,1)S(1)}, u32[]{:S(2)}) copy-start(bf16[208,384]{1,0:T(8,128)(2,1)S(1)} %collective-permute-done.rest_1_.rest_8_) | copy-start | bytes 479236
  53.8 8.3 %collective-permute-start.5 = (bf16[208,384]{1,0:T(8,128)(2,1)S(1)}, bf16[208,384]{1,0:T(8,128)(2,1)S(1)}, u32[]{:S(2)}, u32[]{:S(2)}) collective-permute-start(bf16[208,384]{1,0:T(8,128)(2,1)S(1)} %copy-done.19), channel_id=1, source_target_pairs={{0,6},{1,7},{2,0},{3,1},{4,2},{6,4},{8,14},{9,15},{10,8},{11,9},{1... | collective-permute-start | bytes 479240 | tf_op jit(solution)/shard_map/ppermute | solution.py:448
  55.8 5.4 %copy-start.2 = (bf16[208,384]{1,0:T(8,128)(2,1)}, bf16[208,384]{1,0:T(8,128)(2,1)S(1)}, u32[]{:S(2)}) copy-start(bf16[208,384]{1,0:T(8,128)(2,1)S(1)} %collective-permute-done.1.rest_2_.rest_9_) | copy-start | bytes 479236
  55.8 6.3 %collective-permute-start.6 = (bf16[208,384]{1,0:T(8,128)(2,1)S(1)}, bf16[208,384]{1,0:T(8,128)(2,1)S(1)}, u32[]{:S(2)}, u32[]{:S(2)}) collective-permute-start(bf16[208,384]{1,0:T(8,128)(2,1)S(1)} %copy-done.18), channel_id=1, source_target_pairs={{0,7},{1,0},{2,1},{3,2},{5,4},{7,6},{8,15},{9,8},{10,9},{11,10},{1... | collective-permute-start | bytes 479240 | tf_op jit(solution)/shard_map/ppermute | solution.py:448
  61.8 1.0 copy-start.3
  61.8 1.0 copy-start.4
  61.8 1.0 copy-start.5
  62.1 0.8 copy-start.6
  62.1 0.8 copy-start.7
  72.2 5.0 %collective-permute-start.7 = (bf16[192,384]{1,0:T(8,128)(2,1)}, bf16[192,384]{1,0:T(8,128)(2,1)S(1)}, u32[]{:S(2)}, u32[]{:S(2)}) collective-permute-start(bf16[192,384]{1,0:T(8,128)(2,1)} %get-tuple-element.44), channel_id=1, source_target_pairs={{0,8},{1,9},{2,10},{4,12},{6,14},{7,15},{16,24},{17,25},{18,26},{2... | collective-permute-start | bytes 442376 | tf_op jit(solution)/shard_map/ppermute | solution.py:451
  77.2 0.7 copy-start.16
  79.4 24.4 %collective-permute-start.8 = (bf16[192,384]{1,0:T(8,128)(2,1)}, bf16[192,384]{1,0:T(8,128)(2,1)S(1)}, u32[]{:S(2)}, u32[]{:S(2)}) collective-permute-start(bf16[192,384]{1,0:T(8,128)(2,1)} %get-tuple-element.47), channel_id=1, source_target_pairs={{8,0},{9,1},{10,2},{12,4},{14,6},{15,7},{24,16},{25,17},{26,18},{2... | collective-permute-start | bytes 442376 | tf_op jit(solution)/shard_map/ppermute | solution.py:451
  103.9 0.7 copy-start.8
  114.0 14.7 %collective-permute-start.9 = (bf16[192,384]{1,0:T(8,128)(2,1)}, bf16[192,384]{1,0:T(8,128)(2,1)S(1)}, u32[]{:S(2)}, u32[]{:S(2)}) collective-permute-start(bf16[192,384]{1,0:T(8,128)(2,1)} %get-tuple-element.58), channel_id=1, source_target_pairs={{0,1},{1,2},{2,3},{4,5},{6,7},{7,0},{8,9},{9,10},{10,11},{12,13},{... | collective-permute-start | bytes 442376 | tf_op jit(solution)/shard_map/ppermute | solution.py:448
  116.0 15.0 %collective-permute-start.10 = (bf16[192,384]{1,0:T(8,128)(2,1)}, bf16[192,384]{1,0:T(8,128)(2,1)S(1)}, u32[]{:S(2)}, u32[]{:S(2)}) collective-permute-start(bf16[192,384]{1,0:T(8,128)(2,1)} %get-tuple-element.59), channel_id=1, source_target_pairs={{0,2},{1,3},{2,4},{4,6},{6,0},{7,1},{8,10},{9,11},{10,12},{12,14},... | collective-permute-start | bytes 442376 | tf_op jit(solution)/shard_map/ppermute | solution.py:448
  120.7 15.1 %collective-permute-start.11 = (bf16[192,384]{1,0:T(8,128)(2,1)}, bf16[192,384]{1,0:T(8,128)(2,1)S(1)}, u32[]{:S(2)}, u32[]{:S(2)}) collective-permute-start(bf16[192,384]{1,0:T(8,128)(2,1)} %get-tuple-element.60), channel_id=1, source_target_pairs={{0,3},{1,4},{2,5},{4,7},{6,1},{7,2},{8,11},{9,12},{10,13},{12,15},... | collective-permute-start | bytes 442376 | tf_op jit(solution)/shard_map/ppermute | solution.py:448
  122.0 13.8 %collective-permute-start.12 = (bf16[192,384]{1,0:T(8,128)(2,1)}, bf16[192,384]{1,0:T(8,128)(2,1)S(1)}, u32[]{:S(2)}, u32[]{:S(2)}) collective-permute-start(bf16[192,384]{1,0:T(8,128)(2,1)} %get-tuple-element.61), channel_id=1, source_target_pairs={{0,4},{1,5},{2,6},{4,0},{6,2},{7,3},{8,12},{9,13},{10,14},{12,8},{... | collective-permute-start | bytes 442376 | tf_op jit(solution)/shard_map/ppermute | solution.py:448
  127.5 8.3 %collective-permute-start.13 = (bf16[192,384]{1,0:T(8,128)(2,1)}, bf16[192,384]{1,0:T(8,128)(2,1)S(1)}, u32[]{:S(2)}, u32[]{:S(2)}) collective-permute-start(bf16[192,384]{1,0:T(8,128)(2,1)} %get-tuple-element.62), channel_id=1, source_target_pairs={{0,5},{1,6},{2,7},{4,1},{6,3},{7,4},{8,13},{9,14},{10,15},{12,9},{... | collective-permute-start | bytes 442376 | tf_op jit(solution)/shard_map/ppermute | solution.py:448
  128.8 9.5 %copy-start.9 = (bf16[192,384]{1,0:T(8,128)(2,1)}, bf16[192,384]{1,0:T(8,128)(2,1)S(1)}, u32[]{:S(2)}) copy-start(bf16[192,384]{1,0:T(8,128)(2,1)S(1)} %collective-permute-done.9.rest_1_) | copy-start | bytes 442372
  128.8 7.9 %collective-permute-start.14 = (bf16[192,384]{1,0:T(8,128)(2,1)}, bf16[192,384]{1,0:T(8,128)(2,1)S(1)}, u32[]{:S(2)}, u32[]{:S(2)}) collective-permute-start(bf16[192,384]{1,0:T(8,128)(2,1)} %get-tuple-element.63), channel_id=1, source_target_pairs={{0,6},{1,7},{2,0},{4,2},{6,4},{7,5},{8,14},{9,15},{10,8},{12,10},{... | collective-permute-start | bytes 442376 | tf_op jit(solution)/shard_map/ppermute | solution.py:448
  131.1 7.2 %copy-start.10 = (bf16[192,384]{1,0:T(8,128)(2,1)}, bf16[192,384]{1,0:T(8,128)(2,1)S(1)}, u32[]{:S(2)}) copy-start(bf16[192,384]{1,0:T(8,128)(2,1)S(1)} %collective-permute-done.10.rest_2_) | copy-start | bytes 442372
  131.1 7.2 %collective-permute-start.15 = (bf16[192,384]{1,0:T(8,128)(2,1)}, bf16[192,384]{1,0:T(8,128)(2,1)S(1)}, u32[]{:S(2)}, u32[]{:S(2)}) collective-permute-start(bf16[192,384]{1,0:T(8,128)(2,1)} %get-tuple-element.64), channel_id=1, source_target_pairs={{0,7},{1,0},{2,1},{4,3},{6,5},{7,6},{8,15},{9,8},{10,9},{12,11},{1... | collective-permute-start | bytes 442376 | tf_op jit(solution)/shard_map/ppermute | solution.py:448
  135.8 2.5 %copy-start.11 = (bf16[192,384]{1,0:T(8,128)(2,1)}, bf16[192,384]{1,0:T(8,128)(2,1)S(1)}, u32[]{:S(2)}) copy-start(bf16[192,384]{1,0:T(8,128)(2,1)S(1)} %collective-permute-done.11.rest_3_) | copy-start | bytes 442372
  135.8 2.5 %copy-start.12 = (bf16[192,384]{1,0:T(8,128)(2,1)}, bf16[192,384]{1,0:T(8,128)(2,1)S(1)}, u32[]{:S(2)}) copy-start(bf16[192,384]{1,0:T(8,128)(2,1)S(1)} %collective-permute-done.12.rest_4_) | copy-start | bytes 442372
  135.8 2.5 %copy-start.13 = (bf16[192,384]{1,0:T(8,128)(2,1)}, bf16[192,384]{1,0:T(8,128)(2,1)S(1)}, u32[]{:S(2)}) copy-start(bf16[192,384]{1,0:T(8,128)(2,1)S(1)} %collective-permute-done.13.rest_5_) | copy-start | bytes 442372
  136.7 1.6 %copy-start.14 = (bf16[192,384]{1,0:T(8,128)(2,1)}, bf16[192,384]{1,0:T(8,128)(2,1)S(1)}, u32[]{:S(2)}) copy-start(bf16[192,384]{1,0:T(8,128)(2,1)S(1)} %collective-permute-done.14.rest_6_) | copy-start | bytes 442372
  138.3 0.7 copy-start.15

commit v3 on v1

v3 whole, which is shorter than its diff:
```python
import math

import jax
import jax.numpy as jnp
import numpy as np
from jax import lax
from jax.experimental import pallas as pl
from jax.experimental.pallas import tpu as pltpu
from jax.sharding import PartitionSpec as P

TRANSMIT = 0.985
GROUP = 8
LANES = 128
ROWS = 16
F32 = jnp.float32
BF16 = jnp.bfloat16


def dot(former, latter):
    return jnp.dot(former, latter, preferred_element_type=F32)


def halves(x):
    return x[:, :LANES], x[:, LANES : 2 * LANES], x[:, 2 * LANES :]


def swapped(tail):
    return pltpu.roll(tail, LANES // 2, 1)


def low_half(rows):
    return lax.broadcasted_iota(jnp.int32, (rows, LANES), 1) < LANES // 2


def spread(tail):
    other = swapped(tail)
    low = low_half(tail.shape[0])
    return jnp.where(low, tail, other), jnp.where(low, other, tail)


def signed(tail, minus_low):
    low = low_half(tail.shape[0])
    return jnp.where(low == minus_low, -tail, tail)


def times(a, b):
    a0, a1, at = halves(a)
    b0, b1, bt = halves(b)
    b_real, b_imag = spread(bt)
    tail = at * b_real + signed(swapped(at), True) * b_imag
    return jnp.concatenate([a0 * b0 - a1 * b1, a1 * b0 + a0 * b1, tail], axis=1)


def times_conj(a, *others):
    a0, a1, at = halves(a)
    turned = signed(swapped(at), False)
    results = []
    for b in others:
        b0, b1, bt = halves(b)
        b_real, b_imag = spread(bt)
        tail = at * b_real + turned * b_imag
        results.append(jnp.concatenate([a0 * b0 + a1 * b1, a1 * b0 - a0 * b1, tail], axis=1))
    return results


def joined(both, conj):
    width = both.shape[0] // 2
    u0, u1, ut = halves(both[:width])
    v0, v1, vt = halves(both[width:])
    turned = signed(swapped(vt), not conj)
    if conj:
        return jnp.concatenate([u0 + v1, u1 - v0, ut + turned], axis=1)
    return jnp.concatenate([u0 - v1, u1 + v0, ut + turned], axis=1)


def with_mean(window):
    x = window.astype(F32)
    x0, x1, xt = halves(x)
    mean = jnp.where(low_half(xt.shape[0]), TRANSMIT, 0.0)
    return jnp.concatenate([TRANSMIT + x0, x1, mean + xt], axis=1)


def split2(x):
    high = x.astype(BF16)
    return high, (x - high.astype(F32)).astype(BF16)


def picker(columns, start, high_tail, transposed=False):
    shape = (2 * LANES, columns) if transposed else (columns, 2 * LANES)
    a = lax.broadcasted_iota(jnp.int32, shape, 1 if transposed else 0) - start
    q = lax.broadcasted_iota(jnp.int32, shape, 0 if transposed else 1)
    if high_tail:
        half = LANES // 2
        wanted = jnp.where(q < LANES, q, jnp.where(q < LANES + half, -columns, q - half))
    else:
        wanted = jnp.where(q < LANES + LANES // 2, q, -columns)
    return jnp.where(a == wanted, 1.0, 0.0).astype(BF16)


def row_picker(shape, distance):
    taken = lax.broadcasted_iota(jnp.int32, shape, 1)
    wanted = lax.broadcasted_iota(jnp.int32, shape, 0) + distance
    return jnp.where(taken == wanted, 1.0, 0.0).astype(BF16)


def packed(real, imag, columns, start):
    left = dot(real, picker(columns, start, False))
    right = dot(imag, picker(columns, start, True))
    return jnp.concatenate(
        [left[:, :LANES], right[:, :LANES], left[:, LANES:] + right[:, LANES:]], axis=1
    )


def dft_constant(width):
    counter = np.arange(width)
    angle = (counter[:, None] * counter[None, :] % width) * (2.0 * math.pi / width)
    return (np.stack([np.cos(angle), -np.sin(angle)]) / math.sqrt(width)).astype(np.float32)


def window_kernel(offsets_ref, index_ref, objects_ref, measured_ref, blocks):
    positions, near_rows, width = measured_ref.shape
    extent = objects_ref.shape[-1]
    tag = jnp.full((ROWS, LANES), index_ref[0], jnp.int32).astype(F32).astype(BF16)
    blank = jnp.zeros((ROWS - near_rows, 2 * LANES), F32)
    field = jnp.concatenate([objects_ref[0, 0], objects_ref[0, 1]], axis=1)
    for p in range(positions):
        both = dot(row_picker((width, extent), offsets_ref[p, 0]), field).astype(BF16)
        window = packed(both[:, :extent], both[:, extent:], extent, offsets_ref[p, 1])
        blocks[p, :width, :] = window.astype(BF16)
        high, low = split2(jnp.concatenate([doubled(measured_ref[p]), blank], axis=0))
        for place, part in ((width, high), (width + ROWS, low)):
            blocks[p, place : place + ROWS, : 2 * LANES] = part
            blocks[p, place : place + ROWS, 2 * LANES :] = tag


def doubled(rows):
    tail = jnp.concatenate([rows[:, LANES:]] * 2, axis=1)
    return jnp.concatenate([rows[:, :LANES], tail], axis=1)


def right_table(real, imag):
    width = real.shape[0]
    upper = packed(real, imag, width, 0)
    lower = packed(-imag, real, width, 0)
    return jnp.concatenate([upper[:LANES], lower[:LANES], upper[LANES:], lower[LANES:]], axis=0)


def table_kernel(props_ref, dft_ref, lb_ref, rf_ref, rb_ref, dl_ref, dr_ref, dc_ref):
    width = props_ref.shape[-1]
    for k in range(props_ref.shape[0]):
        real, imag = props_ref[k, 0], props_ref[k, 1]
        lb_ref[k, :width, :] = real.astype(F32).T.astype(BF16)
        lb_ref[k, width:, :] = imag.astype(F32).T.astype(BF16)
        table = right_table(real, -imag)
        rb_ref[k] = table.astype(BF16)
        rf_ref[k] = table.T.astype(BF16)
    for n, (real, imag) in enumerate(zip(split2(dft_ref[0]), split2(dft_ref[1]))):
        dl_ref[n, :width, :] = real
        dl_ref[n, width:, :] = imag
        dr_ref[n] = right_table(real, imag).astype(BF16)
        dc_ref[n] = right_table(real, -imag).astype(BF16)


def forward_steps(blocks, waves, indices, lf, rf):
    sections, _, columns = blocks.shape
    width = columns // 2

    def step(k, carried):
        which = indices[k]
        z = times(waves[k].astype(F32), with_mean(blocks[k, :width, :])).astype(BF16)
        h = joined(dot(lf[which].reshape(columns, width), z), False).astype(BF16)
        waves[k + 1] = dot(h, rf[which]).astype(BF16)
        return carried

    lax.fori_loop(0, sections, step, 0)


def backward_steps(blocks, waves, indices, lb, rb, grads, g):
    sections, _, columns = blocks.shape
    width = columns // 2

    def step(n, carried):
        k = sections - 1 - n
        which = indices[k]
        c = joined(dot(lb[which], g[...]), True).astype(BF16)
        y = dot(c, rb[which])
        grad, passed = times_conj(y, waves[k].astype(F32), with_mean(blocks[k, :width, :]))
        grads[k] = grad.astype(BF16)
        g[...] = passed.astype(BF16)
        return carried

    lax.fori_loop(0, sections, step, 0)


def detector(psi, observed, left, right, right_conj):
    def product(ah, al, bh, bl):
        return dot(ah, bh) + (dot(ah, bl) + dot(al, bh))

    near = joined(dot(left[0], psi) + dot(left[1], psi), False)
    far = product(*split2(near), right[0], right[1])
    f0, f1, ft = halves(far)
    other = swapped(ft)
    main = f0 * f0 + f1 * f1 - observed[:, :LANES]
    tail = ft * ft + other * other - observed[:, LANES:]
    push = jnp.concatenate([main * f0, main * f1, tail * ft], axis=1)
    back = joined(product(left[0], left[1], *split2(push)), True)
    return product(*split2(back), right_conj[0], right_conj[1]).astype(BF16)


def read_indices(blocks, indices, count):
    for k in range(blocks.shape[0]):
        tag = jnp.max(blocks[k, -ROWS:, 2 * LANES :].astype(F32))
        indices[k] = jnp.clip(tag.astype(jnp.int32), 0, count - 1)


def place_in(size):
    rank = lax.axis_index("cuts")
    return lax.rem(rank, size), lax.div(rank, size)


def brought(pairs, sems):
    copies = [pltpu.make_async_copy(source, target, sems.at[n]) for n, (source, target) in enumerate(pairs)]
    for copy in copies:
        copy.start()
    return copies


def all_here(copies):
    for copy in copies:
        copy.wait()


def first_wave(group_ref, probes, probe, size, sem):
    slot, _ = place_in(size)
    which = group_ref[jnp.minimum(slot, group_ref.shape[0] - 1)]
    return pltpu.make_async_copy(probes.at[which], probe, sem)


def forward_kernel(size, stage):
    def kernel(*refs):
        if stage == 0:
            group_ref, probes, blocks_in, lf_in, rf_in, leaving, waves_out = refs[:7]
        else:
            entering, blocks_in, lf_in, rf_in, _, leaving, waves_out = refs[:7]
        blocks, waves, lf, rf, probe, indices, sems = refs[7:]
        _, group = place_in(size)

        @pl.when(group == stage)
        def _():
            copies = brought([(blocks_in, blocks), (lf_in, lf), (rf_in, rf)], sems)
            if stage == 0:
                copies.append(first_wave(group_ref, probes, probe, size, sems.at[3]))
                copies[-1].start()
            all_here(copies)
            read_indices(blocks, indices, lf.shape[0])
            if stage == 0:
                waves[0] = packed(probe[0], probe[1], probe.shape[-1], 0).astype(BF16)
            else:
                waves[0] = entering[...]
            forward_steps(blocks, waves, indices, lf, rf)
            leaving[...] = waves[size]
            all_here(brought([(waves.at[pl.ds(0, size)], waves_out)], sems))

    return kernel


def middle_kernel(size, groups, near_rows):
    def kernel(*refs):
        if groups == 1:
            group_ref, probes, *refs = refs
        else:
            entering, *refs = refs
        earlier, refs = refs[: groups - 1], refs[groups - 1 :]
        blocks_in, tables_in, refs = refs[0], refs[1:8], refs[8:]
        leaving, grads_out, blocks, waves, grads, probe, g, before, observed, indices, *refs = refs
        tables, sems = refs[:7], refs[7]
        lf, rf, lb, rb, left, right, right_conj = tables
        width = waves.shape[1]
        _, group = place_in(size)

        @pl.when(group == groups - 1)
        def _():
            pairs = [(blocks_in, blocks)] + list(zip(tables_in, tables))
            pairs += [(source, before.at[n]) for n, source in enumerate(earlier)]
            copies = brought(pairs, sems)
            if groups == 1:
                copies.insert(3, first_wave(group_ref, probes, probe, size, sems.at[len(pairs)]))
                copies[3].start()
            needed = 3 + (groups == 1)
            all_here(copies[:needed])
            read_indices(blocks, indices, lf.shape[0])
            if groups == 1:
                waves[0] = packed(probe[0], probe[1], width, 0).astype(BF16)
            else:
                waves[0] = entering[...]
            forward_steps(blocks, waves, indices, lf, rf)
            all_here(copies[needed:])

            def observe(at, block):
                high = block[-2 * ROWS : -ROWS, : 2 * LANES].astype(F32)
                low = block[-ROWS:, : 2 * LANES].astype(F32)
                observed[at * near_rows : (at + 1) * near_rows, :] = (high + low)[:near_rows]

            for k in range(size):
                for n in range(groups - 1):
                    observe(n * size + k, before[n, k])
                observe((groups - 1) * size + k, blocks[k, width:])
            g[...] = detector(waves[size], observed[...], left, right, right_conj)
            backward_steps(blocks, waves, indices, lb, rb, grads, g)
            leaving[...] = g[...]
            all_here(brought([(grads, grads_out)], sems))

    return kernel


def backward_kernel(size, stage):
    def kernel(
        arriving, waves_in, blocks_in, lb_in, rb_in, _, leaving, grads_out,
        blocks, waves, grads, lb, rb, g, indices, sems,
    ):
        _, group = place_in(size)

        @pl.when(group == stage)
        def _():
            all_here(brought([(blocks_in, blocks), (waves_in, waves), (lb_in, lb), (rb_in, rb)], sems))
            read_indices(blocks, indices, lb.shape[0])
            g[...] = arriving[...]
            backward_steps(blocks, waves, indices, lb, rb, grads, g)
            leaving[...] = g[...]
            all_here(brought([(grads, grads_out)], sems))

    return kernel


def gather_kernel(offsets_ref, grads_ref, out_ref):
    positions = offsets_ref.shape[0]
    width = grads_ref.shape[1]
    extent = out_ref.shape[-1]
    spread_out = []
    for p in range(positions):
        x0, x1, xt = halves(grads_ref[p])
        spread_out.append(
            jnp.concatenate(
                [
                    dot(
                        jnp.concatenate([main, xt], axis=1),
                        picker(extent, offsets_ref[p, 1], c == 1, transposed=True),
                    ).astype(BF16)
                    for c, main in ((0, x0), (1, x1))
                ],
                axis=1,
            )
        )
    rows = jnp.concatenate(
        [row_picker((extent, width), -offsets_ref[p, 0]) for p in range(positions)], axis=1
    )
    total = dot(rows, jnp.concatenate(spread_out, axis=0))
    out_ref[0, 0] = total[:, :extent]
    out_ref[0, 1] = total[:, extent:]


VMEM = pl.BlockSpec(memory_space=pltpu.VMEM)
SMEM = pl.BlockSpec(memory_space=pltpu.SMEM)
HBM = pl.BlockSpec(memory_space=pl.ANY)
PARAMS = pltpu.CompilerParams(vmem_limit_bytes=56 * 1024 * 1024)


def shards(objects, propagators, prop_index, probes, probe_group, offsets, measured):
    sections = lax.axis_size("cuts")
    width = probes.shape[-1]
    kinds = propagators.shape[0]
    near_rows = measured.shape[1]
    size = GROUP
    groups = sections // size
    rows = width + 2 * ROWS
    members = [list(range(first, first + size)) for first in range(0, sections, size)]

    def struct(*dims, kind=BF16):
        return jax.ShapeDtypeStruct(dims, kind)

    def exchanged(blocks):
        return lax.all_to_all(blocks, "cuts", 0, 0, axis_index_groups=members, tiled=True)

    def handed(block, stage, distance):
        route = [(stage * size + l, (stage + distance) * size + l) for l in range(probe_group.shape[0])]
        return lax.ppermute(block, "cuts", route)

    blocks = pl.pallas_call(
        window_kernel,
        out_shape=struct(size, rows, 2 * width),
        in_specs=[SMEM, SMEM, VMEM, VMEM],
        out_specs=VMEM,
        compiler_params=PARAMS,
        name="windows",
    )(offsets, prop_index, objects, measured)
    blocks = exchanged(blocks)

    tables = pl.pallas_call(
        table_kernel,
        out_shape=[
            struct(kinds, 2 * width, width),
            struct(kinds, 2 * width, 2 * width),
            struct(kinds, 2 * width, 2 * width),
            struct(2, 2 * width, width),
            struct(2, 2 * width, 2 * width),
            struct(2, 2 * width, 2 * width),
        ],
        in_specs=[VMEM, VMEM],
        out_specs=[VMEM] * 6,
        compiler_params=PARAMS,
        cost_estimate=pl.CostEstimate(flops=10**9, bytes_accessed=6 * 10**6, transcendentals=0),
        name="tables",
    )(propagators, jnp.asarray(dft_constant(width)))
    lf, lb, rf, rb = propagators, *tables[:3]
    dft = tables[3:]

    wave = (width, 2 * width)
    block_scratch = pltpu.VMEM((size, rows, 2 * width), BF16)
    waves_scratch = pltpu.VMEM((size + 1,) + wave, BF16)
    grads_scratch = pltpu.VMEM((size,) + wave, BF16)
    probe_scratch = pltpu.VMEM(probes.shape[1:], BF16)
    indices = pltpu.SMEM((size,), jnp.int32)

    def like(*arrays):
        return [pltpu.VMEM(array.shape, array.dtype) for array in arrays]

    entering, waves, nears = None, None, []
    for stage in range(groups - 1):
        nears.append(handed(blocks[:, width:], stage, groups - 1 - stage))
        first = stage == 0
        leaving, waves = pl.pallas_call(
            forward_kernel(size, stage),
            out_shape=[struct(*wave), struct(size, *wave)],
            in_specs=[SMEM] + [HBM] * 4 if first else [VMEM] + [HBM] * 4,
            out_specs=[VMEM, HBM],
            scratch_shapes=[block_scratch, waves_scratch]
            + like(lf, rf)
            + [probe_scratch, indices, pltpu.SemaphoreType.DMA((4,))],
            input_output_aliases={} if first else {4: 1},
            compiler_params=PARAMS,
            name="forward",
        )(*((probe_group, probes, blocks, lf, rf) if first else (entering, blocks, lf, rf, waves)))
        entering = handed(leaving, stage, 1)

    alone = groups == 1
    leaving, grads = pl.pallas_call(
        middle_kernel(size, groups, near_rows),
        out_shape=[struct(*wave), struct(size, *wave)],
        in_specs=([SMEM, HBM] if alone else [VMEM]) + [HBM] * (groups - 1 + 8),
        out_specs=[VMEM, HBM],
        scratch_shapes=[
            block_scratch,
            waves_scratch,
            grads_scratch,
            probe_scratch,
            pltpu.VMEM(wave, BF16),
            pltpu.VMEM((max(groups - 1, 1), size, 2 * ROWS, 2 * width), BF16),
            pltpu.VMEM((width, 2 * LANES), F32),
            indices,
        ]
        + like(lf, rf, lb, rb, *dft)
        + [pltpu.SemaphoreType.DMA((9 + groups,))],
        compiler_params=PARAMS,
        name="middle",
    )(*((probe_group, probes) if alone else (entering,)), *nears, blocks, lf, rf, lb, rb, *dft)

    for stage in range(groups - 2, -1, -1):
        arriving = handed(leaving, stage + 1, -1)
        leaving, grads = pl.pallas_call(
            backward_kernel(size, stage),
            out_shape=[struct(*wave), struct(size, *wave)],
            in_specs=[VMEM] + [HBM] * 5,
            out_specs=[VMEM, HBM],
            scratch_shapes=[block_scratch, pltpu.VMEM((size,) + wave, BF16), grads_scratch]
            + like(lb, rb)
            + [pltpu.VMEM(wave, BF16), indices, pltpu.SemaphoreType.DMA((4,))],
            input_output_aliases={5: 1},
            compiler_params=PARAMS,
            name="backward",
        )(arriving, waves, blocks, lb, rb, grads)

    return pl.pallas_call(
        gather_kernel,
        out_shape=jax.ShapeDtypeStruct(objects.shape, F32),
        in_specs=[SMEM, VMEM],
        out_specs=VMEM,
        compiler_params=PARAMS,
        name="sum_windows",
    )(offsets, exchanged(grads))


def solution(mesh):
    in_specs = (
        P(("parts", "cuts"), None, None, None),
        P(),
        P(("parts", "cuts")),
        P(),
        P(),
        P("parts", None),
        P("parts", "cuts", None),
    )
    out_specs = P(("parts", "cuts"), None, None, None)
    return jax.shard_map(shards, mesh=mesh, in_specs=in_specs, out_specs=out_specs, check_vma=False)
```

time: 172 us -> 113 us (0.66)
  waiting for transfers between devices: 52.6 us -> 23.9 us
  blocking collectives: 67.8 us -> 45.9 us
  local copies, waits for them, and re-layouts: 10.6 us -> 2.76 us
    all_to_all x1 -> x0, waiting for transfers between devices: 52.6 us -> none  [shards(): blocks = lax.all_to_all(blocks, 'cuts', 0, 0, tiled=True)]
    ppermute x0 -> x3, waiting for transfers between devices: none -> 23.9 us  [handed(): return lax.ppermute(block, 'cuts', route)]
    all_to_all x1 -> x2, blocking collectives: 67.8 us -> 45.9 us  [exchanged(): lax.all_to_all(blocks, 'cuts', 0, 0, axis_index_groups=members, tiled=True)]
    unnamed x27 -> x9, local copies, waits for them, and re-layouts: 10.6 us -> 2.74 us
    all_to_all x1 -> x0, starting transfers between devices: 7.55 us -> none  [shards(): blocks = lax.all_to_all(blocks, 'cuts', 0, 0, tiled=True)]
    ppermute x0 -> x3, starting transfers between devices: none -> 7.08 us  [handed(): return lax.ppermute(block, 'cuts', route)]
    pallas_call x2 -> x5, Pallas kernels: 28.5 us -> 28.6 us  [the longest x1 9.61 us: shards(): pl.pallas_call(backward_kernel(size, stage), out_shape=[struct(*wave), st...]
  transfers between devices with their start and end apart: 1 -> 3, of which waited for: 1 -> 2; matrix products, arithmetic and copies ran while one was open for 0% -> 0% of each run, Pallas kernels for 0% -> 12%
where the time goes in v3:
time: 113 us
  blocking collectives  45.9 us (41%)
  Pallas kernels  32.5 us (29%)
  waiting for transfers between devices  23.9 us (21%)
  starting transfers between devices  7.08 us (6%)
  local copies, waits for them, and re-layouts  2.76 us (2%)
    all_to_all x2, blocking collectives, exchanged(): lax.all_to_all(blocks, 'cuts', 0, 0, axis_index_groups=members, tiled=True)  45.9 us
    ppermute x3, waiting for transfers between devices, handed(): return lax.ppermute(block, 'cuts', route)  23.9 us
    pallas_call x1, Pallas kernels, shards(): pl.pallas_call(backward_kernel(size, stage), out_shape=[struct(*wave), st...  9.61 us
    pallas_call x1, Pallas kernels, shards(): pl.pallas_call(forward_kernel(size, stage), out_shape=[struct(*wave), str...  8.91 us
    ppermute x3, starting transfers between devices, handed(): return lax.ppermute(block, 'cuts', route)  7.08 us
    pallas_call x1, Pallas kernels, shards(): pl.pallas_call(window_kernel, out_shape=struct(size, rows, 2 * width), in...  4.25 us
    pallas_call x1, Pallas kernels, shards(): pl.pallas_call(table_kernel, out_shape=[struct(kinds, 2 * width, width),...  4.16 us
    pallas_call x1, Pallas kernels, shards(): pl.pallas_call(gather_kernel, out_shape=jax.ShapeDtypeStruct(objects.shap...  3.91 us
  transfers between devices with their start and end apart: 3, of which 2 were waited for; matrix products, arithmetic and copies ran while one was open for 0% of the time, Pallas kernels for 12%

profile of v3, /device:TPU:0, one launch (start us, length us, event | category | flops | bytes accessed | tf_op | source)
XLA Modules:
  0.0 112.8 jit_solution(11654104014713289559)
XLA Ops:
  0.7 1.3 %copy.11.offsets_ref = s32[6,2]{1,0:T(8,128)} copy(s32[6,2]{0,1:T(2,128)} %param.13) | data formatting | bytes 96 | tf_op args[5]
  2.0 4.3 %windows.1 = bf16[8,224,384]{2,1,0:T(8,128)(2,1)} custom-call(s32[6,2]{1,0:T(8,128)} %copy.11.offsets_ref, s32[1]{0:T(128)S(6)} %copy.13.index_ref, bf16[1,2,384,384]{3,2,1,0:T(8,128)(2,1)} %objects_ref.1, f32[6,12,192]{2,1,0:T(8,128)} %measured_ref.1), custom_call_target="tpu_custom_call" | custom-call | tf_op jit(solution)/shard_map/windows/pallas_call | solution.py:388
  6.3 24.2 %all_to_all.10.refs_2_.blocks_in = bf16[8,224,384]{2,1,0:T(8,128)(2,1)S(1)} all-to-all(bf16[8,224,384]{2,1,0:T(8,128)(2,1)} %windows.1), channel_id=1, replica_groups={{0,1,2,3,4,5,6,7},{8,9,10,11,12,13,14,15},{16,17,18,19,20,21,22,23},{24..., dimensions={0} | all-to-all | bytes 2752512 | tf_op jit(solution)/shard_map/all_to_all | solution.py:382
  30.4 0.0 copy-start
  30.4 4.5 %collective-permute-start.1 = (bf16[8,32,384]{2,1,0:T(8,128)(2,1)S(1)}, bf16[8,32,384]{2,1,0:T(8,128)(2,1)S(1)}, u32[]{:S(2)}, u32[]{:S(2)}) collective-permute-start(bf16[8,32,384]{2,1,0:T(8,128)(2,1)S(1)} %slice.4), channel_id=1, source_target_pairs={{0,8},{1,9},{2,10},{3,11},{4,12},{5,13},{16,24},{17,25},{18,26},{1... | collective-permute-start | bytes 589832 | tf_op jit(solution)/shard_map/ppermute | solution.py:386
  34.9 4.2 %tables.1 = (bf16[4,384,192]{2,1,0:T(8,128)(2,1)}, bf16[4,384,384]{2,1,0:T(8,128)(2,1)}, bf16[4,384,384]{2,1,0:T(8,128)(2,1)}, bf16[2,384,192]{2,1,0:T(8,128)(2,...) custom-call(bf16[4,2,192,192]{3,2,1,0:T(8,128)(2,1)} %refs_3_.3, f32[2,192,192]{2,1,0:T(8,128)} %constant.2.clone.dft_ref), custom_call_target="tpu_custom_call" | custom-call | flops 1000000000 | bytes 6000000 | tf_op jit(solution)/shard_map/tables/pallas_call | solution.py:398
  39.1 0.0 copy-done
  39.1 8.9 %forward.1 = (bf16[192,384]{1,0:T(8,128)(2,1)}, bf16[8,192,384]{2,1,0:T(8,128)(2,1)}) custom-call(s32[6]{0:T(128)} %refs_0_.1, bf16[8,2,192,192]{3,2,1,0:T(8,128)(2,1)} %refs_1_.1, bf16[8,224,384]{2,1,0:T(8,128)(2,1)} %copy-done, bf16[4,2,192,192]{3,2,1,0:T(8,128)(2,1)} %refs_3_.3, bf16[4,384,384]{2,1,0:T(8,128)(2,1)} %get-tuple-element.16.refs_4_), custom_call_target="tpu_custom_call" | custom-call | tf_op jit(solution)/shard_map/forward/pallas_call | solution.py:431
  48.0 1.3 %collective-permute-start = (bf16[192,384]{1,0:T(8,128)(2,1)}, bf16[192,384]{1,0:T(8,128)(2,1)S(1)}, u32[]{:S(2)}, u32[]{:S(2)}) collective-permute-start(bf16[192,384]{1,0:T(8,128)(2,1)} %get-tuple-element.17), channel_id=1, source_target_pairs={{0,8},{1,9},{2,10},{3,11},{4,12},{5,13},{16,24},{17,25},{18,26},{1... | collective-permute-start | bytes 442376 | tf_op jit(solution)/shard_map/ppermute | solution.py:386
  49.3 3.3 %collective-permute-done.refs_0_ = bf16[192,384]{1,0:T(8,128)(2,1)S(1)} collective-permute-done((bf16[192,384]{1,0:T(8,128)(2,1)}, bf16[192,384]{1,0:T(8,128)(2,1)S(1)}, u32[]{:S(2)}, u32[]{:S(2)}) %collective-permute-start) | collective-permute-done | bytes 147488 | tf_op jit(solution)/shard_map/ppermute | solution.py:386
  52.7 0.0 copy-start.3
  52.7 0.0 collective-permute-done.1.refs_1_
  52.7 0.0 copy-start.1
  52.7 0.6 copy-done.3
  53.3 0.1 copy-done.1
  53.4 1.7 %middle.1 = (bf16[192,384]{1,0:T(8,128)(2,1)}, bf16[8,192,384]{2,1,0:T(8,128)(2,1)}) custom-call(bf16[192,384]{1,0:T(8,128)(2,1)} %copy-done.3, bf16[8,32,384]{2,1,0:T(8,128)(2,1)} %copy-done.1, bf16[8,224,384]{2,1,0:T(8,128)(2,1)} %copy-done, bf16[4,2,192,192]{3,2,1,0:T(8,128)(2,1)} %refs_3_.3, bf16[4,384,384]{2,1,0:T(8,128)(2,1)} %get-tuple-element.16.refs_4_, ...), custom_call_target="tpu_custom_call" | custom-call | tf_op jit(solution)/shard_map/middle/pallas_call | solution.py:446
  55.1 1.3 %collective-permute-start.2 = (bf16[192,384]{1,0:T(8,128)(2,1)}, bf16[192,384]{1,0:T(8,128)(2,1)S(1)}, u32[]{:S(2)}, u32[]{:S(2)}) collective-permute-start(bf16[192,384]{1,0:T(8,128)(2,1)} %get-tuple-element.23), channel_id=1, source_target_pairs={{8,0},{9,1},{10,2},{11,3},{12,4},{13,5},{24,16},{25,17},{26,18},{2... | collective-permute-start | bytes 442376 | tf_op jit(solution)/shard_map/ppermute | solution.py:386
  56.4 20.5 %collective-permute-done.2.arriving = bf16[192,384]{1,0:T(8,128)(2,1)S(1)} collective-permute-done((bf16[192,384]{1,0:T(8,128)(2,1)}, bf16[192,384]{1,0:T(8,128)(2,1)S(1)}, u32[]{:S(2)}, u32[]{:S(2)}) %collective-permute-start.2) | collective-permute-done | bytes 147488 | tf_op jit(solution)/shard_map/ppermute | solution.py:386
  76.9 0.0 copy-start.2
  76.9 0.7 copy-done.2
  77.5 9.6 %backward.1 = (bf16[192,384]{1,0:T(8,128)(2,1)}, bf16[8,192,384]{2,1,0:T(8,128)(2,1)}) custom-call(bf16[192,384]{1,0:T(8,128)(2,1)} %copy-done.2, bf16[8,192,384]{2,1,0:T(8,128)(2,1)} %get-tuple-element.24.waves_in, bf16[8,224,384]{2,1,0:T(8,128)(2,1)} %copy-done, ...), custom_call_target="tpu_custom_call", output_to_operand_aliasing={{1}: (5, {})} | custom-call | tf_op jit(solution)/shard_map/backward/pallas_call | solution.py:469
  87.2 21.8 %all_to_all.11.grads_ref = bf16[8,192,384]{2,1,0:T(8,128)(2,1)} all-to-all(bf16[8,192,384]{2,1,0:T(8,128)(2,1)} %get-tuple-element.26), channel_id=1, replica_groups={{0,1,2,3,4,5,6,7},{8,9,10,11,12,13,14,15},{16,17,18,19,20,21,22,23},{24..., dimensions={0} | all-to-all | bytes 2359296 | tf_op jit(solution)/shard_map/all_to_all | solution.py:382
  108.9 3.9 %sum_windows.1 = f32[1,2,384,384]{3,2,1,0:T(8,128)} custom-call(s32[6,2]{1,0:T(8,128)} %copy.11.offsets_ref, bf16[8,192,384]{2,1,0:T(8,128)(2,1)} %all_to_all.11.grads_ref), custom_call_target="tpu_custom_call" | custom-call | tf_op jit(solution)/shard_map/sum_windows/pallas_call | solution.py:482
  (1 shorter events, 0.0 us)
Async XLA Ops:
  30.4 8.7 %copy-start = (bf16[8,224,384]{2,1,0:T(8,128)(2,1)}, bf16[8,224,384]{2,1,0:T(8,128)(2,1)S(1)}, u32[]{:S(2)}) copy-start(bf16[8,224,384]{2,1,0:T(8,128)(2,1)S(1)} %all_to_all.10.refs_2_.blocks_in) | copy-start | bytes 4128772
  30.4 22.2 %collective-permute-start.1 = (bf16[8,32,384]{2,1,0:T(8,128)(2,1)S(1)}, bf16[8,32,384]{2,1,0:T(8,128)(2,1)S(1)}, u32[]{:S(2)}, u32[]{:S(2)}) collective-permute-start(bf16[8,32,384]{2,1,0:T(8,128)(2,1)S(1)} %slice.4), channel_id=1, source_target_pairs={{0,8},{1,9},{2,10},{3,11},{4,12},{5,13},{16,24},{17,25},{18,26},{1... | collective-permute-start | bytes 589832 | tf_op jit(solution)/shard_map/ppermute | solution.py:386
  48.0 4.7 %collective-permute-start = (bf16[192,384]{1,0:T(8,128)(2,1)}, bf16[192,384]{1,0:T(8,128)(2,1)S(1)}, u32[]{:S(2)}, u32[]{:S(2)}) collective-permute-start(bf16[192,384]{1,0:T(8,128)(2,1)} %get-tuple-element.17), channel_id=1, source_target_pairs={{0,8},{1,9},{2,10},{3,11},{4,12},{5,13},{16,24},{17,25},{18,26},{1... | collective-permute-start | bytes 442376 | tf_op jit(solution)/shard_map/ppermute | solution.py:386
  52.7 0.7 copy-start.3
  52.7 0.7 copy-start.1
  55.1 21.8 %collective-permute-start.2 = (bf16[192,384]{1,0:T(8,128)(2,1)}, bf16[192,384]{1,0:T(8,128)(2,1)S(1)}, u32[]{:S(2)}, u32[]{:S(2)}) collective-permute-start(bf16[192,384]{1,0:T(8,128)(2,1)} %get-tuple-element.23), channel_id=1, source_target_pairs={{8,0},{9,1},{10,2},{11,3},{12,4},{13,5},{24,16},{25,17},{26,18},{2... | collective-permute-start | bytes 442376 | tf_op jit(solution)/shard_map/ppermute | solution.py:386
  76.9 0.7 copy-start.2

commit v4 on v3

v4 whole, which is shorter than its diff:
```python
import math

import jax
import jax.numpy as jnp
import numpy as np
from jax import lax
from jax.experimental import pallas as pl
from jax.experimental.pallas import tpu as pltpu
from jax.sharding import PartitionSpec as P

TRANSMIT = 0.985
GROUP = 8
LANES = 128
ROWS = 16
F32 = jnp.float32
BF16 = jnp.bfloat16


def dot(former, latter):
    return jnp.dot(former, latter, preferred_element_type=F32)


def halves(x):
    return x[:, :LANES], x[:, LANES : 2 * LANES], x[:, 2 * LANES :]


def swapped(tail):
    return pltpu.roll(tail, LANES // 2, 1)


def low_half(rows):
    return lax.broadcasted_iota(jnp.int32, (rows, LANES), 1) < LANES // 2


def spread(tail):
    other = swapped(tail)
    low = low_half(tail.shape[0])
    return jnp.where(low, tail, other), jnp.where(low, other, tail)


def signed(tail, minus_low):
    low = low_half(tail.shape[0])
    return jnp.where(low == minus_low, -tail, tail)


def times(a, b):
    a0, a1, at = halves(a)
    b0, b1, bt = halves(b)
    b_real, b_imag = spread(bt)
    tail = at * b_real + signed(swapped(at), True) * b_imag
    return jnp.concatenate([a0 * b0 - a1 * b1, a1 * b0 + a0 * b1, tail], axis=1)


def times_conj(a, *others):
    a0, a1, at = halves(a)
    turned = signed(swapped(at), False)
    results = []
    for b in others:
        b0, b1, bt = halves(b)
        b_real, b_imag = spread(bt)
        tail = at * b_real + turned * b_imag
        results.append(jnp.concatenate([a0 * b0 + a1 * b1, a1 * b0 - a0 * b1, tail], axis=1))
    return results


def joined(both, conj):
    width = both.shape[0] // 2
    u0, u1, ut = halves(both[:width])
    v0, v1, vt = halves(both[width:])
    turned = signed(swapped(vt), not conj)
    if conj:
        return jnp.concatenate([u0 + v1, u1 - v0, ut + turned], axis=1)
    return jnp.concatenate([u0 - v1, u1 + v0, ut + turned], axis=1)


def with_mean(window):
    x = window.astype(F32)
    x0, x1, xt = halves(x)
    mean = jnp.where(low_half(xt.shape[0]), TRANSMIT, 0.0)
    return jnp.concatenate([TRANSMIT + x0, x1, mean + xt], axis=1)


def split2(x):
    high = x.astype(BF16)
    return high, (x - high.astype(F32)).astype(BF16)


def picker(columns, start, high_tail, transposed=False):
    shape = (2 * LANES, columns) if transposed else (columns, 2 * LANES)
    a = lax.broadcasted_iota(jnp.int32, shape, 1 if transposed else 0) - start
    q = lax.broadcasted_iota(jnp.int32, shape, 0 if transposed else 1)
    if high_tail:
        half = LANES // 2
        wanted = jnp.where(q < LANES, q, jnp.where(q < LANES + half, -columns, q - half))
    else:
        wanted = jnp.where(q < LANES + LANES // 2, q, -columns)
    return jnp.where(a == wanted, 1.0, 0.0).astype(BF16)


def row_picker(shape, distance):
    taken = lax.broadcasted_iota(jnp.int32, shape, 1)
    wanted = lax.broadcasted_iota(jnp.int32, shape, 0) + distance
    return jnp.where(taken == wanted, 1.0, 0.0).astype(BF16)


def packed(real, imag, columns, start):
    left = dot(real, picker(columns, start, False))
    right = dot(imag, picker(columns, start, True))
    return jnp.concatenate(
        [left[:, :LANES], right[:, :LANES], left[:, LANES:] + right[:, LANES:]], axis=1
    )


def dft_constant(width):
    counter = np.arange(width)
    angle = (counter[:, None] * counter[None, :] % width) * (2.0 * math.pi / width)
    return (np.stack([np.cos(angle), -np.sin(angle)]) / math.sqrt(width)).astype(np.float32)


def window_kernel(offsets_ref, index_ref, objects_ref, measured_ref, blocks):
    positions, near_rows, width = measured_ref.shape
    extent = objects_ref.shape[-1]
    tag = jnp.full((ROWS, LANES), index_ref[0], jnp.int32).astype(F32).astype(BF16)
    blank = jnp.zeros((ROWS - near_rows, 2 * LANES), F32)
    field = jnp.concatenate([objects_ref[0, 0], objects_ref[0, 1]], axis=1)
    for p in range(positions):
        both = dot(row_picker((width, extent), offsets_ref[0, p]), field).astype(BF16)
        window = packed(both[:, :extent], both[:, extent:], extent, offsets_ref[1, p])
        blocks[p, :width, :] = window.astype(BF16)
        high, low = split2(jnp.concatenate([doubled(measured_ref[p]), blank], axis=0))
        for place, part in ((width, high), (width + ROWS, low)):
            blocks[p, place : place + ROWS, : 2 * LANES] = part
            blocks[p, place : place + ROWS, 2 * LANES :] = tag


def doubled(rows):
    tail = jnp.concatenate([rows[:, LANES:]] * 2, axis=1)
    return jnp.concatenate([rows[:, :LANES], tail], axis=1)


def right_table(real, imag):
    width = real.shape[0]
    upper = packed(real, imag, width, 0)
    lower = packed(-imag, real, width, 0)
    return jnp.concatenate([upper[:LANES], lower[:LANES], upper[LANES:], lower[LANES:]], axis=0)


def transposed(plane):
    return plane.astype(F32).T.astype(BF16)


def forward_tables(props, rf):
    for k in range(props.shape[0]):
        rf[k] = right_table(transposed(props[k, 0]), transposed(props[k, 1])).astype(BF16)


def backward_tables(props, lb, rb):
    width = props.shape[-1]
    for k in range(props.shape[0]):
        real, imag = props[k, 0], props[k, 1]
        lb[k, :width, :] = transposed(real)
        lb[k, width:, :] = transposed(imag)
        rb[k] = right_table(real, -imag).astype(BF16)


def detector_tables(dft, left, right, right_conj):
    width = dft.shape[-1]
    for n, (real, imag) in enumerate(zip(split2(dft[0]), split2(dft[1]))):
        left[n, :width, :] = real
        left[n, width:, :] = imag
        right[n] = right_table(real, imag).astype(BF16)
        right_conj[n] = right_table(real, -imag).astype(BF16)


def forward_steps(blocks, waves, indices, lf, rf):
    sections, _, columns = blocks.shape
    width = columns // 2

    def step(k, carried):
        which = indices[k]
        z = times(waves[k].astype(F32), with_mean(blocks[k, :width, :])).astype(BF16)
        h = joined(dot(lf[which].reshape(columns, width), z), False).astype(BF16)
        waves[k + 1] = dot(h, rf[which]).astype(BF16)
        return carried

    lax.fori_loop(0, sections, step, 0, unroll=2)


def backward_steps(blocks, waves, indices, lb, rb, grads, g):
    sections, _, columns = blocks.shape
    width = columns // 2

    def step(n, carried):
        k = sections - 1 - n
        which = indices[k]
        c = joined(dot(lb[which], g[...]), True).astype(BF16)
        y = dot(c, rb[which])
        grad, passed = times_conj(y, waves[k].astype(F32), with_mean(blocks[k, :width, :]))
        grads[k] = grad.astype(BF16)
        g[...] = passed.astype(BF16)
        return carried

    lax.fori_loop(0, sections, step, 0, unroll=2)


def detector(psi, observed, left, right, right_conj):
    def product(ah, al, bh, bl):
        return dot(ah, bh) + (dot(ah, bl) + dot(al, bh))

    near = joined(dot(left[0], psi) + dot(left[1], psi), False)
    far = product(*split2(near), right[0], right[1])
    f0, f1, ft = halves(far)
    other = swapped(ft)
    main = f0 * f0 + f1 * f1 - observed[:, :LANES]
    tail = ft * ft + other * other - observed[:, LANES:]
    push = jnp.concatenate([main * f0, main * f1, tail * ft], axis=1)
    back = joined(product(left[0], left[1], *split2(push)), True)
    return product(*split2(back), right_conj[0], right_conj[1]).astype(BF16)


def read_indices(blocks, indices, count):
    for k in range(blocks.shape[0]):
        tag = jnp.max(blocks[k, -ROWS:, 2 * LANES :].astype(F32))
        indices[k] = jnp.clip(tag.astype(jnp.int32), 0, count - 1)


def place_in(size):
    rank = lax.axis_index("cuts")
    return lax.rem(rank, size), lax.div(rank, size)


def observe(blocks, near_rows, observed, first):
    for k in range(blocks.shape[0]):
        high = blocks[k, -2 * ROWS : -ROWS, : 2 * LANES].astype(F32)
        low = blocks[k, -ROWS:, : 2 * LANES].astype(F32)
        at = first + k * near_rows
        observed[at : at + near_rows, :] = (high + low)[:near_rows]


def first_kernel(group_ref, probes, blocks, props, dft, leaving, near, waves, lb, rf, rb, left, right, right_conj, probe, indices, sem):
    size = blocks.shape[0]
    slot, group = place_in(size)

    @pl.when(group == 0)
    def _():
        which = group_ref[jnp.minimum(slot, group_ref.shape[0] - 1)]
        copy = pltpu.make_async_copy(probes.at[which], probe, sem)
        copy.start()
        forward_tables(props, rf)
        read_indices(blocks, indices, props.shape[0])
        copy.wait()
        waves[0] = packed(probe[0], probe[1], probe.shape[-1], 0).astype(BF16)
        forward_steps(blocks, waves, indices, props, rf)
        leaving[...] = waves[size]
        observe(blocks, near.shape[0] // size, near, 0)

    @pl.when(group > 0)
    def _():
        forward_tables(props, rf)
        backward_tables(props, lb, rb)
        detector_tables(dft, left, right, right_conj)


def forward_kernel(stage):
    def kernel(entering, blocks, props, rf, waves_in, leaving, near, waves, indices):
        size = blocks.shape[0]
        _, group = place_in(size)

        @pl.when(group == stage)
        def _():
            read_indices(blocks, indices, props.shape[0])
            waves[0] = entering[...]
            forward_steps(blocks, waves, indices, props, rf)
            leaving[...] = waves[size]
            observe(blocks, near.shape[0] // size, near, 0)

        @pl.when(group != stage)
        def _():
            waves[...] = waves_in[...]

    return kernel


def middle_kernel(groups):
    def kernel(entering, *refs):
        earlier, refs = refs[: groups - 1], refs[groups - 1 :]
        blocks, props, lb, rf, rb, left, right, right_conj, leaving, grads, lb_out, rb_out = refs[:12]
        waves, g, observed, indices = refs[12:]
        size = blocks.shape[0]
        _, group = place_in(size)

        @pl.when(group == groups - 1)
        def _():
            read_indices(blocks, indices, props.shape[0])
            waves[0] = entering[...]
            forward_steps(blocks, waves, indices, props, rf)
            rows = earlier[0].shape[0]
            for n, near in enumerate(earlier):
                observed[n * rows : (n + 1) * rows, :] = near[...]
            observe(blocks, rows // size, observed, (groups - 1) * rows)
            g[...] = detector(waves[size], observed[...], left, right, right_conj)
            backward_steps(blocks, waves, indices, lb, rb, grads, g)
            leaving[...] = g[...]

        @pl.when(group < groups - 1)
        def _():
            backward_tables(props, lb_out, rb_out)

    return kernel


def backward_kernel(stage):
    def kernel(arriving, waves, blocks, lb, rb, grads_in, leaving, grads, g, indices):
        _, group = place_in(blocks.shape[0])

        @pl.when(group == stage)
        def _():
            read_indices(blocks, indices, lb.shape[0])
            g[...] = arriving[...]
            backward_steps(blocks, waves, indices, lb, rb, grads, g)
            leaving[...] = g[...]

        @pl.when(group != stage)
        def _():
            grads[...] = grads_in[...]

    return kernel


def gather_kernel(offsets_ref, grads_ref, out_ref):
    positions = offsets_ref.shape[1]
    width = grads_ref.shape[1]
    extent = out_ref.shape[-1]
    spread_out = []
    for p in range(positions):
        x0, x1, xt = halves(grads_ref[p])
        spread_out.append(
            jnp.concatenate(
                [
                    dot(
                        jnp.concatenate([main, xt], axis=1),
                        picker(extent, offsets_ref[1, p], c == 1, transposed=True),
                    ).astype(BF16)
                    for c, main in ((0, x0), (1, x1))
                ],
                axis=1,
            )
        )
    rows = jnp.concatenate(
        [row_picker((extent, width), -offsets_ref[0, p]) for p in range(positions)], axis=1
    )
    total = dot(rows, jnp.concatenate(spread_out, axis=0))
    out_ref[0, 0] = total[:, :extent]
    out_ref[0, 1] = total[:, extent:]


VMEM = pl.BlockSpec(memory_space=pltpu.VMEM)
SMEM = pl.BlockSpec(memory_space=pltpu.SMEM)
HBM = pl.BlockSpec(memory_space=pl.ANY)
PARAMS = pltpu.CompilerParams(vmem_limit_bytes=20 * 1024 * 1024)


def shards(objects, propagators, prop_index, probes, probe_group, offsets, measured):
    sections = lax.axis_size("cuts")
    width = probes.shape[-1]
    kinds = propagators.shape[0]
    near_rows = measured.shape[1]
    size = GROUP
    groups = sections // size
    rows = width + 2 * ROWS
    members = [list(range(first, first + size)) for first in range(0, sections, size)]

    def struct(*dims, kind=BF16):
        return jax.ShapeDtypeStruct(dims, kind)

    def exchanged(blocks):
        return lax.all_to_all(blocks, "cuts", 0, 0, axis_index_groups=members, tiled=True)

    def handed(block, stage, distance):
        route = [(stage * size + l, (stage + distance) * size + l) for l in range(probe_group.shape[0])]
        return lax.ppermute(block, "cuts", route)

    blocks = pl.pallas_call(
        window_kernel,
        out_shape=struct(size, rows, 2 * width),
        in_specs=[SMEM, SMEM, VMEM, VMEM],
        out_specs=VMEM,
        compiler_params=PARAMS,
        name="windows",
    )(offsets.T, prop_index, objects, measured)
    blocks = exchanged(blocks)

    wave = struct(width, 2 * width)
    near = struct(size * near_rows, 2 * LANES, kind=F32)
    waves_shape = struct(size + 1, width, 2 * width)
    grads_shape = struct(size, width, 2 * width)
    left_table = struct(kinds, 2 * width, width)
    square_table = struct(kinds, 2 * width, 2 * width)
    detector_left = struct(2, 2 * width, width)
    detector_right = struct(2, 2 * width, 2 * width)
    indices = pltpu.SMEM((size,), jnp.int32)

    def scratch(shape):
        return pltpu.VMEM(shape.shape, shape.dtype)

    def call(kernel, name, out_shape, in_specs, scratch_shapes, operands):
        return pl.pallas_call(
            kernel,
            out_shape=out_shape,
            in_specs=in_specs,
            out_specs=[VMEM] * len(out_shape),
            scratch_shapes=scratch_shapes,
            compiler_params=PARAMS,
            name=name,
        )(*operands)

    leaving, near_out, waves, lb, rf, rb, *dft = call(
        first_kernel,
        "first_forward",
        [wave, near, waves_shape, left_table, square_table, square_table]
        + [detector_left, detector_right, detector_right],
        [SMEM, HBM, VMEM, VMEM, VMEM],
        [pltpu.VMEM(probes.shape[1:], BF16), indices, pltpu.SemaphoreType.DMA],
        (probe_group, probes, blocks, propagators, jnp.asarray(dft_constant(width))),
    )
    entering = handed(leaving, 0, 1)
    nears = [handed(near_out, 0, groups - 1)]
    for stage in range(1, groups - 1):
        leaving, near_out, waves = call(
            forward_kernel(stage),
            "forward",
            [wave, near, waves_shape],
            [VMEM] * 5,
            [indices],
            (entering, blocks, propagators, rf, waves),
        )
        entering = handed(leaving, stage, 1)
        nears.append(handed(near_out, stage, groups - 1 - stage))

    leaving, grads, lb, rb = call(
        middle_kernel(groups),
        "middle",
        [wave, grads_shape, left_table, square_table],
        [VMEM] * (groups + 8),
        [scratch(waves_shape), scratch(wave), pltpu.VMEM((width, 2 * LANES), F32), indices],
        (entering, *nears, blocks, propagators, lb, rf, rb, *dft),
    )

    for stage in range(groups - 2, -1, -1):
        arriving = handed(leaving, stage + 1, -1)
        leaving, grads = call(
            backward_kernel(stage),
            "backward",
            [wave, grads_shape],
            [VMEM] * 6,
            [scratch(wave), indices],
            (arriving, waves, blocks, lb, rb, grads),
        )

    return pl.pallas_call(
        gather_kernel,
        out_shape=jax.ShapeDtypeStruct(objects.shape, F32),
        in_specs=[SMEM, VMEM],
        out_specs=VMEM,
        compiler_params=PARAMS,
        name="sum_windows",
    )(offsets.T, exchanged(grads))


def solution(mesh):
    in_specs = (
        P(("parts", "cuts"), None, None, None),
        P(),
        P(("parts", "cuts")),
        P(),
        P(),
        P("parts", None),
        P("parts", "cuts", None),
    )
    out_specs = P(("parts", "cuts"), None, None, None)
    return jax.shard_map(shards, mesh=mesh, in_specs=in_specs, out_specs=out_specs, check_vma=False)
```

time: 113 us -> 93.9 us (0.83)
  Pallas kernels: 32.5 us -> 17.5 us
  waiting for transfers between devices: 23.9 us -> 20.7 us
  starting transfers between devices: 7.08 us -> 3.89 us
  blocking collectives: 45.9 us -> 48 us
    pallas_call x4 -> x3, Pallas kernels: 24.3 us -> 11.7 us  [call(): pl.pallas_call(kernel, out_shape=out_shape, in_specs=in_specs, out_specs=...]
    ppermute x3, starting transfers between devices: 7.08 us -> 3.89 us  [handed(): return lax.ppermute(block, 'cuts', route)]
    ppermute x3, waiting for transfers between devices: 23.9 us -> 20.7 us  [handed(): return lax.ppermute(block, 'cuts', route)]
    all_to_all x2, blocking collectives: 45.9 us -> 48 us  [exchanged(): lax.all_to_all(blocks, 'cuts', 0, 0, axis_index_groups=members, tiled=True)]
    pallas_call x1, Pallas kernels: 4.25 us -> 2.63 us  [shards(): pl.pallas_call(window_kernel, out_shape=struct(size, rows, 2 * width), in...]
    unnamed x9 -> x16, local copies, waits for them, and re-layouts: 2.74 us -> 2.65 us
  transfers between devices with their start and end apart: 3 -> 3, of which waited for: 2 -> 2; matrix products, arithmetic and copies ran while one was open for 0% -> 0% of each run, Pallas kernels for 12% -> 0%
where the time goes in v4:
time: 93.9 us; the launch traced here: 93.5 us
  blocking collectives  48 us (51%)
  waiting for transfers between devices  20.7 us (22%)
  Pallas kernels  17.5 us (19%)
  starting transfers between devices  3.89 us (4%)
  local copies, waits for them, and re-layouts  2.65 us (3%)
    all_to_all x2, blocking collectives, exchanged(): lax.all_to_all(blocks, 'cuts', 0, 0, axis_index_groups=members, tiled=True)  48 us
    ppermute x3, waiting for transfers between devices, handed(): return lax.ppermute(block, 'cuts', route)  20.7 us
    pallas_call x3, Pallas kernels, call(): pl.pallas_call(kernel, out_shape=out_shape, in_specs=in_specs, out_specs=...  11.7 us
    ppermute x3, starting transfers between devices, handed(): return lax.ppermute(block, 'cuts', route)  3.89 us
    pallas_call x1, Pallas kernels, shards(): pl.pallas_call(gather_kernel, out_shape=jax.ShapeDtypeStruct(objects.shap...  3.19 us
    unnamed x16, local copies, waits for them, and re-layouts  2.65 us
    pallas_call x1, Pallas kernels, shards(): pl.pallas_call(window_kernel, out_shape=struct(size, rows, 2 * width), in...  2.63 us
  transfers between devices with their start and end apart: 3, of which 2 were waited for; matrix products, arithmetic and copies ran while one was open for 0% of the time, Pallas kernels for 0%

profile of v4, /device:TPU:0, one launch (start us, length us, event | category | flops | bytes accessed | tf_op | source)
XLA Modules:
  0.0 93.5 jit_solution(3389648467718333578)
XLA Ops:
  0.7 0.0 copy-start.2
  0.7 1.1 %copy-done.2 = bf16[1,2,384,384]{3,2,1,0:T(8,128)(2,1)S(1)} copy-done((bf16[1,2,384,384]{3,2,1,0:T(8,128)(2,1)S(1)}, bf16[1,2,384,384]{3,2,1,0:T(8,128)(2,1)}, u32[]{:S(2)}) %copy-start.2) | copy-done | bytes 589848
  1.7 0.0 copy-start.4
  1.7 0.9 copy-done.4
  2.6 0.0 copy-start.5
  2.6 0.7 copy-done.5
  3.3 0.0 copy-start.7
  3.3 2.6 %windows.1 = bf16[8,224,384]{2,1,0:T(8,128)(2,1)S(1)} custom-call(s32[2,6]{1,0:T(2,128)S(1)} %bitcast.1, s32[1]{0:T(128)S(6)} %copy.9.index_ref, bf16[1,2,384,384]{3,2,1,0:T(8,128)(2,1)S(1)} %copy-done.2, f32[6,12,192]{2,1,0:T(8,128)S(1)} %copy-done.4), custom_call_target="tpu_custom_call" | custom-call | tf_op jit(solution)/shard_map/windows/pallas_call | solution.py:383
  5.9 0.0 copy-start
  5.9 0.0 copy-start.1
  6.0 0.0 copy-start.3
  6.0 24.2 %all_to_all.10.blocks.refs_1_ = bf16[8,224,384]{2,1,0:T(8,128)(2,1)S(1)} all-to-all(bf16[8,224,384]{2,1,0:T(8,128)(2,1)S(1)} %windows.1), channel_id=1, replica_groups={{0,1,2,3,4,5,6,7},{8,9,10,11,12,13,14,15},{16,17,18,19,20,21,22,23},{24..., dimensions={0} | all-to-all | bytes 2752512 | tf_op jit(solution)/shard_map/all_to_all | solution.py:377
  30.2 0.0 copy-done.7
  30.2 0.0 copy-done
  30.2 0.0 copy-done.1
  30.2 0.0 copy-done.3
  30.2 6.0 %first_forward.1 = (bf16[192,384]{1,0:T(8,128)(2,1)S(1)}, f32[96,256]{1,0:T(8,128)S(1)}, bf16[9,192,384]{2,1,0:T(8,128)(2,1)S(1)}, bf16[4,384,192]{2,1,0:T(8,128...) custom-call(s32[6]{0:T(128)S(1)} %copy-done.7, ...), custom_call_target="tpu_custom_call" | custom-call | tf_op jit(solution)/shard_map/first_forward/pallas_call | solution.py:407
  36.2 1.3 %collective-permute-start = (bf16[192,384]{1,0:T(8,128)(2,1)S(1)}, bf16[192,384]{1,0:T(8,128)(2,1)S(1)}, u32[]{:S(2)}, u32[]{:S(2)}) collective-permute-start(bf16[192,384]{1,0:T(8,128)(2,1)S(1)} %get-tuple-element.19), channel_id=1, source_target_pairs={{0,8},{1,9},{2,10},{3,11},{4,12},{5,13},{16,24},{17,25},{18,26},{1... | collective-permute-start | bytes 442376 | tf_op jit(solution)/shard_map/ppermute | solution.py:381
  37.5 1.3 %collective-permute-start.1 = (f32[96,256]{1,0:T(8,128)S(1)}, f32[96,256]{1,0:T(8,128)S(1)}, u32[]{:S(2)}, u32[]{:S(2)}) collective-permute-start(f32[96,256]{1,0:T(8,128)S(1)} %get-tuple-element.20), channel_id=1, source_target_pairs={{0,8},{1,9},{2,10},{3,11},{4,12},{5,13},{16,24},{17,25},{18,26},{1... | collective-permute-start | bytes 294920 | tf_op jit(solution)/shard_map/ppermute | solution.py:381
  38.8 4.1 %collective-permute-done.1.refs_0_ = f32[96,256]{1,0:T(8,128)S(1)} collective-permute-done((f32[96,256]{1,0:T(8,128)S(1)}, f32[96,256]{1,0:T(8,128)S(1)}, u32[]{:S(2)}, u32[]{:S(2)}) %collective-permute-start.1) | collective-permute-done | bytes 98336 | tf_op jit(solution)/shard_map/ppermute | solution.py:381
  42.9 0.0 collective-permute-done.entering
  42.9 0.6 middle.1
  43.5 1.3 %collective-permute-start.2 = (bf16[192,384]{1,0:T(8,128)(2,1)S(1)}, bf16[192,384]{1,0:T(8,128)(2,1)S(1)}, u32[]{:S(2)}, u32[]{:S(2)}) collective-permute-start(bf16[192,384]{1,0:T(8,128)(2,1)S(1)} %get-tuple-element.27), channel_id=1, source_target_pairs={{8,0},{9,1},{10,2},{11,3},{12,4},{13,5},{24,16},{25,17},{26,18},{2... | collective-permute-start | bytes 442376 | tf_op jit(solution)/shard_map/ppermute | solution.py:381
  44.8 16.6 %collective-permute-done.2.arriving = bf16[192,384]{1,0:T(8,128)(2,1)S(1)} collective-permute-done((bf16[192,384]{1,0:T(8,128)(2,1)S(1)}, bf16[192,384]{1,0:T(8,128)(2,1)S(1)}, u32[]{:S(2)}, u32[]{:S(2)}) %collective-permute-start.2) | collective-permute-done | bytes 147488 | tf_op jit(solution)/shard_map/ppermute | solution.py:381
  61.4 5.2 %backward.1 = (bf16[192,384]{1,0:T(8,128)(2,1)}, bf16[8,192,384]{2,1,0:T(8,128)(2,1)S(1)}) custom-call(bf16[192,384]{1,0:T(8,128)(2,1)S(1)} %collective-permute-done.2.arriving, bf16[9,192,384]{2,1,0:T(8,128)(2,1)S(1)} %get-tuple-element.28.waves, bf16[8,224,384]{2,1,0:T(8,128)(2,1)S(1)} %all_to_all.10.blocks.refs_1_, ...), custom_call_target="tpu_custom_call" | custom-call | tf_op jit(solution)/shard_map/backward/pallas_call | solution.py:407
  66.6 0.0 copy-start.6
  66.6 23.7 %all_to_all.11.grads_ref = bf16[8,192,384]{2,1,0:T(8,128)(2,1)S(1)} all-to-all(bf16[8,192,384]{2,1,0:T(8,128)(2,1)S(1)} %get-tuple-element.32), channel_id=1, replica_groups={{0,1,2,3,4,5,6,7},{8,9,10,11,12,13,14,15},{16,17,18,19,20,21,22,23},{24..., dimensions={0} | all-to-all | bytes 2359296 | tf_op jit(solution)/shard_map/all_to_all | solution.py:377
  90.3 0.0 copy-done.6
  90.3 3.2 %sum_windows.1 = f32[1,2,384,384]{3,2,1,0:T(8,128)} custom-call(s32[2,6]{1,0:T(2,128)S(1)} %bitcast.2, bf16[8,192,384]{2,1,0:T(8,128)(2,1)S(1)} %all_to_all.11.grads_ref), custom_call_target="tpu_custom_call" | custom-call | tf_op jit(solution)/shard_map/sum_windows/pallas_call | solution.py:460
Async XLA Ops:
  0.7 1.1 %copy-start.2 = (bf16[1,2,384,384]{3,2,1,0:T(8,128)(2,1)S(1)}, bf16[1,2,384,384]{3,2,1,0:T(8,128)(2,1)}, u32[]{:S(2)}) copy-start(bf16[1,2,384,384]{3,2,1,0:T(8,128)(2,1)} %objects_ref.1) | copy-start | bytes 1769476
  1.7 0.9 copy-start.4
  2.6 0.7 copy-start.5
  3.3 26.9 %copy-start.7 = (s32[6]{0:T(128)S(1)}, s32[6]{0:T(128)}, u32[]{:S(2)}) copy-start(s32[6]{0:T(128)} %group_ref.1) | copy-start | bytes 76
  5.9 24.3 %copy-start = (bf16[4,2,192,192]{3,2,1,0:T(8,128)(2,1)S(1)}, bf16[4,2,192,192]{3,2,1,0:T(8,128)(2,1)}, u32[]{:S(2)}) copy-start(bf16[4,2,192,192]{3,2,1,0:T(8,128)(2,1)} %refs_2_.1) | copy-start | bytes 1769476
  5.9 24.3 %copy-start.1 = (bf16[8,2,192,192]{3,2,1,0:T(8,128)(2,1)S(1)}, bf16[8,2,192,192]{3,2,1,0:T(8,128)(2,1)}, u32[]{:S(2)}) copy-start(bf16[8,2,192,192]{3,2,1,0:T(8,128)(2,1)} %probes.1) | copy-start | bytes 3538948
  6.0 24.3 %copy-start.3 = (f32[2,192,192]{2,1,0:T(8,128)S(1)}, f32[2,192,192]{2,1,0:T(8,128)}, u32[]{:S(2)}) copy-start(f32[2,192,192]{2,1,0:T(8,128)} %constant.2.clone.dft) | copy-start | bytes 884740
  36.2 6.7 %collective-permute-start = (bf16[192,384]{1,0:T(8,128)(2,1)S(1)}, bf16[192,384]{1,0:T(8,128)(2,1)S(1)}, u32[]{:S(2)}, u32[]{:S(2)}) collective-permute-start(bf16[192,384]{1,0:T(8,128)(2,1)S(1)} %get-tuple-element.19), channel_id=1, source_target_pairs={{0,8},{1,9},{2,10},{3,11},{4,12},{5,13},{16,24},{17,25},{18,26},{1... | collective-permute-start | bytes 442376 | tf_op jit(solution)/shard_map/ppermute | solution.py:381
  37.5 5.4 %collective-permute-start.1 = (f32[96,256]{1,0:T(8,128)S(1)}, f32[96,256]{1,0:T(8,128)S(1)}, u32[]{:S(2)}, u32[]{:S(2)}) collective-permute-start(f32[96,256]{1,0:T(8,128)S(1)} %get-tuple-element.20), channel_id=1, source_target_pairs={{0,8},{1,9},{2,10},{3,11},{4,12},{5,13},{16,24},{17,25},{18,26},{1... | collective-permute-start | bytes 294920 | tf_op jit(solution)/shard_map/ppermute | solution.py:381
  43.5 17.9 %collective-permute-start.2 = (bf16[192,384]{1,0:T(8,128)(2,1)S(1)}, bf16[192,384]{1,0:T(8,128)(2,1)S(1)}, u32[]{:S(2)}, u32[]{:S(2)}) collective-permute-start(bf16[192,384]{1,0:T(8,128)(2,1)S(1)} %get-tuple-element.27), channel_id=1, source_target_pairs={{8,0},{9,1},{10,2},{11,3},{12,4},{13,5},{24,16},{25,17},{26,18},{2... | collective-permute-start | bytes 442376 | tf_op jit(solution)/shard_map/ppermute | solution.py:381
  66.6 23.7 %copy-start.6 = (s32[6,2]{0,1:T(2,128)S(1)}, s32[6,2]{0,1:T(2,128)}, u32[]{:S(2)}) copy-start(s32[6,2]{0,1:T(2,128)} %param.13) | copy-start | bytes 148

commit v5 on v4

--- a/solution.py
+++ b/solution.py
@@ -117,25 +117,33 @@
     return (np.stack([np.cos(angle), -np.sin(angle)]) / math.sqrt(width)).astype(np.float32)
 
 
-def window_kernel(offsets_ref, index_ref, objects_ref, measured_ref, blocks):
-    positions, near_rows, width = measured_ref.shape
-    extent = objects_ref.shape[-1]
-    tag = jnp.full((ROWS, LANES), index_ref[0], jnp.int32).astype(F32).astype(BF16)
-    blank = jnp.zeros((ROWS - near_rows, 2 * LANES), F32)
-    field = jnp.concatenate([objects_ref[0, 0], objects_ref[0, 1]], axis=1)
-    for p in range(positions):
+def slots_of(positions, size):
+    order = list(range(0, size, 2)) + list(range(1, size, 2))
+    return sorted(order[:positions])
+
+
+def window_kernel(offsets_ref, index_ref, objects_in, measured_in, blocks, objects, measured, sems):
+    positions, near_rows, width = measured.shape
+    extent = objects.shape[-1]
+    copies = [
+        pltpu.make_async_copy(objects_in.at[0, 0], objects.at[0], sems.at[0]),
+        pltpu.make_async_copy(objects_in.at[0, 1], objects.at[1], sems.at[1]),
+        pltpu.make_async_copy(measured_in, measured, sems.at[2]),
+    ]
+    for copy in copies:
+        copy.start()
+    tag = jnp.full((ROWS - near_rows, 2 * width), index_ref[0], jnp.int32).astype(F32)
+    for copy in copies:
+        copy.wait()
+    field = jnp.concatenate([objects[0], objects[1]], axis=1)
+    for p, slot in enumerate(slots_of(positions, blocks.shape[0])):
         both = dot(row_picker((width, extent), offsets_ref[0, p]), field).astype(BF16)
         window = packed(both[:, :extent], both[:, extent:], extent, offsets_ref[1, p])
-        blocks[p, :width, :] = window.astype(BF16)
-        high, low = split2(jnp.concatenate([doubled(measured_ref[p]), blank], axis=0))
-        for place, part in ((width, high), (width + ROWS, low)):
-            blocks[p, place : place + ROWS, : 2 * LANES] = part
-            blocks[p, place : place + ROWS, 2 * LANES :] = tag
-
-
-def doubled(rows):
-    tail = jnp.concatenate([rows[:, LANES:]] * 2, axis=1)
-    return jnp.concatenate([rows[:, :LANES], tail], axis=1)
+        blocks[slot, :width, :] = window.astype(BF16)
+        high = measured[p].astype(BF16).astype(F32)
+        low = measured[p] - high
+        seen = jnp.concatenate([high[:, :LANES], low[:, :LANES], high[:, LANES:], low[:, LANES:]], axis=1)
+        blocks[slot, width:, :] = jnp.concatenate([seen, tag], axis=0).astype(BF16)
 
 
 def right_table(real, imag):
@@ -220,7 +228,7 @@
 
 def read_indices(blocks, indices, count):
     for k in range(blocks.shape[0]):
-        tag = jnp.max(blocks[k, -ROWS:, 2 * LANES :].astype(F32))
+        tag = jnp.max(blocks[k, -ROWS:, :LANES].astype(F32)[ROWS - 1 :])
         indices[k] = jnp.clip(tag.astype(jnp.int32), 0, count - 1)
 
 
@@ -231,19 +239,26 @@
 
 def observe(blocks, near_rows, observed, first):
     for k in range(blocks.shape[0]):
-        high = blocks[k, -2 * ROWS : -ROWS, : 2 * LANES].astype(F32)
-        low = blocks[k, -ROWS:, : 2 * LANES].astype(F32)
+        high, low, tail = halves(blocks[k, -ROWS:, :].astype(F32))
+        rows = jnp.concatenate([high + low, tail + swapped(tail)], axis=1)
         at = first + k * near_rows
-        observed[at : at + near_rows, :] = (high + low)[:near_rows]
-
-
-def first_kernel(group_ref, probes, blocks, props, dft, leaving, near, waves, lb, rf, rb, left, right, right_conj, probe, indices, sem):
+        observed[at : at + near_rows, :] = rows[:near_rows]
+
+
+def near_kernel(blocks, _, near):
+    observe(blocks, near.shape[0] // blocks.shape[0], near, 0)
+
+
+def first_kernel(group_ref, probes, blocks, props, dft, leaving, waves, lb, rf, rb, left, right, right_conj, probe, indices, sem):
     size = blocks.shape[0]
     slot, group = place_in(size)
 
     @pl.when(group == 0)
     def _():
-        which = group_ref[jnp.minimum(slot, group_ref.shape[0] - 1)]
+        position = 0
+        for p, held in enumerate(slots_of(group_ref.shape[0], size)):
+            position = jnp.where(slot == held, p, position)
+        which = group_ref[position]
         copy = pltpu.make_async_copy(probes.at[which], probe, sem)
         copy.start()
         forward_tables(props, rf)
@@ -252,7 +267,6 @@
         waves[0] = packed(probe[0], probe[1], probe.shape[-1], 0).astype(BF16)
         forward_steps(blocks, waves, indices, props, rf)
         leaving[...] = waves[size]
-        observe(blocks, near.shape[0] // size, near, 0)
 
     @pl.when(group > 0)
     def _():
@@ -262,7 +276,7 @@
 
 
 def forward_kernel(stage):
-    def kernel(entering, blocks, props, rf, waves_in, leaving, near, waves, indices):
+    def kernel(entering, blocks, props, rf, waves_in, leaving, waves, indices):
         size = blocks.shape[0]
         _, group = place_in(size)
 
@@ -272,7 +286,6 @@
             waves[0] = entering[...]
             forward_steps(blocks, waves, indices, props, rf)
             leaving[...] = waves[size]
-            observe(blocks, near.shape[0] // size, near, 0)
 
         @pl.when(group != stage)
         def _():
@@ -282,18 +295,15 @@
 
 
 def middle_kernel(groups):
-    def kernel(entering, *refs):
+    def kernel(waves, *refs):
         earlier, refs = refs[: groups - 1], refs[groups - 1 :]
-        blocks, props, lb, rf, rb, left, right, right_conj, leaving, grads, lb_out, rb_out = refs[:12]
-        waves, g, observed, indices = refs[12:]
+        blocks, props, lb, rb, left, right, right_conj, leaving, grads, lb_out, rb_out, g, observed, indices = refs
         size = blocks.shape[0]
         _, group = place_in(size)
 
         @pl.when(group == groups - 1)
         def _():
             read_indices(blocks, indices, props.shape[0])
-            waves[0] = entering[...]
-            forward_steps(blocks, waves, indices, props, rf)
             rows = earlier[0].shape[0]
             for n, near in enumerate(earlier):
                 observed[n * rows : (n + 1) * rows, :] = near[...]
@@ -332,8 +342,8 @@
     width = grads_ref.shape[1]
     extent = out_ref.shape[-1]
     spread_out = []
-    for p in range(positions):
-        x0, x1, xt = halves(grads_ref[p])
+    for p, slot in enumerate(slots_of(positions, grads_ref.shape[0])):
+        x0, x1, xt = halves(grads_ref[slot])
         spread_out.append(
             jnp.concatenate(
                 [
@@ -367,7 +377,8 @@
     near_rows = measured.shape[1]
     size = GROUP
     groups = sections // size
-    rows = width + 2 * ROWS
+    rows = width + ROWS
+    slots = slots_of(probe_group.shape[0], size)
     members = [list(range(first, first + size)) for first in range(0, sections, size)]
 
     def struct(*dims, kind=BF16):
@@ -377,14 +388,19 @@
         return lax.all_to_all(blocks, "cuts", 0, 0, axis_index_groups=members, tiled=True)
 
     def handed(block, stage, distance):
-        route = [(stage * size + l, (stage + distance) * size + l) for l in range(probe_group.shape[0])]
+        route = [(stage * size + l, (stage + distance) * size + l) for l in slots]
         return lax.ppermute(block, "cuts", route)
 
     blocks = pl.pallas_call(
         window_kernel,
         out_shape=struct(size, rows, 2 * width),
-        in_specs=[SMEM, SMEM, VMEM, VMEM],
+        in_specs=[SMEM, SMEM, HBM, HBM],
         out_specs=VMEM,
+        scratch_shapes=[
+            pltpu.VMEM(objects.shape[1:], BF16),
+            pltpu.VMEM(measured.shape, F32),
+            pltpu.SemaphoreType.DMA((3,)),
+        ],
         compiler_params=PARAMS,
         name="windows",
     )(offsets.T, prop_index, objects, measured)
@@ -414,36 +430,37 @@
             name=name,
         )(*operands)
 
-    leaving, near_out, waves, lb, rf, rb, *dft = call(
+    leaving, waves, lb, rf, rb, *dft = call(
         first_kernel,
         "first_forward",
-        [wave, near, waves_shape, left_table, square_table, square_table]
+        [wave, waves_shape, left_table, square_table, square_table]
         + [detector_left, detector_right, detector_right],
         [SMEM, HBM, VMEM, VMEM, VMEM],
         [pltpu.VMEM(probes.shape[1:], BF16), indices, pltpu.SemaphoreType.DMA],
         (probe_group, probes, blocks, propagators, jnp.asarray(dft_constant(width))),
     )
     entering = handed(leaving, 0, 1)
-    nears = [handed(near_out, 0, groups - 1)]
-    for stage in range(1, groups - 1):
-        leaving, near_out, waves = call(
+    (near_out,) = call(near_kernel, "near_rows", [near], [VMEM, HBM], [], (blocks, leaving))
+    nears = [handed(near_out, stage, groups - 1 - stage) for stage in range(groups - 1)]
+    for stage in range(1, groups):
+        leaving, waves = call(
             forward_kernel(stage),
             "forward",
-            [wave, near, waves_shape],
+            [wave, waves_shape],
             [VMEM] * 5,
             [indices],
             (entering, blocks, propagators, rf, waves),
         )
-        entering = handed(leaving, stage, 1)
-        nears.append(handed(near_out, stage, groups - 1 - stage))
+        if stage < groups - 1:
+            entering = handed(leaving, stage, 1)
 
     leaving, grads, lb, rb = call(
         middle_kernel(groups),
         "middle",
         [wave, grads_shape, left_table, square_table],
-        [VMEM] * (groups + 8),
-        [scratch(waves_shape), scratch(wave), pltpu.VMEM((width, 2 * LANES), F32), indices],
-        (entering, *nears, blocks, propagators, lb, rf, rb, *dft),
+        [VMEM] * (groups + 7),
+        [scratch(wave), pltpu.VMEM((width, 2 * LANES), F32), indices],
+        (waves, *nears, blocks, propagators, lb, rb, *dft),
     )
 
     for stage in range(groups - 2, -1, -1):

time: 93.9 us -> 90.5 us (0.964)
  blocking collectives: 48 us -> 44.8 us
  waiting for transfers between devices: 20.7 us -> 19.4 us
  Pallas kernels: 17.5 us -> 18.6 us
    all_to_all x2, blocking collectives: 48 us -> 44.8 us  [exchanged(): lax.all_to_all(blocks, 'cuts', 0, 0, axis_index_groups=members, tiled=True)]
    ppermute x3, waiting for transfers between devices: 20.7 us -> 19.4 us  [handed(): return lax.ppermute(block, 'cuts', route)]
    pallas_call x3 -> x5, Pallas kernels: 11.7 us -> 12.5 us  [call(): pl.pallas_call(kernel, out_shape=out_shape, in_specs=in_specs, out_specs=...]
  transfers between devices with their start and end apart: 3 -> 3, of which waited for: 2 -> 3; matrix products, arithmetic and copies ran while one was open for 0% -> 0% of each run, Pallas kernels for 0% -> 1%
where the time goes in v5:
time: 90.5 us; the launch traced here: 90.1 us
  blocking collectives  44.8 us (50%)
  waiting for transfers between devices  19.4 us (21%)
  Pallas kernels  18.6 us (21%)
  starting transfers between devices  3.89 us (4%)
  local copies, waits for them, and re-layouts  2.65 us (3%)
    all_to_all x2, blocking collectives, exchanged(): lax.all_to_all(blocks, 'cuts', 0, 0, axis_index_groups=members, tiled=True)  44.8 us
    ppermute x3, waiting for transfers between devices, handed(): return lax.ppermute(block, 'cuts', route)  19.4 us
    pallas_call x5, Pallas kernels, call(): pl.pallas_call(kernel, out_shape=out_shape, in_specs=in_specs, out_specs=...  12.5 us
    ppermute x3, starting transfers between devices, handed(): return lax.ppermute(block, 'cuts', route)  3.89 us
    pallas_call x1, Pallas kernels, shards(): pl.pallas_call(gather_kernel, out_shape=jax.ShapeDtypeStruct(objects.shap...  3.19 us
    pallas_call x1, Pallas kernels, shards(): pl.pallas_call(window_kernel, out_shape=struct(size, rows, 2 * width), in...  2.91 us
    unnamed x16, local copies, waits for them, and re-layouts  2.65 us
  transfers between devices with their start and end apart: 3, of which 3 were waited for; matrix products, arithmetic and copies ran while one was open for 0% of the time, Pallas kernels for 1%

profile of v5, /device:TPU:0, one launch (start us, length us, event | category | flops | bytes accessed | tf_op | source)
XLA Modules:
  0.0 90.1 jit_solution(11632818264737774829)
XLA Ops:
  0.7 0.0 copy-start.2
  0.7 1.1 %copy-done.2 = bf16[1,2,384,384]{3,2,1,0:T(8,128)(2,1)S(1)} copy-done((bf16[1,2,384,384]{3,2,1,0:T(8,128)(2,1)S(1)}, bf16[1,2,384,384]{3,2,1,0:T(8,128)(2,1)}, u32[]{:S(2)}) %copy-start.2) | copy-done | bytes 589848
  1.7 0.0 copy-start.4
  1.7 0.9 copy-done.4
  2.6 0.0 copy-start.5
  2.6 0.7 copy-done.5
  3.3 0.0 copy-start.3
  3.3 2.9 %windows.1 = bf16[8,208,384]{2,1,0:T(8,128)(2,1)S(1)} custom-call(s32[2,6]{1,0:T(2,128)S(1)} %bitcast.1, s32[1]{0:T(128)S(6)} %copy.9.index_ref, bf16[1,2,384,384]{3,2,1,0:T(8,128)(2,1)S(1)} %copy-done.2, f32[6,12,192]{2,1,0:T(8,128)S(1)} %copy-done.4), custom_call_target="tpu_custom_call" | custom-call | tf_op jit(solution)/shard_map/windows/pallas_call | solution.py:394
  6.2 0.0 copy-start
  6.2 0.0 copy-start.1
  6.2 0.0 copy-start.7
  6.2 22.4 %all_to_all.10.blocks.refs_1_ = bf16[8,208,384]{2,1,0:T(8,128)(2,1)S(1)} all-to-all(bf16[8,208,384]{2,1,0:T(8,128)(2,1)S(1)} %windows.1), channel_id=1, replica_groups={{0,1,2,3,4,5,6,7},{8,9,10,11,12,13,14,15},{16,17,18,19,20,21,22,23},{24..., dimensions={0} | all-to-all | bytes 2555904 | tf_op jit(solution)/shard_map/all_to_all | solution.py:388
  28.7 0.0 copy-done.3
  28.7 0.0 copy-done
  28.7 0.0 copy-done.1
  28.7 0.0 copy-done.7
  28.7 5.9 %first_forward.1 = (bf16[192,384]{1,0:T(8,128)(2,1)S(1)}, bf16[9,192,384]{2,1,0:T(8,128)(2,1)S(1)}, bf16[4,384,192]{2,1,0:T(8,128)(2,1)S(1)}, bf16[4,384,384]{2,...) custom-call(s32[6]{0:T(128)S(1)} %copy-done.7, ...), custom_call_target="tpu_custom_call" | custom-call | tf_op jit(solution)/shard_map/first_forward/pallas_call | solution.py:423
  34.6 1.3 %collective-permute-start = (bf16[192,384]{1,0:T(8,128)(2,1)S(1)}, bf16[192,384]{1,0:T(8,128)(2,1)S(1)}, u32[]{:S(2)}, u32[]{:S(2)}) collective-permute-start(bf16[192,384]{1,0:T(8,128)(2,1)S(1)} %get-tuple-element.19._), channel_id=1, source_target_pairs={{0,8},{1,9},{2,10},{3,11},{4,12},{6,14},{16,24},{17,25},{18,26},{1... | collective-permute-start | bytes 442376 | tf_op jit(solution)/shard_map/ppermute | solution.py:392
  36.0 0.1 near_rows.1
  36.0 1.3 %collective-permute-start.1 = (f32[96,256]{1,0:T(8,128)S(1)}, f32[96,256]{1,0:T(8,128)S(1)}, u32[]{:S(2)}, u32[]{:S(2)}) collective-permute-start(f32[96,256]{1,0:T(8,128)S(1)} %near_rows.1), channel_id=1, source_target_pairs={{0,8},{1,9},{2,10},{3,11},{4,12},{6,14},{16,24},{17,25},{18,26},{1... | collective-permute-start | bytes 294920 | tf_op jit(solution)/shard_map/ppermute | solution.py:392
  37.3 2.9 %collective-permute-done.entering = bf16[192,384]{1,0:T(8,128)(2,1)S(1)} collective-permute-done((bf16[192,384]{1,0:T(8,128)(2,1)S(1)}, bf16[192,384]{1,0:T(8,128)(2,1)S(1)}, u32[]{:S(2)}, u32[]{:S(2)}) %collective-permute-start) | collective-permute-done | bytes 147488 | tf_op jit(solution)/shard_map/ppermute | solution.py:392
  40.2 0.8 forward.1
  41.0 0.3 collective-permute-done.1.refs_0_
  41.3 0.6 middle.1
  41.9 1.3 %collective-permute-start.2 = (bf16[192,384]{1,0:T(8,128)(2,1)S(1)}, bf16[192,384]{1,0:T(8,128)(2,1)S(1)}, u32[]{:S(2)}, u32[]{:S(2)}) collective-permute-start(bf16[192,384]{1,0:T(8,128)(2,1)S(1)} %get-tuple-element.28), channel_id=1, source_target_pairs={{8,0},{9,1},{10,2},{11,3},{12,4},{14,6},{24,16},{25,17},{26,18},{2... | collective-permute-start | bytes 442376 | tf_op jit(solution)/shard_map/ppermute | solution.py:392
  43.2 16.2 %collective-permute-done.2.arriving = bf16[192,384]{1,0:T(8,128)(2,1)S(1)} collective-permute-done((bf16[192,384]{1,0:T(8,128)(2,1)S(1)}, bf16[192,384]{1,0:T(8,128)(2,1)S(1)}, u32[]{:S(2)}, u32[]{:S(2)}) %collective-permute-start.2) | collective-permute-done | bytes 147488 | tf_op jit(solution)/shard_map/ppermute | solution.py:392
  59.4 5.2 %backward.1 = (bf16[192,384]{1,0:T(8,128)(2,1)}, bf16[8,192,384]{2,1,0:T(8,128)(2,1)S(1)}) custom-call(bf16[192,384]{1,0:T(8,128)(2,1)S(1)} %collective-permute-done.2.arriving, bf16[9,192,384]{2,1,0:T(8,128)(2,1)S(1)} %get-tuple-element.22.waves, bf16[8,208,384]{2,1,0:T(8,128)(2,1)S(1)} %all_to_all.10.blocks.refs_1_, ...), custom_call_target="tpu_custom_call" | custom-call | tf_op jit(solution)/shard_map/backward/pallas_call | solution.py:423
  64.5 0.0 copy-start.6
  64.5 22.4 %all_to_all.11.grads_ref = bf16[8,192,384]{2,1,0:T(8,128)(2,1)S(1)} all-to-all(bf16[8,192,384]{2,1,0:T(8,128)(2,1)S(1)} %get-tuple-element.32), channel_id=1, replica_groups={{0,1,2,3,4,5,6,7},{8,9,10,11,12,13,14,15},{16,17,18,19,20,21,22,23},{24..., dimensions={0} | all-to-all | bytes 2359296 | tf_op jit(solution)/shard_map/all_to_all | solution.py:388
  87.0 0.0 copy-done.6
  87.0 3.2 %sum_windows.1 = f32[1,2,384,384]{3,2,1,0:T(8,128)} custom-call(s32[2,6]{1,0:T(2,128)S(1)} %bitcast.2, bf16[8,192,384]{2,1,0:T(8,128)(2,1)S(1)} %all_to_all.11.grads_ref), custom_call_target="tpu_custom_call" | custom-call | tf_op jit(solution)/shard_map/sum_windows/pallas_call | solution.py:477
Async XLA Ops:
  0.7 1.1 %copy-start.2 = (bf16[1,2,384,384]{3,2,1,0:T(8,128)(2,1)S(1)}, bf16[1,2,384,384]{3,2,1,0:T(8,128)(2,1)}, u32[]{:S(2)}) copy-start(bf16[1,2,384,384]{3,2,1,0:T(8,128)(2,1)} %objects_in.1) | copy-start | bytes 1769476
  1.7 0.9 copy-start.4
  2.6 0.7 copy-start.5
  3.3 25.4 %copy-start.3 = (f32[2,192,192]{2,1,0:T(8,128)S(1)}, f32[2,192,192]{2,1,0:T(8,128)}, u32[]{:S(2)}) copy-start(f32[2,192,192]{2,1,0:T(8,128)} %constant.2.clone.dft) | copy-start | bytes 884740
  6.2 22.5 %copy-start = (bf16[4,2,192,192]{3,2,1,0:T(8,128)(2,1)S(1)}, bf16[4,2,192,192]{3,2,1,0:T(8,128)(2,1)}, u32[]{:S(2)}) copy-start(bf16[4,2,192,192]{3,2,1,0:T(8,128)(2,1)} %refs_2_.1) | copy-start | bytes 1769476
  6.2 22.5 %copy-start.1 = (bf16[8,2,192,192]{3,2,1,0:T(8,128)(2,1)S(1)}, bf16[8,2,192,192]{3,2,1,0:T(8,128)(2,1)}, u32[]{:S(2)}) copy-start(bf16[8,2,192,192]{3,2,1,0:T(8,128)(2,1)} %probes.1) | copy-start | bytes 3538948
  6.2 22.5 %copy-start.7 = (s32[6]{0:T(128)S(1)}, s32[6]{0:T(128)}, u32[]{:S(2)}) copy-start(s32[6]{0:T(128)} %group_ref.1) | copy-start | bytes 76
  34.6 5.6 %collective-permute-start = (bf16[192,384]{1,0:T(8,128)(2,1)S(1)}, bf16[192,384]{1,0:T(8,128)(2,1)S(1)}, u32[]{:S(2)}, u32[]{:S(2)}) collective-permute-start(bf16[192,384]{1,0:T(8,128)(2,1)S(1)} %get-tuple-element.19._), channel_id=1, source_target_pairs={{0,8},{1,9},{2,10},{3,11},{4,12},{6,14},{16,24},{17,25},{18,26},{1... | collective-permute-start | bytes 442376 | tf_op jit(solution)/shard_map/ppermute | solution.py:392
  36.0 5.2 %collective-permute-start.1 = (f32[96,256]{1,0:T(8,128)S(1)}, f32[96,256]{1,0:T(8,128)S(1)}, u32[]{:S(2)}, u32[]{:S(2)}) collective-permute-start(f32[96,256]{1,0:T(8,128)S(1)} %near_rows.1), channel_id=1, source_target_pairs={{0,8},{1,9},{2,10},{3,11},{4,12},{6,14},{16,24},{17,25},{18,26},{1... | collective-permute-start | bytes 294920 | tf_op jit(solution)/shard_map/ppermute | solution.py:392
  41.9 17.5 %collective-permute-start.2 = (bf16[192,384]{1,0:T(8,128)(2,1)S(1)}, bf16[192,384]{1,0:T(8,128)(2,1)S(1)}, u32[]{:S(2)}, u32[]{:S(2)}) collective-permute-start(bf16[192,384]{1,0:T(8,128)(2,1)S(1)} %get-tuple-element.28), channel_id=1, source_target_pairs={{8,0},{9,1},{10,2},{11,3},{12,4},{14,6},{24,16},{25,17},{26,18},{2... | collective-permute-start | bytes 442376 | tf_op jit(solution)/shard_map/ppermute | solution.py:392
  64.5 22.4 %copy-start.6 = (s32[6,2]{0,1:T(2,128)S(1)}, s32[6,2]{0,1:T(2,128)}, u32[]{:S(2)}) copy-start(s32[6,2]{0,1:T(2,128)} %param.13) | copy-start | bytes 148

commit v6 on v5

--- a/solution.py
+++ b/solution.py
@@ -122,7 +122,20 @@
     return sorted(order[:positions])
 
 
-def window_kernel(offsets_ref, index_ref, objects_in, measured_in, blocks, objects, measured, sems):
+def partner(rank, size, r):
+    return lax.bitwise_xor(lax.rem(rank, size), r)
+
+
+def shuffled(pairs, sems):
+    copies = [pltpu.make_async_copy(source, target, sems.at[n]) for n, (source, target) in enumerate(pairs)]
+    for copy in copies:
+        copy.start()
+    for copy in copies:
+        copy.wait()
+
+
+def window_kernel(offsets_ref, index_ref, objects_in, measured_in, *refs):
+    outs, (blocks, objects, measured, sems) = refs[:-4], refs[-4:]
     positions, near_rows, width = measured.shape
     extent = objects.shape[-1]
     copies = [
@@ -144,6 +157,7 @@
         low = measured[p] - high
         seen = jnp.concatenate([high[:, :LANES], low[:, :LANES], high[:, LANES:], low[:, LANES:]], axis=1)
         blocks[slot, width:, :] = jnp.concatenate([seen, tag], axis=0).astype(BF16)
+    shuffled([(blocks.at[partner(lax.axis_index("cuts"), len(outs), r)], out) for r, out in enumerate(outs)], sems)
 
 
 def right_table(real, imag):
@@ -249,8 +263,16 @@
     observe(blocks, near.shape[0] // blocks.shape[0], near, 0)
 
 
-def first_kernel(group_ref, probes, blocks, props, dft, leaving, waves, lb, rf, rb, left, right, right_conj, probe, indices, sem):
+def first_kernel(group_ref, probes, props, dft, *refs):
+    blocks_in, refs = refs[:-13], refs[-13:]
+    leaving, blocks, waves, lb, rf, rb, left, right, right_conj, probe, indices, sem, sems = refs
     size = blocks.shape[0]
+    shifts = [
+        pltpu.make_async_copy(block, blocks.at[partner(lax.axis_index("cuts"), size, r)], sems.at[r])
+        for r, block in enumerate(blocks_in)
+    ]
+    for shift in shifts:
+        shift.start()
     slot, group = place_in(size)
 
     @pl.when(group == 0)
@@ -262,6 +284,8 @@
         copy = pltpu.make_async_copy(probes.at[which], probe, sem)
         copy.start()
         forward_tables(props, rf)
+        for shift in shifts:
+            shift.wait()
         read_indices(blocks, indices, props.shape[0])
         copy.wait()
         waves[0] = packed(probe[0], probe[1], probe.shape[-1], 0).astype(BF16)
@@ -273,6 +297,8 @@
         forward_tables(props, rf)
         backward_tables(props, lb, rb)
         detector_tables(dft, left, right, right_conj)
+        for shift in shifts:
+            shift.wait()
 
 
 def forward_kernel(stage):
@@ -320,8 +346,11 @@
 
 
 def backward_kernel(stage):
-    def kernel(arriving, waves, blocks, lb, rb, grads_in, leaving, grads, g, indices):
-        _, group = place_in(blocks.shape[0])
+    def kernel(arriving, waves, blocks, lb, rb, grads_in, leaving, *refs):
+        outs, (grads, g, indices, sems) = refs[:-4], refs[-4:]
+        size = blocks.shape[0]
+        _, group = place_in(size)
+        order = [partner(lax.axis_index("cuts"), size, r) if stage == 0 else r for r in range(size)]
 
         @pl.when(group == stage)
         def _():
@@ -329,21 +358,26 @@
             g[...] = arriving[...]
             backward_steps(blocks, waves, indices, lb, rb, grads, g)
             leaving[...] = g[...]
+            shuffled([(grads.at[order[r]], out) for r, out in enumerate(outs)], sems)
 
         @pl.when(group != stage)
         def _():
-            grads[...] = grads_in[...]
+            shuffled([(grads_in.at[order[r]], out) for r, out in enumerate(outs)], sems)
 
     return kernel
 
 
-def gather_kernel(offsets_ref, grads_ref, out_ref):
+def gather_kernel(offsets_ref, *refs):
+    grads_in, (out_ref, grads, sems) = refs[:-3], refs[-3:]
+    size = len(grads_in)
+    rank = lax.axis_index("cuts")
+    shuffled([(block, grads.at[partner(rank, size, r)]) for r, block in enumerate(grads_in)], sems)
     positions = offsets_ref.shape[1]
-    width = grads_ref.shape[1]
+    width = grads.shape[1]
     extent = out_ref.shape[-1]
     spread_out = []
-    for p, slot in enumerate(slots_of(positions, grads_ref.shape[0])):
-        x0, x1, xt = halves(grads_ref[slot])
+    for p, slot in enumerate(slots_of(positions, size)):
+        x0, x1, xt = halves(grads[slot])
         spread_out.append(
             jnp.concatenate(
                 [
@@ -379,13 +413,21 @@
     groups = sections // size
     rows = width + ROWS
     slots = slots_of(probe_group.shape[0], size)
-    members = [list(range(first, first + size)) for first in range(0, sections, size)]
 
     def struct(*dims, kind=BF16):
         return jax.ShapeDtypeStruct(dims, kind)
 
-    def exchanged(blocks):
-        return lax.all_to_all(blocks, "cuts", 0, 0, axis_index_groups=members, tiled=True)
+    def exchanged(blocks, inward):
+        results = list(blocks)
+        for r in sorted(range(1, size), key=lambda r: (r % 2, -r)):
+            route = [
+                (first + l, first + (l ^ r))
+                for first in range(0, sections, size)
+                for l in range(size)
+                if (l ^ r if inward else l) in slots
+            ]
+            results[r] = lax.ppermute(blocks[r], "cuts", route)
+        return results
 
     def handed(block, stage, distance):
         route = [(stage * size + l, (stage + distance) * size + l) for l in slots]
@@ -393,18 +435,19 @@
 
     blocks = pl.pallas_call(
         window_kernel,
-        out_shape=struct(size, rows, 2 * width),
+        out_shape=[struct(rows, 2 * width)] * size,
         in_specs=[SMEM, SMEM, HBM, HBM],
-        out_specs=VMEM,
+        out_specs=[VMEM] * size,
         scratch_shapes=[
+            pltpu.VMEM((size, rows, 2 * width), BF16),
             pltpu.VMEM(objects.shape[1:], BF16),
             pltpu.VMEM(measured.shape, F32),
-            pltpu.SemaphoreType.DMA((3,)),
+            pltpu.SemaphoreType.DMA((size,)),
         ],
         compiler_params=PARAMS,
         name="windows",
     )(offsets.T, prop_index, objects, measured)
-    blocks = exchanged(blocks)
+    blocks = exchanged(blocks, True)
 
     wave = struct(width, 2 * width)
     near = struct(size * near_rows, 2 * LANES, kind=F32)
@@ -430,14 +473,14 @@
             name=name,
         )(*operands)
 
-    leaving, waves, lb, rf, rb, *dft = call(
+    leaving, blocks, waves, lb, rf, rb, *dft = call(
         first_kernel,
         "first_forward",
-        [wave, waves_shape, left_table, square_table, square_table]
+        [wave, struct(size, rows, 2 * width), waves_shape, left_table, square_table, square_table]
         + [detector_left, detector_right, detector_right],
-        [SMEM, HBM, VMEM, VMEM, VMEM],
-        [pltpu.VMEM(probes.shape[1:], BF16), indices, pltpu.SemaphoreType.DMA],
-        (probe_group, probes, blocks, propagators, jnp.asarray(dft_constant(width))),
+        [SMEM, HBM, VMEM, VMEM] + [VMEM] * size,
+        [pltpu.VMEM(probes.shape[1:], BF16), indices, pltpu.SemaphoreType.DMA, pltpu.SemaphoreType.DMA((size,))],
+        (probe_group, probes, propagators, jnp.asarray(dft_constant(width)), *blocks),
     )
     entering = handed(leaving, 0, 1)
     (near_out,) = call(near_kernel, "near_rows", [near], [VMEM, HBM], [], (blocks, leaving))
@@ -465,23 +508,26 @@
 
     for stage in range(groups - 2, -1, -1):
         arriving = handed(leaving, stage + 1, -1)
-        leaving, grads = call(
+        last = stage == 0
+        leaving, *grads = call(
             backward_kernel(stage),
             "backward",
-            [wave, grads_shape],
+            [wave] + [struct(width, 2 * width)] * size,
             [VMEM] * 6,
-            [scratch(wave), indices],
+            [scratch(grads_shape), scratch(wave), indices, pltpu.SemaphoreType.DMA((size,))],
             (arriving, waves, blocks, lb, rb, grads),
         )
-
-    return pl.pallas_call(
+        if not last:
+            grads = jnp.stack(grads)
+
+    return call(
         gather_kernel,
-        out_shape=jax.ShapeDtypeStruct(objects.shape, F32),
-        in_specs=[SMEM, VMEM],
-        out_specs=VMEM,
-        compiler_params=PARAMS,
-        name="sum_windows",
-    )(offsets.T, exchanged(grads))
+        "sum_windows",
+        [struct(*objects.shape, kind=F32)],
+        [SMEM] + [VMEM] * size,
+        [scratch(grads_shape), pltpu.SemaphoreType.DMA((size,))],
+        (offsets.T, *exchanged(grads, False)),
+    )[0]
 
 
 def solution(mesh):

time: 90.5 us -> 108 us (1.19)
  blocking collectives: 44.8 us -> 0 us
  starting transfers between devices: 3.89 us -> 39.4 us
  waiting for transfers between devices: 19.4 us -> 34.5 us
  Pallas kernels: 18.6 us -> 25.5 us
  local copies, waits for them, and re-layouts: 2.65 us -> 6.83 us
    all_to_all x2 -> x0, blocking collectives: 44.8 us -> none  [exchanged(): lax.all_to_all(blocks, 'cuts', 0, 0, axis_index_groups=members, tiled=True)]
    ppermute x0 -> x14, starting transfers between devices: none -> 35.4 us  [exchanged(): results[r] = lax.ppermute(blocks[r], 'cuts', route)]
    ppermute x0 -> x14, waiting for transfers between devices: none -> 14.7 us  [exchanged(): results[r] = lax.ppermute(blocks[r], 'cuts', route)]
    pallas_call x5 -> x6, Pallas kernels: 12.5 us -> 20.9 us  [call(): pl.pallas_call(kernel, out_shape=out_shape, in_specs=in_specs, out_specs=...]
    unnamed x16 -> x18, local copies, waits for them, and re-layouts: 2.65 us -> 6.83 us
    pallas_call x2 -> x1, Pallas kernels: 6.09 us -> 4.61 us  [shards(): pl.pallas_call(window_kernel, out_shape=[struct(rows, 2 * width)] * size,...]
  transfers between devices with their start and end apart: 3 -> 17, of which waited for: 3 -> 8; matrix products, arithmetic and copies ran while one was open for 0% -> 0% of each run, Pallas kernels for 1% -> 1%
where the time goes in v6:
time: 108 us; the launch traced here: 107 us
  starting transfers between devices  39.4 us (36%)
  waiting for transfers between devices  34.5 us (32%)
  Pallas kernels  25.5 us (24%)
  local copies, waits for them, and re-layouts  6.83 us (6%)
    ppermute x14, starting transfers between devices, exchanged(): results[r] = lax.ppermute(blocks[r], 'cuts', route)  35.4 us
    pallas_call x6, Pallas kernels, call(): pl.pallas_call(kernel, out_shape=out_shape, in_specs=in_specs, out_specs=...  20.9 us
    ppermute x3, waiting for transfers between devices, handed(): return lax.ppermute(block, 'cuts', route)  19.8 us
    ppermute x14, waiting for transfers between devices, exchanged(): results[r] = lax.ppermute(blocks[r], 'cuts', route)  14.7 us
    unnamed x18, local copies, waits for them, and re-layouts  6.83 us
    pallas_call x1, Pallas kernels, shards(): pl.pallas_call(window_kernel, out_shape=[struct(rows, 2 * width)] * size,...  4.61 us
    ppermute x3, starting transfers between devices, handed(): return lax.ppermute(block, 'cuts', route)  4.02 us
  transfers between devices with their start and end apart: 17, of which 8 were waited for; matrix products, arithmetic and copies ran while one was open for 0% of the time, Pallas kernels for 1%

profile of v6, /device:TPU:0, one launch (start us, length us, event | category | flops | bytes accessed | tf_op | source)
XLA Modules:
  0.0 107.2 jit_solution(11130917178931615467)
XLA Ops:
  0.7 1.1 copy-done.3
  1.7 0.9 copy-done.5
  2.6 0.7 copy-done.6
  3.3 4.6 %windows.1 = (bf16[208,384]{1,0:T(8,128)(2,1)S(1)}, bf16[208,384]{1,0:T(8,128)(2,1)S(1)}, bf16[208,384]{1,0:T(8,128)(2,1)S(1)}, bf16[208,384]{1,0:T(8,128)(2,1)S...) custom-call(s32[2,6]{1,0:T(2,128)S(1)} %bitcast.1, ...), custom_call_target="tpu_custom_call" | custom-call | tf_op jit(solution)/shard_map/windows/pallas_call | solution.py:436
  7.9 2.4 %collective-permute-start = (bf16[208,384]{1,0:T(8,128)(2,1)S(1)}, bf16[208,384]{1,0:T(8,128)(2,1)S(1)}, u32[]{:S(2)}, u32[]{:S(2)}) collective-permute-start(bf16[208,384]{1,0:T(8,128)(2,1)S(1)} %get-tuple-element.36), channel_id=1, source_target_pairs={{0,1},{1,0},{2,3},{3,2},{5,4},{7,6},{8,9},{9,8},{10,11},{11,10},{1... | collective-permute-start | bytes 479240 | tf_op jit(solution)/shard_map/ppermute | solution.py:429
  10.3 4.4 %collective-permute-start.1 = (bf16[208,384]{1,0:T(8,128)(2,1)S(1)}, bf16[208,384]{1,0:T(8,128)(2,1)S(1)}, u32[]{:S(2)}, u32[]{:S(2)}) collective-permute-start(bf16[208,384]{1,0:T(8,128)(2,1)S(1)} %get-tuple-element.37), channel_id=1, source_target_pairs={{0,2},{1,3},{2,0},{3,1},{4,6},{6,4},{8,10},{9,11},{10,8},{11,9},{1... | collective-permute-start | bytes 479240 | tf_op jit(solution)/shard_map/ppermute | solution.py:429
  14.7 2.0 %collective-permute-start.2 = (bf16[208,384]{1,0:T(8,128)(2,1)S(1)}, bf16[208,384]{1,0:T(8,128)(2,1)S(1)}, u32[]{:S(2)}, u32[]{:S(2)}) collective-permute-start(bf16[208,384]{1,0:T(8,128)(2,1)S(1)} %get-tuple-element.38), channel_id=1, source_target_pairs={{0,3},{1,2},{2,1},{3,0},{5,6},{7,4},{8,11},{9,10},{10,9},{11,8},{1... | collective-permute-start | bytes 479240 | tf_op jit(solution)/shard_map/ppermute | solution.py:429
  16.7 2.1 %collective-permute-start.3 = (bf16[208,384]{1,0:T(8,128)(2,1)S(1)}, bf16[208,384]{1,0:T(8,128)(2,1)S(1)}, u32[]{:S(2)}, u32[]{:S(2)}) collective-permute-start(bf16[208,384]{1,0:T(8,128)(2,1)S(1)} %get-tuple-element.39), channel_id=1, source_target_pairs={{0,4},{2,6},{4,0},{5,1},{6,2},{7,3},{8,12},{10,14},{12,8},{13,9},{... | collective-permute-start | bytes 479240 | tf_op jit(solution)/shard_map/ppermute | solution.py:429
  18.9 1.3 %collective-permute-start.4 = (bf16[208,384]{1,0:T(8,128)(2,1)S(1)}, bf16[208,384]{1,0:T(8,128)(2,1)S(1)}, u32[]{:S(2)}, u32[]{:S(2)}) collective-permute-start(bf16[208,384]{1,0:T(8,128)(2,1)S(1)} %get-tuple-element.40), channel_id=1, source_target_pairs={{1,4},{3,6},{4,1},{5,0},{6,3},{7,2},{9,12},{11,14},{12,9},{13,8},{... | collective-permute-start | bytes 479240 | tf_op jit(solution)/shard_map/ppermute | solution.py:429
  20.2 0.0 collective-permute-done.refs_1_
  20.2 5.5 %collective-permute-start.5 = (bf16[208,384]{1,0:T(8,128)(2,1)S(1)}, bf16[208,384]{1,0:T(8,128)(2,1)S(1)}, u32[]{:S(2)}, u32[]{:S(2)}) collective-permute-start(bf16[208,384]{1,0:T(8,128)(2,1)S(1)} %get-tuple-element.41), channel_id=1, source_target_pairs={{0,6},{2,4},{4,2},{5,3},{6,0},{7,1},{8,14},{10,12},{12,10},{13,11}... | collective-permute-start | bytes 479240 | tf_op jit(solution)/shard_map/ppermute | solution.py:429
  25.7 0.0 collective-permute-done.1.refs_2_
  25.7 1.3 %collective-permute-start.6 = (bf16[208,384]{1,0:T(8,128)(2,1)S(1)}, bf16[208,384]{1,0:T(8,128)(2,1)S(1)}, u32[]{:S(2)}, u32[]{:S(2)}) collective-permute-start(bf16[208,384]{1,0:T(8,128)(2,1)S(1)} %get-tuple-element.42), channel_id=1, source_target_pairs={{1,6},{3,4},{4,3},{5,2},{6,1},{7,0},{9,14},{11,12},{12,11},{13,10}... | collective-permute-start | bytes 479240 | tf_op jit(solution)/shard_map/ppermute | solution.py:429
  27.0 0.0 collective-permute-done.2.refs_3_
  27.0 0.0 collective-permute-done.3.refs_4_
  27.0 0.3 collective-permute-done.4.refs_5_
  27.4 6.2 %collective-permute-done.5.refs_6_ = bf16[208,384]{1,0:T(8,128)(2,1)S(1)} collective-permute-done((bf16[208,384]{1,0:T(8,128)(2,1)S(1)}, bf16[208,384]{1,0:T(8,128)(2,1)S(1)}, u32[]{:S(2)}, u32[]{:S(2)}) %collective-permute-start.5) | collective-permute-done | bytes 159776 | tf_op jit(solution)/shard_map/ppermute | solution.py:429
  33.6 2.2 %collective-permute-done.6.refs_7_ = bf16[208,384]{1,0:T(8,128)(2,1)S(1)} collective-permute-done((bf16[208,384]{1,0:T(8,128)(2,1)S(1)}, bf16[208,384]{1,0:T(8,128)(2,1)S(1)}, u32[]{:S(2)}, u32[]{:S(2)}) %collective-permute-start.6) | collective-permute-done | bytes 159776 | tf_op jit(solution)/shard_map/ppermute | solution.py:429
  35.8 1.1 %copy-done = bf16[4,2,192,192]{3,2,1,0:T(8,128)(2,1)S(1)} copy-done((bf16[4,2,192,192]{3,2,1,0:T(8,128)(2,1)S(1)}, bf16[4,2,192,192]{3,2,1,0:T(8,128)(2,1)}, u32[]{:S(2)}) %copy-start) | copy-done | bytes 589848
  36.9 1.4 %copy-done.2 = bf16[8,2,192,192]{3,2,1,0:T(8,128)(2,1)S(1)} copy-done((bf16[8,2,192,192]{3,2,1,0:T(8,128)(2,1)S(1)}, bf16[8,2,192,192]{3,2,1,0:T(8,128)(2,1)}, u32[]{:S(2)}) %copy-start.2) | copy-done | bytes 1179672
  38.3 1.0 copy-done.4
  39.3 0.7 copy-done.8
  40.0 7.9 %first_forward.1 = (bf16[192,384]{1,0:T(8,128)(2,1)S(1)}, bf16[8,208,384]{2,1,0:T(8,128)(2,1)S(1)}, bf16[9,192,384]{2,1,0:T(8,128)(2,1)S(1)}, bf16[4,384,192]{2,...) custom-call(s32[6]{0:T(128)S(1)} %copy-done.8, ...), custom_call_target="tpu_custom_call" | custom-call | tf_op jit(solution)/shard_map/first_forward/pallas_call | solution.py:466
  47.8 0.0 copy-start.1
  47.9 1.4 %collective-permute-start.7 = (bf16[192,384]{1,0:T(8,128)(2,1)S(1)}, bf16[192,384]{1,0:T(8,128)(2,1)S(1)}, u32[]{:S(2)}, u32[]{:S(2)}) collective-permute-start(bf16[192,384]{1,0:T(8,128)(2,1)S(1)} %get-tuple-element.43._), channel_id=1, source_target_pairs={{0,8},{1,9},{2,10},{3,11},{4,12},{6,14},{16,24},{17,25},{18,26},{1... | collective-permute-start | bytes 442376 | tf_op jit(solution)/shard_map/ppermute | solution.py:434
  49.3 0.1 near_rows.1
  49.4 1.3 %collective-permute-start.8 = (f32[96,256]{1,0:T(8,128)S(1)}, f32[96,256]{1,0:T(8,128)S(1)}, u32[]{:S(2)}, u32[]{:S(2)}) collective-permute-start(f32[96,256]{1,0:T(8,128)S(1)} %near_rows.1), channel_id=1, source_target_pairs={{0,8},{1,9},{2,10},{3,11},{4,12},{6,14},{16,24},{17,25},{18,26},{1... | collective-permute-start | bytes 294920 | tf_op jit(solution)/shard_map/ppermute | solution.py:434
  50.7 2.8 %collective-permute-done.7.entering = bf16[192,384]{1,0:T(8,128)(2,1)S(1)} collective-permute-done((bf16[192,384]{1,0:T(8,128)(2,1)S(1)}, bf16[192,384]{1,0:T(8,128)(2,1)S(1)}, u32[]{:S(2)}, u32[]{:S(2)}) %collective-permute-start.7) | collective-permute-done | bytes 147488 | tf_op jit(solution)/shard_map/ppermute | solution.py:434
  53.5 0.8 forward.1
  54.3 1.1 %collective-permute-done.8.refs_0_ = f32[96,256]{1,0:T(8,128)S(1)} collective-permute-done((f32[96,256]{1,0:T(8,128)S(1)}, f32[96,256]{1,0:T(8,128)S(1)}, u32[]{:S(2)}, u32[]{:S(2)}) %collective-permute-start.8) | collective-permute-done | bytes 98336 | tf_op jit(solution)/shard_map/ppermute | solution.py:434
  55.4 0.6 middle.1
  55.9 1.3 %collective-permute-start.9 = (bf16[192,384]{1,0:T(8,128)(2,1)S(1)}, bf16[192,384]{1,0:T(8,128)(2,1)S(1)}, u32[]{:S(2)}, u32[]{:S(2)}) collective-permute-start(bf16[192,384]{1,0:T(8,128)(2,1)S(1)} %get-tuple-element.53), channel_id=1, source_target_pairs={{8,0},{9,1},{10,2},{11,3},{12,4},{14,6},{24,16},{25,17},{26,18},{2... | collective-permute-start | bytes 442376 | tf_op jit(solution)/shard_map/ppermute | solution.py:434
  57.2 15.9 %collective-permute-done.9.arriving = bf16[192,384]{1,0:T(8,128)(2,1)S(1)} collective-permute-done((bf16[192,384]{1,0:T(8,128)(2,1)S(1)}, bf16[192,384]{1,0:T(8,128)(2,1)S(1)}, u32[]{:S(2)}, u32[]{:S(2)}) %collective-permute-start.9) | collective-permute-done | bytes 147488 | tf_op jit(solution)/shard_map/ppermute | solution.py:434
  73.1 6.8 %backward.1 = (bf16[192,384]{1,0:T(8,128)(2,1)}, bf16[192,384]{1,0:T(8,128)(2,1)S(1)}, bf16[192,384]{1,0:T(8,128)(2,1)S(1)}, bf16[192,384]{1,0:T(8,128)(2,1)S(1)...) custom-call(bf16[192,384]{1,0:T(8,128)(2,1)S(1)} %collective-permute, ...), custom_call_target="tpu_custom_call" | custom-call | tf_op jit(solution)/shard_map/backward/pallas_call | solution.py:466
  79.9 1.9 %collective-permute-start.10 = (bf16[192,384]{1,0:T(8,128)(2,1)S(1)}, bf16[192,384]{1,0:T(8,128)(2,1)S(1)}, u32[]{:S(2)}, u32[]{:S(2)}) collective-permute-start(bf16[192,384]{1,0:T(8,128)(2,1)S(1)} %get-tuple-element.58), channel_id=1, source_target_pairs={{0,1},{1,0},{2,3},{3,2},{4,5},{6,7},{8,9},{9,8},{10,11},{11,10},{1... | collective-permute-start | bytes 442376 | tf_op jit(solution)/shard_map/ppermute | solution.py:429
  81.8 2.2 %collective-permute-start.11 = (bf16[192,384]{1,0:T(8,128)(2,1)S(1)}, bf16[192,384]{1,0:T(8,128)(2,1)S(1)}, u32[]{:S(2)}, u32[]{:S(2)}) collective-permute-start(bf16[192,384]{1,0:T(8,128)(2,1)S(1)} %get-tuple-element.59), channel_id=1, source_target_pairs={{0,2},{1,3},{2,0},{3,1},{4,6},{6,4},{8,10},{9,11},{10,8},{11,9},{1... | collective-permute-start | bytes 442376 | tf_op jit(solution)/shard_map/ppermute | solution.py:429
  84.1 3.5 %collective-permute-start.12 = (bf16[192,384]{1,0:T(8,128)(2,1)S(1)}, bf16[192,384]{1,0:T(8,128)(2,1)S(1)}, u32[]{:S(2)}, u32[]{:S(2)}) collective-permute-start(bf16[192,384]{1,0:T(8,128)(2,1)S(1)} %get-tuple-element.60), channel_id=1, source_target_pairs={{0,3},{1,2},{2,1},{3,0},{4,7},{6,5},{8,11},{9,10},{10,9},{11,8},{1... | collective-permute-start | bytes 442376 | tf_op jit(solution)/shard_map/ppermute | solution.py:429
  87.5 2.7 %collective-permute-start.13 = (bf16[192,384]{1,0:T(8,128)(2,1)S(1)}, bf16[192,384]{1,0:T(8,128)(2,1)S(1)}, u32[]{:S(2)}, u32[]{:S(2)}) collective-permute-start(bf16[192,384]{1,0:T(8,128)(2,1)S(1)} %get-tuple-element.61), channel_id=1, source_target_pairs={{0,4},{1,5},{2,6},{3,7},{4,0},{6,2},{8,12},{9,13},{10,14},{11,15},... | collective-permute-start | bytes 442376 | tf_op jit(solution)/shard_map/ppermute | solution.py:429
  90.3 1.3 %collective-permute-start.14 = (bf16[192,384]{1,0:T(8,128)(2,1)S(1)}, bf16[192,384]{1,0:T(8,128)(2,1)S(1)}, u32[]{:S(2)}, u32[]{:S(2)}) collective-permute-start(bf16[192,384]{1,0:T(8,128)(2,1)S(1)} %get-tuple-element.62), channel_id=1, source_target_pairs={{0,5},{1,4},{2,7},{3,6},{4,1},{6,3},{8,13},{9,12},{10,15},{11,14},... | collective-permute-start | bytes 442376 | tf_op jit(solution)/shard_map/ppermute | solution.py:429
  91.6 0.0 collective-permute-done.10.refs_1_
  91.6 3.5 %collective-permute-start.15 = (bf16[192,384]{1,0:T(8,128)(2,1)S(1)}, bf16[192,384]{1,0:T(8,128)(2,1)S(1)}, u32[]{:S(2)}, u32[]{:S(2)}) collective-permute-start(bf16[192,384]{1,0:T(8,128)(2,1)S(1)} %get-tuple-element.63), channel_id=1, source_target_pairs={{0,6},{1,7},{2,4},{3,5},{4,2},{6,0},{8,14},{9,15},{10,12},{11,13},... | collective-permute-start | bytes 442376 | tf_op jit(solution)/shard_map/ppermute | solution.py:429
  95.1 0.0 collective-permute-done.11.refs_2_
  95.1 1.3 %collective-permute-start.16 = (bf16[192,384]{1,0:T(8,128)(2,1)S(1)}, bf16[192,384]{1,0:T(8,128)(2,1)S(1)}, u32[]{:S(2)}, u32[]{:S(2)}) collective-permute-start(bf16[192,384]{1,0:T(8,128)(2,1)S(1)} %get-tuple-element.64), channel_id=1, source_target_pairs={{0,7},{1,6},{2,5},{3,4},{4,3},{6,1},{8,15},{9,14},{10,13},{11,12},... | collective-permute-start | bytes 442376 | tf_op jit(solution)/shard_map/ppermute | solution.py:429
  96.4 0.0 collective-permute-done.13.refs_4_
  96.4 0.0 collective-permute-done.14.refs_5_
  96.4 3.1 %collective-permute-done.15.refs_6_ = bf16[192,384]{1,0:T(8,128)(2,1)S(1)} collective-permute-done((bf16[192,384]{1,0:T(8,128)(2,1)S(1)}, bf16[192,384]{1,0:T(8,128)(2,1)S(1)}, u32[]{:S(2)}, u32[]{:S(2)}) %collective-permute-start.15) | collective-permute-done | bytes 147488 | tf_op jit(solution)/shard_map/ppermute | solution.py:429
  99.5 2.9 %collective-permute-done.16.refs_7_ = bf16[192,384]{1,0:T(8,128)(2,1)S(1)} collective-permute-done((bf16[192,384]{1,0:T(8,128)(2,1)S(1)}, bf16[192,384]{1,0:T(8,128)(2,1)S(1)}, u32[]{:S(2)}, u32[]{:S(2)}) %collective-permute-start.16) | collective-permute-done | bytes 147488 | tf_op jit(solution)/shard_map/ppermute | solution.py:429
  102.4 4.8 %sum_windows.1 = f32[1,2,384,384]{3,2,1,0:T(8,128)} custom-call(s32[2,6]{1,0:T(2,128)S(1)} %bitcast.2, bf16[192,384]{1,0:T(8,128)(2,1)S(1)} %get-tuple-element.57.refs_0_, bf16[192,384]{1,0:T(8,128)(2,1)S(1)} %collective-permute-done.10.refs_1_, bf16[192,384]{1,0:T(8,128)(2,1)S(1)} %collective-permute-done.11.refs_2_, ...), custom_call_target="tpu_custom_call" | custom-call | tf_op jit(solution)/shard_map/sum_windows/pallas_call | solution.py:466
  (11 shorter events, 0.0 us)
Async XLA Ops:
  0.7 1.1 copy-start.3
  1.7 0.9 copy-start.5
  2.6 0.7 copy-start.6
  7.9 12.3 %collective-permute-start = (bf16[208,384]{1,0:T(8,128)(2,1)S(1)}, bf16[208,384]{1,0:T(8,128)(2,1)S(1)}, u32[]{:S(2)}, u32[]{:S(2)}) collective-permute-start(bf16[208,384]{1,0:T(8,128)(2,1)S(1)} %get-tuple-element.36), channel_id=1, source_target_pairs={{0,1},{1,0},{2,3},{3,2},{5,4},{7,6},{8,9},{9,8},{10,11},{11,10},{1... | collective-permute-start | bytes 479240 | tf_op jit(solution)/shard_map/ppermute | solution.py:429
  10.3 15.4 %collective-permute-start.1 = (bf16[208,384]{1,0:T(8,128)(2,1)S(1)}, bf16[208,384]{1,0:T(8,128)(2,1)S(1)}, u32[]{:S(2)}, u32[]{:S(2)}) collective-permute-start(bf16[208,384]{1,0:T(8,128)(2,1)S(1)} %get-tuple-element.37), channel_id=1, source_target_pairs={{0,2},{1,3},{2,0},{3,1},{4,6},{6,4},{8,10},{9,11},{10,8},{11,9},{1... | collective-permute-start | bytes 479240 | tf_op jit(solution)/shard_map/ppermute | solution.py:429
  14.7 12.3 %collective-permute-start.2 = (bf16[208,384]{1,0:T(8,128)(2,1)S(1)}, bf16[208,384]{1,0:T(8,128)(2,1)S(1)}, u32[]{:S(2)}, u32[]{:S(2)}) collective-permute-start(bf16[208,384]{1,0:T(8,128)(2,1)S(1)} %get-tuple-element.38), channel_id=1, source_target_pairs={{0,3},{1,2},{2,1},{3,0},{5,6},{7,4},{8,11},{9,10},{10,9},{11,8},{1... | collective-permute-start | bytes 479240 | tf_op jit(solution)/shard_map/ppermute | solution.py:429
  16.7 10.3 %collective-permute-start.3 = (bf16[208,384]{1,0:T(8,128)(2,1)S(1)}, bf16[208,384]{1,0:T(8,128)(2,1)S(1)}, u32[]{:S(2)}, u32[]{:S(2)}) collective-permute-start(bf16[208,384]{1,0:T(8,128)(2,1)S(1)} %get-tuple-element.39), channel_id=1, source_target_pairs={{0,4},{2,6},{4,0},{5,1},{6,2},{7,3},{8,12},{10,14},{12,8},{13,9},{... | collective-permute-start | bytes 479240 | tf_op jit(solution)/shard_map/ppermute | solution.py:429
  18.9 8.5 %collective-permute-start.4 = (bf16[208,384]{1,0:T(8,128)(2,1)S(1)}, bf16[208,384]{1,0:T(8,128)(2,1)S(1)}, u32[]{:S(2)}, u32[]{:S(2)}) collective-permute-start(bf16[208,384]{1,0:T(8,128)(2,1)S(1)} %get-tuple-element.40), channel_id=1, source_target_pairs={{1,4},{3,6},{4,1},{5,0},{6,3},{7,2},{9,12},{11,14},{12,9},{13,8},{... | collective-permute-start | bytes 479240 | tf_op jit(solution)/shard_map/ppermute | solution.py:429
  20.2 13.4 %collective-permute-start.5 = (bf16[208,384]{1,0:T(8,128)(2,1)S(1)}, bf16[208,384]{1,0:T(8,128)(2,1)S(1)}, u32[]{:S(2)}, u32[]{:S(2)}) collective-permute-start(bf16[208,384]{1,0:T(8,128)(2,1)S(1)} %get-tuple-element.41), channel_id=1, source_target_pairs={{0,6},{2,4},{4,2},{5,3},{6,0},{7,1},{8,14},{10,12},{12,10},{13,11}... | collective-permute-start | bytes 479240 | tf_op jit(solution)/shard_map/ppermute | solution.py:429
  25.7 10.0 %collective-permute-start.6 = (bf16[208,384]{1,0:T(8,128)(2,1)S(1)}, bf16[208,384]{1,0:T(8,128)(2,1)S(1)}, u32[]{:S(2)}, u32[]{:S(2)}) collective-permute-start(bf16[208,384]{1,0:T(8,128)(2,1)S(1)} %get-tuple-element.42), channel_id=1, source_target_pairs={{1,6},{3,4},{4,3},{5,2},{6,1},{7,0},{9,14},{11,12},{12,11},{13,10}... | collective-permute-start | bytes 479240 | tf_op jit(solution)/shard_map/ppermute | solution.py:429
  35.8 1.1 %copy-start = (bf16[4,2,192,192]{3,2,1,0:T(8,128)(2,1)S(1)}, bf16[4,2,192,192]{3,2,1,0:T(8,128)(2,1)}, u32[]{:S(2)}) copy-start(bf16[4,2,192,192]{3,2,1,0:T(8,128)(2,1)} %refs_2_.1) | copy-start | bytes 1769476
  36.9 1.4 %copy-start.2 = (bf16[8,2,192,192]{3,2,1,0:T(8,128)(2,1)S(1)}, bf16[8,2,192,192]{3,2,1,0:T(8,128)(2,1)}, u32[]{:S(2)}) copy-start(bf16[8,2,192,192]{3,2,1,0:T(8,128)(2,1)} %probes.1) | copy-start | bytes 3538948
  38.3 1.0 copy-start.4
  39.3 0.7 copy-start.8
  47.8 5.7 %copy-start.1 = (bf16[4,2,192,192]{3,2,1,0:T(8,128)(2,1)S(1)}, bf16[4,2,192,192]{3,2,1,0:T(8,128)(2,1)}, u32[]{:S(2)}) copy-start(bf16[4,2,192,192]{3,2,1,0:T(8,128)(2,1)} %refs_2_.1) | copy-start | bytes 1769476
  47.9 5.7 %collective-permute-start.7 = (bf16[192,384]{1,0:T(8,128)(2,1)S(1)}, bf16[192,384]{1,0:T(8,128)(2,1)S(1)}, u32[]{:S(2)}, u32[]{:S(2)}) collective-permute-start(bf16[192,384]{1,0:T(8,128)(2,1)S(1)} %get-tuple-element.43._), channel_id=1, source_target_pairs={{0,8},{1,9},{2,10},{3,11},{4,12},{6,14},{16,24},{17,25},{18,26},{1... | collective-permute-start | bytes 442376 | tf_op jit(solution)/shard_map/ppermute | solution.py:434
  49.4 6.0 %collective-permute-start.8 = (f32[96,256]{1,0:T(8,128)S(1)}, f32[96,256]{1,0:T(8,128)S(1)}, u32[]{:S(2)}, u32[]{:S(2)}) collective-permute-start(f32[96,256]{1,0:T(8,128)S(1)} %near_rows.1), channel_id=1, source_target_pairs={{0,8},{1,9},{2,10},{3,11},{4,12},{6,14},{16,24},{17,25},{18,26},{1... | collective-permute-start | bytes 294920 | tf_op jit(solution)/shard_map/ppermute | solution.py:434
  55.9 17.2 %collective-permute-start.9 = (bf16[192,384]{1,0:T(8,128)(2,1)S(1)}, bf16[192,384]{1,0:T(8,128)(2,1)S(1)}, u32[]{:S(2)}, u32[]{:S(2)}) collective-permute-start(bf16[192,384]{1,0:T(8,128)(2,1)S(1)} %get-tuple-element.53), channel_id=1, source_target_pairs={{8,0},{9,1},{10,2},{11,3},{12,4},{14,6},{24,16},{25,17},{26,18},{2... | collective-permute-start | bytes 442376 | tf_op jit(solution)/shard_map/ppermute | solution.py:434
  73.1 29.3 %copy-start.7 = (s32[6,2]{0,1:T(2,128)S(1)}, s32[6,2]{0,1:T(2,128)}, u32[]{:S(2)}) copy-start(s32[6,2]{0,1:T(2,128)} %param.13) | copy-start | bytes 148
  79.9 11.7 %collective-permute-start.10 = (bf16[192,384]{1,0:T(8,128)(2,1)S(1)}, bf16[192,384]{1,0:T(8,128)(2,1)S(1)}, u32[]{:S(2)}, u32[]{:S(2)}) collective-permute-start(bf16[192,384]{1,0:T(8,128)(2,1)S(1)} %get-tuple-element.58), channel_id=1, source_target_pairs={{0,1},{1,0},{2,3},{3,2},{4,5},{6,7},{8,9},{9,8},{10,11},{11,10},{1... | collective-permute-start | bytes 442376 | tf_op jit(solution)/shard_map/ppermute | solution.py:429
  81.8 13.2 %collective-permute-start.11 = (bf16[192,384]{1,0:T(8,128)(2,1)S(1)}, bf16[192,384]{1,0:T(8,128)(2,1)S(1)}, u32[]{:S(2)}, u32[]{:S(2)}) collective-permute-start(bf16[192,384]{1,0:T(8,128)(2,1)S(1)} %get-tuple-element.59), channel_id=1, source_target_pairs={{0,2},{1,3},{2,0},{3,1},{4,6},{6,4},{8,10},{9,11},{10,8},{11,9},{1... | collective-permute-start | bytes 442376 | tf_op jit(solution)/shard_map/ppermute | solution.py:429
  84.1 12.3 %collective-permute-start.12 = (bf16[192,384]{1,0:T(8,128)(2,1)S(1)}, bf16[192,384]{1,0:T(8,128)(2,1)S(1)}, u32[]{:S(2)}, u32[]{:S(2)}) collective-permute-start(bf16[192,384]{1,0:T(8,128)(2,1)S(1)} %get-tuple-element.60), channel_id=1, source_target_pairs={{0,3},{1,2},{2,1},{3,0},{4,7},{6,5},{8,11},{9,10},{10,9},{11,8},{1... | collective-permute-start | bytes 442376 | tf_op jit(solution)/shard_map/ppermute | solution.py:429
  87.5 8.9 %collective-permute-start.13 = (bf16[192,384]{1,0:T(8,128)(2,1)S(1)}, bf16[192,384]{1,0:T(8,128)(2,1)S(1)}, u32[]{:S(2)}, u32[]{:S(2)}) collective-permute-start(bf16[192,384]{1,0:T(8,128)(2,1)S(1)} %get-tuple-element.61), channel_id=1, source_target_pairs={{0,4},{1,5},{2,6},{3,7},{4,0},{6,2},{8,12},{9,13},{10,14},{11,15},... | collective-permute-start | bytes 442376 | tf_op jit(solution)/shard_map/ppermute | solution.py:429
  90.3 6.1 %collective-permute-start.14 = (bf16[192,384]{1,0:T(8,128)(2,1)S(1)}, bf16[192,384]{1,0:T(8,128)(2,1)S(1)}, u32[]{:S(2)}, u32[]{:S(2)}) collective-permute-start(bf16[192,384]{1,0:T(8,128)(2,1)S(1)} %get-tuple-element.62), channel_id=1, source_target_pairs={{0,5},{1,4},{2,7},{3,6},{4,1},{6,3},{8,13},{9,12},{10,15},{11,14},... | collective-permute-start | bytes 442376 | tf_op jit(solution)/shard_map/ppermute | solution.py:429
  91.6 7.9 %collective-permute-start.15 = (bf16[192,384]{1,0:T(8,128)(2,1)S(1)}, bf16[192,384]{1,0:T(8,128)(2,1)S(1)}, u32[]{:S(2)}, u32[]{:S(2)}) collective-permute-start(bf16[192,384]{1,0:T(8,128)(2,1)S(1)} %get-tuple-element.63), channel_id=1, source_target_pairs={{0,6},{1,7},{2,4},{3,5},{4,2},{6,0},{8,14},{9,15},{10,12},{11,13},... | collective-permute-start | bytes 442376 | tf_op jit(solution)/shard_map/ppermute | solution.py:429
  95.1 7.3 %collective-permute-start.16 = (bf16[192,384]{1,0:T(8,128)(2,1)S(1)}, bf16[192,384]{1,0:T(8,128)(2,1)S(1)}, u32[]{:S(2)}, u32[]{:S(2)}) collective-permute-start(bf16[192,384]{1,0:T(8,128)(2,1)S(1)} %get-tuple-element.64), channel_id=1, source_target_pairs={{0,7},{1,6},{2,5},{3,4},{4,3},{6,1},{8,15},{9,14},{10,13},{11,12},... | collective-permute-start | bytes 442376 | tf_op jit(solution)/shard_map/ppermute | solution.py:429

commit v7 on v5

--- a/solution.py
+++ b/solution.py
@@ -122,13 +122,14 @@
     return sorted(order[:positions])
 
 
-def window_kernel(offsets_ref, index_ref, objects_in, measured_in, blocks, objects, measured, sems):
+def window_kernel(offsets_in, index_ref, objects_in, measured_in, blocks, offsets_ref, objects, measured, sems):
     positions, near_rows, width = measured.shape
     extent = objects.shape[-1]
     copies = [
         pltpu.make_async_copy(objects_in.at[0, 0], objects.at[0], sems.at[0]),
         pltpu.make_async_copy(objects_in.at[0, 1], objects.at[1], sems.at[1]),
         pltpu.make_async_copy(measured_in, measured, sems.at[2]),
+        pltpu.make_async_copy(offsets_in, offsets_ref, sems.at[3]),
     ]
     for copy in copies:
         copy.start()
@@ -191,7 +192,7 @@
         waves[k + 1] = dot(h, rf[which]).astype(BF16)
         return carried
 
-    lax.fori_loop(0, sections, step, 0, unroll=2)
+    lax.fori_loop(0, sections, step, 0, unroll=True)
 
 
 def backward_steps(blocks, waves, indices, lb, rb, grads, g):
@@ -208,7 +209,7 @@
         g[...] = passed.astype(BF16)
         return carried
 
-    lax.fori_loop(0, sections, step, 0, unroll=2)
+    lax.fori_loop(0, sections, step, 0, unroll=True)
 
 
 def detector(psi, observed, left, right, right_conj):
@@ -367,6 +368,7 @@
 VMEM = pl.BlockSpec(memory_space=pltpu.VMEM)
 SMEM = pl.BlockSpec(memory_space=pltpu.SMEM)
 HBM = pl.BlockSpec(memory_space=pl.ANY)
+ALONE = pltpu.CompilerParams(vmem_limit_bytes=60 * 1024 * 1024)
 PARAMS = pltpu.CompilerParams(vmem_limit_bytes=20 * 1024 * 1024)
 
 
@@ -394,14 +396,15 @@
     blocks = pl.pallas_call(
         window_kernel,
         out_shape=struct(size, rows, 2 * width),
-        in_specs=[SMEM, SMEM, HBM, HBM],
+        in_specs=[HBM, SMEM, HBM, HBM],
         out_specs=VMEM,
         scratch_shapes=[
+            pltpu.SMEM(offsets.shape[::-1], jnp.int32),
             pltpu.VMEM(objects.shape[1:], BF16),
             pltpu.VMEM(measured.shape, F32),
-            pltpu.SemaphoreType.DMA((3,)),
+            pltpu.SemaphoreType.DMA((4,)),
         ],
-        compiler_params=PARAMS,
+        compiler_params=ALONE,
         name="windows",
     )(offsets.T, prop_index, objects, measured)
     blocks = exchanged(blocks)

time: 90.5 us -> 88.9 us (0.982)
  local copies, waits for them, and re-layouts: 2.65 us -> 0.03 us
  Pallas kernels: 18.6 us -> 19.8 us
    unnamed x16 -> x10, local copies, waits for them, and re-layouts: 2.65 us -> 0.03 us
    pallas_call x1, Pallas kernels: 2.91 us -> 4.3 us  [shards(): pl.pallas_call(window_kernel, out_shape=struct(size, rows, 2 * width), in...]
where the time goes in v7:
time: 88.9 us; the launch traced here: 88.6 us
  blocking collectives  45.1 us (51%)
  Pallas kernels  19.8 us (22%)
  waiting for transfers between devices  19.1 us (21%)
  starting transfers between devices  3.89 us (4%)
    all_to_all x2, blocking collectives, exchanged(): lax.all_to_all(blocks, 'cuts', 0, 0, axis_index_groups=members, tiled=True)  45.1 us
    ppermute x3, waiting for transfers between devices, handed(): return lax.ppermute(block, 'cuts', route)  19.1 us
    pallas_call x5, Pallas kernels, call(): pl.pallas_call(kernel, out_shape=out_shape, in_specs=in_specs, out_specs=...  12.3 us
    pallas_call x1, Pallas kernels, shards(): pl.pallas_call(window_kernel, out_shape=struct(size, rows, 2 * width), in...  4.3 us
    ppermute x3, starting transfers between devices, handed(): return lax.ppermute(block, 'cuts', route)  3.89 us
    pallas_call x1, Pallas kernels, shards(): pl.pallas_call(gather_kernel, out_shape=jax.ShapeDtypeStruct(objects.shap...  3.18 us
  transfers between devices with their start and end apart: 3, of which 3 were waited for; matrix products, arithmetic and copies ran while one was open for 0% of the time, Pallas kernels for 1%

profile of v7, /device:TPU:0, one launch (start us, length us, event | category | flops | bytes accessed | tf_op | source)
XLA Modules:
  0.0 88.6 jit_solution(9242297719619317009)
XLA Ops:
  0.7 0.0 copy-start.2
  0.7 4.3 %windows.1 = bf16[8,208,384]{2,1,0:T(8,128)(2,1)} custom-call(s32[2,6]{1,0:T(2,128)} %bitcast.1, s32[1]{0:T(128)S(6)} %copy.9.index_ref, bf16[1,2,384,384]{3,2,1,0:T(8,128)(2,1)} %objects_in.1, f32[6,12,192]{2,1,0:T(8,128)} %measured_in.1), custom_call_target="tpu_custom_call" | custom-call | tf_op jit(solution)/shard_map/windows/pallas_call | solution.py:396
  5.0 0.0 copy-start
  5.0 0.0 copy-start.1
  5.0 0.0 copy-start.4
  5.0 22.6 %all_to_all.10.blocks.refs_1_ = bf16[8,208,384]{2,1,0:T(8,128)(2,1)S(1)} all-to-all(bf16[8,208,384]{2,1,0:T(8,128)(2,1)} %windows.1), channel_id=1, replica_groups={{0,1,2,3,4,5,6,7},{8,9,10,11,12,13,14,15},{16,17,18,19,20,21,22,23},{24..., dimensions={0} | all-to-all | bytes 2555904 | tf_op jit(solution)/shard_map/all_to_all | solution.py:390
  27.6 0.0 copy-done.2
  27.7 0.0 copy-done
  27.7 0.0 copy-done.1
  27.7 0.0 copy-done.4
  27.7 5.8 %first_forward.1 = (bf16[192,384]{1,0:T(8,128)(2,1)S(1)}, bf16[9,192,384]{2,1,0:T(8,128)(2,1)S(1)}, bf16[4,384,192]{2,1,0:T(8,128)(2,1)S(1)}, bf16[4,384,384]{2,...) custom-call(s32[6]{0:T(128)S(1)} %copy-done.4, ...), custom_call_target="tpu_custom_call" | custom-call | tf_op jit(solution)/shard_map/first_forward/pallas_call | solution.py:426
  33.5 1.3 %collective-permute-start = (bf16[192,384]{1,0:T(8,128)(2,1)S(1)}, bf16[192,384]{1,0:T(8,128)(2,1)S(1)}, u32[]{:S(2)}, u32[]{:S(2)}) collective-permute-start(bf16[192,384]{1,0:T(8,128)(2,1)S(1)} %get-tuple-element.19._), channel_id=1, source_target_pairs={{0,8},{1,9},{2,10},{3,11},{4,12},{6,14},{16,24},{17,25},{18,26},{1... | collective-permute-start | bytes 442376 | tf_op jit(solution)/shard_map/ppermute | solution.py:394
  34.8 0.1 near_rows.1
  34.9 1.3 %collective-permute-start.1 = (f32[96,256]{1,0:T(8,128)S(1)}, f32[96,256]{1,0:T(8,128)S(1)}, u32[]{:S(2)}, u32[]{:S(2)}) collective-permute-start(f32[96,256]{1,0:T(8,128)S(1)} %near_rows.1), channel_id=1, source_target_pairs={{0,8},{1,9},{2,10},{3,11},{4,12},{6,14},{16,24},{17,25},{18,26},{1... | collective-permute-start | bytes 294920 | tf_op jit(solution)/shard_map/ppermute | solution.py:394
  36.2 2.9 %collective-permute-done.entering = bf16[192,384]{1,0:T(8,128)(2,1)S(1)} collective-permute-done((bf16[192,384]{1,0:T(8,128)(2,1)S(1)}, bf16[192,384]{1,0:T(8,128)(2,1)S(1)}, u32[]{:S(2)}, u32[]{:S(2)}) %collective-permute-start) | collective-permute-done | bytes 147488 | tf_op jit(solution)/shard_map/ppermute | solution.py:394
  39.0 0.8 forward.1
  39.8 0.3 collective-permute-done.1.refs_0_
  40.1 0.6 middle.1
  40.7 1.3 %collective-permute-start.2 = (bf16[192,384]{1,0:T(8,128)(2,1)S(1)}, bf16[192,384]{1,0:T(8,128)(2,1)S(1)}, u32[]{:S(2)}, u32[]{:S(2)}) collective-permute-start(bf16[192,384]{1,0:T(8,128)(2,1)S(1)} %get-tuple-element.28), channel_id=1, source_target_pairs={{8,0},{9,1},{10,2},{11,3},{12,4},{14,6},{24,16},{25,17},{26,18},{2... | collective-permute-start | bytes 442376 | tf_op jit(solution)/shard_map/ppermute | solution.py:394
  42.0 15.9 %collective-permute-done.2.arriving = bf16[192,384]{1,0:T(8,128)(2,1)S(1)} collective-permute-done((bf16[192,384]{1,0:T(8,128)(2,1)S(1)}, bf16[192,384]{1,0:T(8,128)(2,1)S(1)}, u32[]{:S(2)}, u32[]{:S(2)}) %collective-permute-start.2) | collective-permute-done | bytes 147488 | tf_op jit(solution)/shard_map/ppermute | solution.py:394
  57.9 5.1 %backward.1 = (bf16[192,384]{1,0:T(8,128)(2,1)}, bf16[8,192,384]{2,1,0:T(8,128)(2,1)S(1)}) custom-call(bf16[192,384]{1,0:T(8,128)(2,1)S(1)} %collective-permute-done.2.arriving, bf16[9,192,384]{2,1,0:T(8,128)(2,1)S(1)} %get-tuple-element.22.waves, bf16[8,208,384]{2,1,0:T(8,128)(2,1)S(1)} %all_to_all.10.blocks.refs_1_, ...), custom_call_target="tpu_custom_call" | custom-call | tf_op jit(solution)/shard_map/backward/pallas_call | solution.py:426
  63.0 0.0 copy-start.3
  63.0 22.4 %all_to_all.11.grads_ref = bf16[8,192,384]{2,1,0:T(8,128)(2,1)S(1)} all-to-all(bf16[8,192,384]{2,1,0:T(8,128)(2,1)S(1)} %get-tuple-element.32), channel_id=1, replica_groups={{0,1,2,3,4,5,6,7},{8,9,10,11,12,13,14,15},{16,17,18,19,20,21,22,23},{24..., dimensions={0} | all-to-all | bytes 2359296 | tf_op jit(solution)/shard_map/all_to_all | solution.py:390
  85.4 0.0 copy-done.3
  85.4 3.2 %sum_windows.1 = f32[1,2,384,384]{3,2,1,0:T(8,128)} custom-call(s32[2,6]{1,0:T(2,128)S(1)} %bitcast.2, bf16[8,192,384]{2,1,0:T(8,128)(2,1)S(1)} %all_to_all.11.grads_ref), custom_call_target="tpu_custom_call" | custom-call | tf_op jit(solution)/shard_map/sum_windows/pallas_call | solution.py:480
Async XLA Ops:
  0.7 27.0 %copy-start.2 = (f32[2,192,192]{2,1,0:T(8,128)S(1)}, f32[2,192,192]{2,1,0:T(8,128)}, u32[]{:S(2)}) copy-start(f32[2,192,192]{2,1,0:T(8,128)} %constant.2.clone.dft) | copy-start | bytes 884740
  5.0 22.7 %copy-start = (bf16[4,2,192,192]{3,2,1,0:T(8,128)(2,1)S(1)}, bf16[4,2,192,192]{3,2,1,0:T(8,128)(2,1)}, u32[]{:S(2)}) copy-start(bf16[4,2,192,192]{3,2,1,0:T(8,128)(2,1)} %refs_2_.1) | copy-start | bytes 1769476
  5.0 22.7 %copy-start.1 = (bf16[8,2,192,192]{3,2,1,0:T(8,128)(2,1)S(1)}, bf16[8,2,192,192]{3,2,1,0:T(8,128)(2,1)}, u32[]{:S(2)}) copy-start(bf16[8,2,192,192]{3,2,1,0:T(8,128)(2,1)} %probes.1) | copy-start | bytes 3538948
  5.0 22.7 %copy-start.4 = (s32[6]{0:T(128)S(1)}, s32[6]{0:T(128)}, u32[]{:S(2)}) copy-start(s32[6]{0:T(128)} %group_ref.1) | copy-start | bytes 76
  33.5 5.6 %collective-permute-start = (bf16[192,384]{1,0:T(8,128)(2,1)S(1)}, bf16[192,384]{1,0:T(8,128)(2,1)S(1)}, u32[]{:S(2)}, u32[]{:S(2)}) collective-permute-start(bf16[192,384]{1,0:T(8,128)(2,1)S(1)} %get-tuple-element.19._), channel_id=1, source_target_pairs={{0,8},{1,9},{2,10},{3,11},{4,12},{6,14},{16,24},{17,25},{18,26},{1... | collective-permute-start | bytes 442376 | tf_op jit(solution)/shard_map/ppermute | solution.py:394
  34.9 5.3 %collective-permute-start.1 = (f32[96,256]{1,0:T(8,128)S(1)}, f32[96,256]{1,0:T(8,128)S(1)}, u32[]{:S(2)}, u32[]{:S(2)}) collective-permute-start(f32[96,256]{1,0:T(8,128)S(1)} %near_rows.1), channel_id=1, source_target_pairs={{0,8},{1,9},{2,10},{3,11},{4,12},{6,14},{16,24},{17,25},{18,26},{1... | collective-permute-start | bytes 294920 | tf_op jit(solution)/shard_map/ppermute | solution.py:394
  40.7 17.2 %collective-permute-start.2 = (bf16[192,384]{1,0:T(8,128)(2,1)S(1)}, bf16[192,384]{1,0:T(8,128)(2,1)S(1)}, u32[]{:S(2)}, u32[]{:S(2)}) collective-permute-start(bf16[192,384]{1,0:T(8,128)(2,1)S(1)} %get-tuple-element.28), channel_id=1, source_target_pairs={{8,0},{9,1},{10,2},{11,3},{12,4},{14,6},{24,16},{25,17},{26,18},{2... | collective-permute-start | bytes 442376 | tf_op jit(solution)/shard_map/ppermute | solution.py:394
  63.0 22.4 %copy-start.3 = (s32[6,2]{0,1:T(2,128)S(1)}, s32[6,2]{0,1:T(2,128)}, u32[]{:S(2)}) copy-start(s32[6,2]{0,1:T(2,128)} %param.13) | copy-start | bytes 148

commit v8 on v7

--- a/solution.py
+++ b/solution.py
@@ -103,6 +103,19 @@
     return jnp.where(taken == wanted, 1.0, 0.0).astype(BF16)
 
 
+def rows_near(x, start, count):
+    limit = x.shape[0] - count
+    bit = 1 << (limit.bit_length() - 1)
+    while bit >= ROWS:
+        length = count + bit
+        short = bit + length - x.shape[0]
+        if short > 0:
+            x = jnp.concatenate([x, jnp.zeros((short, x.shape[1]), x.dtype)], axis=0)
+        x = jnp.where(lax.bitwise_and(start, bit) != 0, x[bit : bit + length], x[:length])
+        bit //= 2
+    return x
+
+
 def packed(real, imag, columns, start):
     left = dot(real, picker(columns, start, False))
     right = dot(imag, picker(columns, start, True))
@@ -118,11 +131,11 @@
 
 
 def slots_of(positions, size):
-    order = list(range(0, size, 2)) + list(range(1, size, 2))
+    order = list(range(0, size, 2)) + list(range(size - 1, 0, -2))
     return sorted(order[:positions])
 
 
-def window_kernel(offsets_in, index_ref, objects_in, measured_in, blocks, offsets_ref, objects, measured, sems):
+def window_kernel(offsets_in, index_ref, objects_in, measured_in, blocks_out, blocks, offsets_ref, objects, measured, sems):
     positions, near_rows, width = measured.shape
     extent = objects.shape[-1]
     copies = [
@@ -133,18 +146,24 @@
     ]
     for copy in copies:
         copy.start()
-    tag = jnp.full((ROWS - near_rows, 2 * width), index_ref[0], jnp.int32).astype(F32)
+    tag = jnp.full((ROWS, LANES), index_ref[0], jnp.int32).astype(F32)
     for copy in copies:
         copy.wait()
-    field = jnp.concatenate([objects[0], objects[1]], axis=1)
+    sending = []
     for p, slot in enumerate(slots_of(positions, blocks.shape[0])):
-        both = dot(row_picker((width, extent), offsets_ref[0, p]), field).astype(BF16)
-        window = packed(both[:, :extent], both[:, extent:], extent, offsets_ref[1, p])
-        blocks[slot, :width, :] = window.astype(BF16)
-        high = measured[p].astype(BF16).astype(F32)
-        low = measured[p] - high
-        seen = jnp.concatenate([high[:, :LANES], low[:, :LANES], high[:, LANES:], low[:, LANES:]], axis=1)
-        blocks[slot, width:, :] = jnp.concatenate([seen, tag], axis=0).astype(BF16)
+        start = offsets_ref[0, p]
+        real, imag = (rows_near(objects[c], start, width) for c in range(2))
+        window = packed(real, imag, extent, offsets_ref[1, p]).astype(BF16)
+        shift = lax.bitwise_and(start, ROWS - 1)
+        blocks[slot, :width, :] = dot(row_picker((width, width + ROWS), shift), window).astype(BF16)
+        tail = measured[p, :, LANES:]
+        seen = jnp.concatenate([measured[p, :, :LANES], tail, tail, tag[:near_rows]], axis=1)
+        left_over = jnp.concatenate([tag[near_rows:]] * 3, axis=1)
+        blocks[slot, width:, :] = jnp.concatenate([seen, left_over], axis=0).astype(BF16)
+        sending.append(pltpu.make_async_copy(blocks.at[slot], blocks_out.at[slot], sems.at[4 + p]))
+        sending[-1].start()
+    for copy in sending:
+        copy.wait()
 
 
 def right_table(real, imag):
@@ -229,7 +248,7 @@
 
 def read_indices(blocks, indices, count):
     for k in range(blocks.shape[0]):
-        tag = jnp.max(blocks[k, -ROWS:, :LANES].astype(F32)[ROWS - 1 :])
+        tag = jnp.max(blocks[k, -ROWS:, 2 * LANES :].astype(F32))
         indices[k] = jnp.clip(tag.astype(jnp.int32), 0, count - 1)
 
 
@@ -240,14 +259,13 @@
 
 def observe(blocks, near_rows, observed, first):
     for k in range(blocks.shape[0]):
-        high, low, tail = halves(blocks[k, -ROWS:, :].astype(F32))
-        rows = jnp.concatenate([high + low, tail + swapped(tail)], axis=1)
         at = first + k * near_rows
-        observed[at : at + near_rows, :] = rows[:near_rows]
-
-
-def near_kernel(blocks, _, near):
-    observe(blocks, near.shape[0] // blocks.shape[0], near, 0)
+        observed[at : at + near_rows, :] = blocks[k, -ROWS:, : 2 * LANES].astype(F32)[:near_rows]
+
+
+def near_kernel(blocks, _, near, observed):
+    observe(blocks, near.shape[0] // blocks.shape[0], observed, 0)
+    near[...] = observed[...].astype(BF16)
 
 
 def first_kernel(group_ref, probes, blocks, props, dft, leaving, waves, lb, rf, rb, left, right, right_conj, probe, indices, sem):
@@ -307,7 +325,7 @@
             read_indices(blocks, indices, props.shape[0])
             rows = earlier[0].shape[0]
             for n, near in enumerate(earlier):
-                observed[n * rows : (n + 1) * rows, :] = near[...]
+                observed[n * rows : (n + 1) * rows, :] = near[...].astype(F32)
             observe(blocks, rows // size, observed, (groups - 1) * rows)
             g[...] = detector(waves[size], observed[...], left, right, right_conj)
             backward_steps(blocks, waves, indices, lb, rb, grads, g)
@@ -397,12 +415,13 @@
         window_kernel,
         out_shape=struct(size, rows, 2 * width),
         in_specs=[HBM, SMEM, HBM, HBM],
-        out_specs=VMEM,
+        out_specs=HBM,
         scratch_shapes=[
+            pltpu.VMEM((size, rows, 2 * width), BF16),
             pltpu.SMEM(offsets.shape[::-1], jnp.int32),
             pltpu.VMEM(objects.shape[1:], BF16),
             pltpu.VMEM(measured.shape, F32),
-            pltpu.SemaphoreType.DMA((4,)),
+            pltpu.SemaphoreType.DMA((4 + len(slots),)),
         ],
         compiler_params=ALONE,
         name="windows",
@@ -410,7 +429,7 @@
     blocks = exchanged(blocks)
 
     wave = struct(width, 2 * width)
-    near = struct(size * near_rows, 2 * LANES, kind=F32)
+    near = struct(size * near_rows, 2 * LANES)
     waves_shape = struct(size + 1, width, 2 * width)
     grads_shape = struct(size, width, 2 * width)
     left_table = struct(kinds, 2 * width, width)
@@ -422,7 +441,7 @@
     def scratch(shape):
         return pltpu.VMEM(shape.shape, shape.dtype)
 
-    def call(kernel, name, out_shape, in_specs, scratch_shapes, operands):
+    def call(kernel, name, out_shape, in_specs, scratch_shapes, operands, slices=0):
         return pl.pallas_call(
             kernel,
             out_shape=out_shape,
@@ -430,6 +449,11 @@
             out_specs=[VMEM] * len(out_shape),
             scratch_shapes=scratch_shapes,
             compiler_params=PARAMS,
+            cost_estimate=pl.CostEstimate(
+                flops=16 * slices * width**3,
+                bytes_accessed=sum(math.prod(x.shape) * x.dtype.itemsize for x in list(operands) + out_shape),
+                transcendentals=0,
+            ),
             name=name,
         )(*operands)
 
@@ -441,9 +465,10 @@
         [SMEM, HBM, VMEM, VMEM, VMEM],
         [pltpu.VMEM(probes.shape[1:], BF16), indices, pltpu.SemaphoreType.DMA],
         (probe_group, probes, blocks, propagators, jnp.asarray(dft_constant(width))),
+        size,
     )
     entering = handed(leaving, 0, 1)
-    (near_out,) = call(near_kernel, "near_rows", [near], [VMEM, HBM], [], (blocks, leaving))
+    (near_out,) = call(near_kernel, "near_rows", [near], [VMEM, HBM], [pltpu.VMEM(near.shape, F32)], (blocks, leaving))
     nears = [handed(near_out, stage, groups - 1 - stage) for stage in range(groups - 1)]
     for stage in range(1, groups):
         leaving, waves = call(
@@ -453,6 +478,7 @@
             [VMEM] * 5,
             [indices],
             (entering, blocks, propagators, rf, waves),
+            size,
         )
         if stage < groups - 1:
             entering = handed(leaving, stage, 1)
@@ -464,6 +490,7 @@
         [VMEM] * (groups + 7),
         [scratch(wave), pltpu.VMEM((width, 2 * LANES), F32), indices],
         (waves, *nears, blocks, propagators, lb, rb, *dft),
+        size,
     )
 
     for stage in range(groups - 2, -1, -1):
@@ -475,6 +502,7 @@
             [VMEM] * 6,
             [scratch(wave), indices],
             (arriving, waves, blocks, lb, rb, grads),
+            size,
         )
 
     return pl.pallas_call(

time: 88.9 us -> 86.9 us (0.978)
  waiting for transfers between devices: 19.1 us -> 17.5 us
    ppermute x3, waiting for transfers between devices: 19.1 us -> 17.5 us  [handed(): return lax.ppermute(block, 'cuts', route)]
  transfers between devices with their start and end apart: 3 -> 3, of which waited for: 3 -> 2; matrix products, arithmetic and copies ran while one was open for 0% -> 0% of each run, Pallas kernels for 1% -> 1%
where the time goes in v8:
time: 86.9 us; the launch traced here: 86.6 us
  blocking collectives  45 us (52%)
  Pallas kernels  19.4 us (22%)
  waiting for transfers between devices  17.5 us (20%)
  starting transfers between devices  3.88 us (4%)
    all_to_all x2, blocking collectives, exchanged(): lax.all_to_all(blocks, 'cuts', 0, 0, axis_index_groups=members, tiled=True)  45 us
    ppermute x3, waiting for transfers between devices, handed(): return lax.ppermute(block, 'cuts', route)  17.5 us
    pallas_call x5, Pallas kernels, call(): pl.pallas_call(kernel, out_shape=out_shape, in_specs=in_specs, out_specs=...  12.3 us
    pallas_call x1, Pallas kernels, shards(): pl.pallas_call(window_kernel, out_shape=struct(size, rows, 2 * width), in...  3.99 us
    ppermute x3, starting transfers between devices, handed(): return lax.ppermute(block, 'cuts', route)  3.88 us
    pallas_call x1, Pallas kernels, shards(): pl.pallas_call(gather_kernel, out_shape=jax.ShapeDtypeStruct(objects.shap...  3.18 us
  transfers between devices with their start and end apart: 3, of which 2 were waited for; matrix products, arithmetic and copies ran while one was open for 0% of the time, Pallas kernels for 1%

profile of v8, /device:TPU:0, one launch (start us, length us, event | category | flops | bytes accessed | tf_op | source)
XLA Modules:
  0.0 86.6 jit_solution(4805130103655631500)
XLA Ops:
  0.7 0.0 copy-start.2
  0.7 4.0 %windows.1 = bf16[8,208,384]{2,1,0:T(8,128)(2,1)} custom-call(s32[2,6]{1,0:T(2,128)} %bitcast.1, s32[1]{0:T(128)S(6)} %copy.9.index_ref, bf16[1,2,384,384]{3,2,1,0:T(8,128)(2,1)} %objects_in.1, f32[6,12,192]{2,1,0:T(8,128)} %measured_in.1), custom_call_target="tpu_custom_call" | custom-call | tf_op jit(solution)/shard_map/windows/pallas_call | solution.py:414
  4.7 0.0 copy-start
  4.7 0.0 copy-start.1
  4.7 0.0 copy-start.4
  4.7 22.6 %all_to_all.10.blocks.refs_1_ = bf16[8,208,384]{2,1,0:T(8,128)(2,1)S(1)} all-to-all(bf16[8,208,384]{2,1,0:T(8,128)(2,1)} %windows.1), channel_id=1, replica_groups={{0,1,2,3,4,5,6,7},{8,9,10,11,12,13,14,15},{16,17,18,19,20,21,22,23},{24..., dimensions={0} | all-to-all | bytes 2555904 | tf_op jit(solution)/shard_map/all_to_all | solution.py:408
  27.3 0.0 copy-done.2
  27.3 0.0 copy-done
  27.3 0.0 copy-done.1
  27.3 0.0 copy-done.4
  27.3 5.8 %first_forward.1 = (bf16[192,384]{1,0:T(8,128)(2,1)S(1)}, bf16[9,192,384]{2,1,0:T(8,128)(2,1)S(1)}, bf16[4,384,192]{2,1,0:T(8,128)(2,1)S(1)}, bf16[4,384,384]{2,...) custom-call(s32[6]{0:T(128)S(1)} %copy-done.4, ...), custom_call_target="tpu_custom_call" | custom-call | flops 905969664 | bytes 9240600 | tf_op jit(solution)/shard_map/first_forward/pallas_call | solution.py:445
  33.1 1.3 %collective-permute-start = (bf16[192,384]{1,0:T(8,128)(2,1)S(1)}, bf16[192,384]{1,0:T(8,128)(2,1)S(1)}, u32[]{:S(2)}, u32[]{:S(2)}) collective-permute-start(bf16[192,384]{1,0:T(8,128)(2,1)S(1)} %get-tuple-element.19._), channel_id=1, source_target_pairs={{0,8},{2,10},{4,12},{5,13},{6,14},{7,15},{16,24},{18,26},{20,28},{... | collective-permute-start | bytes 442376 | tf_op jit(solution)/shard_map/ppermute | solution.py:412
  34.5 1.3 %collective-permute-start.1 = (bf16[96,256]{1,0:T(8,128)(2,1)S(1)}, bf16[96,256]{1,0:T(8,128)(2,1)S(1)}, u32[]{:S(2)}, u32[]{:S(2)}) collective-permute-start(bf16[96,256]{1,0:T(8,128)(2,1)S(1)} %near_rows.1), channel_id=1, source_target_pairs={{0,8},{2,10},{4,12},{5,13},{6,14},{7,15},{16,24},{18,26},{20,28},{... | collective-permute-start | bytes 147464 | tf_op jit(solution)/shard_map/ppermute | solution.py:412
  35.8 1.4 %collective-permute-done.entering = bf16[192,384]{1,0:T(8,128)(2,1)S(1)} collective-permute-done((bf16[192,384]{1,0:T(8,128)(2,1)S(1)}, bf16[192,384]{1,0:T(8,128)(2,1)S(1)}, u32[]{:S(2)}, u32[]{:S(2)}) %collective-permute-start) | collective-permute-done | bytes 147488 | tf_op jit(solution)/shard_map/ppermute | solution.py:412
  37.1 0.8 forward.1
  37.9 0.0 collective-permute-done.1.refs_0_
  37.9 0.6 middle.1
  38.5 1.3 %collective-permute-start.2 = (bf16[192,384]{1,0:T(8,128)(2,1)S(1)}, bf16[192,384]{1,0:T(8,128)(2,1)S(1)}, u32[]{:S(2)}, u32[]{:S(2)}) collective-permute-start(bf16[192,384]{1,0:T(8,128)(2,1)S(1)} %get-tuple-element.28), channel_id=1, source_target_pairs={{8,0},{10,2},{12,4},{13,5},{14,6},{15,7},{24,16},{26,18},{28,20},{... | collective-permute-start | bytes 442376 | tf_op jit(solution)/shard_map/ppermute | solution.py:412
  39.8 16.2 %collective-permute-done.2.arriving = bf16[192,384]{1,0:T(8,128)(2,1)S(1)} collective-permute-done((bf16[192,384]{1,0:T(8,128)(2,1)S(1)}, bf16[192,384]{1,0:T(8,128)(2,1)S(1)}, u32[]{:S(2)}, u32[]{:S(2)}) %collective-permute-start.2) | collective-permute-done | bytes 147488 | tf_op jit(solution)/shard_map/ppermute | solution.py:412
  56.0 5.1 %backward.1 = (bf16[192,384]{1,0:T(8,128)(2,1)}, bf16[8,192,384]{2,1,0:T(8,128)(2,1)S(1)}) custom-call(bf16[192,384]{1,0:T(8,128)(2,1)S(1)} %collective-permute-done.2.arriving, bf16[9,192,384]{2,1,0:T(8,128)(2,1)S(1)} %get-tuple-element.22.waves, bf16[8,208,384]{2,1,0:T(8,128)(2,1)S(1)} %all_to_all.10.blocks.refs_1_, ...), custom_call_target="tpu_custom_call" | custom-call | flops 905969664 | bytes 7028736 | tf_op jit(solution)/shard_map/backward/pallas_call | solution.py:445
  61.1 0.0 copy-start.3
  61.1 22.3 %all_to_all.11.grads_ref = bf16[8,192,384]{2,1,0:T(8,128)(2,1)S(1)} all-to-all(bf16[8,192,384]{2,1,0:T(8,128)(2,1)S(1)} %get-tuple-element.32), channel_id=1, replica_groups={{0,1,2,3,4,5,6,7},{8,9,10,11,12,13,14,15},{16,17,18,19,20,21,22,23},{24..., dimensions={0} | all-to-all | bytes 2359296 | tf_op jit(solution)/shard_map/all_to_all | solution.py:408
  83.4 0.0 copy-done.3
  83.4 3.2 %sum_windows.1 = f32[1,2,384,384]{3,2,1,0:T(8,128)} custom-call(s32[2,6]{1,0:T(2,128)S(1)} %bitcast.2, bf16[8,192,384]{2,1,0:T(8,128)(2,1)S(1)} %all_to_all.11.grads_ref), custom_call_target="tpu_custom_call" | custom-call | tf_op jit(solution)/shard_map/sum_windows/pallas_call | solution.py:508
  (1 shorter events, 0.0 us)
Async XLA Ops:
  0.7 26.7 %copy-start.2 = (f32[2,192,192]{2,1,0:T(8,128)S(1)}, f32[2,192,192]{2,1,0:T(8,128)}, u32[]{:S(2)}) copy-start(f32[2,192,192]{2,1,0:T(8,128)} %constant.2.clone.dft) | copy-start | bytes 884740
  4.7 22.7 %copy-start = (bf16[4,2,192,192]{3,2,1,0:T(8,128)(2,1)S(1)}, bf16[4,2,192,192]{3,2,1,0:T(8,128)(2,1)}, u32[]{:S(2)}) copy-start(bf16[4,2,192,192]{3,2,1,0:T(8,128)(2,1)} %refs_2_.1) | copy-start | bytes 1769476
  4.7 22.7 %copy-start.1 = (bf16[8,2,192,192]{3,2,1,0:T(8,128)(2,1)S(1)}, bf16[8,2,192,192]{3,2,1,0:T(8,128)(2,1)}, u32[]{:S(2)}) copy-start(bf16[8,2,192,192]{3,2,1,0:T(8,128)(2,1)} %probes.1) | copy-start | bytes 3538948
  4.7 22.7 %copy-start.4 = (s32[6]{0:T(128)S(1)}, s32[6]{0:T(128)}, u32[]{:S(2)}) copy-start(s32[6]{0:T(128)} %group_ref.1) | copy-start | bytes 76
  33.1 4.0 %collective-permute-start = (bf16[192,384]{1,0:T(8,128)(2,1)S(1)}, bf16[192,384]{1,0:T(8,128)(2,1)S(1)}, u32[]{:S(2)}, u32[]{:S(2)}) collective-permute-start(bf16[192,384]{1,0:T(8,128)(2,1)S(1)} %get-tuple-element.19._), channel_id=1, source_target_pairs={{0,8},{2,10},{4,12},{5,13},{6,14},{7,15},{16,24},{18,26},{20,28},{... | collective-permute-start | bytes 442376 | tf_op jit(solution)/shard_map/ppermute | solution.py:412
  34.5 3.4 %collective-permute-start.1 = (bf16[96,256]{1,0:T(8,128)(2,1)S(1)}, bf16[96,256]{1,0:T(8,128)(2,1)S(1)}, u32[]{:S(2)}, u32[]{:S(2)}) collective-permute-start(bf16[96,256]{1,0:T(8,128)(2,1)S(1)} %near_rows.1), channel_id=1, source_target_pairs={{0,8},{2,10},{4,12},{5,13},{6,14},{7,15},{16,24},{18,26},{20,28},{... | collective-permute-start | bytes 147464 | tf_op jit(solution)/shard_map/ppermute | solution.py:412
  38.5 17.5 %collective-permute-start.2 = (bf16[192,384]{1,0:T(8,128)(2,1)S(1)}, bf16[192,384]{1,0:T(8,128)(2,1)S(1)}, u32[]{:S(2)}, u32[]{:S(2)}) collective-permute-start(bf16[192,384]{1,0:T(8,128)(2,1)S(1)} %get-tuple-element.28), channel_id=1, source_target_pairs={{8,0},{10,2},{12,4},{13,5},{14,6},{15,7},{24,16},{26,18},{28,20},{... | collective-permute-start | bytes 442376 | tf_op jit(solution)/shard_map/ppermute | solution.py:412
  61.1 22.4 %copy-start.3 = (s32[6,2]{0,1:T(2,128)S(1)}, s32[6,2]{0,1:T(2,128)}, u32[]{:S(2)}) copy-start(s32[6,2]{0,1:T(2,128)} %param.13) | copy-start | bytes 148

commit v9 on v8

--- a/solution.py
+++ b/solution.py
@@ -43,24 +43,23 @@
     return jnp.where(low == minus_low, -tail, tail)
 
 
-def times(a, b):
+def factor(b):
+    b0, b1, bt = halves(b)
+    return (b0, b1) + spread(bt)
+
+
+def times(a, parts):
     a0, a1, at = halves(a)
-    b0, b1, bt = halves(b)
-    b_real, b_imag = spread(bt)
+    b0, b1, b_real, b_imag = parts
     tail = at * b_real + signed(swapped(at), True) * b_imag
     return jnp.concatenate([a0 * b0 - a1 * b1, a1 * b0 + a0 * b1, tail], axis=1)
 
 
-def times_conj(a, *others):
+def times_conj(a, turned, parts):
     a0, a1, at = halves(a)
-    turned = signed(swapped(at), False)
-    results = []
-    for b in others:
-        b0, b1, bt = halves(b)
-        b_real, b_imag = spread(bt)
-        tail = at * b_real + turned * b_imag
-        results.append(jnp.concatenate([a0 * b0 + a1 * b1, a1 * b0 - a0 * b1, tail], axis=1))
-    return results
+    b0, b1, b_real, b_imag = parts
+    tail = at * b_real + turned * b_imag
+    return jnp.concatenate([a0 * b0 + a1 * b1, a1 * b0 - a0 * b1, tail], axis=1)
 
 
 def joined(both, conj):
@@ -197,38 +196,47 @@
         left[n, :width, :] = real
         left[n, width:, :] = imag
         right[n] = right_table(real, imag).astype(BF16)
-        right_conj[n] = right_table(real, -imag).astype(BF16)
+        if n == 0:
+            right_conj[...] = right_table(real, -imag).astype(BF16)
 
 
 def forward_steps(blocks, waves, indices, lf, rf):
     sections, _, columns = blocks.shape
     width = columns // 2
-
-    def step(k, carried):
+    psi = waves[0]
+    parts = factor(with_mean(blocks[0, :width, :]))
+    for k in range(sections):
         which = indices[k]
-        z = times(waves[k].astype(F32), with_mean(blocks[k, :width, :])).astype(BF16)
+        z = times(psi.astype(F32), parts).astype(BF16)
         h = joined(dot(lf[which].reshape(columns, width), z), False).astype(BF16)
-        waves[k + 1] = dot(h, rf[which]).astype(BF16)
-        return carried
-
-    lax.fori_loop(0, sections, step, 0, unroll=True)
+        if k + 1 < sections:
+            parts = factor(with_mean(blocks[k + 1, :width, :]))
+        psi = dot(h, rf[which]).astype(BF16)
+        waves[k + 1] = psi
 
 
 def backward_steps(blocks, waves, indices, lb, rb, grads, g):
     sections, _, columns = blocks.shape
     width = columns // 2
 
-    def step(n, carried):
-        k = sections - 1 - n
+    def leave(k, y, turned, wave_parts):
+        grads[k] = times_conj(y, turned, wave_parts).astype(BF16)
+
+    late = None
+    for k in reversed(range(sections)):
         which = indices[k]
-        c = joined(dot(lb[which], g[...]), True).astype(BF16)
+        both = dot(lb[which], g)
+        if late is not None:
+            leave(*late)
+        c = joined(both, True).astype(BF16)
+        wave_parts = factor(waves[k].astype(F32))
+        window_parts = factor(with_mean(blocks[k, :width, :]))
         y = dot(c, rb[which])
-        grad, passed = times_conj(y, waves[k].astype(F32), with_mean(blocks[k, :width, :]))
-        grads[k] = grad.astype(BF16)
-        g[...] = passed.astype(BF16)
-        return carried
-
-    lax.fori_loop(0, sections, step, 0, unroll=True)
+        turned = signed(swapped(halves(y)[2]), False)
+        g = times_conj(y, turned, window_parts).astype(BF16)
+        late = (k, y, turned, wave_parts)
+    leave(*late)
+    return g
 
 
 def detector(psi, observed, left, right, right_conj):
@@ -242,8 +250,8 @@
     main = f0 * f0 + f1 * f1 - observed[:, :LANES]
     tail = ft * ft + other * other - observed[:, LANES:]
     push = jnp.concatenate([main * f0, main * f1, tail * ft], axis=1)
-    back = joined(product(left[0], left[1], *split2(push)), True)
-    return product(*split2(back), right_conj[0], right_conj[1]).astype(BF16)
+    back = joined(dot(left[0], push.astype(BF16)), True)
+    return dot(back.astype(BF16), right_conj[...]).astype(BF16)
 
 
 def read_indices(blocks, indices, count):
@@ -316,7 +324,7 @@
 def middle_kernel(groups):
     def kernel(waves, *refs):
         earlier, refs = refs[: groups - 1], refs[groups - 1 :]
-        blocks, props, lb, rb, left, right, right_conj, leaving, grads, lb_out, rb_out, g, observed, indices = refs
+        blocks, props, lb, rb, left, right, right_conj, leaving, grads, lb_out, rb_out, observed, indices = refs
         size = blocks.shape[0]
         _, group = place_in(size)
 
@@ -327,9 +335,8 @@
             for n, near in enumerate(earlier):
                 observed[n * rows : (n + 1) * rows, :] = near[...].astype(F32)
             observe(blocks, rows // size, observed, (groups - 1) * rows)
-            g[...] = detector(waves[size], observed[...], left, right, right_conj)
-            backward_steps(blocks, waves, indices, lb, rb, grads, g)
-            leaving[...] = g[...]
+            g = detector(waves[size], observed[...], left, right, right_conj)
+            leaving[...] = backward_steps(blocks, waves, indices, lb, rb, grads, g)
 
         @pl.when(group < groups - 1)
         def _():
@@ -339,15 +346,13 @@
 
 
 def backward_kernel(stage):
-    def kernel(arriving, waves, blocks, lb, rb, grads_in, leaving, grads, g, indices):
+    def kernel(arriving, waves, blocks, lb, rb, grads_in, leaving, grads, indices):
         _, group = place_in(blocks.shape[0])
 
         @pl.when(group == stage)
         def _():
             read_indices(blocks, indices, lb.shape[0])
-            g[...] = arriving[...]
-            backward_steps(blocks, waves, indices, lb, rb, grads, g)
-            leaving[...] = g[...]
+            leaving[...] = backward_steps(blocks, waves, indices, lb, rb, grads, arriving[...])
 
         @pl.when(group != stage)
         def _():
@@ -438,9 +443,6 @@
     detector_right = struct(2, 2 * width, 2 * width)
     indices = pltpu.SMEM((size,), jnp.int32)
 
-    def scratch(shape):
-        return pltpu.VMEM(shape.shape, shape.dtype)
-
     def call(kernel, name, out_shape, in_specs, scratch_shapes, operands, slices=0):
         return pl.pallas_call(
             kernel,
@@ -461,7 +463,7 @@
         first_kernel,
         "first_forward",
         [wave, waves_shape, left_table, square_table, square_table]
-        + [detector_left, detector_right, detector_right],
+        + [detector_left, detector_right, struct(2 * width, 2 * width)],
         [SMEM, HBM, VMEM, VMEM, VMEM],
         [pltpu.VMEM(probes.shape[1:], BF16), indices, pltpu.SemaphoreType.DMA],
         (probe_group, probes, blocks, propagators, jnp.asarray(dft_constant(width))),
@@ -488,7 +490,7 @@
         "middle",
         [wave, grads_shape, left_table, square_table],
         [VMEM] * (groups + 7),
-        [scratch(wave), pltpu.VMEM((width, 2 * LANES), F32), indices],
+        [pltpu.VMEM((width, 2 * LANES), F32), indices],
         (waves, *nears, blocks, propagators, lb, rb, *dft),
         size,
     )
@@ -500,7 +502,7 @@
             "backward",
             [wave, grads_shape],
             [VMEM] * 6,
-            [scratch(wave), indices],
+            [indices],
             (arriving, waves, blocks, lb, rb, grads),
             size,
         )

time: 86.9 us -> 85.9 us (0.988)
  no operation moved by 1% of the time
where the time goes in v9:
time: 85.9 us; the launch traced here: 85.6 us
  blocking collectives  45 us (52%)
  Pallas kernels  19.3 us (22%)
  waiting for transfers between devices  16.8 us (20%)
  starting transfers between devices  3.88 us (5%)
    all_to_all x2, blocking collectives, exchanged(): lax.all_to_all(blocks, 'cuts', 0, 0, axis_index_groups=members, tiled=True)  45 us
    ppermute x3, waiting for transfers between devices, handed(): return lax.ppermute(block, 'cuts', route)  16.8 us
    pallas_call x5, Pallas kernels, call(): pl.pallas_call(kernel, out_shape=out_shape, in_specs=in_specs, out_specs=...  12.1 us
    pallas_call x1, Pallas kernels, shards(): pl.pallas_call(window_kernel, out_shape=struct(size, rows, 2 * width), in...  3.99 us
    ppermute x3, starting transfers between devices, handed(): return lax.ppermute(block, 'cuts', route)  3.88 us
    pallas_call x1, Pallas kernels, shards(): pl.pallas_call(gather_kernel, out_shape=jax.ShapeDtypeStruct(objects.shap...  3.18 us
  transfers between devices with their start and end apart: 3, of which 2 were waited for; matrix products, arithmetic and copies ran while one was open for 0% of the time, Pallas kernels for 1%

profile of v9, /device:TPU:0, one launch (start us, length us, event | category | flops | bytes accessed | tf_op | source)
XLA Modules:
  0.0 85.6 jit_solution(17941339722510591461)
XLA Ops:
  0.7 0.0 copy-start.2
  0.7 4.0 %windows.1 = bf16[8,208,384]{2,1,0:T(8,128)(2,1)} custom-call(s32[2,6]{1,0:T(2,128)} %bitcast.1, s32[1]{0:T(128)S(6)} %copy.9.index_ref, bf16[1,2,384,384]{3,2,1,0:T(8,128)(2,1)} %objects_in.1, f32[6,12,192]{2,1,0:T(8,128)} %measured_in.1), custom_call_target="tpu_custom_call" | custom-call | tf_op jit(solution)/shard_map/windows/pallas_call | solution.py:419
  4.7 0.0 copy-start
  4.7 0.0 copy-start.1
  4.7 0.0 copy-start.4
  4.7 22.6 %all_to_all.10.blocks.refs_1_ = bf16[8,208,384]{2,1,0:T(8,128)(2,1)S(1)} all-to-all(bf16[8,208,384]{2,1,0:T(8,128)(2,1)} %windows.1), channel_id=1, replica_groups={{0,1,2,3,4,5,6,7},{8,9,10,11,12,13,14,15},{16,17,18,19,20,21,22,23},{24..., dimensions={0} | all-to-all | bytes 2555904 | tf_op jit(solution)/shard_map/all_to_all | solution.py:413
  27.3 0.0 copy-done.2
  27.3 0.0 copy-done
  27.3 0.0 copy-done.1
  27.3 0.0 copy-done.4
  27.3 5.8 %first_forward.1 = (bf16[192,384]{1,0:T(8,128)(2,1)S(1)}, bf16[9,192,384]{2,1,0:T(8,128)(2,1)S(1)}, bf16[4,384,192]{2,1,0:T(8,128)(2,1)S(1)}, bf16[4,384,384]{2,...) custom-call(s32[6]{0:T(128)S(1)} %copy-done.4, ...), custom_call_target="tpu_custom_call" | custom-call | flops 905969664 | bytes 8945688 | tf_op jit(solution)/shard_map/first_forward/pallas_call | solution.py:447
  33.1 1.3 %collective-permute-start = (bf16[192,384]{1,0:T(8,128)(2,1)S(1)}, bf16[192,384]{1,0:T(8,128)(2,1)S(1)}, u32[]{:S(2)}, u32[]{:S(2)}) collective-permute-start(bf16[192,384]{1,0:T(8,128)(2,1)S(1)} %get-tuple-element.19._), channel_id=1, source_target_pairs={{0,8},{2,10},{4,12},{5,13},{6,14},{7,15},{16,24},{18,26},{20,28},{... | collective-permute-start | bytes 442376 | tf_op jit(solution)/shard_map/ppermute | solution.py:417
  34.4 1.3 %collective-permute-start.1 = (bf16[96,256]{1,0:T(8,128)(2,1)S(1)}, bf16[96,256]{1,0:T(8,128)(2,1)S(1)}, u32[]{:S(2)}, u32[]{:S(2)}) collective-permute-start(bf16[96,256]{1,0:T(8,128)(2,1)S(1)} %near_rows.1), channel_id=1, source_target_pairs={{0,8},{2,10},{4,12},{5,13},{6,14},{7,15},{16,24},{18,26},{20,28},{... | collective-permute-start | bytes 147464 | tf_op jit(solution)/shard_map/ppermute | solution.py:417
  35.7 1.4 %collective-permute-done.entering = bf16[192,384]{1,0:T(8,128)(2,1)S(1)} collective-permute-done((bf16[192,384]{1,0:T(8,128)(2,1)S(1)}, bf16[192,384]{1,0:T(8,128)(2,1)S(1)}, u32[]{:S(2)}, u32[]{:S(2)}) %collective-permute-start) | collective-permute-done | bytes 147488 | tf_op jit(solution)/shard_map/ppermute | solution.py:417
  37.1 0.8 forward.1
  37.9 0.0 collective-permute-done.1.refs_0_
  37.9 0.6 middle.1
  38.5 1.3 %collective-permute-start.2 = (bf16[192,384]{1,0:T(8,128)(2,1)S(1)}, bf16[192,384]{1,0:T(8,128)(2,1)S(1)}, u32[]{:S(2)}, u32[]{:S(2)}) collective-permute-start(bf16[192,384]{1,0:T(8,128)(2,1)S(1)} %get-tuple-element.28), channel_id=1, source_target_pairs={{8,0},{10,2},{12,4},{13,5},{14,6},{15,7},{24,16},{26,18},{28,20},{... | collective-permute-start | bytes 442376 | tf_op jit(solution)/shard_map/ppermute | solution.py:417
  39.8 15.4 %collective-permute-done.2.arriving = bf16[192,384]{1,0:T(8,128)(2,1)S(1)} collective-permute-done((bf16[192,384]{1,0:T(8,128)(2,1)S(1)}, bf16[192,384]{1,0:T(8,128)(2,1)S(1)}, u32[]{:S(2)}, u32[]{:S(2)}) %collective-permute-start.2) | collective-permute-done | bytes 147488 | tf_op jit(solution)/shard_map/ppermute | solution.py:417
  55.2 5.0 %backward.1 = (bf16[192,384]{1,0:T(8,128)(2,1)}, bf16[8,192,384]{2,1,0:T(8,128)(2,1)S(1)}) custom-call(bf16[192,384]{1,0:T(8,128)(2,1)S(1)} %collective-permute-done.2.arriving, bf16[9,192,384]{2,1,0:T(8,128)(2,1)S(1)} %get-tuple-element.22.waves, bf16[8,208,384]{2,1,0:T(8,128)(2,1)S(1)} %all_to_all.10.blocks.refs_1_, ...), custom_call_target="tpu_custom_call" | custom-call | flops 905969664 | bytes 7028736 | tf_op jit(solution)/shard_map/backward/pallas_call | solution.py:447
  60.1 0.0 copy-start.3
  60.1 22.3 %all_to_all.11.grads_ref = bf16[8,192,384]{2,1,0:T(8,128)(2,1)S(1)} all-to-all(bf16[8,192,384]{2,1,0:T(8,128)(2,1)S(1)} %get-tuple-element.32), channel_id=1, replica_groups={{0,1,2,3,4,5,6,7},{8,9,10,11,12,13,14,15},{16,17,18,19,20,21,22,23},{24..., dimensions={0} | all-to-all | bytes 2359296 | tf_op jit(solution)/shard_map/all_to_all | solution.py:413
  82.5 0.0 copy-done.3
  82.5 3.2 %sum_windows.1 = f32[1,2,384,384]{3,2,1,0:T(8,128)} custom-call(s32[2,6]{1,0:T(2,128)S(1)} %bitcast.2, bf16[8,192,384]{2,1,0:T(8,128)(2,1)S(1)} %all_to_all.11.grads_ref), custom_call_target="tpu_custom_call" | custom-call | tf_op jit(solution)/shard_map/sum_windows/pallas_call | solution.py:510
  (1 shorter events, 0.0 us)
Async XLA Ops:
  0.7 26.7 %copy-start.2 = (f32[2,192,192]{2,1,0:T(8,128)S(1)}, f32[2,192,192]{2,1,0:T(8,128)}, u32[]{:S(2)}) copy-start(f32[2,192,192]{2,1,0:T(8,128)} %constant.2.clone.dft) | copy-start | bytes 884740
  4.7 22.7 %copy-start = (bf16[4,2,192,192]{3,2,1,0:T(8,128)(2,1)S(1)}, bf16[4,2,192,192]{3,2,1,0:T(8,128)(2,1)}, u32[]{:S(2)}) copy-start(bf16[4,2,192,192]{3,2,1,0:T(8,128)(2,1)} %refs_2_.1) | copy-start | bytes 1769476
  4.7 22.7 %copy-start.1 = (bf16[8,2,192,192]{3,2,1,0:T(8,128)(2,1)S(1)}, bf16[8,2,192,192]{3,2,1,0:T(8,128)(2,1)}, u32[]{:S(2)}) copy-start(bf16[8,2,192,192]{3,2,1,0:T(8,128)(2,1)} %probes.1) | copy-start | bytes 3538948
  4.7 22.7 %copy-start.4 = (s32[6]{0:T(128)S(1)}, s32[6]{0:T(128)}, u32[]{:S(2)}) copy-start(s32[6]{0:T(128)} %group_ref.1) | copy-start | bytes 76
  33.1 4.0 %collective-permute-start = (bf16[192,384]{1,0:T(8,128)(2,1)S(1)}, bf16[192,384]{1,0:T(8,128)(2,1)S(1)}, u32[]{:S(2)}, u32[]{:S(2)}) collective-permute-start(bf16[192,384]{1,0:T(8,128)(2,1)S(1)} %get-tuple-element.19._), channel_id=1, source_target_pairs={{0,8},{2,10},{4,12},{5,13},{6,14},{7,15},{16,24},{18,26},{20,28},{... | collective-permute-start | bytes 442376 | tf_op jit(solution)/shard_map/ppermute | solution.py:417
  34.4 3.4 %collective-permute-start.1 = (bf16[96,256]{1,0:T(8,128)(2,1)S(1)}, bf16[96,256]{1,0:T(8,128)(2,1)S(1)}, u32[]{:S(2)}, u32[]{:S(2)}) collective-permute-start(bf16[96,256]{1,0:T(8,128)(2,1)S(1)} %near_rows.1), channel_id=1, source_target_pairs={{0,8},{2,10},{4,12},{5,13},{6,14},{7,15},{16,24},{18,26},{20,28},{... | collective-permute-start | bytes 147464 | tf_op jit(solution)/shard_map/ppermute | solution.py:417
  38.5 16.7 %collective-permute-start.2 = (bf16[192,384]{1,0:T(8,128)(2,1)S(1)}, bf16[192,384]{1,0:T(8,128)(2,1)S(1)}, u32[]{:S(2)}, u32[]{:S(2)}) collective-permute-start(bf16[192,384]{1,0:T(8,128)(2,1)S(1)} %get-tuple-element.28), channel_id=1, source_target_pairs={{8,0},{10,2},{12,4},{13,5},{14,6},{15,7},{24,16},{26,18},{28,20},{... | collective-permute-start | bytes 442376 | tf_op jit(solution)/shard_map/ppermute | solution.py:417
  60.1 22.3 %copy-start.3 = (s32[6,2]{0,1:T(2,128)S(1)}, s32[6,2]{0,1:T(2,128)}, u32[]{:S(2)}) copy-start(s32[6,2]{0,1:T(2,128)} %param.13) | copy-start | bytes 148

commit v10 on v9

--- a/solution.py
+++ b/solution.py
@@ -70,6 +70,18 @@
     if conj:
         return jnp.concatenate([u0 + v1, u1 - v0, ut + turned], axis=1)
     return jnp.concatenate([u0 - v1, u1 + v0, ut + turned], axis=1)
+
+
+def stacked(x):
+    x0, x1, xt = halves(x)
+    half = LANES // 2
+    return jnp.concatenate(
+        [
+            jnp.concatenate([x0, xt[:, :half]], axis=1),
+            jnp.concatenate([x1, swapped(xt)[:, :half]], axis=1),
+        ],
+        axis=0,
+    )
 
 
 def with_mean(window):
@@ -165,20 +177,13 @@
         copy.wait()
 
 
-def right_table(real, imag):
-    width = real.shape[0]
-    upper = packed(real, imag, width, 0)
-    lower = packed(-imag, real, width, 0)
-    return jnp.concatenate([upper[:LANES], lower[:LANES], upper[LANES:], lower[LANES:]], axis=0)
-
-
 def transposed(plane):
     return plane.astype(F32).T.astype(BF16)
 
 
 def forward_tables(props, rf):
     for k in range(props.shape[0]):
-        rf[k] = right_table(transposed(props[k, 0]), transposed(props[k, 1])).astype(BF16)
+        rf[k] = packed(transposed(props[k, 0]), transposed(props[k, 1]), props.shape[-1], 0).astype(BF16)
 
 
 def backward_tables(props, lb, rb):
@@ -187,7 +192,7 @@
         real, imag = props[k, 0], props[k, 1]
         lb[k, :width, :] = transposed(real)
         lb[k, width:, :] = transposed(imag)
-        rb[k] = right_table(real, -imag).astype(BF16)
+        rb[k] = packed(real, -imag, width, 0).astype(BF16)
 
 
 def detector_tables(dft, left, right, right_conj):
@@ -195,9 +200,9 @@
     for n, (real, imag) in enumerate(zip(split2(dft[0]), split2(dft[1]))):
         left[n, :width, :] = real
         left[n, width:, :] = imag
-        right[n] = right_table(real, imag).astype(BF16)
+        right[n] = packed(real, imag, width, 0).astype(BF16)
         if n == 0:
-            right_conj[...] = right_table(real, -imag).astype(BF16)
+            right_conj[...] = packed(real, -imag, width, 0).astype(BF16)
 
 
 def forward_steps(blocks, waves, indices, lf, rf):
@@ -208,10 +213,10 @@
     for k in range(sections):
         which = indices[k]
         z = times(psi.astype(F32), parts).astype(BF16)
-        h = joined(dot(lf[which].reshape(columns, width), z), False).astype(BF16)
+        h = joined(dot(lf[which].reshape(columns, width), z), False)
         if k + 1 < sections:
             parts = factor(with_mean(blocks[k + 1, :width, :]))
-        psi = dot(h, rf[which]).astype(BF16)
+        psi = joined(dot(stacked(h).astype(BF16), rf[which]), False).astype(BF16)
         waves[k + 1] = psi
 
 
@@ -228,10 +233,10 @@
         both = dot(lb[which], g)
         if late is not None:
             leave(*late)
-        c = joined(both, True).astype(BF16)
+        c = joined(both, True)
         wave_parts = factor(waves[k].astype(F32))
         window_parts = factor(with_mean(blocks[k, :width, :]))
-        y = dot(c, rb[which])
+        y = joined(dot(stacked(c).astype(BF16), rb[which]), False)
         turned = signed(swapped(halves(y)[2]), False)
         g = times_conj(y, turned, window_parts).astype(BF16)
         late = (k, y, turned, wave_parts)
@@ -244,14 +249,14 @@
         return dot(ah, bh) + (dot(ah, bl) + dot(al, bh))
 
     near = joined(dot(left[0], psi) + dot(left[1], psi), False)
-    far = product(*split2(near), right[0], right[1])
+    far = joined(product(*split2(stacked(near)), right[0], right[1]), False)
     f0, f1, ft = halves(far)
     other = swapped(ft)
     main = f0 * f0 + f1 * f1 - observed[:, :LANES]
     tail = ft * ft + other * other - observed[:, LANES:]
     push = jnp.concatenate([main * f0, main * f1, tail * ft], axis=1)
     back = joined(dot(left[0], push.astype(BF16)), True)
-    return dot(back.astype(BF16), right_conj[...]).astype(BF16)
+    return joined(dot(stacked(back).astype(BF16), right_conj[...]), False).astype(BF16)
 
 
 def read_indices(blocks, indices, count):
@@ -438,9 +443,9 @@
     waves_shape = struct(size + 1, width, 2 * width)
     grads_shape = struct(size, width, 2 * width)
     left_table = struct(kinds, 2 * width, width)
-    square_table = struct(kinds, 2 * width, 2 * width)
+    right_table = struct(kinds, width, 2 * width)
     detector_left = struct(2, 2 * width, width)
-    detector_right = struct(2, 2 * width, 2 * width)
+    detector_right = struct(2, width, 2 * width)
     indices = pltpu.SMEM((size,), jnp.int32)
 
     def call(kernel, name, out_shape, in_specs, scratch_shapes, operands, slices=0):
@@ -462,8 +467,8 @@
     leaving, waves, lb, rf, rb, *dft = call(
         first_kernel,
         "first_forward",
-        [wave, waves_shape, left_table, square_table, square_table]
-        + [detector_left, detector_right, struct(2 * width, 2 * width)],
+        [wave, waves_shape, left_table, right_table, right_table]
+        + [detector_left, detector_right, wave],
         [SMEM, HBM, VMEM, VMEM, VMEM],
         [pltpu.VMEM(probes.shape[1:], BF16), indices, pltpu.SemaphoreType.DMA],
         (probe_group, probes, blocks, propagators, jnp.asarray(dft_constant(width))),
@@ -488,7 +493,7 @@
     leaving, grads, lb, rb = call(
         middle_kernel(groups),
         "middle",
-        [wave, grads_shape, left_table, square_table],
+        [wave, grads_shape, left_table, right_table],
         [VMEM] * (groups + 7),
         [pltpu.VMEM((width, 2 * LANES), F32), indices],
         (waves, *nears, blocks, propagators, lb, rb, *dft),

time: 85.9 us -> 90.6 us (1.055)
  waiting for transfers between devices: 16.8 us -> 19.6 us
  Pallas kernels: 19.3 us -> 21.1 us
    ppermute x3, waiting for transfers between devices: 16.8 us -> 19.6 us  [handed(): return lax.ppermute(block, 'cuts', route)]
    pallas_call x5, Pallas kernels: 12.1 us -> 13.9 us  [call(): pl.pallas_call(kernel, out_shape=out_shape, in_specs=in_specs, out_specs=...]
where the time goes in v10:
time: 90.6 us; the launch traced here: 90.3 us
  blocking collectives  45 us (50%)
  Pallas kernels  21.1 us (23%)
  waiting for transfers between devices  19.6 us (22%)
  starting transfers between devices  3.88 us (4%)
    all_to_all x2, blocking collectives, exchanged(): lax.all_to_all(blocks, 'cuts', 0, 0, axis_index_groups=members, tiled=True)  45 us
    ppermute x3, waiting for transfers between devices, handed(): return lax.ppermute(block, 'cuts', route)  19.6 us
    pallas_call x5, Pallas kernels, call(): pl.pallas_call(kernel, out_shape=out_shape, in_specs=in_specs, out_specs=...  13.9 us
    pallas_call x1, Pallas kernels, shards(): pl.pallas_call(window_kernel, out_shape=struct(size, rows, 2 * width), in...  3.99 us
    ppermute x3, starting transfers between devices, handed(): return lax.ppermute(block, 'cuts', route)  3.88 us
    pallas_call x1, Pallas kernels, shards(): pl.pallas_call(gather_kernel, out_shape=jax.ShapeDtypeStruct(objects.shap...  3.19 us
  transfers between devices with their start and end apart: 3, of which 2 were waited for; matrix products, arithmetic and copies ran while one was open for 0% of the time, Pallas kernels for 1%

profile of v10, /device:TPU:0, one launch (start us, length us, event | category | flops | bytes accessed | tf_op | source)
XLA Modules:
  0.0 90.3 jit_solution(17061907929139180060)
XLA Ops:
  0.7 0.0 copy-start.2
  0.7 4.0 %windows.1 = bf16[8,208,384]{2,1,0:T(8,128)(2,1)} custom-call(s32[2,6]{1,0:T(2,128)} %bitcast.1, s32[1]{0:T(128)S(6)} %copy.9.index_ref, bf16[1,2,384,384]{3,2,1,0:T(8,128)(2,1)} %objects_in.1, f32[6,12,192]{2,1,0:T(8,128)} %measured_in.1), custom_call_target="tpu_custom_call" | custom-call | tf_op jit(solution)/shard_map/windows/pallas_call | solution.py:424
  4.7 0.0 copy-start
  4.7 0.0 copy-start.1
  4.7 0.0 copy-start.4
  4.7 22.6 %all_to_all.10.blocks.refs_1_ = bf16[8,208,384]{2,1,0:T(8,128)(2,1)S(1)} all-to-all(bf16[8,208,384]{2,1,0:T(8,128)(2,1)} %windows.1), channel_id=1, replica_groups={{0,1,2,3,4,5,6,7},{8,9,10,11,12,13,14,15},{16,17,18,19,20,21,22,23},{24..., dimensions={0} | all-to-all | bytes 2555904 | tf_op jit(solution)/shard_map/all_to_all | solution.py:418
  27.3 0.0 copy-done.2
  27.3 0.0 copy-done
  27.3 0.0 copy-done.1
  27.3 0.0 copy-done.4
  27.3 6.7 %first_forward.1 = (bf16[192,384]{1,0:T(8,128)(2,1)S(1)}, bf16[9,192,384]{2,1,0:T(8,128)(2,1)S(1)}, bf16[4,384,192]{2,1,0:T(8,128)(2,1)S(1)}, bf16[4,192,384]{2,...) custom-call(s32[6]{0:T(128)S(1)} %copy-done.4, ...), custom_call_target="tpu_custom_call" | custom-call | flops 905969664 | bytes 7323672 | tf_op jit(solution)/shard_map/first_forward/pallas_call | solution.py:452
  34.0 1.3 %collective-permute-start = (bf16[192,384]{1,0:T(8,128)(2,1)S(1)}, bf16[192,384]{1,0:T(8,128)(2,1)S(1)}, u32[]{:S(2)}, u32[]{:S(2)}) collective-permute-start(bf16[192,384]{1,0:T(8,128)(2,1)S(1)} %get-tuple-element.19._), channel_id=1, source_target_pairs={{0,8},{2,10},{4,12},{5,13},{6,14},{7,15},{16,24},{18,26},{20,28},{... | collective-permute-start | bytes 442376 | tf_op jit(solution)/shard_map/ppermute | solution.py:422
  35.4 1.3 %collective-permute-start.1 = (bf16[96,256]{1,0:T(8,128)(2,1)S(1)}, bf16[96,256]{1,0:T(8,128)(2,1)S(1)}, u32[]{:S(2)}, u32[]{:S(2)}) collective-permute-start(bf16[96,256]{1,0:T(8,128)(2,1)S(1)} %near_rows.1), channel_id=1, source_target_pairs={{0,8},{2,10},{4,12},{5,13},{6,14},{7,15},{16,24},{18,26},{20,28},{... | collective-permute-start | bytes 147464 | tf_op jit(solution)/shard_map/ppermute | solution.py:422
  36.7 1.4 %collective-permute-done.entering = bf16[192,384]{1,0:T(8,128)(2,1)S(1)} collective-permute-done((bf16[192,384]{1,0:T(8,128)(2,1)S(1)}, bf16[192,384]{1,0:T(8,128)(2,1)S(1)}, u32[]{:S(2)}, u32[]{:S(2)}) %collective-permute-start) | collective-permute-done | bytes 147488 | tf_op jit(solution)/shard_map/ppermute | solution.py:422
  38.0 0.8 forward.1
  38.8 0.0 collective-permute-done.1.refs_0_
  38.8 0.4 middle.1
  39.2 1.3 %collective-permute-start.2 = (bf16[192,384]{1,0:T(8,128)(2,1)S(1)}, bf16[192,384]{1,0:T(8,128)(2,1)S(1)}, u32[]{:S(2)}, u32[]{:S(2)}) collective-permute-start(bf16[192,384]{1,0:T(8,128)(2,1)S(1)} %get-tuple-element.28), channel_id=1, source_target_pairs={{8,0},{10,2},{12,4},{13,5},{14,6},{15,7},{24,16},{26,18},{28,20},{... | collective-permute-start | bytes 442376 | tf_op jit(solution)/shard_map/ppermute | solution.py:422
  40.5 18.2 %collective-permute-done.2.arriving = bf16[192,384]{1,0:T(8,128)(2,1)S(1)} collective-permute-done((bf16[192,384]{1,0:T(8,128)(2,1)S(1)}, bf16[192,384]{1,0:T(8,128)(2,1)S(1)}, u32[]{:S(2)}, u32[]{:S(2)}) %collective-permute-start.2) | collective-permute-done | bytes 147488 | tf_op jit(solution)/shard_map/ppermute | solution.py:422
  58.7 6.1 %backward.1 = (bf16[192,384]{1,0:T(8,128)(2,1)}, bf16[8,192,384]{2,1,0:T(8,128)(2,1)S(1)}) custom-call(bf16[192,384]{1,0:T(8,128)(2,1)S(1)} %collective-permute-done.2.arriving, bf16[9,192,384]{2,1,0:T(8,128)(2,1)S(1)} %get-tuple-element.22.waves, bf16[8,208,384]{2,1,0:T(8,128)(2,1)S(1)} %all_to_all.10.blocks.refs_1_, ...), custom_call_target="tpu_custom_call" | custom-call | flops 905969664 | bytes 6438912 | tf_op jit(solution)/shard_map/backward/pallas_call | solution.py:452
  64.7 0.0 copy-start.3
  64.7 22.3 %all_to_all.11.grads_ref = bf16[8,192,384]{2,1,0:T(8,128)(2,1)S(1)} all-to-all(bf16[8,192,384]{2,1,0:T(8,128)(2,1)S(1)} %get-tuple-element.32), channel_id=1, replica_groups={{0,1,2,3,4,5,6,7},{8,9,10,11,12,13,14,15},{16,17,18,19,20,21,22,23},{24..., dimensions={0} | all-to-all | bytes 2359296 | tf_op jit(solution)/shard_map/all_to_all | solution.py:418
  87.1 0.0 copy-done.3
  87.1 3.2 %sum_windows.1 = f32[1,2,384,384]{3,2,1,0:T(8,128)} custom-call(s32[2,6]{1,0:T(2,128)S(1)} %bitcast.2, bf16[8,192,384]{2,1,0:T(8,128)(2,1)S(1)} %all_to_all.11.grads_ref), custom_call_target="tpu_custom_call" | custom-call | tf_op jit(solution)/shard_map/sum_windows/pallas_call | solution.py:515
  (1 shorter events, 0.0 us)
Async XLA Ops:
  0.7 26.7 %copy-start.2 = (f32[2,192,192]{2,1,0:T(8,128)S(1)}, f32[2,192,192]{2,1,0:T(8,128)}, u32[]{:S(2)}) copy-start(f32[2,192,192]{2,1,0:T(8,128)} %constant.2.clone.dft) | copy-start | bytes 884740
  4.7 22.7 %copy-start = (bf16[4,2,192,192]{3,2,1,0:T(8,128)(2,1)S(1)}, bf16[4,2,192,192]{3,2,1,0:T(8,128)(2,1)}, u32[]{:S(2)}) copy-start(bf16[4,2,192,192]{3,2,1,0:T(8,128)(2,1)} %refs_2_.1) | copy-start | bytes 1769476
  4.7 22.7 %copy-start.1 = (bf16[8,2,192,192]{3,2,1,0:T(8,128)(2,1)S(1)}, bf16[8,2,192,192]{3,2,1,0:T(8,128)(2,1)}, u32[]{:S(2)}) copy-start(bf16[8,2,192,192]{3,2,1,0:T(8,128)(2,1)} %probes.1) | copy-start | bytes 3538948
  4.7 22.7 %copy-start.4 = (s32[6]{0:T(128)S(1)}, s32[6]{0:T(128)}, u32[]{:S(2)}) copy-start(s32[6]{0:T(128)} %group_ref.1) | copy-start | bytes 76
  34.0 4.0 %collective-permute-start = (bf16[192,384]{1,0:T(8,128)(2,1)S(1)}, bf16[192,384]{1,0:T(8,128)(2,1)S(1)}, u32[]{:S(2)}, u32[]{:S(2)}) collective-permute-start(bf16[192,384]{1,0:T(8,128)(2,1)S(1)} %get-tuple-element.19._), channel_id=1, source_target_pairs={{0,8},{2,10},{4,12},{5,13},{6,14},{7,15},{16,24},{18,26},{20,28},{... | collective-permute-start | bytes 442376 | tf_op jit(solution)/shard_map/ppermute | solution.py:422
  35.4 3.4 %collective-permute-start.1 = (bf16[96,256]{1,0:T(8,128)(2,1)S(1)}, bf16[96,256]{1,0:T(8,128)(2,1)S(1)}, u32[]{:S(2)}, u32[]{:S(2)}) collective-permute-start(bf16[96,256]{1,0:T(8,128)(2,1)S(1)} %near_rows.1), channel_id=1, source_target_pairs={{0,8},{2,10},{4,12},{5,13},{6,14},{7,15},{16,24},{18,26},{20,28},{... | collective-permute-start | bytes 147464 | tf_op jit(solution)/shard_map/ppermute | solution.py:422
  39.2 19.5 %collective-permute-start.2 = (bf16[192,384]{1,0:T(8,128)(2,1)S(1)}, bf16[192,384]{1,0:T(8,128)(2,1)S(1)}, u32[]{:S(2)}, u32[]{:S(2)}) collective-permute-start(bf16[192,384]{1,0:T(8,128)(2,1)S(1)} %get-tuple-element.28), channel_id=1, source_target_pairs={{8,0},{10,2},{12,4},{13,5},{14,6},{15,7},{24,16},{26,18},{28,20},{... | collective-permute-start | bytes 442376 | tf_op jit(solution)/shard_map/ppermute | solution.py:422
  64.7 22.3 %copy-start.3 = (s32[6,2]{0,1:T(2,128)S(1)}, s32[6,2]{0,1:T(2,128)}, u32[]{:S(2)}) copy-start(s32[6,2]{0,1:T(2,128)} %param.13) | copy-start | bytes 148

commit v11 on v9

--- a/solution.py
+++ b/solution.py
@@ -32,51 +32,43 @@
     return lax.broadcasted_iota(jnp.int32, (rows, LANES), 1) < LANES // 2
 
 
-def spread(tail):
-    other = swapped(tail)
-    low = low_half(tail.shape[0])
-    return jnp.where(low, tail, other), jnp.where(low, other, tail)
-
-
-def signed(tail, minus_low):
-    low = low_half(tail.shape[0])
-    return jnp.where(low == minus_low, -tail, tail)
-
-
-def factor(b):
-    b0, b1, bt = halves(b)
-    return (b0, b1) + spread(bt)
-
-
-def times(a, parts):
-    a0, a1, at = halves(a)
-    b0, b1, b_real, b_imag = parts
-    tail = at * b_real + signed(swapped(at), True) * b_imag
-    return jnp.concatenate([a0 * b0 - a1 * b1, a1 * b0 + a0 * b1, tail], axis=1)
-
-
-def times_conj(a, turned, parts):
-    a0, a1, at = halves(a)
-    b0, b1, b_real, b_imag = parts
-    tail = at * b_real + turned * b_imag
-    return jnp.concatenate([a0 * b0 + a1 * b1, a1 * b0 - a0 * b1, tail], axis=1)
-
-
-def joined(both, conj):
-    width = both.shape[0] // 2
-    u0, u1, ut = halves(both[:width])
-    v0, v1, vt = halves(both[width:])
-    turned = signed(swapped(vt), not conj)
-    if conj:
-        return jnp.concatenate([u0 + v1, u1 - v0, ut + turned], axis=1)
-    return jnp.concatenate([u0 - v1, u1 + v0, ut + turned], axis=1)
-
-
-def with_mean(window):
-    x = window.astype(F32)
+def wide(x):
     x0, x1, xt = halves(x)
-    mean = jnp.where(low_half(xt.shape[0]), TRANSMIT, 0.0)
-    return jnp.concatenate([TRANSMIT + x0, x1, mean + xt], axis=1)
+    low = low_half(xt.shape[0])
+    return jnp.concatenate([x0, jnp.where(low, xt, 0.0), x1, jnp.where(low, swapped(xt), 0.0)], axis=1)
+
+
+def narrow(x):
+    x0, xt, x1, yt = (x[:, n * LANES : (n + 1) * LANES] for n in range(4))
+    return jnp.concatenate([x0, x1, jnp.where(low_half(xt.shape[0]), xt, swapped(yt))], axis=1)
+
+
+def parts(x):
+    return x[:, : 2 * LANES], x[:, 2 * LANES :]
+
+
+def upright(x):
+    return jnp.concatenate(parts(x), axis=0)
+
+
+def abreast(x):
+    half = x.shape[0] // 2
+    return jnp.concatenate([x[:half], x[half:]], axis=1)
+
+
+def times(a, b):
+    (ar, ai), (br, bi) = parts(a), parts(b)
+    return jnp.concatenate([ar * br - ai * bi, ai * br + ar * bi], axis=1)
+
+
+def times_conj(a, b):
+    (ar, ai), (br, bi) = parts(a), parts(b)
+    return jnp.concatenate([ar * br + ai * bi, ai * br - ar * bi], axis=1)
+
+
+def transmission(window):
+    real, imag = parts(wide(window.astype(F32)))
+    return jnp.concatenate([TRANSMIT + real, imag], axis=1)
 
 
 def split2(x):
@@ -165,93 +157,92 @@
         copy.wait()
 
 
-def right_table(real, imag):
+def left_table(table, at, real, imag):
     width = real.shape[0]
-    upper = packed(real, imag, width, 0)
-    lower = packed(-imag, real, width, 0)
-    return jnp.concatenate([upper[:LANES], lower[:LANES], upper[LANES:], lower[LANES:]], axis=0)
-
-
-def transposed(plane):
-    return plane.astype(F32).T.astype(BF16)
-
-
-def forward_tables(props, rf):
+    table[at, :width, :] = jnp.concatenate([real, -imag], axis=1).astype(BF16)
+    table[at, width:, :] = jnp.concatenate([imag, real], axis=1).astype(BF16)
+
+
+def right_table(table, at, real, imag):
+    width = real.shape[0]
+    second = 2 * LANES
+    table[at] = jnp.zeros(table.shape[1:], BF16)
+    for row, column, plane in (
+        (0, 0, real),
+        (0, second, imag),
+        (second, 0, -imag),
+        (second, second, real),
+    ):
+        table[at, row : row + width, column : column + width] = plane.astype(BF16)
+
+
+def forward_tables(props, lf, rf):
     for k in range(props.shape[0]):
-        rf[k] = right_table(transposed(props[k, 0]), transposed(props[k, 1])).astype(BF16)
+        real, imag = props[k, 0].astype(F32), props[k, 1].astype(F32)
+        left_table(lf, k, real, imag)
+        right_table(rf, k, real.T, imag.T)
 
 
 def backward_tables(props, lb, rb):
-    width = props.shape[-1]
     for k in range(props.shape[0]):
-        real, imag = props[k, 0], props[k, 1]
-        lb[k, :width, :] = transposed(real)
-        lb[k, width:, :] = transposed(imag)
-        rb[k] = right_table(real, -imag).astype(BF16)
-
-
-def detector_tables(dft, left, right, right_conj):
-    width = dft.shape[-1]
+        real, imag = props[k, 0].astype(F32), props[k, 1].astype(F32)
+        left_table(lb, k, real.T, -imag.T)
+        right_table(rb, k, real, -imag)
+
+
+def detector_tables(dft, left, right):
     for n, (real, imag) in enumerate(zip(split2(dft[0]), split2(dft[1]))):
-        left[n, :width, :] = real
-        left[n, width:, :] = imag
-        right[n] = right_table(real, imag).astype(BF16)
-        if n == 0:
-            right_conj[...] = right_table(real, -imag).astype(BF16)
+        real, imag = real.astype(F32), imag.astype(F32)
+        for at, sign in ((n, 1.0), (n + 2, -1.0)):
+            if at < 3:
+                left_table(left, at, real, sign * imag)
+                right_table(right, at, real, sign * imag)
 
 
 def forward_steps(blocks, waves, indices, lf, rf):
     sections, _, columns = blocks.shape
     width = columns // 2
     psi = waves[0]
-    parts = factor(with_mean(blocks[0, :width, :]))
     for k in range(sections):
         which = indices[k]
-        z = times(psi.astype(F32), parts).astype(BF16)
-        h = joined(dot(lf[which].reshape(columns, width), z), False).astype(BF16)
-        if k + 1 < sections:
-            parts = factor(with_mean(blocks[k + 1, :width, :]))
-        psi = dot(h, rf[which]).astype(BF16)
+        z = times(psi.astype(F32), transmission(blocks[k, :width, :])).astype(BF16)
+        h = dot(lf[which], upright(z)).astype(BF16)
+        psi = dot(abreast(h), rf[which]).astype(BF16)
         waves[k + 1] = psi
 
 
 def backward_steps(blocks, waves, indices, lb, rb, grads, g):
     sections, _, columns = blocks.shape
     width = columns // 2
-
-    def leave(k, y, turned, wave_parts):
-        grads[k] = times_conj(y, turned, wave_parts).astype(BF16)
-
-    late = None
     for k in reversed(range(sections)):
         which = indices[k]
-        both = dot(lb[which], g)
-        if late is not None:
-            leave(*late)
-        c = joined(both, True).astype(BF16)
-        wave_parts = factor(waves[k].astype(F32))
-        window_parts = factor(with_mean(blocks[k, :width, :]))
-        y = dot(c, rb[which])
-        turned = signed(swapped(halves(y)[2]), False)
-        g = times_conj(y, turned, window_parts).astype(BF16)
-        late = (k, y, turned, wave_parts)
-    leave(*late)
+        c = dot(lb[which], upright(g)).astype(BF16)
+        y = dot(abreast(c), rb[which])
+        g = times_conj(y, transmission(blocks[k, :width, :])).astype(BF16)
+        grads[k] = narrow(times_conj(y, waves[k].astype(F32))).astype(BF16)
     return g
 
 
-def detector(psi, observed, left, right, right_conj):
+def sent(wave):
+    return narrow(wave.astype(F32)).astype(BF16)
+
+
+def received(wave):
+    return wide(wave.astype(F32)).astype(BF16)
+
+
+def detector(psi, observed, left, right):
     def product(ah, al, bh, bl):
         return dot(ah, bh) + (dot(ah, bl) + dot(al, bh))
 
-    near = joined(dot(left[0], psi) + dot(left[1], psi), False)
+    psi = upright(psi)
+    near = abreast(dot(left[0], psi) + dot(left[1], psi))
     far = product(*split2(near), right[0], right[1])
-    f0, f1, ft = halves(far)
-    other = swapped(ft)
-    main = f0 * f0 + f1 * f1 - observed[:, :LANES]
-    tail = ft * ft + other * other - observed[:, LANES:]
-    push = jnp.concatenate([main * f0, main * f1, tail * ft], axis=1)
-    back = joined(dot(left[0], push.astype(BF16)), True)
-    return dot(back.astype(BF16), right_conj[...]).astype(BF16)
+    real, imag = parts(far)
+    misfit = real * real + imag * imag - observed
+    push = jnp.concatenate([misfit * real, misfit * imag], axis=0)
+    back = dot(left[2], push.astype(BF16)).astype(BF16)
+    return dot(abreast(back), right[2]).astype(BF16)
 
 
 def read_indices(blocks, indices, count):
@@ -276,7 +267,7 @@
     near[...] = observed[...].astype(BF16)
 
 
-def first_kernel(group_ref, probes, blocks, props, dft, leaving, waves, lb, rf, rb, left, right, right_conj, probe, indices, sem):
+def first_kernel(group_ref, probes, blocks, props, dft, leaving, waves, lf, rf, lb, rb, left, right, probe, indices, sem):
     size = blocks.shape[0]
     slot, group = place_in(size)
 
@@ -288,31 +279,31 @@
         which = group_ref[position]
         copy = pltpu.make_async_copy(probes.at[which], probe, sem)
         copy.start()
-        forward_tables(props, rf)
+        forward_tables(props, lf, rf)
         read_indices(blocks, indices, props.shape[0])
         copy.wait()
-        waves[0] = packed(probe[0], probe[1], probe.shape[-1], 0).astype(BF16)
-        forward_steps(blocks, waves, indices, props, rf)
-        leaving[...] = waves[size]
+        waves[0] = wide(packed(probe[0], probe[1], probe.shape[-1], 0)).astype(BF16)
+        forward_steps(blocks, waves, indices, lf, rf)
+        leaving[...] = sent(waves[size])
 
     @pl.when(group > 0)
     def _():
-        forward_tables(props, rf)
+        forward_tables(props, lf, rf)
         backward_tables(props, lb, rb)
-        detector_tables(dft, left, right, right_conj)
+        detector_tables(dft, left, right)
 
 
 def forward_kernel(stage):
-    def kernel(entering, blocks, props, rf, waves_in, leaving, waves, indices):
+    def kernel(entering, blocks, lf, rf, waves_in, leaving, waves, indices):
         size = blocks.shape[0]
         _, group = place_in(size)
 
         @pl.when(group == stage)
         def _():
-            read_indices(blocks, indices, props.shape[0])
-            waves[0] = entering[...]
-            forward_steps(blocks, waves, indices, props, rf)
-            leaving[...] = waves[size]
+            read_indices(blocks, indices, lf.shape[0])
+            waves[0] = received(entering[...])
+            forward_steps(blocks, waves, indices, lf, rf)
+            leaving[...] = sent(waves[size])
 
         @pl.when(group != stage)
         def _():
@@ -324,7 +315,7 @@
 def middle_kernel(groups):
     def kernel(waves, *refs):
         earlier, refs = refs[: groups - 1], refs[groups - 1 :]
-        blocks, props, lb, rb, left, right, right_conj, leaving, grads, lb_out, rb_out, observed, indices = refs
+        blocks, props, lb, rb, left, right, leaving, grads, lb_out, rb_out, observed, indices = refs
         size = blocks.shape[0]
         _, group = place_in(size)
 
@@ -335,8 +326,8 @@
             for n, near in enumerate(earlier):
                 observed[n * rows : (n + 1) * rows, :] = near[...].astype(F32)
             observe(blocks, rows // size, observed, (groups - 1) * rows)
-            g = detector(waves[size], observed[...], left, right, right_conj)
-            leaving[...] = backward_steps(blocks, waves, indices, lb, rb, grads, g)
+            g = detector(waves[size], observed[...], left, right)
+            leaving[...] = sent(backward_steps(blocks, waves, indices, lb, rb, grads, g))
 
         @pl.when(group < groups - 1)
         def _():
@@ -352,7 +343,8 @@
         @pl.when(group == stage)
         def _():
             read_indices(blocks, indices, lb.shape[0])
-            leaving[...] = backward_steps(blocks, waves, indices, lb, rb, grads, arriving[...])
+            g = received(arriving[...])
+            leaving[...] = sent(backward_steps(blocks, waves, indices, lb, rb, grads, g))
 
         @pl.when(group != stage)
         def _():
@@ -435,12 +427,11 @@
 
     wave = struct(width, 2 * width)
     near = struct(size * near_rows, 2 * LANES)
-    waves_shape = struct(size + 1, width, 2 * width)
+    full = 4 * LANES
+    waves_shape = struct(size + 1, width, full)
     grads_shape = struct(size, width, 2 * width)
-    left_table = struct(kinds, 2 * width, width)
-    square_table = struct(kinds, 2 * width, 2 * width)
-    detector_left = struct(2, 2 * width, width)
-    detector_right = struct(2, 2 * width, 2 * width)
+    lefts, rights = struct(kinds, 2 * width, 2 * width), struct(kinds, full, full)
+    detector_tables_shapes = [struct(3, 2 * width, 2 * width), struct(3, full, full)]
     indices = pltpu.SMEM((size,), jnp.int32)
 
     def call(kernel, name, out_shape, in_specs, scratch_shapes, operands, slices=0):
@@ -459,11 +450,10 @@
             name=name,
         )(*operands)
 
-    leaving, waves, lb, rf, rb, *dft = call(
+    leaving, waves, lf, rf, lb, rb, *dft = call(
         first_kernel,
         "first_forward",
-        [wave, waves_shape, left_table, square_table, square_table]
-        + [detector_left, detector_right, struct(2 * width, 2 * width)],
+        [wave, waves_shape, lefts, rights, lefts, rights] + detector_tables_shapes,
         [SMEM, HBM, VMEM, VMEM, VMEM],
         [pltpu.VMEM(probes.shape[1:], BF16), indices, pltpu.SemaphoreType.DMA],
         (probe_group, probes, blocks, propagators, jnp.asarray(dft_constant(width))),
@@ -479,7 +469,7 @@
             [wave, waves_shape],
             [VMEM] * 5,
             [indices],
-            (entering, blocks, propagators, rf, waves),
+            (entering, blocks, lf, rf, waves),
             size,
         )
         if stage < groups - 1:
@@ -488,8 +478,8 @@
     leaving, grads, lb, rb = call(
         middle_kernel(groups),
         "middle",
-        [wave, grads_shape, left_table, square_table],
-        [VMEM] * (groups + 7),
+        [wave, grads_shape, lefts, rights],
+        [VMEM] * (groups + 6),
         [pltpu.VMEM((width, 2 * LANES), F32), indices],
         (waves, *nears, blocks, propagators, lb, rb, *dft),
         size,

time: 85.9 us -> 89 us (1.036)
  Pallas kernels: 19.3 us -> 20.8 us
  waiting for transfers between devices: 16.8 us -> 18.3 us
    pallas_call x5, Pallas kernels: 12.1 us -> 13.6 us  [call(): pl.pallas_call(kernel, out_shape=out_shape, in_specs=in_specs, out_specs=...]
    ppermute x3, waiting for transfers between devices: 16.8 us -> 18.3 us  [handed(): return lax.ppermute(block, 'cuts', route)]
where the time goes in v11:
time: 89 us; the launch traced here: 88.7 us
  blocking collectives  45 us (51%)
  Pallas kernels  20.8 us (23%)
  waiting for transfers between devices  18.3 us (21%)
  starting transfers between devices  3.88 us (4%)
    all_to_all x2, blocking collectives, exchanged(): lax.all_to_all(blocks, 'cuts', 0, 0, axis_index_groups=members, tiled=True)  45 us
    ppermute x3, waiting for transfers between devices, handed(): return lax.ppermute(block, 'cuts', route)  18.3 us
    pallas_call x5, Pallas kernels, call(): pl.pallas_call(kernel, out_shape=out_shape, in_specs=in_specs, out_specs=...  13.6 us
    pallas_call x1, Pallas kernels, shards(): pl.pallas_call(window_kernel, out_shape=struct(size, rows, 2 * width), in...  3.99 us
    ppermute x3, starting transfers between devices, handed(): return lax.ppermute(block, 'cuts', route)  3.88 us
    pallas_call x1, Pallas kernels, shards(): pl.pallas_call(gather_kernel, out_shape=jax.ShapeDtypeStruct(objects.shap...  3.19 us
  transfers between devices with their start and end apart: 3, of which 2 were waited for; matrix products, arithmetic and copies ran while one was open for 0% of the time, Pallas kernels for 1%

profile of v11, /device:TPU:0, one launch (start us, length us, event | category | flops | bytes accessed | tf_op | source)
XLA Modules:
  0.0 88.7 jit_solution(9220602159093750307)
XLA Ops:
  0.7 0.0 copy-start.2
  0.7 4.0 %windows.1 = bf16[8,208,384]{2,1,0:T(8,128)(2,1)} custom-call(s32[2,6]{1,0:T(2,128)} %bitcast.1, s32[1]{0:T(128)S(6)} %copy.9.index_ref, bf16[1,2,384,384]{3,2,1,0:T(8,128)(2,1)} %objects_in.1, f32[6,12,192]{2,1,0:T(8,128)} %measured_in.1), custom_call_target="tpu_custom_call" | custom-call | tf_op jit(solution)/shard_map/windows/pallas_call | solution.py:411
  4.7 0.0 copy-start
  4.7 0.0 copy-start.1
  4.7 0.0 copy-start.4
  4.7 22.6 %all_to_all.10.blocks.refs_1_ = bf16[8,208,384]{2,1,0:T(8,128)(2,1)S(1)} all-to-all(bf16[8,208,384]{2,1,0:T(8,128)(2,1)} %windows.1), channel_id=1, replica_groups={{0,1,2,3,4,5,6,7},{8,9,10,11,12,13,14,15},{16,17,18,19,20,21,22,23},{24..., dimensions={0} | all-to-all | bytes 2555904 | tf_op jit(solution)/shard_map/all_to_all | solution.py:405
  27.3 0.0 copy-done.2
  27.3 0.0 copy-done
  27.3 0.0 copy-done.1
  27.3 0.0 copy-done.4
  27.3 6.5 %first_forward.1 = (bf16[192,384]{1,0:T(8,128)(2,1)S(1)}, bf16[9,192,512]{2,1,0:T(8,128)(2,1)S(1)}, bf16[4,384,384]{2,1,0:T(8,128)(2,1)S(1)}, bf16[4,512,512]{2,...) custom-call(s32[6]{0:T(128)S(1)} %copy-done.4, ...), custom_call_target="tpu_custom_call" | custom-call | flops 905969664 | bytes 14270488 | tf_op jit(solution)/shard_map/first_forward/pallas_call | solution.py:438
  33.8 1.3 %collective-permute-start = (bf16[192,384]{1,0:T(8,128)(2,1)S(1)}, bf16[192,384]{1,0:T(8,128)(2,1)S(1)}, u32[]{:S(2)}, u32[]{:S(2)}) collective-permute-start(bf16[192,384]{1,0:T(8,128)(2,1)S(1)} %get-tuple-element.19._), channel_id=1, source_target_pairs={{0,8},{2,10},{4,12},{5,13},{6,14},{7,15},{16,24},{18,26},{20,28},{... | collective-permute-start | bytes 442376 | tf_op jit(solution)/shard_map/ppermute | solution.py:409
  35.1 1.3 %collective-permute-start.1 = (bf16[96,256]{1,0:T(8,128)(2,1)S(1)}, bf16[96,256]{1,0:T(8,128)(2,1)S(1)}, u32[]{:S(2)}, u32[]{:S(2)}) collective-permute-start(bf16[96,256]{1,0:T(8,128)(2,1)S(1)} %near_rows.1), channel_id=1, source_target_pairs={{0,8},{2,10},{4,12},{5,13},{6,14},{7,15},{16,24},{18,26},{20,28},{... | collective-permute-start | bytes 147464 | tf_op jit(solution)/shard_map/ppermute | solution.py:409
  36.4 1.4 %collective-permute-done.entering = bf16[192,384]{1,0:T(8,128)(2,1)S(1)} collective-permute-done((bf16[192,384]{1,0:T(8,128)(2,1)S(1)}, bf16[192,384]{1,0:T(8,128)(2,1)S(1)}, u32[]{:S(2)}, u32[]{:S(2)}) %collective-permute-start) | collective-permute-done | bytes 147488 | tf_op jit(solution)/shard_map/ppermute | solution.py:409
  37.8 0.8 forward.1
  38.6 0.0 collective-permute-done.1.refs_0_
  38.6 0.7 middle.1
  39.3 1.3 %collective-permute-start.2 = (bf16[192,384]{1,0:T(8,128)(2,1)S(1)}, bf16[192,384]{1,0:T(8,128)(2,1)S(1)}, u32[]{:S(2)}, u32[]{:S(2)}) collective-permute-start(bf16[192,384]{1,0:T(8,128)(2,1)S(1)} %get-tuple-element.28), channel_id=1, source_target_pairs={{8,0},{10,2},{12,4},{13,5},{14,6},{15,7},{24,16},{26,18},{28,20},{... | collective-permute-start | bytes 442376 | tf_op jit(solution)/shard_map/ppermute | solution.py:409
  40.6 16.9 %collective-permute-done.2.arriving = bf16[192,384]{1,0:T(8,128)(2,1)S(1)} collective-permute-done((bf16[192,384]{1,0:T(8,128)(2,1)S(1)}, bf16[192,384]{1,0:T(8,128)(2,1)S(1)}, u32[]{:S(2)}, u32[]{:S(2)}) %collective-permute-start.2) | collective-permute-done | bytes 147488 | tf_op jit(solution)/shard_map/ppermute | solution.py:409
  57.5 5.7 %backward.1 = (bf16[192,384]{1,0:T(8,128)(2,1)}, bf16[8,192,384]{2,1,0:T(8,128)(2,1)S(1)}) custom-call(bf16[192,384]{1,0:T(8,128)(2,1)S(1)} %collective-permute-done.2.arriving, bf16[9,192,512]{2,1,0:T(8,128)(2,1)S(1)} %get-tuple-element.23.waves, bf16[8,208,384]{2,1,0:T(8,128)(2,1)S(1)} %all_to_all.10.blocks.refs_1_, ...), custom_call_target="tpu_custom_call" | custom-call | flops 905969664 | bytes 8978432 | tf_op jit(solution)/shard_map/backward/pallas_call | solution.py:438
  63.2 0.0 copy-start.3
  63.2 22.3 %all_to_all.11.grads_ref = bf16[8,192,384]{2,1,0:T(8,128)(2,1)S(1)} all-to-all(bf16[8,192,384]{2,1,0:T(8,128)(2,1)S(1)} %get-tuple-element.32), channel_id=1, replica_groups={{0,1,2,3,4,5,6,7},{8,9,10,11,12,13,14,15},{16,17,18,19,20,21,22,23},{24..., dimensions={0} | all-to-all | bytes 2359296 | tf_op jit(solution)/shard_map/all_to_all | solution.py:405
  85.5 0.0 copy-done.3
  85.5 3.2 %sum_windows.1 = f32[1,2,384,384]{3,2,1,0:T(8,128)} custom-call(s32[2,6]{1,0:T(2,128)S(1)} %bitcast.2, bf16[8,192,384]{2,1,0:T(8,128)(2,1)S(1)} %all_to_all.11.grads_ref), custom_call_target="tpu_custom_call" | custom-call | tf_op jit(solution)/shard_map/sum_windows/pallas_call | solution.py:500
  (1 shorter events, 0.0 us)
Async XLA Ops:
  0.7 26.7 %copy-start.2 = (f32[2,192,192]{2,1,0:T(8,128)S(1)}, f32[2,192,192]{2,1,0:T(8,128)}, u32[]{:S(2)}) copy-start(f32[2,192,192]{2,1,0:T(8,128)} %constant.2.clone.dft) | copy-start | bytes 884740
  4.7 22.7 %copy-start = (bf16[4,2,192,192]{3,2,1,0:T(8,128)(2,1)S(1)}, bf16[4,2,192,192]{3,2,1,0:T(8,128)(2,1)}, u32[]{:S(2)}) copy-start(bf16[4,2,192,192]{3,2,1,0:T(8,128)(2,1)} %refs_2_.1) | copy-start | bytes 1769476
  4.7 22.7 %copy-start.1 = (bf16[8,2,192,192]{3,2,1,0:T(8,128)(2,1)S(1)}, bf16[8,2,192,192]{3,2,1,0:T(8,128)(2,1)}, u32[]{:S(2)}) copy-start(bf16[8,2,192,192]{3,2,1,0:T(8,128)(2,1)} %probes.1) | copy-start | bytes 3538948
  4.7 22.7 %copy-start.4 = (s32[6]{0:T(128)S(1)}, s32[6]{0:T(128)}, u32[]{:S(2)}) copy-start(s32[6]{0:T(128)} %group_ref.1) | copy-start | bytes 76
  33.8 4.0 %collective-permute-start = (bf16[192,384]{1,0:T(8,128)(2,1)S(1)}, bf16[192,384]{1,0:T(8,128)(2,1)S(1)}, u32[]{:S(2)}, u32[]{:S(2)}) collective-permute-start(bf16[192,384]{1,0:T(8,128)(2,1)S(1)} %get-tuple-element.19._), channel_id=1, source_target_pairs={{0,8},{2,10},{4,12},{5,13},{6,14},{7,15},{16,24},{18,26},{20,28},{... | collective-permute-start | bytes 442376 | tf_op jit(solution)/shard_map/ppermute | solution.py:409
  35.1 3.4 %collective-permute-start.1 = (bf16[96,256]{1,0:T(8,128)(2,1)S(1)}, bf16[96,256]{1,0:T(8,128)(2,1)S(1)}, u32[]{:S(2)}, u32[]{:S(2)}) collective-permute-start(bf16[96,256]{1,0:T(8,128)(2,1)S(1)} %near_rows.1), channel_id=1, source_target_pairs={{0,8},{2,10},{4,12},{5,13},{6,14},{7,15},{16,24},{18,26},{20,28},{... | collective-permute-start | bytes 147464 | tf_op jit(solution)/shard_map/ppermute | solution.py:409
  39.3 18.2 %collective-permute-start.2 = (bf16[192,384]{1,0:T(8,128)(2,1)S(1)}, bf16[192,384]{1,0:T(8,128)(2,1)S(1)}, u32[]{:S(2)}, u32[]{:S(2)}) collective-permute-start(bf16[192,384]{1,0:T(8,128)(2,1)S(1)} %get-tuple-element.28), channel_id=1, source_target_pairs={{8,0},{10,2},{12,4},{13,5},{14,6},{15,7},{24,16},{26,18},{28,20},{... | collective-permute-start | bytes 442376 | tf_op jit(solution)/shard_map/ppermute | solution.py:409
  63.2 22.3 %copy-start.3 = (s32[6,2]{0,1:T(2,128)S(1)}, s32[6,2]{0,1:T(2,128)}, u32[]{:S(2)}) copy-start(s32[6,2]{0,1:T(2,128)} %param.13) | copy-start | bytes 148

commit v12 on v9

--- a/solution.py
+++ b/solution.py
@@ -84,16 +84,12 @@
     return high, (x - high.astype(F32)).astype(BF16)
 
 
-def picker(columns, start, high_tail, transposed=False):
-    shape = (2 * LANES, columns) if transposed else (columns, 2 * LANES)
-    a = lax.broadcasted_iota(jnp.int32, shape, 1 if transposed else 0) - start
-    q = lax.broadcasted_iota(jnp.int32, shape, 0 if transposed else 1)
-    if high_tail:
-        half = LANES // 2
-        wanted = jnp.where(q < LANES, q, jnp.where(q < LANES + half, -columns, q - half))
-    else:
-        wanted = jnp.where(q < LANES + LANES // 2, q, -columns)
-    return jnp.where(a == wanted, 1.0, 0.0).astype(BF16)
+def picker(shape, start):
+    columns, across = (0, 1) if shape[0] > shape[1] else (1, 0)
+    taken = lax.broadcasted_iota(jnp.int32, shape, columns) - start
+    place = lax.broadcasted_iota(jnp.int32, shape, across)
+    wanted = jnp.where(place < LANES + LANES // 2, place, -shape[columns])
+    return jnp.where(taken == wanted, 1.0, 0.0).astype(BF16)
 
 
 def row_picker(shape, distance):
@@ -115,12 +111,8 @@
     return x
 
 
-def packed(real, imag, columns, start):
-    left = dot(real, picker(columns, start, False))
-    right = dot(imag, picker(columns, start, True))
-    return jnp.concatenate(
-        [left[:, :LANES], right[:, :LANES], left[:, LANES:] + right[:, LANES:]], axis=1
-    )
+def packed(real, imag):
+    return jnp.concatenate([real[:, :LANES], imag[:, :LANES], real[:, LANES:], imag[:, LANES:]], axis=1)
 
 
 def dft_constant(width):
@@ -130,8 +122,14 @@
 
 
 def slots_of(positions, size):
-    order = list(range(0, size, 2)) + list(range(size - 1, 0, -2))
-    return sorted(order[:positions])
+    half = size // 2
+    order = list(range(half, size)) + list(range(0, half, 2)) + list(range(1, half, 2))
+    return order[:positions]
+
+
+def slots_in(group, positions, size):
+    flip = (group % 2) * (size // 2)
+    return [slot ^ flip for slot in slots_of(positions, size)]
 
 
 def window_kernel(offsets_in, index_ref, objects_in, measured_in, blocks_out, blocks, offsets_ref, objects, measured, sems):
@@ -148,46 +146,47 @@
     tag = jnp.full((ROWS, LANES), index_ref[0], jnp.int32).astype(F32)
     for copy in copies:
         copy.wait()
+    size = blocks_out.shape[0]
+    _, group = place_in(size)
+    flip = lax.rem(group, 2) * (size // 2)
     sending = []
-    for p, slot in enumerate(slots_of(positions, blocks.shape[0])):
+    for p, slot in enumerate(slots_of(positions, size)):
         start = offsets_ref[0, p]
-        real, imag = (rows_near(objects[c], start, width) for c in range(2))
-        window = packed(real, imag, extent, offsets_ref[1, p]).astype(BF16)
+        both = jnp.concatenate([rows_near(objects[c], start, width) for c in range(2)], axis=0)
+        picked = dot(both, picker((extent, 2 * LANES), offsets_ref[1, p]))
+        real, imag = picked[: width + ROWS], picked[width + ROWS :]
+        tail = jnp.where(low_half(width + ROWS), real[:, LANES:], swapped(imag[:, LANES:]))
+        window = jnp.concatenate([real[:, :LANES], imag[:, :LANES], tail], axis=1).astype(BF16)
         shift = lax.bitwise_and(start, ROWS - 1)
-        blocks[slot, :width, :] = dot(row_picker((width, width + ROWS), shift), window).astype(BF16)
+        blocks[p, :width, :] = dot(row_picker((width, width + ROWS), shift), window).astype(BF16)
         tail = measured[p, :, LANES:]
         seen = jnp.concatenate([measured[p, :, :LANES], tail, tail, tag[:near_rows]], axis=1)
         left_over = jnp.concatenate([tag[near_rows:]] * 3, axis=1)
-        blocks[slot, width:, :] = jnp.concatenate([seen, left_over], axis=0).astype(BF16)
-        sending.append(pltpu.make_async_copy(blocks.at[slot], blocks_out.at[slot], sems.at[4 + p]))
+        blocks[p, width:, :] = jnp.concatenate([seen, left_over], axis=0).astype(BF16)
+        target = blocks_out.at[lax.bitwise_xor(slot, flip)]
+        sending.append(pltpu.make_async_copy(blocks.at[p], target, sems.at[4 + p]))
         sending[-1].start()
     for copy in sending:
         copy.wait()
 
 
 def right_table(real, imag):
-    width = real.shape[0]
-    upper = packed(real, imag, width, 0)
-    lower = packed(-imag, real, width, 0)
-    return jnp.concatenate([upper[:LANES], lower[:LANES], upper[LANES:], lower[LANES:]], axis=0)
-
-
-def transposed(plane):
-    return plane.astype(F32).T.astype(BF16)
+    upper, lower = packed(real, imag), packed(-imag, real)
+    return jnp.concatenate([upper[:LANES], lower[:LANES], upper[LANES:], lower[LANES:]], axis=0).astype(BF16)
 
 
 def forward_tables(props, rf):
     for k in range(props.shape[0]):
-        rf[k] = right_table(transposed(props[k, 0]), transposed(props[k, 1])).astype(BF16)
+        rf[k] = right_table(props[k, 0].astype(F32).T, props[k, 1].astype(F32).T)
 
 
 def backward_tables(props, lb, rb):
     width = props.shape[-1]
     for k in range(props.shape[0]):
-        real, imag = props[k, 0], props[k, 1]
-        lb[k, :width, :] = transposed(real)
-        lb[k, width:, :] = transposed(imag)
-        rb[k] = right_table(real, -imag).astype(BF16)
+        real, imag = props[k, 0].astype(F32), props[k, 1].astype(F32)
+        lb[k, :width, :] = real.T.astype(BF16)
+        lb[k, width:, :] = imag.T.astype(BF16)
+        rb[k] = right_table(real, -imag)
 
 
 def detector_tables(dft, left, right, right_conj):
@@ -195,9 +194,10 @@
     for n, (real, imag) in enumerate(zip(split2(dft[0]), split2(dft[1]))):
         left[n, :width, :] = real
         left[n, width:, :] = imag
-        right[n] = right_table(real, imag).astype(BF16)
+        real, imag = real.astype(F32), imag.astype(F32)
+        right[n] = right_table(real, imag)
         if n == 0:
-            right_conj[...] = right_table(real, -imag).astype(BF16)
+            right_conj[...] = right_table(real, -imag)
 
 
 def forward_steps(blocks, waves, indices, lf, rf):
@@ -291,7 +291,7 @@
         forward_tables(props, rf)
         read_indices(blocks, indices, props.shape[0])
         copy.wait()
-        waves[0] = packed(probe[0], probe[1], probe.shape[-1], 0).astype(BF16)
+        waves[0] = packed(probe[0].astype(F32), probe[1].astype(F32)).astype(BF16)
         forward_steps(blocks, waves, indices, props, rf)
         leaving[...] = waves[size]
 
@@ -361,31 +361,31 @@
     return kernel
 
 
-def gather_kernel(offsets_ref, grads_ref, out_ref):
+def gather_kernel(offsets_ref, grads_ref, out_ref, planes, sems):
     positions = offsets_ref.shape[1]
-    width = grads_ref.shape[1]
+    size, width, _ = grads_ref.shape
     extent = out_ref.shape[-1]
+    _, group = place_in(size)
+    flip = lax.rem(group, 2) * (size // 2)
     spread_out = []
-    for p, slot in enumerate(slots_of(positions, grads_ref.shape[0])):
-        x0, x1, xt = halves(grads_ref[slot])
-        spread_out.append(
-            jnp.concatenate(
-                [
-                    dot(
-                        jnp.concatenate([main, xt], axis=1),
-                        picker(extent, offsets_ref[1, p], c == 1, transposed=True),
-                    ).astype(BF16)
-                    for c, main in ((0, x0), (1, x1))
-                ],
-                axis=1,
-            )
+    for p, slot in enumerate(slots_of(positions, size)):
+        x0, x1, xt = halves(grads_ref[lax.bitwise_xor(slot, flip)])
+        other = swapped(xt.astype(F32)).astype(BF16)
+        both = jnp.concatenate(
+            [jnp.concatenate([x0, xt], axis=1), jnp.concatenate([x1, other], axis=1)], axis=0
         )
+        spread_out.append(dot(both, picker((2 * LANES, extent), offsets_ref[1, p])).astype(BF16))
     rows = jnp.concatenate(
         [row_picker((extent, width), -offsets_ref[0, p]) for p in range(positions)], axis=1
     )
-    total = dot(rows, jnp.concatenate(spread_out, axis=0))
-    out_ref[0, 0] = total[:, :extent]
-    out_ref[0, 1] = total[:, extent:]
+    copies = []
+    for c in range(2):
+        here = slice(c * width, (c + 1) * width)
+        planes[c] = dot(rows, jnp.concatenate([x[here] for x in spread_out], axis=0))
+        copies.append(pltpu.make_async_copy(planes.at[c], out_ref.at[0, c], sems.at[c]))
+        copies[-1].start()
+    for copy in copies:
+        copy.wait()
 
 
 VMEM = pl.BlockSpec(memory_space=pltpu.VMEM)
@@ -413,7 +413,8 @@
         return lax.all_to_all(blocks, "cuts", 0, 0, axis_index_groups=members, tiled=True)
 
     def handed(block, stage, distance):
-        route = [(stage * size + l, (stage + distance) * size + l) for l in slots]
+        ends = (slots_in(at, len(slots), size) for at in (stage, stage + distance))
+        route = [(stage * size + l, (stage + distance) * size + m) for l, m in zip(*ends)]
         return lax.ppermute(block, "cuts", route)
 
     blocks = pl.pallas_call(
@@ -511,7 +512,8 @@
         gather_kernel,
         out_shape=jax.ShapeDtypeStruct(objects.shape, F32),
         in_specs=[SMEM, VMEM],
-        out_specs=VMEM,
+        out_specs=HBM,
+        scratch_shapes=[pltpu.VMEM(objects.shape[1:], F32), pltpu.SemaphoreType.DMA((2,))],
         compiler_params=PARAMS,
         name="sum_windows",
     )(offsets.T, exchanged(grads))

time: 85.9 us -> 86.8 us (1.010)
  waiting for transfers between devices: 16.8 us -> 17.9 us
    ppermute x3, waiting for transfers between devices: 16.8 us -> 17.9 us  [handed(): return lax.ppermute(block, 'cuts', route)]
where the time goes in v12:
time: 86.8 us; the launch traced here: 86.5 us
  blocking collectives  44.3 us (51%)
  Pallas kernels  19.5 us (22%)
  waiting for transfers between devices  17.9 us (21%)
  starting transfers between devices  3.88 us (4%)
  between operations  0.91 us (1%)
    all_to_all x2, blocking collectives, exchanged(): lax.all_to_all(blocks, 'cuts', 0, 0, axis_index_groups=members, tiled=True)  44.3 us
    ppermute x3, waiting for transfers between devices, handed(): return lax.ppermute(block, 'cuts', route)  17.9 us
    pallas_call x5, Pallas kernels, call(): pl.pallas_call(kernel, out_shape=out_shape, in_specs=in_specs, out_specs=...  11.7 us
    pallas_call x1, Pallas kernels, shards(): pl.pallas_call(window_kernel, out_shape=struct(size, rows, 2 * width), in...  4.7 us
    ppermute x3, starting transfers between devices, handed(): return lax.ppermute(block, 'cuts', route)  3.88 us
    pallas_call x1, Pallas kernels, shards(): pl.pallas_call(gather_kernel, out_shape=jax.ShapeDtypeStruct(objects.shap...  3.17 us
  transfers between devices with their start and end apart: 3, of which 2 were waited for; matrix products, arithmetic and copies ran while one was open for 0% of the time, Pallas kernels for 1%

profile of v12, /device:TPU:0, one launch (start us, length us, event | category | flops | bytes accessed | tf_op | source)
XLA Modules:
  0.0 86.5 jit_solution(280835820474616304)
XLA Ops:
  0.7 0.0 copy-start.2
  0.7 4.7 %windows.1 = bf16[8,208,384]{2,1,0:T(8,128)(2,1)} custom-call(s32[2,6]{1,0:T(2,128)} %bitcast.1, s32[1]{0:T(128)S(6)} %copy.9.index_ref, bf16[1,2,384,384]{3,2,1,0:T(8,128)(2,1)} %objects_in.1, f32[6,12,192]{2,1,0:T(8,128)} %measured_in.1), custom_call_target="tpu_custom_call" | custom-call | tf_op jit(solution)/shard_map/windows/pallas_call | solution.py:420
  5.4 0.0 copy-start
  5.4 0.0 copy-start.1
  5.4 0.0 copy-start.4
  5.4 22.6 %all_to_all.10.blocks.refs_1_ = bf16[8,208,384]{2,1,0:T(8,128)(2,1)S(1)} all-to-all(bf16[8,208,384]{2,1,0:T(8,128)(2,1)} %windows.1), channel_id=1, replica_groups={{0,1,2,3,4,5,6,7},{8,9,10,11,12,13,14,15},{16,17,18,19,20,21,22,23},{24..., dimensions={0} | all-to-all | bytes 2555904 | tf_op jit(solution)/shard_map/all_to_all | solution.py:413
  28.0 0.0 copy-done.2
  28.1 0.0 copy-done
  28.1 0.0 copy-done.1
  28.1 0.0 copy-done.4
  28.1 5.5 %first_forward.1 = (bf16[192,384]{1,0:T(8,128)(2,1)S(1)}, bf16[9,192,384]{2,1,0:T(8,128)(2,1)S(1)}, bf16[4,384,192]{2,1,0:T(8,128)(2,1)S(1)}, bf16[4,384,384]{2,...) custom-call(s32[6]{0:T(128)S(1)} %copy-done.4, ...), custom_call_target="tpu_custom_call" | custom-call | flops 905969664 | bytes 8945688 | tf_op jit(solution)/shard_map/first_forward/pallas_call | solution.py:448
  33.6 1.3 %collective-permute-start = (bf16[192,384]{1,0:T(8,128)(2,1)S(1)}, bf16[192,384]{1,0:T(8,128)(2,1)S(1)}, u32[]{:S(2)}, u32[]{:S(2)}) collective-permute-start(bf16[192,384]{1,0:T(8,128)(2,1)S(1)} %get-tuple-element.19._), channel_id=1, source_target_pairs={{4,8},{5,9},{6,10},{7,11},{0,12},{2,14},{20,24},{21,25},{22,26},{2... | collective-permute-start | bytes 442376 | tf_op jit(solution)/shard_map/ppermute | solution.py:418
  34.9 1.3 %collective-permute-start.1 = (bf16[96,256]{1,0:T(8,128)(2,1)S(1)}, bf16[96,256]{1,0:T(8,128)(2,1)S(1)}, u32[]{:S(2)}, u32[]{:S(2)}) collective-permute-start(bf16[96,256]{1,0:T(8,128)(2,1)S(1)} %near_rows.1), channel_id=1, source_target_pairs={{4,8},{5,9},{6,10},{7,11},{0,12},{2,14},{20,24},{21,25},{22,26},{2... | collective-permute-start | bytes 147464 | tf_op jit(solution)/shard_map/ppermute | solution.py:418
  36.2 1.4 %collective-permute-done.entering = bf16[192,384]{1,0:T(8,128)(2,1)S(1)} collective-permute-done((bf16[192,384]{1,0:T(8,128)(2,1)S(1)}, bf16[192,384]{1,0:T(8,128)(2,1)S(1)}, u32[]{:S(2)}, u32[]{:S(2)}) %collective-permute-start) | collective-permute-done | bytes 147488 | tf_op jit(solution)/shard_map/ppermute | solution.py:418
  37.5 0.8 forward.1
  38.3 0.0 collective-permute-done.1.refs_0_
  38.3 0.4 middle.1
  38.8 1.3 %collective-permute-start.2 = (bf16[192,384]{1,0:T(8,128)(2,1)S(1)}, bf16[192,384]{1,0:T(8,128)(2,1)S(1)}, u32[]{:S(2)}, u32[]{:S(2)}) collective-permute-start(bf16[192,384]{1,0:T(8,128)(2,1)S(1)} %get-tuple-element.28), channel_id=1, source_target_pairs={{8,4},{9,5},{10,6},{11,7},{12,0},{14,2},{24,20},{25,21},{26,22},{2... | collective-permute-start | bytes 442376 | tf_op jit(solution)/shard_map/ppermute | solution.py:418
  40.1 16.5 %collective-permute-done.2.arriving = bf16[192,384]{1,0:T(8,128)(2,1)S(1)} collective-permute-done((bf16[192,384]{1,0:T(8,128)(2,1)S(1)}, bf16[192,384]{1,0:T(8,128)(2,1)S(1)}, u32[]{:S(2)}, u32[]{:S(2)}) %collective-permute-start.2) | collective-permute-done | bytes 147488 | tf_op jit(solution)/shard_map/ppermute | solution.py:418
  56.6 5.0 %backward.1 = (bf16[192,384]{1,0:T(8,128)(2,1)}, bf16[8,192,384]{2,1,0:T(8,128)(2,1)S(1)}) custom-call(bf16[192,384]{1,0:T(8,128)(2,1)S(1)} %collective-permute-done.2.arriving, bf16[9,192,384]{2,1,0:T(8,128)(2,1)S(1)} %get-tuple-element.22.waves, bf16[8,208,384]{2,1,0:T(8,128)(2,1)S(1)} %all_to_all.10.blocks.refs_1_, ...), custom_call_target="tpu_custom_call" | custom-call | flops 905969664 | bytes 7028736 | tf_op jit(solution)/shard_map/backward/pallas_call | solution.py:448
  61.6 0.0 copy-start.3
  61.6 21.6 %all_to_all.11.grads_ref = bf16[8,192,384]{2,1,0:T(8,128)(2,1)S(1)} all-to-all(bf16[8,192,384]{2,1,0:T(8,128)(2,1)S(1)} %get-tuple-element.32), channel_id=1, replica_groups={{0,1,2,3,4,5,6,7},{8,9,10,11,12,13,14,15},{16,17,18,19,20,21,22,23},{24..., dimensions={0} | all-to-all | bytes 2359296 | tf_op jit(solution)/shard_map/all_to_all | solution.py:413
  83.2 0.0 copy-done.3
  83.2 3.2 %sum_windows.1 = f32[1,2,384,384]{3,2,1,0:T(8,128)} custom-call(s32[2,6]{1,0:T(2,128)S(1)} %bitcast.2, bf16[8,192,384]{2,1,0:T(8,128)(2,1)S(1)} %all_to_all.11.grads_ref), custom_call_target="tpu_custom_call" | custom-call | tf_op jit(solution)/shard_map/sum_windows/pallas_call | solution.py:511
  (1 shorter events, 0.0 us)
Async XLA Ops:
  0.7 27.4 %copy-start.2 = (f32[2,192,192]{2,1,0:T(8,128)S(1)}, f32[2,192,192]{2,1,0:T(8,128)}, u32[]{:S(2)}) copy-start(f32[2,192,192]{2,1,0:T(8,128)} %constant.2.clone.dft) | copy-start | bytes 884740
  5.4 22.7 %copy-start = (bf16[4,2,192,192]{3,2,1,0:T(8,128)(2,1)S(1)}, bf16[4,2,192,192]{3,2,1,0:T(8,128)(2,1)}, u32[]{:S(2)}) copy-start(bf16[4,2,192,192]{3,2,1,0:T(8,128)(2,1)} %refs_2_.1) | copy-start | bytes 1769476
  5.4 22.7 %copy-start.1 = (bf16[8,2,192,192]{3,2,1,0:T(8,128)(2,1)S(1)}, bf16[8,2,192,192]{3,2,1,0:T(8,128)(2,1)}, u32[]{:S(2)}) copy-start(bf16[8,2,192,192]{3,2,1,0:T(8,128)(2,1)} %probes.1) | copy-start | bytes 3538948
  5.4 22.7 %copy-start.4 = (s32[6]{0:T(128)S(1)}, s32[6]{0:T(128)}, u32[]{:S(2)}) copy-start(s32[6]{0:T(128)} %group_ref.1) | copy-start | bytes 76
  33.6 4.0 %collective-permute-start = (bf16[192,384]{1,0:T(8,128)(2,1)S(1)}, bf16[192,384]{1,0:T(8,128)(2,1)S(1)}, u32[]{:S(2)}, u32[]{:S(2)}) collective-permute-start(bf16[192,384]{1,0:T(8,128)(2,1)S(1)} %get-tuple-element.19._), channel_id=1, source_target_pairs={{4,8},{5,9},{6,10},{7,11},{0,12},{2,14},{20,24},{21,25},{22,26},{2... | collective-permute-start | bytes 442376 | tf_op jit(solution)/shard_map/ppermute | solution.py:418
  34.9 3.4 %collective-permute-start.1 = (bf16[96,256]{1,0:T(8,128)(2,1)S(1)}, bf16[96,256]{1,0:T(8,128)(2,1)S(1)}, u32[]{:S(2)}, u32[]{:S(2)}) collective-permute-start(bf16[96,256]{1,0:T(8,128)(2,1)S(1)} %near_rows.1), channel_id=1, source_target_pairs={{4,8},{5,9},{6,10},{7,11},{0,12},{2,14},{20,24},{21,25},{22,26},{2... | collective-permute-start | bytes 147464 | tf_op jit(solution)/shard_map/ppermute | solution.py:418
  38.8 17.8 %collective-permute-start.2 = (bf16[192,384]{1,0:T(8,128)(2,1)S(1)}, bf16[192,384]{1,0:T(8,128)(2,1)S(1)}, u32[]{:S(2)}, u32[]{:S(2)}) collective-permute-start(bf16[192,384]{1,0:T(8,128)(2,1)S(1)} %get-tuple-element.28), channel_id=1, source_target_pairs={{8,4},{9,5},{10,6},{11,7},{12,0},{14,2},{24,20},{25,21},{26,22},{2... | collective-permute-start | bytes 442376 | tf_op jit(solution)/shard_map/ppermute | solution.py:418
  61.6 21.6 %copy-start.3 = (s32[6,2]{0,1:T(2,128)S(1)}, s32[6,2]{0,1:T(2,128)}, u32[]{:S(2)}) copy-start(s32[6,2]{0,1:T(2,128)} %param.13) | copy-start | bytes 148

commit v13 on v12

--- a/solution.py
+++ b/solution.py
@@ -62,14 +62,19 @@
     return jnp.concatenate([a0 * b0 + a1 * b1, a1 * b0 - a0 * b1, tail], axis=1)
 
 
-def joined(both, conj):
-    width = both.shape[0] // 2
-    u0, u1, ut = halves(both[:width])
-    v0, v1, vt = halves(both[width:])
+def left_product(table, x, conj):
+    width = x.shape[0]
+    u0, u1, ut = halves(dot(table[:width], x))
+    v0, v1, vt = halves(dot(table[width:], x))
     turned = signed(swapped(vt), not conj)
     if conj:
         return jnp.concatenate([u0 + v1, u1 - v0, ut + turned], axis=1)
     return jnp.concatenate([u0 - v1, u1 + v0, ut + turned], axis=1)
+
+
+def right_product(x, table):
+    half = x.shape[0] // 2
+    return jnp.concatenate([dot(x[:half], table), dot(x[half:], table)], axis=0)
 
 
 def with_mean(window):
@@ -84,11 +89,15 @@
     return high, (x - high.astype(F32)).astype(BF16)
 
 
-def picker(shape, start):
+def picker(shape, start, high_tail=False):
     columns, across = (0, 1) if shape[0] > shape[1] else (1, 0)
+    half = LANES // 2
     taken = lax.broadcasted_iota(jnp.int32, shape, columns) - start
     place = lax.broadcasted_iota(jnp.int32, shape, across)
-    wanted = jnp.where(place < LANES + LANES // 2, place, -shape[columns])
+    if high_tail:
+        wanted = jnp.where(place < LANES, place, jnp.where(place < LANES + half, -shape[columns], place - half))
+    else:
+        wanted = jnp.where(place < LANES + half, place, -shape[columns])
     return jnp.where(taken == wanted, 1.0, 0.0).astype(BF16)
 
 
@@ -152,10 +161,11 @@
     sending = []
     for p, slot in enumerate(slots_of(positions, size)):
         start = offsets_ref[0, p]
-        both = jnp.concatenate([rows_near(objects[c], start, width) for c in range(2)], axis=0)
-        picked = dot(both, picker((extent, 2 * LANES), offsets_ref[1, p]))
-        real, imag = picked[: width + ROWS], picked[width + ROWS :]
-        tail = jnp.where(low_half(width + ROWS), real[:, LANES:], swapped(imag[:, LANES:]))
+        real, imag = (
+            dot(rows_near(objects[c], start, width), picker((extent, 2 * LANES), offsets_ref[1, p], c == 1))
+            for c in range(2)
+        )
+        tail = real[:, LANES:] + imag[:, LANES:]
         window = jnp.concatenate([real[:, :LANES], imag[:, :LANES], tail], axis=1).astype(BF16)
         shift = lax.bitwise_and(start, ROWS - 1)
         blocks[p, :width, :] = dot(row_picker((width, width + ROWS), shift), window).astype(BF16)
@@ -208,10 +218,10 @@
     for k in range(sections):
         which = indices[k]
         z = times(psi.astype(F32), parts).astype(BF16)
-        h = joined(dot(lf[which].reshape(columns, width), z), False).astype(BF16)
+        h = left_product(lf[which].reshape(columns, width), z, False).astype(BF16)
         if k + 1 < sections:
             parts = factor(with_mean(blocks[k + 1, :width, :]))
-        psi = dot(h, rf[which]).astype(BF16)
+        psi = right_product(h, rf[which]).astype(BF16)
         waves[k + 1] = psi
 
 
@@ -225,13 +235,12 @@
     late = None
     for k in reversed(range(sections)):
         which = indices[k]
-        both = dot(lb[which], g)
+        c = left_product(lb[which], g, True).astype(BF16)
         if late is not None:
             leave(*late)
-        c = joined(both, True).astype(BF16)
         wave_parts = factor(waves[k].astype(F32))
         window_parts = factor(with_mean(blocks[k, :width, :]))
-        y = dot(c, rb[which])
+        y = right_product(c, rb[which])
         turned = signed(swapped(halves(y)[2]), False)
         g = times_conj(y, turned, window_parts).astype(BF16)
         late = (k, y, turned, wave_parts)
@@ -243,14 +252,14 @@
     def product(ah, al, bh, bl):
         return dot(ah, bh) + (dot(ah, bl) + dot(al, bh))
 
-    near = joined(dot(left[0], psi) + dot(left[1], psi), False)
+    near = left_product(left[0], psi, False) + left_product(left[1], psi, False)
     far = product(*split2(near), right[0], right[1])
     f0, f1, ft = halves(far)
     other = swapped(ft)
     main = f0 * f0 + f1 * f1 - observed[:, :LANES]
     tail = ft * ft + other * other - observed[:, LANES:]
     push = jnp.concatenate([main * f0, main * f1, tail * ft], axis=1)
-    back = joined(dot(left[0], push.astype(BF16)), True)
+    back = left_product(left[0], push.astype(BF16), True)
     return dot(back.astype(BF16), right_conj[...]).astype(BF16)
 
 

time: 86.8 us -> 86.6 us (level)
  no operation moved by 1% of the time
where the time goes in v13:
time: 86.6 us; the launch traced here: 86.3 us
  blocking collectives  44.2 us (51%)
  Pallas kernels  19.1 us (22%)
  waiting for transfers between devices  18.1 us (21%)
  starting transfers between devices  3.88 us (4%)
  between operations  0.91 us (1%)
    all_to_all x2, blocking collectives, exchanged(): lax.all_to_all(blocks, 'cuts', 0, 0, axis_index_groups=members, tiled=True)  44.2 us
    ppermute x3, waiting for transfers between devices, handed(): return lax.ppermute(block, 'cuts', route)  18.1 us
    pallas_call x5, Pallas kernels, call(): pl.pallas_call(kernel, out_shape=out_shape, in_specs=in_specs, out_specs=...  11.9 us
    pallas_call x1, Pallas kernels, shards(): pl.pallas_call(window_kernel, out_shape=struct(size, rows, 2 * width), in...  3.98 us
    ppermute x3, starting transfers between devices, handed(): return lax.ppermute(block, 'cuts', route)  3.88 us
    pallas_call x1, Pallas kernels, shards(): pl.pallas_call(gather_kernel, out_shape=jax.ShapeDtypeStruct(objects.shap...  3.16 us
  transfers between devices with their start and end apart: 3, of which 2 were waited for; matrix products, arithmetic and copies ran while one was open for 0% of the time, Pallas kernels for 1%

profile of v13, /device:TPU:0, one launch (start us, length us, event | category | flops | bytes accessed | tf_op | source)
XLA Modules:
  0.0 86.3 jit_solution(18099474075932715269)
XLA Ops:
  0.7 0.0 copy-start.2
  0.7 4.0 %windows.1 = bf16[8,208,384]{2,1,0:T(8,128)(2,1)} custom-call(s32[2,6]{1,0:T(2,128)} %bitcast.1, s32[1]{0:T(128)S(6)} %copy.9.index_ref, bf16[1,2,384,384]{3,2,1,0:T(8,128)(2,1)} %objects_in.1, f32[6,12,192]{2,1,0:T(8,128)} %measured_in.1), custom_call_target="tpu_custom_call" | custom-call | tf_op jit(solution)/shard_map/windows/pallas_call | solution.py:429
  4.7 0.0 copy-start
  4.7 0.0 copy-start.1
  4.7 0.0 copy-start.4
  4.7 22.6 %all_to_all.10.blocks.refs_1_ = bf16[8,208,384]{2,1,0:T(8,128)(2,1)S(1)} all-to-all(bf16[8,208,384]{2,1,0:T(8,128)(2,1)} %windows.1), channel_id=1, replica_groups={{0,1,2,3,4,5,6,7},{8,9,10,11,12,13,14,15},{16,17,18,19,20,21,22,23},{24..., dimensions={0} | all-to-all | bytes 2555904 | tf_op jit(solution)/shard_map/all_to_all | solution.py:422
  27.3 0.0 copy-done.2
  27.3 0.0 copy-done
  27.3 0.0 copy-done.1
  27.3 0.0 copy-done.4
  27.3 5.6 %first_forward.1 = (bf16[192,384]{1,0:T(8,128)(2,1)S(1)}, bf16[9,192,384]{2,1,0:T(8,128)(2,1)S(1)}, bf16[4,384,192]{2,1,0:T(8,128)(2,1)S(1)}, bf16[4,384,384]{2,...) custom-call(s32[6]{0:T(128)S(1)} %copy-done.4, ...), custom_call_target="tpu_custom_call" | custom-call | flops 905969664 | bytes 8945688 | tf_op jit(solution)/shard_map/first_forward/pallas_call | solution.py:457
  33.0 1.3 %collective-permute-start = (bf16[192,384]{1,0:T(8,128)(2,1)S(1)}, bf16[192,384]{1,0:T(8,128)(2,1)S(1)}, u32[]{:S(2)}, u32[]{:S(2)}) collective-permute-start(bf16[192,384]{1,0:T(8,128)(2,1)S(1)} %get-tuple-element.19._), channel_id=1, source_target_pairs={{4,8},{5,9},{6,10},{7,11},{0,12},{2,14},{20,24},{21,25},{22,26},{2... | collective-permute-start | bytes 442376 | tf_op jit(solution)/shard_map/ppermute | solution.py:427
  34.3 1.3 %collective-permute-start.1 = (bf16[96,256]{1,0:T(8,128)(2,1)S(1)}, bf16[96,256]{1,0:T(8,128)(2,1)S(1)}, u32[]{:S(2)}, u32[]{:S(2)}) collective-permute-start(bf16[96,256]{1,0:T(8,128)(2,1)S(1)} %near_rows.1), channel_id=1, source_target_pairs={{4,8},{5,9},{6,10},{7,11},{0,12},{2,14},{20,24},{21,25},{22,26},{2... | collective-permute-start | bytes 147464 | tf_op jit(solution)/shard_map/ppermute | solution.py:427
  35.6 1.4 %collective-permute-done.entering = bf16[192,384]{1,0:T(8,128)(2,1)S(1)} collective-permute-done((bf16[192,384]{1,0:T(8,128)(2,1)S(1)}, bf16[192,384]{1,0:T(8,128)(2,1)S(1)}, u32[]{:S(2)}, u32[]{:S(2)}) %collective-permute-start) | collective-permute-done | bytes 147488 | tf_op jit(solution)/shard_map/ppermute | solution.py:427
  37.0 0.8 forward.1
  37.8 0.0 collective-permute-done.1.refs_0_
  37.8 0.4 middle.1
  38.2 1.3 %collective-permute-start.2 = (bf16[192,384]{1,0:T(8,128)(2,1)S(1)}, bf16[192,384]{1,0:T(8,128)(2,1)S(1)}, u32[]{:S(2)}, u32[]{:S(2)}) collective-permute-start(bf16[192,384]{1,0:T(8,128)(2,1)S(1)} %get-tuple-element.28), channel_id=1, source_target_pairs={{8,4},{9,5},{10,6},{11,7},{12,0},{14,2},{24,20},{25,21},{26,22},{2... | collective-permute-start | bytes 442376 | tf_op jit(solution)/shard_map/ppermute | solution.py:427
  39.5 16.8 %collective-permute-done.2.arriving = bf16[192,384]{1,0:T(8,128)(2,1)S(1)} collective-permute-done((bf16[192,384]{1,0:T(8,128)(2,1)S(1)}, bf16[192,384]{1,0:T(8,128)(2,1)S(1)}, u32[]{:S(2)}, u32[]{:S(2)}) %collective-permute-start.2) | collective-permute-done | bytes 147488 | tf_op jit(solution)/shard_map/ppermute | solution.py:427
  56.3 5.1 %backward.1 = (bf16[192,384]{1,0:T(8,128)(2,1)}, bf16[8,192,384]{2,1,0:T(8,128)(2,1)S(1)}) custom-call(bf16[192,384]{1,0:T(8,128)(2,1)S(1)} %collective-permute-done.2.arriving, bf16[9,192,384]{2,1,0:T(8,128)(2,1)S(1)} %get-tuple-element.22.waves, bf16[8,208,384]{2,1,0:T(8,128)(2,1)S(1)} %all_to_all.10.blocks.refs_1_, ...), custom_call_target="tpu_custom_call" | custom-call | flops 905969664 | bytes 7028736 | tf_op jit(solution)/shard_map/backward/pallas_call | solution.py:457
  61.4 0.0 copy-start.3
  61.4 21.6 %all_to_all.11.grads_ref = bf16[8,192,384]{2,1,0:T(8,128)(2,1)S(1)} all-to-all(bf16[8,192,384]{2,1,0:T(8,128)(2,1)S(1)} %get-tuple-element.32), channel_id=1, replica_groups={{0,1,2,3,4,5,6,7},{8,9,10,11,12,13,14,15},{16,17,18,19,20,21,22,23},{24..., dimensions={0} | all-to-all | bytes 2359296 | tf_op jit(solution)/shard_map/all_to_all | solution.py:422
  83.0 0.0 copy-done.3
  83.0 3.2 %sum_windows.1 = f32[1,2,384,384]{3,2,1,0:T(8,128)} custom-call(s32[2,6]{1,0:T(2,128)S(1)} %bitcast.2, bf16[8,192,384]{2,1,0:T(8,128)(2,1)S(1)} %all_to_all.11.grads_ref), custom_call_target="tpu_custom_call" | custom-call | tf_op jit(solution)/shard_map/sum_windows/pallas_call | solution.py:520
  (1 shorter events, 0.0 us)
Async XLA Ops:
  0.7 26.7 %copy-start.2 = (f32[2,192,192]{2,1,0:T(8,128)S(1)}, f32[2,192,192]{2,1,0:T(8,128)}, u32[]{:S(2)}) copy-start(f32[2,192,192]{2,1,0:T(8,128)} %constant.2.clone.dft) | copy-start | bytes 884740
  4.7 22.7 %copy-start = (bf16[4,2,192,192]{3,2,1,0:T(8,128)(2,1)S(1)}, bf16[4,2,192,192]{3,2,1,0:T(8,128)(2,1)}, u32[]{:S(2)}) copy-start(bf16[4,2,192,192]{3,2,1,0:T(8,128)(2,1)} %refs_2_.1) | copy-start | bytes 1769476
  4.7 22.7 %copy-start.1 = (bf16[8,2,192,192]{3,2,1,0:T(8,128)(2,1)S(1)}, bf16[8,2,192,192]{3,2,1,0:T(8,128)(2,1)}, u32[]{:S(2)}) copy-start(bf16[8,2,192,192]{3,2,1,0:T(8,128)(2,1)} %probes.1) | copy-start | bytes 3538948
  4.7 22.7 %copy-start.4 = (s32[6]{0:T(128)S(1)}, s32[6]{0:T(128)}, u32[]{:S(2)}) copy-start(s32[6]{0:T(128)} %group_ref.1) | copy-start | bytes 76
  33.0 4.0 %collective-permute-start = (bf16[192,384]{1,0:T(8,128)(2,1)S(1)}, bf16[192,384]{1,0:T(8,128)(2,1)S(1)}, u32[]{:S(2)}, u32[]{:S(2)}) collective-permute-start(bf16[192,384]{1,0:T(8,128)(2,1)S(1)} %get-tuple-element.19._), channel_id=1, source_target_pairs={{4,8},{5,9},{6,10},{7,11},{0,12},{2,14},{20,24},{21,25},{22,26},{2... | collective-permute-start | bytes 442376 | tf_op jit(solution)/shard_map/ppermute | solution.py:427
  34.3 3.4 %collective-permute-start.1 = (bf16[96,256]{1,0:T(8,128)(2,1)S(1)}, bf16[96,256]{1,0:T(8,128)(2,1)S(1)}, u32[]{:S(2)}, u32[]{:S(2)}) collective-permute-start(bf16[96,256]{1,0:T(8,128)(2,1)S(1)} %near_rows.1), channel_id=1, source_target_pairs={{4,8},{5,9},{6,10},{7,11},{0,12},{2,14},{20,24},{21,25},{22,26},{2... | collective-permute-start | bytes 147464 | tf_op jit(solution)/shard_map/ppermute | solution.py:427
  38.2 18.1 %collective-permute-start.2 = (bf16[192,384]{1,0:T(8,128)(2,1)S(1)}, bf16[192,384]{1,0:T(8,128)(2,1)S(1)}, u32[]{:S(2)}, u32[]{:S(2)}) collective-permute-start(bf16[192,384]{1,0:T(8,128)(2,1)S(1)} %get-tuple-element.28), channel_id=1, source_target_pairs={{8,4},{9,5},{10,6},{11,7},{12,0},{14,2},{24,20},{25,21},{26,22},{2... | collective-permute-start | bytes 442376 | tf_op jit(solution)/shard_map/ppermute | solution.py:427
  61.4 21.6 %copy-start.3 = (s32[6,2]{0,1:T(2,128)S(1)}, s32[6,2]{0,1:T(2,128)}, u32[]{:S(2)}) copy-start(s32[6,2]{0,1:T(2,128)} %param.13) | copy-start | bytes 148

commit v14 on v13

--- a/solution.py
+++ b/solution.py
@@ -48,33 +48,46 @@
     return (b0, b1) + spread(bt)
 
 
-def times(a, parts):
+def upright(real, real_tail, imag, imag_tail):
+    return jnp.concatenate(
+        [jnp.concatenate([real, real_tail], axis=1), jnp.concatenate([imag, imag_tail], axis=1)], axis=0
+    ).astype(BF16)
+
+
+def from_upright(x):
+    width = x.shape[0] // 2
+    real, imag = x[:width], x[width:]
+    tail = jnp.where(low_half(width), real[:, LANES:], swapped(imag[:, LANES:]))
+    return jnp.concatenate([real[:, :LANES], imag[:, :LANES], tail], axis=1)
+
+
+def to_upright(x):
+    x0, x1, xt = halves(x)
+    return upright(x0, xt, x1, swapped(xt))
+
+
+def times_upright(a, parts):
     a0, a1, at = halves(a)
     b0, b1, b_real, b_imag = parts
-    tail = at * b_real + signed(swapped(at), True) * b_imag
-    return jnp.concatenate([a0 * b0 - a1 * b1, a1 * b0 + a0 * b1, tail], axis=1)
-
-
-def times_conj(a, turned, parts):
+    other = swapped(at)
+    return upright(
+        a0 * b0 - a1 * b1, at * b_real - other * b_imag, a1 * b0 + a0 * b1, other * b_real + at * b_imag
+    )
+
+
+def times_conj_upright(a, other, parts):
     a0, a1, at = halves(a)
     b0, b1, b_real, b_imag = parts
-    tail = at * b_real + turned * b_imag
+    return upright(
+        a0 * b0 + a1 * b1, at * b_real + other * b_imag, a1 * b0 - a0 * b1, other * b_real - at * b_imag
+    )
+
+
+def times_conj(a, other, parts):
+    a0, a1, at = halves(a)
+    b0, b1, b_real, b_imag = parts
+    tail = at * b_real + signed(other, False) * b_imag
     return jnp.concatenate([a0 * b0 + a1 * b1, a1 * b0 - a0 * b1, tail], axis=1)
-
-
-def left_product(table, x, conj):
-    width = x.shape[0]
-    u0, u1, ut = halves(dot(table[:width], x))
-    v0, v1, vt = halves(dot(table[width:], x))
-    turned = signed(swapped(vt), not conj)
-    if conj:
-        return jnp.concatenate([u0 + v1, u1 - v0, ut + turned], axis=1)
-    return jnp.concatenate([u0 - v1, u1 + v0, ut + turned], axis=1)
-
-
-def right_product(x, table):
-    half = x.shape[0] // 2
-    return jnp.concatenate([dot(x[:half], table), dot(x[half:], table)], axis=0)
 
 
 def with_mean(window):
@@ -185,82 +198,75 @@
     return jnp.concatenate([upper[:LANES], lower[:LANES], upper[LANES:], lower[LANES:]], axis=0).astype(BF16)
 
 
-def forward_tables(props, rf):
-    for k in range(props.shape[0]):
-        rf[k] = right_table(props[k, 0].astype(F32).T, props[k, 1].astype(F32).T)
-
-
-def backward_tables(props, lb, rb):
-    width = props.shape[-1]
+def left_table(real, imag):
+    return jnp.concatenate(
+        [jnp.concatenate([real, -imag], axis=1), jnp.concatenate([imag, real], axis=1)], axis=0
+    ).astype(BF16)
+
+
+def forward_tables(props, lf, rf):
     for k in range(props.shape[0]):
         real, imag = props[k, 0].astype(F32), props[k, 1].astype(F32)
-        lb[k, :width, :] = real.T.astype(BF16)
-        lb[k, width:, :] = imag.T.astype(BF16)
+        lf[k] = left_table(real, imag)
+        rf[k] = right_table(real.T, imag.T)
+
+
+def backward_tables(props, lb, rb):
+    for k in range(props.shape[0]):
+        real, imag = props[k, 0].astype(F32), props[k, 1].astype(F32)
+        lb[k] = left_table(real.T, -imag.T)
         rb[k] = right_table(real, -imag)
 
 
-def detector_tables(dft, left, right, right_conj):
-    width = dft.shape[-1]
+def detector_tables(dft, left, right):
     for n, (real, imag) in enumerate(zip(split2(dft[0]), split2(dft[1]))):
-        left[n, :width, :] = real
-        left[n, width:, :] = imag
         real, imag = real.astype(F32), imag.astype(F32)
+        left[n] = left_table(real, imag)
         right[n] = right_table(real, imag)
         if n == 0:
-            right_conj[...] = right_table(real, -imag)
+            left[2] = left_table(real, -imag)
+            right[2] = right_table(real, -imag)
 
 
 def forward_steps(blocks, waves, indices, lf, rf):
     sections, _, columns = blocks.shape
     width = columns // 2
     psi = waves[0]
-    parts = factor(with_mean(blocks[0, :width, :]))
     for k in range(sections):
         which = indices[k]
-        z = times(psi.astype(F32), parts).astype(BF16)
-        h = left_product(lf[which].reshape(columns, width), z, False).astype(BF16)
-        if k + 1 < sections:
-            parts = factor(with_mean(blocks[k + 1, :width, :]))
-        psi = right_product(h, rf[which]).astype(BF16)
+        z = times_upright(psi.astype(F32), factor(with_mean(blocks[k, :width, :])))
+        h = from_upright(dot(lf[which], z)).astype(BF16)
+        psi = dot(h, rf[which]).astype(BF16)
         waves[k + 1] = psi
 
 
 def backward_steps(blocks, waves, indices, lb, rb, grads, g):
     sections, _, columns = blocks.shape
     width = columns // 2
-
-    def leave(k, y, turned, wave_parts):
-        grads[k] = times_conj(y, turned, wave_parts).astype(BF16)
-
-    late = None
     for k in reversed(range(sections)):
         which = indices[k]
-        c = left_product(lb[which], g, True).astype(BF16)
-        if late is not None:
-            leave(*late)
-        wave_parts = factor(waves[k].astype(F32))
-        window_parts = factor(with_mean(blocks[k, :width, :]))
-        y = right_product(c, rb[which])
-        turned = signed(swapped(halves(y)[2]), False)
-        g = times_conj(y, turned, window_parts).astype(BF16)
-        late = (k, y, turned, wave_parts)
-    leave(*late)
-    return g
-
-
-def detector(psi, observed, left, right, right_conj):
+        c = from_upright(dot(lb[which], g)).astype(BF16)
+        y = dot(c, rb[which])
+        other = swapped(halves(y)[2])
+        g = times_conj_upright(y, other, factor(with_mean(blocks[k, :width, :])))
+        grads[k] = times_conj(y, other, factor(waves[k].astype(F32))).astype(BF16)
+    return from_upright(g.astype(F32)).astype(BF16)
+
+
+def detector(psi, observed, left, right):
     def product(ah, al, bh, bl):
         return dot(ah, bh) + (dot(ah, bl) + dot(al, bh))
 
-    near = left_product(left[0], psi, False) + left_product(left[1], psi, False)
+    psi = to_upright(psi.astype(F32))
+    near = from_upright(dot(left[0], psi) + dot(left[1], psi))
     far = product(*split2(near), right[0], right[1])
     f0, f1, ft = halves(far)
     other = swapped(ft)
     main = f0 * f0 + f1 * f1 - observed[:, :LANES]
     tail = ft * ft + other * other - observed[:, LANES:]
-    push = jnp.concatenate([main * f0, main * f1, tail * ft], axis=1)
-    back = left_product(left[0], push.astype(BF16), True)
-    return dot(back.astype(BF16), right_conj[...]).astype(BF16)
+    push = upright(main * f0, tail * ft, main * f1, tail * other)
+    back = from_upright(dot(left[2], push)).astype(BF16)
+    return to_upright(dot(back, right[2]))
 
 
 def read_indices(blocks, indices, count):
@@ -285,7 +291,7 @@
     near[...] = observed[...].astype(BF16)
 
 
-def first_kernel(group_ref, probes, blocks, props, dft, leaving, waves, lb, rf, rb, left, right, right_conj, probe, indices, sem):
+def first_kernel(group_ref, probes, blocks, props, dft, leaving, waves, lf, rf, lb, rb, left, right, probe, indices, sem):
     size = blocks.shape[0]
     slot, group = place_in(size)
 
@@ -297,30 +303,30 @@
         which = group_ref[position]
         copy = pltpu.make_async_copy(probes.at[which], probe, sem)
         copy.start()
-        forward_tables(props, rf)
+        forward_tables(props, lf, rf)
         read_indices(blocks, indices, props.shape[0])
         copy.wait()
         waves[0] = packed(probe[0].astype(F32), probe[1].astype(F32)).astype(BF16)
-        forward_steps(blocks, waves, indices, props, rf)
+        forward_steps(blocks, waves, indices, lf, rf)
         leaving[...] = waves[size]
 
     @pl.when(group > 0)
     def _():
-        forward_tables(props, rf)
+        forward_tables(props, lf, rf)
         backward_tables(props, lb, rb)
-        detector_tables(dft, left, right, right_conj)
+        detector_tables(dft, left, right)
 
 
 def forward_kernel(stage):
-    def kernel(entering, blocks, props, rf, waves_in, leaving, waves, indices):
+    def kernel(entering, blocks, lf, rf, waves_in, leaving, waves, indices):
         size = blocks.shape[0]
         _, group = place_in(size)
 
         @pl.when(group == stage)
         def _():
-            read_indices(blocks, indices, props.shape[0])
+            read_indices(blocks, indices, lf.shape[0])
             waves[0] = entering[...]
-            forward_steps(blocks, waves, indices, props, rf)
+            forward_steps(blocks, waves, indices, lf, rf)
             leaving[...] = waves[size]
 
         @pl.when(group != stage)
@@ -333,7 +339,7 @@
 def middle_kernel(groups):
     def kernel(waves, *refs):
         earlier, refs = refs[: groups - 1], refs[groups - 1 :]
-        blocks, props, lb, rb, left, right, right_conj, leaving, grads, lb_out, rb_out, observed, indices = refs
+        blocks, props, lb, rb, left, right, leaving, grads, lb_out, rb_out, observed, indices = refs
         size = blocks.shape[0]
         _, group = place_in(size)
 
@@ -344,7 +350,7 @@
             for n, near in enumerate(earlier):
                 observed[n * rows : (n + 1) * rows, :] = near[...].astype(F32)
             observe(blocks, rows // size, observed, (groups - 1) * rows)
-            g = detector(waves[size], observed[...], left, right, right_conj)
+            g = detector(waves[size], observed[...], left, right)
             leaving[...] = backward_steps(blocks, waves, indices, lb, rb, grads, g)
 
         @pl.when(group < groups - 1)
@@ -361,7 +367,8 @@
         @pl.when(group == stage)
         def _():
             read_indices(blocks, indices, lb.shape[0])
-            leaving[...] = backward_steps(blocks, waves, indices, lb, rb, grads, arriving[...])
+            g = to_upright(arriving[...].astype(F32))
+            leaving[...] = backward_steps(blocks, waves, indices, lb, rb, grads, g)
 
         @pl.when(group != stage)
         def _():
@@ -447,10 +454,8 @@
     near = struct(size * near_rows, 2 * LANES)
     waves_shape = struct(size + 1, width, 2 * width)
     grads_shape = struct(size, width, 2 * width)
-    left_table = struct(kinds, 2 * width, width)
-    square_table = struct(kinds, 2 * width, 2 * width)
-    detector_left = struct(2, 2 * width, width)
-    detector_right = struct(2, 2 * width, 2 * width)
+    table = struct(kinds, 2 * width, 2 * width)
+    detector_table = struct(3, 2 * width, 2 * width)
     indices = pltpu.SMEM((size,), jnp.int32)
 
     def call(kernel, name, out_shape, in_specs, scratch_shapes, operands, slices=0):
@@ -469,11 +474,10 @@
             name=name,
         )(*operands)
 
-    leaving, waves, lb, rf, rb, *dft = call(
+    leaving, waves, lf, rf, lb, rb, *dft = call(
         first_kernel,
         "first_forward",
-        [wave, waves_shape, left_table, square_table, square_table]
-        + [detector_left, detector_right, struct(2 * width, 2 * width)],
+        [wave, waves_shape, table, table, table, table, detector_table, detector_table],
         [SMEM, HBM, VMEM, VMEM, VMEM],
         [pltpu.VMEM(probes.shape[1:], BF16), indices, pltpu.SemaphoreType.DMA],
         (probe_group, probes, blocks, propagators, jnp.asarray(dft_constant(width))),
@@ -489,7 +493,7 @@
             [wave, waves_shape],
             [VMEM] * 5,
             [indices],
-            (entering, blocks, propagators, rf, waves),
+            (entering, blocks, lf, rf, waves),
             size,
         )
         if stage < groups - 1:
@@ -498,8 +502,8 @@
     leaving, grads, lb, rb = call(
         middle_kernel(groups),
         "middle",
-        [wave, grads_shape, left_table, square_table],
-        [VMEM] * (groups + 7),
+        [wave, grads_shape, table, table],
+        [VMEM] * (groups + 6),
         [pltpu.VMEM((width, 2 * LANES), F32), indices],
         (waves, *nears, blocks, propagators, lb, rb, *dft),
         size,

time: 86.6 us -> 92.3 us (1.066)
  Pallas kernels: 19.1 us -> 22 us
  waiting for transfers between devices: 18.1 us -> 20.9 us
    pallas_call x5, Pallas kernels: 11.9 us -> 14.9 us  [call(): pl.pallas_call(kernel, out_shape=out_shape, in_specs=in_specs, out_specs=...]
    ppermute x3, waiting for transfers between devices: 18.1 us -> 20.9 us  [handed(): return lax.ppermute(block, 'cuts', route)]
where the time goes in v14:
time: 92.3 us; the launch traced here: 92 us
  blocking collectives  44.3 us (48%)
  Pallas kernels  22 us (24%)
  waiting for transfers between devices  20.9 us (23%)
  starting transfers between devices  3.88 us (4%)
    all_to_all x2, blocking collectives, exchanged(): lax.all_to_all(blocks, 'cuts', 0, 0, axis_index_groups=members, tiled=True)  44.3 us
    ppermute x3, waiting for transfers between devices, handed(): return lax.ppermute(block, 'cuts', route)  20.9 us
    pallas_call x5, Pallas kernels, call(): pl.pallas_call(kernel, out_shape=out_shape, in_specs=in_specs, out_specs=...  14.9 us
    pallas_call x1, Pallas kernels, shards(): pl.pallas_call(window_kernel, out_shape=struct(size, rows, 2 * width), in...  3.98 us
    ppermute x3, starting transfers between devices, handed(): return lax.ppermute(block, 'cuts', route)  3.88 us
    pallas_call x1, Pallas kernels, shards(): pl.pallas_call(gather_kernel, out_shape=jax.ShapeDtypeStruct(objects.shap...  3.16 us
  transfers between devices with their start and end apart: 3, of which 2 were waited for; matrix products, arithmetic and copies ran while one was open for 0% of the time, Pallas kernels for 1%

profile of v14, /device:TPU:0, one launch (start us, length us, event | category | flops | bytes accessed | tf_op | source)
XLA Modules:
  0.0 92.0 jit_solution(1361898789095086970)
XLA Ops:
  0.7 0.0 copy-start.2
  0.7 4.0 %windows.1 = bf16[8,208,384]{2,1,0:T(8,128)(2,1)} custom-call(s32[2,6]{1,0:T(2,128)} %bitcast.1, s32[1]{0:T(128)S(6)} %copy.9.index_ref, bf16[1,2,384,384]{3,2,1,0:T(8,128)(2,1)} %objects_in.1, f32[6,12,192]{2,1,0:T(8,128)} %measured_in.1), custom_call_target="tpu_custom_call" | custom-call | tf_op jit(solution)/shard_map/windows/pallas_call | solution.py:436
  4.7 0.0 copy-start
  4.7 0.0 copy-start.1
  4.7 0.0 copy-start.4
  4.7 22.6 %all_to_all.10.blocks.refs_1_ = bf16[8,208,384]{2,1,0:T(8,128)(2,1)S(1)} all-to-all(bf16[8,208,384]{2,1,0:T(8,128)(2,1)} %windows.1), channel_id=1, replica_groups={{0,1,2,3,4,5,6,7},{8,9,10,11,12,13,14,15},{16,17,18,19,20,21,22,23},{24..., dimensions={0} | all-to-all | bytes 2555904 | tf_op jit(solution)/shard_map/all_to_all | solution.py:429
  27.3 0.0 copy-done.2
  27.3 0.0 copy-done
  27.3 0.0 copy-done.1
  27.3 0.0 copy-done.4
  27.3 7.1 %first_forward.1 = (bf16[192,384]{1,0:T(8,128)(2,1)S(1)}, bf16[9,192,384]{2,1,0:T(8,128)(2,1)S(1)}, bf16[4,384,384]{2,1,0:T(8,128)(2,1)S(1)}, bf16[4,384,384]{2,...) custom-call(s32[6]{0:T(128)S(1)} %copy-done.4, ...), custom_call_target="tpu_custom_call" | custom-call | flops 905969664 | bytes 11304984 | tf_op jit(solution)/shard_map/first_forward/pallas_call | solution.py:462
  34.5 1.3 %collective-permute-start = (bf16[192,384]{1,0:T(8,128)(2,1)S(1)}, bf16[192,384]{1,0:T(8,128)(2,1)S(1)}, u32[]{:S(2)}, u32[]{:S(2)}) collective-permute-start(bf16[192,384]{1,0:T(8,128)(2,1)S(1)} %get-tuple-element.19._), channel_id=1, source_target_pairs={{4,8},{5,9},{6,10},{7,11},{0,12},{2,14},{20,24},{21,25},{22,26},{2... | collective-permute-start | bytes 442376 | tf_op jit(solution)/shard_map/ppermute | solution.py:434
  35.8 1.3 %collective-permute-start.1 = (bf16[96,256]{1,0:T(8,128)(2,1)S(1)}, bf16[96,256]{1,0:T(8,128)(2,1)S(1)}, u32[]{:S(2)}, u32[]{:S(2)}) collective-permute-start(bf16[96,256]{1,0:T(8,128)(2,1)S(1)} %near_rows.1), channel_id=1, source_target_pairs={{4,8},{5,9},{6,10},{7,11},{0,12},{2,14},{20,24},{21,25},{22,26},{2... | collective-permute-start | bytes 147464 | tf_op jit(solution)/shard_map/ppermute | solution.py:434
  37.1 1.4 %collective-permute-done.entering = bf16[192,384]{1,0:T(8,128)(2,1)S(1)} collective-permute-done((bf16[192,384]{1,0:T(8,128)(2,1)S(1)}, bf16[192,384]{1,0:T(8,128)(2,1)S(1)}, u32[]{:S(2)}, u32[]{:S(2)}) %collective-permute-start) | collective-permute-done | bytes 147488 | tf_op jit(solution)/shard_map/ppermute | solution.py:434
  38.4 0.8 forward.1
  39.2 0.0 collective-permute-done.1.refs_0_
  39.2 0.7 middle.1
  39.9 1.3 %collective-permute-start.2 = (bf16[192,384]{1,0:T(8,128)(2,1)S(1)}, bf16[192,384]{1,0:T(8,128)(2,1)S(1)}, u32[]{:S(2)}, u32[]{:S(2)}) collective-permute-start(bf16[192,384]{1,0:T(8,128)(2,1)S(1)} %get-tuple-element.28), channel_id=1, source_target_pairs={{8,4},{9,5},{10,6},{11,7},{12,0},{14,2},{24,20},{25,21},{26,22},{2... | collective-permute-start | bytes 442376 | tf_op jit(solution)/shard_map/ppermute | solution.py:434
  41.2 19.6 %collective-permute-done.2.arriving = bf16[192,384]{1,0:T(8,128)(2,1)S(1)} collective-permute-done((bf16[192,384]{1,0:T(8,128)(2,1)S(1)}, bf16[192,384]{1,0:T(8,128)(2,1)S(1)}, u32[]{:S(2)}, u32[]{:S(2)}) %collective-permute-start.2) | collective-permute-done | bytes 147488 | tf_op jit(solution)/shard_map/ppermute | solution.py:434
  60.8 6.3 %backward.1 = (bf16[192,384]{1,0:T(8,128)(2,1)}, bf16[8,192,384]{2,1,0:T(8,128)(2,1)S(1)}) custom-call(bf16[192,384]{1,0:T(8,128)(2,1)S(1)} %collective-permute-done.2.arriving, bf16[9,192,384]{2,1,0:T(8,128)(2,1)S(1)} %get-tuple-element.23.waves, bf16[8,208,384]{2,1,0:T(8,128)(2,1)S(1)} %all_to_all.10.blocks.refs_1_, ...), custom_call_target="tpu_custom_call" | custom-call | flops 905969664 | bytes 7618560 | tf_op jit(solution)/shard_map/backward/pallas_call | solution.py:462
  67.1 0.0 copy-start.3
  67.1 21.6 %all_to_all.11.grads_ref = bf16[8,192,384]{2,1,0:T(8,128)(2,1)S(1)} all-to-all(bf16[8,192,384]{2,1,0:T(8,128)(2,1)S(1)} %get-tuple-element.32), channel_id=1, replica_groups={{0,1,2,3,4,5,6,7},{8,9,10,11,12,13,14,15},{16,17,18,19,20,21,22,23},{24..., dimensions={0} | all-to-all | bytes 2359296 | tf_op jit(solution)/shard_map/all_to_all | solution.py:429
  88.7 0.0 copy-done.3
  88.7 3.2 %sum_windows.1 = f32[1,2,384,384]{3,2,1,0:T(8,128)} custom-call(s32[2,6]{1,0:T(2,128)S(1)} %bitcast.2, bf16[8,192,384]{2,1,0:T(8,128)(2,1)S(1)} %all_to_all.11.grads_ref), custom_call_target="tpu_custom_call" | custom-call | tf_op jit(solution)/shard_map/sum_windows/pallas_call | solution.py:524
  (1 shorter events, 0.0 us)
Async XLA Ops:
  0.7 26.7 %copy-start.2 = (f32[2,192,192]{2,1,0:T(8,128)S(1)}, f32[2,192,192]{2,1,0:T(8,128)}, u32[]{:S(2)}) copy-start(f32[2,192,192]{2,1,0:T(8,128)} %constant.2.clone.dft) | copy-start | bytes 884740
  4.7 22.7 %copy-start = (bf16[4,2,192,192]{3,2,1,0:T(8,128)(2,1)S(1)}, bf16[4,2,192,192]{3,2,1,0:T(8,128)(2,1)}, u32[]{:S(2)}) copy-start(bf16[4,2,192,192]{3,2,1,0:T(8,128)(2,1)} %refs_2_.1) | copy-start | bytes 1769476
  4.7 22.7 %copy-start.1 = (bf16[8,2,192,192]{3,2,1,0:T(8,128)(2,1)S(1)}, bf16[8,2,192,192]{3,2,1,0:T(8,128)(2,1)}, u32[]{:S(2)}) copy-start(bf16[8,2,192,192]{3,2,1,0:T(8,128)(2,1)} %probes.1) | copy-start | bytes 3538948
  4.7 22.7 %copy-start.4 = (s32[6]{0:T(128)S(1)}, s32[6]{0:T(128)}, u32[]{:S(2)}) copy-start(s32[6]{0:T(128)} %group_ref.1) | copy-start | bytes 76
  34.5 4.0 %collective-permute-start = (bf16[192,384]{1,0:T(8,128)(2,1)S(1)}, bf16[192,384]{1,0:T(8,128)(2,1)S(1)}, u32[]{:S(2)}, u32[]{:S(2)}) collective-permute-start(bf16[192,384]{1,0:T(8,128)(2,1)S(1)} %get-tuple-element.19._), channel_id=1, source_target_pairs={{4,8},{5,9},{6,10},{7,11},{0,12},{2,14},{20,24},{21,25},{22,26},{2... | collective-permute-start | bytes 442376 | tf_op jit(solution)/shard_map/ppermute | solution.py:434
  35.8 3.4 %collective-permute-start.1 = (bf16[96,256]{1,0:T(8,128)(2,1)S(1)}, bf16[96,256]{1,0:T(8,128)(2,1)S(1)}, u32[]{:S(2)}, u32[]{:S(2)}) collective-permute-start(bf16[96,256]{1,0:T(8,128)(2,1)S(1)} %near_rows.1), channel_id=1, source_target_pairs={{4,8},{5,9},{6,10},{7,11},{0,12},{2,14},{20,24},{21,25},{22,26},{2... | collective-permute-start | bytes 147464 | tf_op jit(solution)/shard_map/ppermute | solution.py:434
  39.9 20.9 %collective-permute-start.2 = (bf16[192,384]{1,0:T(8,128)(2,1)S(1)}, bf16[192,384]{1,0:T(8,128)(2,1)S(1)}, u32[]{:S(2)}, u32[]{:S(2)}) collective-permute-start(bf16[192,384]{1,0:T(8,128)(2,1)S(1)} %get-tuple-element.28), channel_id=1, source_target_pairs={{8,4},{9,5},{10,6},{11,7},{12,0},{14,2},{24,20},{25,21},{26,22},{2... | collective-permute-start | bytes 442376 | tf_op jit(solution)/shard_map/ppermute | solution.py:434
  67.1 21.6 %copy-start.3 = (s32[6,2]{0,1:T(2,128)S(1)}, s32[6,2]{0,1:T(2,128)}, u32[]{:S(2)}) copy-start(s32[6,2]{0,1:T(2,128)} %param.13) | copy-start | bytes 148

commit v15 on v13

--- a/solution.py
+++ b/solution.py
@@ -64,24 +64,31 @@
 
 def left_product(table, x, conj):
     width = x.shape[0]
-    u0, u1, ut = halves(dot(table[:width], x))
-    v0, v1, vt = halves(dot(table[width:], x))
+    both = dot(table, x)
+    u0, u1, ut = halves(both[:width])
+    v0, v1, vt = halves(both[width:])
     turned = signed(swapped(vt), not conj)
     if conj:
         return jnp.concatenate([u0 + v1, u1 - v0, ut + turned], axis=1)
     return jnp.concatenate([u0 - v1, u1 + v0, ut + turned], axis=1)
 
 
-def right_product(x, table):
-    half = x.shape[0] // 2
-    return jnp.concatenate([dot(x[:half], table), dot(x[half:], table)], axis=0)
-
-
-def with_mean(window):
-    x = window.astype(F32)
-    x0, x1, xt = halves(x)
-    mean = jnp.where(low_half(xt.shape[0]), TRANSMIT, 0.0)
-    return jnp.concatenate([TRANSMIT + x0, x1, mean + xt], axis=1)
+def spread_tails(blocks, tails):
+    size, _, columns = blocks.shape
+    for k in range(size):
+        pair = spread(blocks[k, : columns // 2, 2 * LANES :].astype(F32))
+        tails[k] = jnp.concatenate(pair, axis=1).astype(BF16)
+
+
+def transmission(blocks, tails, k):
+    window = blocks[k, : blocks.shape[2] // 2, :].astype(F32)
+    b0, b1, bt = halves(window)
+    if tails is None:
+        b_real, b_imag = spread(bt)
+    else:
+        pair = tails[k].astype(F32)
+        b_real, b_imag = pair[:, :LANES], pair[:, LANES:]
+    return TRANSMIT + b0, b1, TRANSMIT + b_real, b_imag
 
 
 def split2(x):
@@ -210,22 +217,22 @@
             right_conj[...] = right_table(real, -imag)
 
 
-def forward_steps(blocks, waves, indices, lf, rf):
+def forward_steps(blocks, tails, waves, indices, lf, rf):
     sections, _, columns = blocks.shape
     width = columns // 2
     psi = waves[0]
-    parts = factor(with_mean(blocks[0, :width, :]))
+    parts = transmission(blocks, tails, 0)
     for k in range(sections):
         which = indices[k]
         z = times(psi.astype(F32), parts).astype(BF16)
         h = left_product(lf[which].reshape(columns, width), z, False).astype(BF16)
         if k + 1 < sections:
-            parts = factor(with_mean(blocks[k + 1, :width, :]))
-        psi = right_product(h, rf[which]).astype(BF16)
+            parts = transmission(blocks, tails, k + 1)
+        psi = dot(h, rf[which]).astype(BF16)
         waves[k + 1] = psi
 
 
-def backward_steps(blocks, waves, indices, lb, rb, grads, g):
+def backward_steps(blocks, tails, waves, indices, lb, rb, grads, g):
     sections, _, columns = blocks.shape
     width = columns // 2
 
@@ -239,8 +246,8 @@
         if late is not None:
             leave(*late)
         wave_parts = factor(waves[k].astype(F32))
-        window_parts = factor(with_mean(blocks[k, :width, :]))
-        y = right_product(c, rb[which])
+        window_parts = transmission(blocks, tails, k)
+        y = dot(c, rb[which])
         turned = signed(swapped(halves(y)[2]), False)
         g = times_conj(y, turned, window_parts).astype(BF16)
         late = (k, y, turned, wave_parts)
@@ -285,7 +292,7 @@
     near[...] = observed[...].astype(BF16)
 
 
-def first_kernel(group_ref, probes, blocks, props, dft, leaving, waves, lb, rf, rb, left, right, right_conj, probe, indices, sem):
+def first_kernel(group_ref, probes, blocks, props, dft, leaving, waves, tails, lb, rf, rb, left, right, right_conj, probe, indices, sem):
     size = blocks.shape[0]
     slot, group = place_in(size)
 
@@ -301,18 +308,19 @@
         read_indices(blocks, indices, props.shape[0])
         copy.wait()
         waves[0] = packed(probe[0].astype(F32), probe[1].astype(F32)).astype(BF16)
-        forward_steps(blocks, waves, indices, props, rf)
+        forward_steps(blocks, None, waves, indices, props, rf)
         leaving[...] = waves[size]
 
     @pl.when(group > 0)
     def _():
+        spread_tails(blocks, tails)
         forward_tables(props, rf)
         backward_tables(props, lb, rb)
         detector_tables(dft, left, right, right_conj)
 
 
 def forward_kernel(stage):
-    def kernel(entering, blocks, props, rf, waves_in, leaving, waves, indices):
+    def kernel(entering, blocks, tails, props, rf, waves_in, leaving, waves, first_tails, indices):
         size = blocks.shape[0]
         _, group = place_in(size)
 
@@ -320,12 +328,16 @@
         def _():
             read_indices(blocks, indices, props.shape[0])
             waves[0] = entering[...]
-            forward_steps(blocks, waves, indices, props, rf)
+            forward_steps(blocks, tails, waves, indices, props, rf)
             leaving[...] = waves[size]
 
         @pl.when(group != stage)
         def _():
             waves[...] = waves_in[...]
+
+        @pl.when(group == 0)
+        def _():
+            spread_tails(blocks, first_tails)
 
     return kernel
 
@@ -333,7 +345,7 @@
 def middle_kernel(groups):
     def kernel(waves, *refs):
         earlier, refs = refs[: groups - 1], refs[groups - 1 :]
-        blocks, props, lb, rb, left, right, right_conj, leaving, grads, lb_out, rb_out, observed, indices = refs
+        blocks, tails, props, lb, rb, left, right, right_conj, leaving, grads, lb_out, rb_out, observed, indices = refs
         size = blocks.shape[0]
         _, group = place_in(size)
 
@@ -345,7 +357,7 @@
                 observed[n * rows : (n + 1) * rows, :] = near[...].astype(F32)
             observe(blocks, rows // size, observed, (groups - 1) * rows)
             g = detector(waves[size], observed[...], left, right, right_conj)
-            leaving[...] = backward_steps(blocks, waves, indices, lb, rb, grads, g)
+            leaving[...] = backward_steps(blocks, tails, waves, indices, lb, rb, grads, g)
 
         @pl.when(group < groups - 1)
         def _():
@@ -355,13 +367,13 @@
 
 
 def backward_kernel(stage):
-    def kernel(arriving, waves, blocks, lb, rb, grads_in, leaving, grads, indices):
+    def kernel(arriving, waves, blocks, tails, lb, rb, grads_in, leaving, grads, indices):
         _, group = place_in(blocks.shape[0])
 
         @pl.when(group == stage)
         def _():
             read_indices(blocks, indices, lb.shape[0])
-            leaving[...] = backward_steps(blocks, waves, indices, lb, rb, grads, arriving[...])
+            leaving[...] = backward_steps(blocks, tails, waves, indices, lb, rb, grads, arriving[...])
 
         @pl.when(group != stage)
         def _():
@@ -447,6 +459,7 @@
     near = struct(size * near_rows, 2 * LANES)
     waves_shape = struct(size + 1, width, 2 * width)
     grads_shape = struct(size, width, 2 * width)
+    tails_shape = struct(size, width, 2 * LANES)
     left_table = struct(kinds, 2 * width, width)
     square_table = struct(kinds, 2 * width, 2 * width)
     detector_left = struct(2, 2 * width, width)
@@ -469,10 +482,10 @@
             name=name,
         )(*operands)
 
-    leaving, waves, lb, rf, rb, *dft = call(
+    leaving, waves, tails, lb, rf, rb, *dft = call(
         first_kernel,
         "first_forward",
-        [wave, waves_shape, left_table, square_table, square_table]
+        [wave, waves_shape, tails_shape, left_table, square_table, square_table]
         + [detector_left, detector_right, struct(2 * width, 2 * width)],
         [SMEM, HBM, VMEM, VMEM, VMEM],
         [pltpu.VMEM(probes.shape[1:], BF16), indices, pltpu.SemaphoreType.DMA],
@@ -483,13 +496,13 @@
     (near_out,) = call(near_kernel, "near_rows", [near], [VMEM, HBM], [pltpu.VMEM(near.shape, F32)], (blocks, leaving))
     nears = [handed(near_out, stage, groups - 1 - stage) for stage in range(groups - 1)]
     for stage in range(1, groups):
-        leaving, waves = call(
+        leaving, waves, first_tails = call(
             forward_kernel(stage),
             "forward",
-            [wave, waves_shape],
-            [VMEM] * 5,
+            [wave, waves_shape, tails_shape],
+            [VMEM] * 6,
             [indices],
-            (entering, blocks, propagators, rf, waves),
+            (entering, blocks, tails, propagators, rf, waves),
             size,
         )
         if stage < groups - 1:
@@ -499,9 +512,9 @@
         middle_kernel(groups),
         "middle",
         [wave, grads_shape, left_table, square_table],
-        [VMEM] * (groups + 7),
+        [VMEM] * (groups + 8),
         [pltpu.VMEM((width, 2 * LANES), F32), indices],
-        (waves, *nears, blocks, propagators, lb, rb, *dft),
+        (waves, *nears, blocks, tails, propagators, lb, rb, *dft),
         size,
     )
 
@@ -511,9 +524,9 @@
             backward_kernel(stage),
             "backward",
             [wave, grads_shape],
-            [VMEM] * 6,
+            [VMEM] * 7,
             [indices],
-            (arriving, waves, blocks, lb, rb, grads),
+            (arriving, waves, blocks, first_tails if stage == 0 else tails, lb, rb, grads),
             size,
         )
 

time: 86.6 us -> 86.1 us (level)
  no operation moved by 1% of the time
where the time goes in v15:
time: 86.1 us; the launch traced here: 85.8 us
  blocking collectives  44.3 us (51%)
  Pallas kernels  19 us (22%)
  waiting for transfers between devices  17.7 us (21%)
  starting transfers between devices  3.88 us (5%)
  between operations  0.91 us (1%)
    all_to_all x2, blocking collectives, exchanged(): lax.all_to_all(blocks, 'cuts', 0, 0, axis_index_groups=members, tiled=True)  44.3 us
    ppermute x3, waiting for transfers between devices, handed(): return lax.ppermute(block, 'cuts', route)  17.7 us
    pallas_call x5, Pallas kernels, call(): pl.pallas_call(kernel, out_shape=out_shape, in_specs=in_specs, out_specs=...  11.9 us
    pallas_call x1, Pallas kernels, shards(): pl.pallas_call(window_kernel, out_shape=struct(size, rows, 2 * width), in...  3.98 us
    ppermute x3, starting transfers between devices, handed(): return lax.ppermute(block, 'cuts', route)  3.88 us
    pallas_call x1, Pallas kernels, shards(): pl.pallas_call(gather_kernel, out_shape=jax.ShapeDtypeStruct(objects.shap...  3.17 us
  transfers between devices with their start and end apart: 3, of which 2 were waited for; matrix products, arithmetic and copies ran while one was open for 0% of the time, Pallas kernels for 1%

profile of v15, /device:TPU:0, one launch (start us, length us, event | category | flops | bytes accessed | tf_op | source)
XLA Modules:
  0.0 85.8 jit_solution(1582215393269687117)
XLA Ops:
  0.7 0.0 copy-start.2
  0.7 4.0 %windows.1 = bf16[8,208,384]{2,1,0:T(8,128)(2,1)} custom-call(s32[2,6]{1,0:T(2,128)} %bitcast.1, s32[1]{0:T(128)S(6)} %copy.9.index_ref, bf16[1,2,384,384]{3,2,1,0:T(8,128)(2,1)} %objects_in.1, f32[6,12,192]{2,1,0:T(8,128)} %measured_in.1), custom_call_target="tpu_custom_call" | custom-call | tf_op jit(solution)/shard_map/windows/pallas_call | solution.py:441
  4.7 0.0 copy-start
  4.7 0.0 copy-start.1
  4.7 0.0 copy-start.4
  4.7 22.6 %all_to_all.10.blocks.refs_1_ = bf16[8,208,384]{2,1,0:T(8,128)(2,1)S(1)} all-to-all(bf16[8,208,384]{2,1,0:T(8,128)(2,1)} %windows.1), channel_id=1, replica_groups={{0,1,2,3,4,5,6,7},{8,9,10,11,12,13,14,15},{16,17,18,19,20,21,22,23},{24..., dimensions={0} | all-to-all | bytes 2555904 | tf_op jit(solution)/shard_map/all_to_all | solution.py:434
  27.3 0.0 copy-done.2
  27.3 0.0 copy-done
  27.3 0.0 copy-done.1
  27.3 0.0 copy-done.4
  27.3 5.5 %first_forward.1 = (bf16[192,384]{1,0:T(8,128)(2,1)S(1)}, bf16[9,192,384]{2,1,0:T(8,128)(2,1)S(1)}, bf16[8,192,256]{2,1,0:T(8,128)(2,1)S(1)}, bf16[4,384,192]{2,...) custom-call(s32[6]{0:T(128)S(1)} %copy-done.4, ...), custom_call_target="tpu_custom_call" | custom-call | flops 905969664 | bytes 9732120 | tf_op jit(solution)/shard_map/first_forward/pallas_call | solution.py:470
  32.8 1.3 %collective-permute-start = (bf16[192,384]{1,0:T(8,128)(2,1)S(1)}, bf16[192,384]{1,0:T(8,128)(2,1)S(1)}, u32[]{:S(2)}, u32[]{:S(2)}) collective-permute-start(bf16[192,384]{1,0:T(8,128)(2,1)S(1)} %get-tuple-element.21._), channel_id=1, source_target_pairs={{4,8},{5,9},{6,10},{7,11},{0,12},{2,14},{20,24},{21,25},{22,26},{2... | collective-permute-start | bytes 442376 | tf_op jit(solution)/shard_map/ppermute | solution.py:439
  34.2 1.3 %collective-permute-start.1 = (bf16[96,256]{1,0:T(8,128)(2,1)S(1)}, bf16[96,256]{1,0:T(8,128)(2,1)S(1)}, u32[]{:S(2)}, u32[]{:S(2)}) collective-permute-start(bf16[96,256]{1,0:T(8,128)(2,1)S(1)} %near_rows.1), channel_id=1, source_target_pairs={{4,8},{5,9},{6,10},{7,11},{0,12},{2,14},{20,24},{21,25},{22,26},{2... | collective-permute-start | bytes 147464 | tf_op jit(solution)/shard_map/ppermute | solution.py:439
  35.5 1.4 %collective-permute-done.entering = bf16[192,384]{1,0:T(8,128)(2,1)S(1)} collective-permute-done((bf16[192,384]{1,0:T(8,128)(2,1)S(1)}, bf16[192,384]{1,0:T(8,128)(2,1)S(1)}, u32[]{:S(2)}, u32[]{:S(2)}) %collective-permute-start) | collective-permute-done | bytes 147488 | tf_op jit(solution)/shard_map/ppermute | solution.py:439
  36.8 1.0 %forward.1 = (bf16[192,384]{1,0:T(8,128)(2,1)}, bf16[9,192,384]{2,1,0:T(8,128)(2,1)S(1)}, bf16[8,192,256]{2,1,0:T(8,128)(2,1)S(1)}) custom-call(bf16[192,384]{1,0:T(8,128)(2,1)S(1)} %collective-permute-done.entering, bf16[8,208,384]{2,1,0:T(8,128)(2,1)S(1)} %all_to_all.10.blocks.refs_1_, bf16[8,192,256]{2,1,0:T(8,128)(2,1)S(1)} %get-tuple-element.22.tails.refs_2_, ...), custom_call_target="tpu_custom_call" | custom-call | flops 905969664 | bytes 7569408 | tf_op jit(solution)/shard_map/forward/pallas_call | solution.py:470
  37.8 0.0 collective-permute-done.1.refs_0_
  37.8 0.4 middle.1
  38.2 1.3 %collective-permute-start.2 = (bf16[192,384]{1,0:T(8,128)(2,1)S(1)}, bf16[192,384]{1,0:T(8,128)(2,1)S(1)}, u32[]{:S(2)}, u32[]{:S(2)}) collective-permute-start(bf16[192,384]{1,0:T(8,128)(2,1)S(1)} %get-tuple-element.31), channel_id=1, source_target_pairs={{8,4},{9,5},{10,6},{11,7},{12,0},{14,2},{24,20},{25,21},{26,22},{2... | collective-permute-start | bytes 442376 | tf_op jit(solution)/shard_map/ppermute | solution.py:439
  39.5 16.4 %collective-permute-done.2.arriving = bf16[192,384]{1,0:T(8,128)(2,1)S(1)} collective-permute-done((bf16[192,384]{1,0:T(8,128)(2,1)S(1)}, bf16[192,384]{1,0:T(8,128)(2,1)S(1)}, u32[]{:S(2)}, u32[]{:S(2)}) %collective-permute-start.2) | collective-permute-done | bytes 147488 | tf_op jit(solution)/shard_map/ppermute | solution.py:439
  55.9 5.0 %backward.1 = (bf16[192,384]{1,0:T(8,128)(2,1)}, bf16[8,192,384]{2,1,0:T(8,128)(2,1)S(1)}) custom-call(bf16[192,384]{1,0:T(8,128)(2,1)S(1)} %collective-permute-done.2.arriving, bf16[9,192,384]{2,1,0:T(8,128)(2,1)S(1)} %get-tuple-element.25.waves, bf16[8,208,384]{2,1,0:T(8,128)(2,1)S(1)} %all_to_all.10.blocks.refs_1_, ...), custom_call_target="tpu_custom_call" | custom-call | flops 905969664 | bytes 7815168 | tf_op jit(solution)/shard_map/backward/pallas_call | solution.py:470
  60.9 0.0 copy-start.3
  60.9 21.6 %all_to_all.11.grads_ref = bf16[8,192,384]{2,1,0:T(8,128)(2,1)S(1)} all-to-all(bf16[8,192,384]{2,1,0:T(8,128)(2,1)S(1)} %get-tuple-element.36), channel_id=1, replica_groups={{0,1,2,3,4,5,6,7},{8,9,10,11,12,13,14,15},{16,17,18,19,20,21,22,23},{24..., dimensions={0} | all-to-all | bytes 2359296 | tf_op jit(solution)/shard_map/all_to_all | solution.py:434
  82.5 0.0 copy-done.3
  82.5 3.2 %sum_windows.1 = f32[1,2,384,384]{3,2,1,0:T(8,128)} custom-call(s32[2,6]{1,0:T(2,128)S(1)} %bitcast.2, bf16[8,192,384]{2,1,0:T(8,128)(2,1)S(1)} %all_to_all.11.grads_ref), custom_call_target="tpu_custom_call" | custom-call | tf_op jit(solution)/shard_map/sum_windows/pallas_call | solution.py:533
  (1 shorter events, 0.0 us)
Async XLA Ops:
  0.7 26.7 %copy-start.2 = (f32[2,192,192]{2,1,0:T(8,128)S(1)}, f32[2,192,192]{2,1,0:T(8,128)}, u32[]{:S(2)}) copy-start(f32[2,192,192]{2,1,0:T(8,128)} %constant.2.clone.dft) | copy-start | bytes 884740
  4.7 22.7 %copy-start = (bf16[4,2,192,192]{3,2,1,0:T(8,128)(2,1)S(1)}, bf16[4,2,192,192]{3,2,1,0:T(8,128)(2,1)}, u32[]{:S(2)}) copy-start(bf16[4,2,192,192]{3,2,1,0:T(8,128)(2,1)} %refs_3_.1) | copy-start | bytes 1769476
  4.7 22.7 %copy-start.1 = (bf16[8,2,192,192]{3,2,1,0:T(8,128)(2,1)S(1)}, bf16[8,2,192,192]{3,2,1,0:T(8,128)(2,1)}, u32[]{:S(2)}) copy-start(bf16[8,2,192,192]{3,2,1,0:T(8,128)(2,1)} %probes.1) | copy-start | bytes 3538948
  4.7 22.7 %copy-start.4 = (s32[6]{0:T(128)S(1)}, s32[6]{0:T(128)}, u32[]{:S(2)}) copy-start(s32[6]{0:T(128)} %group_ref.1) | copy-start | bytes 76
  32.8 4.0 %collective-permute-start = (bf16[192,384]{1,0:T(8,128)(2,1)S(1)}, bf16[192,384]{1,0:T(8,128)(2,1)S(1)}, u32[]{:S(2)}, u32[]{:S(2)}) collective-permute-start(bf16[192,384]{1,0:T(8,128)(2,1)S(1)} %get-tuple-element.21._), channel_id=1, source_target_pairs={{4,8},{5,9},{6,10},{7,11},{0,12},{2,14},{20,24},{21,25},{22,26},{2... | collective-permute-start | bytes 442376 | tf_op jit(solution)/shard_map/ppermute | solution.py:439
  34.2 3.6 %collective-permute-start.1 = (bf16[96,256]{1,0:T(8,128)(2,1)S(1)}, bf16[96,256]{1,0:T(8,128)(2,1)S(1)}, u32[]{:S(2)}, u32[]{:S(2)}) collective-permute-start(bf16[96,256]{1,0:T(8,128)(2,1)S(1)} %near_rows.1), channel_id=1, source_target_pairs={{4,8},{5,9},{6,10},{7,11},{0,12},{2,14},{20,24},{21,25},{22,26},{2... | collective-permute-start | bytes 147464 | tf_op jit(solution)/shard_map/ppermute | solution.py:439
  38.2 17.7 %collective-permute-start.2 = (bf16[192,384]{1,0:T(8,128)(2,1)S(1)}, bf16[192,384]{1,0:T(8,128)(2,1)S(1)}, u32[]{:S(2)}, u32[]{:S(2)}) collective-permute-start(bf16[192,384]{1,0:T(8,128)(2,1)S(1)} %get-tuple-element.31), channel_id=1, source_target_pairs={{8,4},{9,5},{10,6},{11,7},{12,0},{14,2},{24,20},{25,21},{26,22},{2... | collective-permute-start | bytes 442376 | tf_op jit(solution)/shard_map/ppermute | solution.py:439
  60.9 21.6 %copy-start.3 = (s32[6,2]{0,1:T(2,128)S(1)}, s32[6,2]{0,1:T(2,128)}, u32[]{:S(2)}) copy-start(s32[6,2]{0,1:T(2,128)} %param.13) | copy-start | bytes 148

commit v16 on v15

--- a/solution.py
+++ b/solution.py
@@ -148,7 +148,7 @@
     return [slot ^ flip for slot in slots_of(positions, size)]
 
 
-def window_kernel(offsets_in, index_ref, objects_in, measured_in, blocks_out, blocks, offsets_ref, objects, measured, sems):
+def window_kernel(offsets_in, index_ref, objects_in, measured_in, blocks_out, blocks, offsets_ref, objects, measured, pickers, sems):
     positions, near_rows, width = measured.shape
     extent = objects.shape[-1]
     copies = [
@@ -157,19 +157,23 @@
         pltpu.make_async_copy(measured_in, measured, sems.at[2]),
         pltpu.make_async_copy(offsets_in, offsets_ref, sems.at[3]),
     ]
-    for copy in copies:
+    for copy in reversed(copies):
         copy.start()
     tag = jnp.full((ROWS, LANES), index_ref[0], jnp.int32).astype(F32)
-    for copy in copies:
-        copy.wait()
     size = blocks_out.shape[0]
     _, group = place_in(size)
     flip = lax.rem(group, 2) * (size // 2)
+    copies.pop().wait()
+    for p in range(positions):
+        for c in range(2):
+            pickers[p, c] = picker((extent, 2 * LANES), offsets_ref[1, p], c == 1)
+    for copy in copies:
+        copy.wait()
     sending = []
     for p, slot in enumerate(slots_of(positions, size)):
         start = offsets_ref[0, p]
         real, imag = (
-            dot(rows_near(objects[c], start, width), picker((extent, 2 * LANES), offsets_ref[1, p], c == 1))
+            dot(rows_near(objects[c], start, width), pickers[p, c])
             for c in range(2)
         )
         tail = real[:, LANES:] + imag[:, LANES:]
@@ -448,6 +452,7 @@
             pltpu.SMEM(offsets.shape[::-1], jnp.int32),
             pltpu.VMEM(objects.shape[1:], BF16),
             pltpu.VMEM(measured.shape, F32),
+            pltpu.VMEM((len(slots), 2, objects.shape[-1], 2 * LANES), BF16),
             pltpu.SemaphoreType.DMA((4 + len(slots),)),
         ],
         compiler_params=ALONE,

time: 86.1 us -> 86.1 us (level)
  no operation moved by 1% of the time
where the time goes in v16:
time: 86.1 us; the launch traced here: 85.8 us
  blocking collectives  44.3 us (51%)
  Pallas kernels  19 us (22%)
  waiting for transfers between devices  17.7 us (21%)
  starting transfers between devices  3.88 us (5%)
  between operations  0.91 us (1%)
    all_to_all x2, blocking collectives, exchanged(): lax.all_to_all(blocks, 'cuts', 0, 0, axis_index_groups=members, tiled=True)  44.3 us
    ppermute x3, waiting for transfers between devices, handed(): return lax.ppermute(block, 'cuts', route)  17.7 us
    pallas_call x5, Pallas kernels, call(): pl.pallas_call(kernel, out_shape=out_shape, in_specs=in_specs, out_specs=...  11.9 us
    pallas_call x1, Pallas kernels, shards(): pl.pallas_call(window_kernel, out_shape=struct(size, rows, 2 * width), in...  3.93 us
    ppermute x3, starting transfers between devices, handed(): return lax.ppermute(block, 'cuts', route)  3.88 us
    pallas_call x1, Pallas kernels, shards(): pl.pallas_call(gather_kernel, out_shape=jax.ShapeDtypeStruct(objects.shap...  3.17 us
  transfers between devices with their start and end apart: 3, of which 2 were waited for; matrix products, arithmetic and copies ran while one was open for 0% of the time, Pallas kernels for 1%

profile of v16, /device:TPU:0, one launch (start us, length us, event | category | flops | bytes accessed | tf_op | source)
XLA Modules:
  0.0 85.8 jit_solution(3129616754840804479)
XLA Ops:
  0.7 0.0 copy-start.2
  0.7 3.9 %windows.1 = bf16[8,208,384]{2,1,0:T(8,128)(2,1)} custom-call(s32[2,6]{1,0:T(2,128)} %bitcast.1, s32[1]{0:T(128)S(6)} %copy.9.index_ref, bf16[1,2,384,384]{3,2,1,0:T(8,128)(2,1)} %objects_in.1, f32[6,12,192]{2,1,0:T(8,128)} %measured_in.1), custom_call_target="tpu_custom_call" | custom-call | tf_op jit(solution)/shard_map/windows/pallas_call | solution.py:445
  4.6 0.0 copy-start
  4.6 0.0 copy-start.1
  4.6 0.0 copy-start.4
  4.6 22.6 %all_to_all.10.blocks.refs_1_ = bf16[8,208,384]{2,1,0:T(8,128)(2,1)S(1)} all-to-all(bf16[8,208,384]{2,1,0:T(8,128)(2,1)} %windows.1), channel_id=1, replica_groups={{0,1,2,3,4,5,6,7},{8,9,10,11,12,13,14,15},{16,17,18,19,20,21,22,23},{24..., dimensions={0} | all-to-all | bytes 2555904 | tf_op jit(solution)/shard_map/all_to_all | solution.py:438
  27.3 0.0 copy-done.2
  27.3 0.0 copy-done
  27.3 0.0 copy-done.1
  27.3 0.0 copy-done.4
  27.3 5.5 %first_forward.1 = (bf16[192,384]{1,0:T(8,128)(2,1)S(1)}, bf16[9,192,384]{2,1,0:T(8,128)(2,1)S(1)}, bf16[8,192,256]{2,1,0:T(8,128)(2,1)S(1)}, bf16[4,384,192]{2,...) custom-call(s32[6]{0:T(128)S(1)} %copy-done.4, ...), custom_call_target="tpu_custom_call" | custom-call | flops 905969664 | bytes 9732120 | tf_op jit(solution)/shard_map/first_forward/pallas_call | solution.py:475
  32.8 1.3 %collective-permute-start = (bf16[192,384]{1,0:T(8,128)(2,1)S(1)}, bf16[192,384]{1,0:T(8,128)(2,1)S(1)}, u32[]{:S(2)}, u32[]{:S(2)}) collective-permute-start(bf16[192,384]{1,0:T(8,128)(2,1)S(1)} %get-tuple-element.21._), channel_id=1, source_target_pairs={{4,8},{5,9},{6,10},{7,11},{0,12},{2,14},{20,24},{21,25},{22,26},{2... | collective-permute-start | bytes 442376 | tf_op jit(solution)/shard_map/ppermute | solution.py:443
  34.1 1.3 %collective-permute-start.1 = (bf16[96,256]{1,0:T(8,128)(2,1)S(1)}, bf16[96,256]{1,0:T(8,128)(2,1)S(1)}, u32[]{:S(2)}, u32[]{:S(2)}) collective-permute-start(bf16[96,256]{1,0:T(8,128)(2,1)S(1)} %near_rows.1), channel_id=1, source_target_pairs={{4,8},{5,9},{6,10},{7,11},{0,12},{2,14},{20,24},{21,25},{22,26},{2... | collective-permute-start | bytes 147464 | tf_op jit(solution)/shard_map/ppermute | solution.py:443
  35.4 1.4 %collective-permute-done.entering = bf16[192,384]{1,0:T(8,128)(2,1)S(1)} collective-permute-done((bf16[192,384]{1,0:T(8,128)(2,1)S(1)}, bf16[192,384]{1,0:T(8,128)(2,1)S(1)}, u32[]{:S(2)}, u32[]{:S(2)}) %collective-permute-start) | collective-permute-done | bytes 147488 | tf_op jit(solution)/shard_map/ppermute | solution.py:443
  36.8 1.0 %forward.1 = (bf16[192,384]{1,0:T(8,128)(2,1)}, bf16[9,192,384]{2,1,0:T(8,128)(2,1)S(1)}, bf16[8,192,256]{2,1,0:T(8,128)(2,1)S(1)}) custom-call(bf16[192,384]{1,0:T(8,128)(2,1)S(1)} %collective-permute-done.entering, bf16[8,208,384]{2,1,0:T(8,128)(2,1)S(1)} %all_to_all.10.blocks.refs_1_, bf16[8,192,256]{2,1,0:T(8,128)(2,1)S(1)} %get-tuple-element.22.tails.refs_2_, ...), custom_call_target="tpu_custom_call" | custom-call | flops 905969664 | bytes 7569408 | tf_op jit(solution)/shard_map/forward/pallas_call | solution.py:475
  37.7 0.0 collective-permute-done.1.refs_0_
  37.7 0.4 middle.1
  38.2 1.3 %collective-permute-start.2 = (bf16[192,384]{1,0:T(8,128)(2,1)S(1)}, bf16[192,384]{1,0:T(8,128)(2,1)S(1)}, u32[]{:S(2)}, u32[]{:S(2)}) collective-permute-start(bf16[192,384]{1,0:T(8,128)(2,1)S(1)} %get-tuple-element.31), channel_id=1, source_target_pairs={{8,4},{9,5},{10,6},{11,7},{12,0},{14,2},{24,20},{25,21},{26,22},{2... | collective-permute-start | bytes 442376 | tf_op jit(solution)/shard_map/ppermute | solution.py:443
  39.5 16.4 %collective-permute-done.2.arriving = bf16[192,384]{1,0:T(8,128)(2,1)S(1)} collective-permute-done((bf16[192,384]{1,0:T(8,128)(2,1)S(1)}, bf16[192,384]{1,0:T(8,128)(2,1)S(1)}, u32[]{:S(2)}, u32[]{:S(2)}) %collective-permute-start.2) | collective-permute-done | bytes 147488 | tf_op jit(solution)/shard_map/ppermute | solution.py:443
  55.8 5.0 %backward.1 = (bf16[192,384]{1,0:T(8,128)(2,1)}, bf16[8,192,384]{2,1,0:T(8,128)(2,1)S(1)}) custom-call(bf16[192,384]{1,0:T(8,128)(2,1)S(1)} %collective-permute-done.2.arriving, bf16[9,192,384]{2,1,0:T(8,128)(2,1)S(1)} %get-tuple-element.25.waves, bf16[8,208,384]{2,1,0:T(8,128)(2,1)S(1)} %all_to_all.10.blocks.refs_1_, ...), custom_call_target="tpu_custom_call" | custom-call | flops 905969664 | bytes 7815168 | tf_op jit(solution)/shard_map/backward/pallas_call | solution.py:475
  60.8 0.0 copy-start.3
  60.8 21.6 %all_to_all.11.grads_ref = bf16[8,192,384]{2,1,0:T(8,128)(2,1)S(1)} all-to-all(bf16[8,192,384]{2,1,0:T(8,128)(2,1)S(1)} %get-tuple-element.36), channel_id=1, replica_groups={{0,1,2,3,4,5,6,7},{8,9,10,11,12,13,14,15},{16,17,18,19,20,21,22,23},{24..., dimensions={0} | all-to-all | bytes 2359296 | tf_op jit(solution)/shard_map/all_to_all | solution.py:438
  82.5 0.0 copy-done.3
  82.5 3.2 %sum_windows.1 = f32[1,2,384,384]{3,2,1,0:T(8,128)} custom-call(s32[2,6]{1,0:T(2,128)S(1)} %bitcast.2, bf16[8,192,384]{2,1,0:T(8,128)(2,1)S(1)} %all_to_all.11.grads_ref), custom_call_target="tpu_custom_call" | custom-call | tf_op jit(solution)/shard_map/sum_windows/pallas_call | solution.py:538
  (1 shorter events, 0.0 us)
Async XLA Ops:
  0.7 26.6 %copy-start.2 = (f32[2,192,192]{2,1,0:T(8,128)S(1)}, f32[2,192,192]{2,1,0:T(8,128)}, u32[]{:S(2)}) copy-start(f32[2,192,192]{2,1,0:T(8,128)} %constant.2.clone.dft) | copy-start | bytes 884740
  4.6 22.7 %copy-start = (bf16[4,2,192,192]{3,2,1,0:T(8,128)(2,1)S(1)}, bf16[4,2,192,192]{3,2,1,0:T(8,128)(2,1)}, u32[]{:S(2)}) copy-start(bf16[4,2,192,192]{3,2,1,0:T(8,128)(2,1)} %refs_3_.1) | copy-start | bytes 1769476
  4.6 22.7 %copy-start.1 = (bf16[8,2,192,192]{3,2,1,0:T(8,128)(2,1)S(1)}, bf16[8,2,192,192]{3,2,1,0:T(8,128)(2,1)}, u32[]{:S(2)}) copy-start(bf16[8,2,192,192]{3,2,1,0:T(8,128)(2,1)} %probes.1) | copy-start | bytes 3538948
  4.6 22.7 %copy-start.4 = (s32[6]{0:T(128)S(1)}, s32[6]{0:T(128)}, u32[]{:S(2)}) copy-start(s32[6]{0:T(128)} %group_ref.1) | copy-start | bytes 76
  32.8 4.0 %collective-permute-start = (bf16[192,384]{1,0:T(8,128)(2,1)S(1)}, bf16[192,384]{1,0:T(8,128)(2,1)S(1)}, u32[]{:S(2)}, u32[]{:S(2)}) collective-permute-start(bf16[192,384]{1,0:T(8,128)(2,1)S(1)} %get-tuple-element.21._), channel_id=1, source_target_pairs={{4,8},{5,9},{6,10},{7,11},{0,12},{2,14},{20,24},{21,25},{22,26},{2... | collective-permute-start | bytes 442376 | tf_op jit(solution)/shard_map/ppermute | solution.py:443
  34.1 3.6 %collective-permute-start.1 = (bf16[96,256]{1,0:T(8,128)(2,1)S(1)}, bf16[96,256]{1,0:T(8,128)(2,1)S(1)}, u32[]{:S(2)}, u32[]{:S(2)}) collective-permute-start(bf16[96,256]{1,0:T(8,128)(2,1)S(1)} %near_rows.1), channel_id=1, source_target_pairs={{4,8},{5,9},{6,10},{7,11},{0,12},{2,14},{20,24},{21,25},{22,26},{2... | collective-permute-start | bytes 147464 | tf_op jit(solution)/shard_map/ppermute | solution.py:443
  38.2 17.7 %collective-permute-start.2 = (bf16[192,384]{1,0:T(8,128)(2,1)S(1)}, bf16[192,384]{1,0:T(8,128)(2,1)S(1)}, u32[]{:S(2)}, u32[]{:S(2)}) collective-permute-start(bf16[192,384]{1,0:T(8,128)(2,1)S(1)} %get-tuple-element.31), channel_id=1, source_target_pairs={{8,4},{9,5},{10,6},{11,7},{12,0},{14,2},{24,20},{25,21},{26,22},{2... | collective-permute-start | bytes 442376 | tf_op jit(solution)/shard_map/ppermute | solution.py:443
  60.8 21.6 %copy-start.3 = (s32[6,2]{0,1:T(2,128)S(1)}, s32[6,2]{0,1:T(2,128)}, u32[]{:S(2)}) copy-start(s32[6,2]{0,1:T(2,128)} %param.13) | copy-start | bytes 148

commit v17 on v16

--- a/solution.py
+++ b/solution.py
@@ -148,16 +148,20 @@
     return [slot ^ flip for slot in slots_of(positions, size)]
 
 
-def window_kernel(offsets_in, index_ref, objects_in, measured_in, blocks_out, blocks, offsets_ref, objects, measured, pickers, sems):
+def window_kernel(
+    offsets_in, index_ref, objects_in, measured_in, props_in, blocks_out, rf_out,
+    blocks, rf, offsets_ref, objects, measured, props, pickers, sems,
+):
     positions, near_rows, width = measured.shape
     extent = objects.shape[-1]
     copies = [
         pltpu.make_async_copy(objects_in.at[0, 0], objects.at[0], sems.at[0]),
         pltpu.make_async_copy(objects_in.at[0, 1], objects.at[1], sems.at[1]),
         pltpu.make_async_copy(measured_in, measured, sems.at[2]),
-        pltpu.make_async_copy(offsets_in, offsets_ref, sems.at[3]),
+        pltpu.make_async_copy(props_in, props, sems.at[3]),
+        pltpu.make_async_copy(offsets_in, offsets_ref, sems.at[4]),
     ]
-    for copy in reversed(copies):
+    for copy in copies[-1:] + copies[:-1]:
         copy.start()
     tag = jnp.full((ROWS, LANES), index_ref[0], jnp.int32).astype(F32)
     size = blocks_out.shape[0]
@@ -185,8 +189,12 @@
         left_over = jnp.concatenate([tag[near_rows:]] * 3, axis=1)
         blocks[p, width:, :] = jnp.concatenate([seen, left_over], axis=0).astype(BF16)
         target = blocks_out.at[lax.bitwise_xor(slot, flip)]
-        sending.append(pltpu.make_async_copy(blocks.at[p], target, sems.at[4 + p]))
+        sending.append(pltpu.make_async_copy(blocks.at[p], target, sems.at[5 + p]))
         sending[-1].start()
+        for k in range(p, props.shape[0], positions):
+            rf[k] = right_table(props[k, 0].astype(F32).T, props[k, 1].astype(F32).T)
+            sending.append(pltpu.make_async_copy(rf.at[k], rf_out.at[k], sems.at[5 + positions + k]))
+            sending[-1].start()
     for copy in sending:
         copy.wait()
 
@@ -194,11 +202,6 @@
 def right_table(real, imag):
     upper, lower = packed(real, imag), packed(-imag, real)
     return jnp.concatenate([upper[:LANES], lower[:LANES], upper[LANES:], lower[LANES:]], axis=0).astype(BF16)
-
-
-def forward_tables(props, rf):
-    for k in range(props.shape[0]):
-        rf[k] = right_table(props[k, 0].astype(F32).T, props[k, 1].astype(F32).T)
 
 
 def backward_tables(props, lb, rb):
@@ -296,7 +299,7 @@
     near[...] = observed[...].astype(BF16)
 
 
-def first_kernel(group_ref, probes, blocks, props, dft, leaving, waves, tails, lb, rf, rb, left, right, right_conj, probe, indices, sem):
+def first_kernel(group_ref, probes, blocks, props, rf, dft, leaving, waves, tails, lb, rb, left, right, right_conj, probe, indices, sem):
     size = blocks.shape[0]
     slot, group = place_in(size)
 
@@ -308,7 +311,6 @@
         which = group_ref[position]
         copy = pltpu.make_async_copy(probes.at[which], probe, sem)
         copy.start()
-        forward_tables(props, rf)
         read_indices(blocks, indices, props.shape[0])
         copy.wait()
         waves[0] = packed(probe[0].astype(F32), probe[1].astype(F32)).astype(BF16)
@@ -318,7 +320,6 @@
     @pl.when(group > 0)
     def _():
         spread_tails(blocks, tails)
-        forward_tables(props, rf)
         backward_tables(props, lb, rb)
         detector_tables(dft, left, right, right_conj)
 
@@ -442,22 +443,24 @@
         route = [(stage * size + l, (stage + distance) * size + m) for l, m in zip(*ends)]
         return lax.ppermute(block, "cuts", route)
 
-    blocks = pl.pallas_call(
+    blocks, rf = pl.pallas_call(
         window_kernel,
-        out_shape=struct(size, rows, 2 * width),
-        in_specs=[HBM, SMEM, HBM, HBM],
-        out_specs=HBM,
+        out_shape=[struct(size, rows, 2 * width), struct(kinds, 2 * width, 2 * width)],
+        in_specs=[HBM, SMEM, HBM, HBM, HBM],
+        out_specs=[HBM, HBM],
         scratch_shapes=[
             pltpu.VMEM((size, rows, 2 * width), BF16),
+            pltpu.VMEM((kinds, 2 * width, 2 * width), BF16),
             pltpu.SMEM(offsets.shape[::-1], jnp.int32),
             pltpu.VMEM(objects.shape[1:], BF16),
             pltpu.VMEM(measured.shape, F32),
+            pltpu.VMEM(propagators.shape, BF16),
             pltpu.VMEM((len(slots), 2, objects.shape[-1], 2 * LANES), BF16),
-            pltpu.SemaphoreType.DMA((4 + len(slots),)),
+            pltpu.SemaphoreType.DMA((5 + len(slots) + kinds,)),
         ],
         compiler_params=ALONE,
         name="windows",
-    )(offsets.T, prop_index, objects, measured)
+    )(offsets.T, prop_index, objects, measured, propagators)
     blocks = exchanged(blocks)
 
     wave = struct(width, 2 * width)
@@ -487,14 +490,14 @@
             name=name,
         )(*operands)
 
-    leaving, waves, tails, lb, rf, rb, *dft = call(
+    leaving, waves, tails, lb, rb, *dft = call(
         first_kernel,
         "first_forward",
-        [wave, waves_shape, tails_shape, left_table, square_table, square_table]
+        [wave, waves_shape, tails_shape, left_table, square_table]
         + [detector_left, detector_right, struct(2 * width, 2 * width)],
-        [SMEM, HBM, VMEM, VMEM, VMEM],
+        [SMEM, HBM, VMEM, VMEM, VMEM, VMEM],
         [pltpu.VMEM(probes.shape[1:], BF16), indices, pltpu.SemaphoreType.DMA],
-        (probe_group, probes, blocks, propagators, jnp.asarray(dft_constant(width))),
+        (probe_group, probes, blocks, propagators, rf, jnp.asarray(dft_constant(width))),
         size,
     )
     entering = handed(leaving, 0, 1)

time: 86.1 us -> 86.4 us (level)
  no operation moved by 1% of the time
where the time goes in v17:
time: 86.4 us; the launch traced here: 86.1 us
  blocking collectives  44.2 us (51%)
  Pallas kernels  19.3 us (22%)
  waiting for transfers between devices  17.7 us (20%)
  starting transfers between devices  3.88 us (4%)
  between operations  0.93 us (1%)
    all_to_all x2, blocking collectives, exchanged(): lax.all_to_all(blocks, 'cuts', 0, 0, axis_index_groups=members, tiled=True)  44.2 us
    ppermute x3, waiting for transfers between devices, handed(): return lax.ppermute(block, 'cuts', route)  17.7 us
    pallas_call x5, Pallas kernels, call(): pl.pallas_call(kernel, out_shape=out_shape, in_specs=in_specs, out_specs=...  11.5 us
    pallas_call x1, Pallas kernels, shards(): pl.pallas_call(window_kernel, out_shape=[struct(size, rows, 2 * width), s...  4.59 us
    ppermute x3, starting transfers between devices, handed(): return lax.ppermute(block, 'cuts', route)  3.88 us
    pallas_call x1, Pallas kernels, shards(): pl.pallas_call(gather_kernel, out_shape=jax.ShapeDtypeStruct(objects.shap...  3.17 us
  transfers between devices with their start and end apart: 3, of which 2 were waited for; matrix products, arithmetic and copies ran while one was open for 0% of the time, Pallas kernels for 1%

profile of v17, /device:TPU:0, one launch (start us, length us, event | category | flops | bytes accessed | tf_op | source)
XLA Modules:
  0.0 86.1 jit_solution(10172166747243695336)
XLA Ops:
  0.7 0.0 copy-start.2
  0.7 4.6 %windows.1 = (bf16[8,208,384]{2,1,0:T(8,128)(2,1)}, bf16[4,384,384]{2,1,0:T(8,128)(2,1)}) custom-call(s32[2,6]{1,0:T(2,128)} %bitcast.1, s32[1]{0:T(128)S(6)} %copy.9.index_ref, bf16[1,2,384,384]{3,2,1,0:T(8,128)(2,1)} %objects_in.1, f32[6,12,192]{2,1,0:T(8,128)} %measured_in.1, bf16[4,2,192,192]{3,2,1,0:T(8,128)(2,1)} %refs_3_.1), custom_call_target="tpu_custom_call" | custom-call | tf_op jit(solution)/shard_map/windows/pallas_call | solution.py:446
  5.3 0.0 copy-start
  5.3 0.0 copy-start.1
  5.3 0.0 copy-start.3
  5.3 0.0 copy-start.5
  5.3 22.6 %all_to_all.10.blocks.refs_1_ = bf16[8,208,384]{2,1,0:T(8,128)(2,1)S(1)} all-to-all(bf16[8,208,384]{2,1,0:T(8,128)(2,1)} %get-tuple-element.22), channel_id=1, replica_groups={{0,1,2,3,4,5,6,7},{8,9,10,11,12,13,14,15},{16,17,18,19,20,21,22,23},{24..., dimensions={0} | all-to-all | bytes 2555904 | tf_op jit(solution)/shard_map/all_to_all | solution.py:439
  28.0 0.0 copy-done.2
  28.0 0.0 copy-done
  28.0 0.0 copy-done.1
  28.0 0.0 copy-done.3
  28.0 0.0 copy-done.5
  28.0 5.1 %first_forward.1 = (bf16[192,384]{1,0:T(8,128)(2,1)S(1)}, bf16[9,192,384]{2,1,0:T(8,128)(2,1)S(1)}, bf16[8,192,256]{2,1,0:T(8,128)(2,1)S(1)}, bf16[4,384,192]{2,...) custom-call(s32[6]{0:T(128)S(1)} %copy-done.5, ...), custom_call_target="tpu_custom_call" | custom-call | flops 905969664 | bytes 9732120 | tf_op jit(solution)/shard_map/first_forward/pallas_call | solution.py:478
  33.1 1.3 %collective-permute-start = (bf16[192,384]{1,0:T(8,128)(2,1)S(1)}, bf16[192,384]{1,0:T(8,128)(2,1)S(1)}, u32[]{:S(2)}, u32[]{:S(2)}) collective-permute-start(bf16[192,384]{1,0:T(8,128)(2,1)S(1)} %get-tuple-element.24._), channel_id=1, source_target_pairs={{4,8},{5,9},{6,10},{7,11},{0,12},{2,14},{20,24},{21,25},{22,26},{2... | collective-permute-start | bytes 442376 | tf_op jit(solution)/shard_map/ppermute | solution.py:444
  34.5 1.3 %collective-permute-start.1 = (bf16[96,256]{1,0:T(8,128)(2,1)S(1)}, bf16[96,256]{1,0:T(8,128)(2,1)S(1)}, u32[]{:S(2)}, u32[]{:S(2)}) collective-permute-start(bf16[96,256]{1,0:T(8,128)(2,1)S(1)} %near_rows.1), channel_id=1, source_target_pairs={{4,8},{5,9},{6,10},{7,11},{0,12},{2,14},{20,24},{21,25},{22,26},{2... | collective-permute-start | bytes 147464 | tf_op jit(solution)/shard_map/ppermute | solution.py:444
  35.8 1.4 %collective-permute-done.entering = bf16[192,384]{1,0:T(8,128)(2,1)S(1)} collective-permute-done((bf16[192,384]{1,0:T(8,128)(2,1)S(1)}, bf16[192,384]{1,0:T(8,128)(2,1)S(1)}, u32[]{:S(2)}, u32[]{:S(2)}) %collective-permute-start) | collective-permute-done | bytes 147488 | tf_op jit(solution)/shard_map/ppermute | solution.py:444
  37.1 1.0 %forward.1 = (bf16[192,384]{1,0:T(8,128)(2,1)}, bf16[9,192,384]{2,1,0:T(8,128)(2,1)S(1)}, bf16[8,192,256]{2,1,0:T(8,128)(2,1)S(1)}) custom-call(bf16[192,384]{1,0:T(8,128)(2,1)S(1)} %collective-permute-done.entering, bf16[8,208,384]{2,1,0:T(8,128)(2,1)S(1)} %all_to_all.10.blocks.refs_1_, bf16[8,192,256]{2,1,0:T(8,128)(2,1)S(1)} %get-tuple-element.25.tails.refs_2_, ...), custom_call_target="tpu_custom_call" | custom-call | flops 905969664 | bytes 7569408 | tf_op jit(solution)/shard_map/forward/pallas_call | solution.py:478
  38.1 0.0 collective-permute-done.1.refs_0_
  38.1 0.4 middle.1
  38.5 1.3 %collective-permute-start.2 = (bf16[192,384]{1,0:T(8,128)(2,1)S(1)}, bf16[192,384]{1,0:T(8,128)(2,1)S(1)}, u32[]{:S(2)}, u32[]{:S(2)}) collective-permute-start(bf16[192,384]{1,0:T(8,128)(2,1)S(1)} %get-tuple-element.33), channel_id=1, source_target_pairs={{8,4},{9,5},{10,6},{11,7},{12,0},{14,2},{24,20},{25,21},{26,22},{2... | collective-permute-start | bytes 442376 | tf_op jit(solution)/shard_map/ppermute | solution.py:444
  39.8 16.4 %collective-permute-done.2.arriving = bf16[192,384]{1,0:T(8,128)(2,1)S(1)} collective-permute-done((bf16[192,384]{1,0:T(8,128)(2,1)S(1)}, bf16[192,384]{1,0:T(8,128)(2,1)S(1)}, u32[]{:S(2)}, u32[]{:S(2)}) %collective-permute-start.2) | collective-permute-done | bytes 147488 | tf_op jit(solution)/shard_map/ppermute | solution.py:444
  56.2 5.0 %backward.1 = (bf16[192,384]{1,0:T(8,128)(2,1)}, bf16[8,192,384]{2,1,0:T(8,128)(2,1)S(1)}) custom-call(bf16[192,384]{1,0:T(8,128)(2,1)S(1)} %collective-permute-done.2.arriving, bf16[9,192,384]{2,1,0:T(8,128)(2,1)S(1)} %get-tuple-element.27.waves, bf16[8,208,384]{2,1,0:T(8,128)(2,1)S(1)} %all_to_all.10.blocks.refs_1_, ...), custom_call_target="tpu_custom_call" | custom-call | flops 905969664 | bytes 7815168 | tf_op jit(solution)/shard_map/backward/pallas_call | solution.py:478
  61.2 0.0 copy-start.4
  61.2 21.6 %all_to_all.11.grads_ref = bf16[8,192,384]{2,1,0:T(8,128)(2,1)S(1)} all-to-all(bf16[8,192,384]{2,1,0:T(8,128)(2,1)S(1)} %get-tuple-element.38), channel_id=1, replica_groups={{0,1,2,3,4,5,6,7},{8,9,10,11,12,13,14,15},{16,17,18,19,20,21,22,23},{24..., dimensions={0} | all-to-all | bytes 2359296 | tf_op jit(solution)/shard_map/all_to_all | solution.py:439
  82.8 0.0 copy-done.4
  82.8 3.2 %sum_windows.1 = f32[1,2,384,384]{3,2,1,0:T(8,128)} custom-call(s32[2,6]{1,0:T(2,128)S(1)} %bitcast.2, bf16[8,192,384]{2,1,0:T(8,128)(2,1)S(1)} %all_to_all.11.grads_ref), custom_call_target="tpu_custom_call" | custom-call | tf_op jit(solution)/shard_map/sum_windows/pallas_call | solution.py:541
  (1 shorter events, 0.0 us)
Async XLA Ops:
  0.7 27.3 %copy-start.2 = (bf16[8,2,192,192]{3,2,1,0:T(8,128)(2,1)S(1)}, bf16[8,2,192,192]{3,2,1,0:T(8,128)(2,1)}, u32[]{:S(2)}) copy-start(bf16[8,2,192,192]{3,2,1,0:T(8,128)(2,1)} %probes.1) | copy-start | bytes 3538948
  5.3 22.7 %copy-start = (bf16[4,2,192,192]{3,2,1,0:T(8,128)(2,1)S(1)}, bf16[4,2,192,192]{3,2,1,0:T(8,128)(2,1)}, u32[]{:S(2)}) copy-start(bf16[4,2,192,192]{3,2,1,0:T(8,128)(2,1)} %refs_3_.1) | copy-start | bytes 1769476
  5.3 22.7 %copy-start.1 = (bf16[4,384,384]{2,1,0:T(8,128)(2,1)S(1)}, bf16[4,384,384]{2,1,0:T(8,128)(2,1)}, u32[]{:S(2)}) copy-start(bf16[4,384,384]{2,1,0:T(8,128)(2,1)} %get-tuple-element.23.rf) | copy-start | bytes 3538948
  5.3 22.7 %copy-start.3 = (f32[2,192,192]{2,1,0:T(8,128)S(1)}, f32[2,192,192]{2,1,0:T(8,128)}, u32[]{:S(2)}) copy-start(f32[2,192,192]{2,1,0:T(8,128)} %constant.2.clone.dft) | copy-start | bytes 884740
  5.3 22.7 %copy-start.5 = (s32[6]{0:T(128)S(1)}, s32[6]{0:T(128)}, u32[]{:S(2)}) copy-start(s32[6]{0:T(128)} %group_ref.1) | copy-start | bytes 76
  33.1 4.0 %collective-permute-start = (bf16[192,384]{1,0:T(8,128)(2,1)S(1)}, bf16[192,384]{1,0:T(8,128)(2,1)S(1)}, u32[]{:S(2)}, u32[]{:S(2)}) collective-permute-start(bf16[192,384]{1,0:T(8,128)(2,1)S(1)} %get-tuple-element.24._), channel_id=1, source_target_pairs={{4,8},{5,9},{6,10},{7,11},{0,12},{2,14},{20,24},{21,25},{22,26},{2... | collective-permute-start | bytes 442376 | tf_op jit(solution)/shard_map/ppermute | solution.py:444
  34.5 3.6 %collective-permute-start.1 = (bf16[96,256]{1,0:T(8,128)(2,1)S(1)}, bf16[96,256]{1,0:T(8,128)(2,1)S(1)}, u32[]{:S(2)}, u32[]{:S(2)}) collective-permute-start(bf16[96,256]{1,0:T(8,128)(2,1)S(1)} %near_rows.1), channel_id=1, source_target_pairs={{4,8},{5,9},{6,10},{7,11},{0,12},{2,14},{20,24},{21,25},{22,26},{2... | collective-permute-start | bytes 147464 | tf_op jit(solution)/shard_map/ppermute | solution.py:444
  38.5 17.7 %collective-permute-start.2 = (bf16[192,384]{1,0:T(8,128)(2,1)S(1)}, bf16[192,384]{1,0:T(8,128)(2,1)S(1)}, u32[]{:S(2)}, u32[]{:S(2)}) collective-permute-start(bf16[192,384]{1,0:T(8,128)(2,1)S(1)} %get-tuple-element.33), channel_id=1, source_target_pairs={{8,4},{9,5},{10,6},{11,7},{12,0},{14,2},{24,20},{25,21},{26,22},{2... | collective-permute-start | bytes 442376 | tf_op jit(solution)/shard_map/ppermute | solution.py:444
  61.2 21.6 %copy-start.4 = (s32[6,2]{0,1:T(2,128)S(1)}, s32[6,2]{0,1:T(2,128)}, u32[]{:S(2)}) copy-start(s32[6,2]{0,1:T(2,128)} %param.13) | copy-start | bytes 148

commit v18 on v16

--- a/solution.py
+++ b/solution.py
@@ -12,6 +12,7 @@
 GROUP = 8
 LANES = 128
 ROWS = 16
+EXTRA = 8
 F32 = jnp.float32
 BF16 = jnp.bfloat16
 
@@ -159,7 +160,8 @@
     ]
     for copy in reversed(copies):
         copy.start()
-    tag = jnp.full((ROWS, LANES), index_ref[0], jnp.int32).astype(F32)
+    half = (near_rows + 1) // 2
+    tag = jnp.full((EXTRA - half, 2 * width), index_ref[0], jnp.int32).astype(F32)
     size = blocks_out.shape[0]
     _, group = place_in(size)
     flip = lax.rem(group, 2) * (size // 2)
@@ -180,10 +182,9 @@
         window = jnp.concatenate([real[:, :LANES], imag[:, :LANES], tail], axis=1).astype(BF16)
         shift = lax.bitwise_and(start, ROWS - 1)
         blocks[p, :width, :] = dot(row_picker((width, width + ROWS), shift), window).astype(BF16)
-        tail = measured[p, :, LANES:]
-        seen = jnp.concatenate([measured[p, :, :LANES], tail, tail, tag[:near_rows]], axis=1)
-        left_over = jnp.concatenate([tag[near_rows:]] * 3, axis=1)
-        blocks[p, width:, :] = jnp.concatenate([seen, left_over], axis=0).astype(BF16)
+        rows = jnp.concatenate([measured[p], measured[p, : 2 * half - near_rows]], axis=0) if near_rows % 2 else measured[p]
+        seen = packed(rows[:half], rows[half:])
+        blocks[p, width:, :] = jnp.concatenate([seen, tag], axis=0).astype(BF16)
         target = blocks_out.at[lax.bitwise_xor(slot, flip)]
         sending.append(pltpu.make_async_copy(blocks.at[p], target, sems.at[4 + p]))
         sending[-1].start()
@@ -276,7 +277,7 @@
 
 def read_indices(blocks, indices, count):
     for k in range(blocks.shape[0]):
-        tag = jnp.max(blocks[k, -ROWS:, 2 * LANES :].astype(F32))
+        tag = jnp.max(blocks[k, -EXTRA:, :LANES].astype(F32)[EXTRA - 1 :])
         indices[k] = jnp.clip(tag.astype(jnp.int32), 0, count - 1)
 
 
@@ -286,9 +287,13 @@
 
 
 def observe(blocks, near_rows, observed, first):
+    half = (near_rows + 1) // 2
     for k in range(blocks.shape[0]):
+        early, late, tail = halves(blocks[k, -EXTRA:, :].astype(F32))
+        early_tail, late_tail = spread(tail)
         at = first + k * near_rows
-        observed[at : at + near_rows, :] = blocks[k, -ROWS:, : 2 * LANES].astype(F32)[:near_rows]
+        observed[at : at + half, :] = jnp.concatenate([early, early_tail], axis=1)[:half]
+        observed[at + half : at + near_rows, :] = jnp.concatenate([late, late_tail], axis=1)[: near_rows - half]
 
 
 def near_kernel(blocks, _, near, observed):
@@ -427,7 +432,7 @@
     near_rows = measured.shape[1]
     size = GROUP
     groups = sections // size
-    rows = width + ROWS
+    rows = width + EXTRA
     slots = slots_of(probe_group.shape[0], size)
     members = [list(range(first, first + size)) for first in range(0, sections, size)]
 

time: 86.1 us -> 85.7 us (level)
  no operation moved by 1% of the time
where the time goes in v18:
time: 85.7 us; the launch traced here: 85.4 us
  blocking collectives  43.9 us (51%)
  Pallas kernels  19 us (22%)
  waiting for transfers between devices  17.7 us (21%)
  starting transfers between devices  3.88 us (5%)
  between operations  0.91 us (1%)
    all_to_all x2, blocking collectives, exchanged(): lax.all_to_all(blocks, 'cuts', 0, 0, axis_index_groups=members, tiled=True)  43.9 us
    ppermute x3, waiting for transfers between devices, handed(): return lax.ppermute(block, 'cuts', route)  17.7 us
    pallas_call x5, Pallas kernels, call(): pl.pallas_call(kernel, out_shape=out_shape, in_specs=in_specs, out_specs=...  12 us
    pallas_call x1, Pallas kernels, shards(): pl.pallas_call(window_kernel, out_shape=struct(size, rows, 2 * width), in...  3.9 us
    ppermute x3, starting transfers between devices, handed(): return lax.ppermute(block, 'cuts', route)  3.88 us
    pallas_call x1, Pallas kernels, shards(): pl.pallas_call(gather_kernel, out_shape=jax.ShapeDtypeStruct(objects.shap...  3.17 us
  transfers between devices with their start and end apart: 3, of which 2 were waited for; matrix products, arithmetic and copies ran while one was open for 0% of the time, Pallas kernels for 1%

profile of v18, /device:TPU:0, one launch (start us, length us, event | category | flops | bytes accessed | tf_op | source)
XLA Modules:
  0.0 85.4 jit_solution(594981139693714802)
XLA Ops:
  0.7 0.0 copy-start.2
  0.7 3.9 %windows.1 = bf16[8,200,384]{2,1,0:T(8,128)(2,1)} custom-call(s32[2,6]{1,0:T(2,128)} %bitcast.1, s32[1]{0:T(128)S(6)} %copy.9.index_ref, bf16[1,2,384,384]{3,2,1,0:T(8,128)(2,1)} %objects_in.1, f32[6,12,192]{2,1,0:T(8,128)} %measured_in.1), custom_call_target="tpu_custom_call" | custom-call | tf_op jit(solution)/shard_map/windows/pallas_call | solution.py:450
  4.6 0.0 copy-start
  4.6 0.0 copy-start.1
  4.6 0.0 copy-start.4
  4.6 22.4 %all_to_all.10.blocks.refs_1_ = bf16[8,200,384]{2,1,0:T(8,128)(2,1)S(1)} all-to-all(bf16[8,200,384]{2,1,0:T(8,128)(2,1)} %windows.1), channel_id=1, replica_groups={{0,1,2,3,4,5,6,7},{8,9,10,11,12,13,14,15},{16,17,18,19,20,21,22,23},{24..., dimensions={0} | all-to-all | bytes 2457600 | tf_op jit(solution)/shard_map/all_to_all | solution.py:443
  27.0 0.0 copy-done.2
  27.0 0.0 copy-done
  27.0 0.0 copy-done.1
  27.0 0.0 copy-done.4
  27.0 5.5 %first_forward.1 = (bf16[192,384]{1,0:T(8,128)(2,1)S(1)}, bf16[9,192,384]{2,1,0:T(8,128)(2,1)S(1)}, bf16[8,192,256]{2,1,0:T(8,128)(2,1)S(1)}, bf16[4,384,192]{2,...) custom-call(s32[6]{0:T(128)S(1)} %copy-done.4, ...), custom_call_target="tpu_custom_call" | custom-call | flops 905969664 | bytes 9682968 | tf_op jit(solution)/shard_map/first_forward/pallas_call | solution.py:480
  32.5 1.3 %collective-permute-start = (bf16[192,384]{1,0:T(8,128)(2,1)S(1)}, bf16[192,384]{1,0:T(8,128)(2,1)S(1)}, u32[]{:S(2)}, u32[]{:S(2)}) collective-permute-start(bf16[192,384]{1,0:T(8,128)(2,1)S(1)} %get-tuple-element.21._), channel_id=1, source_target_pairs={{4,8},{5,9},{6,10},{7,11},{0,12},{2,14},{20,24},{21,25},{22,26},{2... | collective-permute-start | bytes 442376 | tf_op jit(solution)/shard_map/ppermute | solution.py:448
  33.8 0.1 near_rows.1
  33.9 1.3 %collective-permute-start.1 = (bf16[96,256]{1,0:T(8,128)(2,1)S(1)}, bf16[96,256]{1,0:T(8,128)(2,1)S(1)}, u32[]{:S(2)}, u32[]{:S(2)}) collective-permute-start(bf16[96,256]{1,0:T(8,128)(2,1)S(1)} %near_rows.1), channel_id=1, source_target_pairs={{4,8},{5,9},{6,10},{7,11},{0,12},{2,14},{20,24},{21,25},{22,26},{2... | collective-permute-start | bytes 147464 | tf_op jit(solution)/shard_map/ppermute | solution.py:448
  35.2 1.3 %collective-permute-done.entering = bf16[192,384]{1,0:T(8,128)(2,1)S(1)} collective-permute-done((bf16[192,384]{1,0:T(8,128)(2,1)S(1)}, bf16[192,384]{1,0:T(8,128)(2,1)S(1)}, u32[]{:S(2)}, u32[]{:S(2)}) %collective-permute-start) | collective-permute-done | bytes 147488 | tf_op jit(solution)/shard_map/ppermute | solution.py:448
  36.5 1.0 %forward.1 = (bf16[192,384]{1,0:T(8,128)(2,1)}, bf16[9,192,384]{2,1,0:T(8,128)(2,1)S(1)}, bf16[8,192,256]{2,1,0:T(8,128)(2,1)S(1)}) custom-call(bf16[192,384]{1,0:T(8,128)(2,1)S(1)} %collective-permute-done.entering, bf16[8,200,384]{2,1,0:T(8,128)(2,1)S(1)} %all_to_all.10.blocks.refs_1_, bf16[8,192,256]{2,1,0:T(8,128)(2,1)S(1)} %get-tuple-element.22.tails.refs_2_, ...), custom_call_target="tpu_custom_call" | custom-call | flops 905969664 | bytes 7520256 | tf_op jit(solution)/shard_map/forward/pallas_call | solution.py:480
  37.4 0.0 collective-permute-done.1.refs_0_
  37.4 0.4 middle.1
  37.9 1.3 %collective-permute-start.2 = (bf16[192,384]{1,0:T(8,128)(2,1)S(1)}, bf16[192,384]{1,0:T(8,128)(2,1)S(1)}, u32[]{:S(2)}, u32[]{:S(2)}) collective-permute-start(bf16[192,384]{1,0:T(8,128)(2,1)S(1)} %get-tuple-element.31), channel_id=1, source_target_pairs={{8,4},{9,5},{10,6},{11,7},{12,0},{14,2},{24,20},{25,21},{26,22},{2... | collective-permute-start | bytes 442376 | tf_op jit(solution)/shard_map/ppermute | solution.py:448
  39.2 16.4 %collective-permute-done.2.arriving = bf16[192,384]{1,0:T(8,128)(2,1)S(1)} collective-permute-done((bf16[192,384]{1,0:T(8,128)(2,1)S(1)}, bf16[192,384]{1,0:T(8,128)(2,1)S(1)}, u32[]{:S(2)}, u32[]{:S(2)}) %collective-permute-start.2) | collective-permute-done | bytes 147488 | tf_op jit(solution)/shard_map/ppermute | solution.py:448
  55.6 5.0 %backward.1 = (bf16[192,384]{1,0:T(8,128)(2,1)}, bf16[8,192,384]{2,1,0:T(8,128)(2,1)S(1)}) custom-call(bf16[192,384]{1,0:T(8,128)(2,1)S(1)} %collective-permute-done.2.arriving, bf16[9,192,384]{2,1,0:T(8,128)(2,1)S(1)} %get-tuple-element.25.waves, bf16[8,200,384]{2,1,0:T(8,128)(2,1)S(1)} %all_to_all.10.blocks.refs_1_, ...), custom_call_target="tpu_custom_call" | custom-call | flops 905969664 | bytes 7766016 | tf_op jit(solution)/shard_map/backward/pallas_call | solution.py:480
  60.5 0.0 copy-start.3
  60.5 21.5 %all_to_all.11.grads_ref = bf16[8,192,384]{2,1,0:T(8,128)(2,1)S(1)} all-to-all(bf16[8,192,384]{2,1,0:T(8,128)(2,1)S(1)} %get-tuple-element.36), channel_id=1, replica_groups={{0,1,2,3,4,5,6,7},{8,9,10,11,12,13,14,15},{16,17,18,19,20,21,22,23},{24..., dimensions={0} | all-to-all | bytes 2359296 | tf_op jit(solution)/shard_map/all_to_all | solution.py:443
  82.0 0.0 copy-done.3
  82.0 3.2 %sum_windows.1 = f32[1,2,384,384]{3,2,1,0:T(8,128)} custom-call(s32[2,6]{1,0:T(2,128)S(1)} %bitcast.2, bf16[8,192,384]{2,1,0:T(8,128)(2,1)S(1)} %all_to_all.11.grads_ref), custom_call_target="tpu_custom_call" | custom-call | tf_op jit(solution)/shard_map/sum_windows/pallas_call | solution.py:543
Async XLA Ops:
  0.7 26.3 %copy-start.2 = (f32[2,192,192]{2,1,0:T(8,128)S(1)}, f32[2,192,192]{2,1,0:T(8,128)}, u32[]{:S(2)}) copy-start(f32[2,192,192]{2,1,0:T(8,128)} %constant.2.clone.dft) | copy-start | bytes 884740
  4.6 22.4 %copy-start = (bf16[4,2,192,192]{3,2,1,0:T(8,128)(2,1)S(1)}, bf16[4,2,192,192]{3,2,1,0:T(8,128)(2,1)}, u32[]{:S(2)}) copy-start(bf16[4,2,192,192]{3,2,1,0:T(8,128)(2,1)} %refs_3_.1) | copy-start | bytes 1769476
  4.6 22.4 %copy-start.1 = (bf16[8,2,192,192]{3,2,1,0:T(8,128)(2,1)S(1)}, bf16[8,2,192,192]{3,2,1,0:T(8,128)(2,1)}, u32[]{:S(2)}) copy-start(bf16[8,2,192,192]{3,2,1,0:T(8,128)(2,1)} %probes.1) | copy-start | bytes 3538948
  4.6 22.4 %copy-start.4 = (s32[6]{0:T(128)S(1)}, s32[6]{0:T(128)}, u32[]{:S(2)}) copy-start(s32[6]{0:T(128)} %group_ref.1) | copy-start | bytes 76
  32.5 4.0 %collective-permute-start = (bf16[192,384]{1,0:T(8,128)(2,1)S(1)}, bf16[192,384]{1,0:T(8,128)(2,1)S(1)}, u32[]{:S(2)}, u32[]{:S(2)}) collective-permute-start(bf16[192,384]{1,0:T(8,128)(2,1)S(1)} %get-tuple-element.21._), channel_id=1, source_target_pairs={{4,8},{5,9},{6,10},{7,11},{0,12},{2,14},{20,24},{21,25},{22,26},{2... | collective-permute-start | bytes 442376 | tf_op jit(solution)/shard_map/ppermute | solution.py:448
  33.9 3.6 %collective-permute-start.1 = (bf16[96,256]{1,0:T(8,128)(2,1)S(1)}, bf16[96,256]{1,0:T(8,128)(2,1)S(1)}, u32[]{:S(2)}, u32[]{:S(2)}) collective-permute-start(bf16[96,256]{1,0:T(8,128)(2,1)S(1)} %near_rows.1), channel_id=1, source_target_pairs={{4,8},{5,9},{6,10},{7,11},{0,12},{2,14},{20,24},{21,25},{22,26},{2... | collective-permute-start | bytes 147464 | tf_op jit(solution)/shard_map/ppermute | solution.py:448
  37.9 17.7 %collective-permute-start.2 = (bf16[192,384]{1,0:T(8,128)(2,1)S(1)}, bf16[192,384]{1,0:T(8,128)(2,1)S(1)}, u32[]{:S(2)}, u32[]{:S(2)}) collective-permute-start(bf16[192,384]{1,0:T(8,128)(2,1)S(1)} %get-tuple-element.31), channel_id=1, source_target_pairs={{8,4},{9,5},{10,6},{11,7},{12,0},{14,2},{24,20},{25,21},{26,22},{2... | collective-permute-start | bytes 442376 | tf_op jit(solution)/shard_map/ppermute | solution.py:448
  60.5 21.5 %copy-start.3 = (s32[6,2]{0,1:T(2,128)S(1)}, s32[6,2]{0,1:T(2,128)}, u32[]{:S(2)}) copy-start(s32[6,2]{0,1:T(2,128)} %param.13) | copy-start | bytes 148

commit v19 on v16

--- a/solution.py
+++ b/solution.py
@@ -291,7 +291,14 @@
         observed[at : at + near_rows, :] = blocks[k, -ROWS:, : 2 * LANES].astype(F32)[:near_rows]
 
 
-def near_kernel(blocks, _, near, observed):
+def near_kernel(blocks, props, _, near, tails, lb, rb, observed):
+    _, group = place_in(blocks.shape[0])
+
+    @pl.when(group == 0)
+    def _():
+        spread_tails(blocks, tails)
+        backward_tables(props, lb, rb)
+
     observe(blocks, near.shape[0] // blocks.shape[0], observed, 0)
     near[...] = observed[...].astype(BF16)
 
@@ -324,7 +331,7 @@
 
 
 def forward_kernel(stage):
-    def kernel(entering, blocks, tails, props, rf, waves_in, leaving, waves, first_tails, indices):
+    def kernel(entering, blocks, tails, props, rf, waves_in, leaving, waves, indices):
         size = blocks.shape[0]
         _, group = place_in(size)
 
@@ -339,17 +346,13 @@
         def _():
             waves[...] = waves_in[...]
 
-        @pl.when(group == 0)
-        def _():
-            spread_tails(blocks, first_tails)
-
     return kernel
 
 
 def middle_kernel(groups):
     def kernel(waves, *refs):
         earlier, refs = refs[: groups - 1], refs[groups - 1 :]
-        blocks, tails, props, lb, rb, left, right, right_conj, leaving, grads, lb_out, rb_out, observed, indices = refs
+        blocks, tails, props, lb, rb, left, right, right_conj, leaving, grads, observed, indices = refs
         size = blocks.shape[0]
         _, group = place_in(size)
 
@@ -362,10 +365,6 @@
             observe(blocks, rows // size, observed, (groups - 1) * rows)
             g = detector(waves[size], observed[...], left, right, right_conj)
             leaving[...] = backward_steps(blocks, tails, waves, indices, lb, rb, grads, g)
-
-        @pl.when(group < groups - 1)
-        def _():
-            backward_tables(props, lb_out, rb_out)
 
     return kernel
 
@@ -498,13 +497,20 @@
         size,
     )
     entering = handed(leaving, 0, 1)
-    (near_out,) = call(near_kernel, "near_rows", [near], [VMEM, HBM], [pltpu.VMEM(near.shape, F32)], (blocks, leaving))
+    near_out, *first_back = call(
+        near_kernel,
+        "near_rows",
+        [near, tails_shape, left_table, square_table],
+        [VMEM, VMEM, HBM],
+        [pltpu.VMEM(near.shape, F32)],
+        (blocks, propagators, leaving),
+    )
     nears = [handed(near_out, stage, groups - 1 - stage) for stage in range(groups - 1)]
     for stage in range(1, groups):
-        leaving, waves, first_tails = call(
+        leaving, waves = call(
             forward_kernel(stage),
             "forward",
-            [wave, waves_shape, tails_shape],
+            [wave, waves_shape],
             [VMEM] * 6,
             [indices],
             (entering, blocks, tails, propagators, rf, waves),
@@ -513,10 +519,10 @@
         if stage < groups - 1:
             entering = handed(leaving, stage, 1)
 
-    leaving, grads, lb, rb = call(
+    leaving, grads = call(
         middle_kernel(groups),
         "middle",
-        [wave, grads_shape, left_table, square_table],
+        [wave, grads_shape],
         [VMEM] * (groups + 8),
         [pltpu.VMEM((width, 2 * LANES), F32), indices],
         (waves, *nears, blocks, tails, propagators, lb, rb, *dft),
@@ -531,7 +537,7 @@
             [wave, grads_shape],
             [VMEM] * 7,
             [indices],
-            (arriving, waves, blocks, first_tails if stage == 0 else tails, lb, rb, grads),
+            (arriving, waves, blocks, *(first_back if stage == 0 else (tails, lb, rb)), grads),
             size,
         )
 

time: 86.1 us -> 86.1 us (level)
  transfers between devices with their start and end apart: 3 -> 3, of which waited for: 2 -> 3; matrix products, arithmetic and copies ran while one was open for 0% -> 0% of each run, Pallas kernels for 1% -> 2%
where the time goes in v19:
time: 86.1 us; the launch traced here: 85.8 us
  blocking collectives  44.2 us (51%)
  Pallas kernels  18.9 us (22%)
  waiting for transfers between devices  17.8 us (21%)
  starting transfers between devices  3.87 us (4%)
  between operations  0.9 us (1%)
    all_to_all x2, blocking collectives, exchanged(): lax.all_to_all(blocks, 'cuts', 0, 0, axis_index_groups=members, tiled=True)  44.2 us
    ppermute x3, waiting for transfers between devices, handed(): return lax.ppermute(block, 'cuts', route)  17.8 us
    pallas_call x5, Pallas kernels, call(): pl.pallas_call(kernel, out_shape=out_shape, in_specs=in_specs, out_specs=...  11.8 us
    pallas_call x1, Pallas kernels, shards(): pl.pallas_call(window_kernel, out_shape=struct(size, rows, 2 * width), in...  3.92 us
    ppermute x3, starting transfers between devices, handed(): return lax.ppermute(block, 'cuts', route)  3.87 us
    pallas_call x1, Pallas kernels, shards(): pl.pallas_call(gather_kernel, out_shape=jax.ShapeDtypeStruct(objects.shap...  3.17 us
  transfers between devices with their start and end apart: 3, of which 3 were waited for; matrix products, arithmetic and copies ran while one was open for 0% of the time, Pallas kernels for 2%

profile of v19, /device:TPU:0, one launch (start us, length us, event | category | flops | bytes accessed | tf_op | source)
XLA Modules:
  0.0 85.8 jit_solution(10763831576022811786)
XLA Ops:
  0.7 0.0 copy-start.2
  0.7 3.9 %windows.1 = bf16[8,208,384]{2,1,0:T(8,128)(2,1)} custom-call(s32[2,6]{1,0:T(2,128)} %bitcast.1, s32[1]{0:T(128)S(6)} %copy.9.index_ref, bf16[1,2,384,384]{3,2,1,0:T(8,128)(2,1)} %objects_in.1, f32[6,12,192]{2,1,0:T(8,128)} %measured_in.1), custom_call_target="tpu_custom_call" | custom-call | tf_op jit(solution)/shard_map/windows/pallas_call | solution.py:444
  4.6 0.0 copy-start
  4.6 0.0 copy-start.1
  4.6 0.0 copy-start.4
  4.6 22.6 %all_to_all.10.blocks.refs_1_ = bf16[8,208,384]{2,1,0:T(8,128)(2,1)S(1)} all-to-all(bf16[8,208,384]{2,1,0:T(8,128)(2,1)} %windows.1), channel_id=1, replica_groups={{0,1,2,3,4,5,6,7},{8,9,10,11,12,13,14,15},{16,17,18,19,20,21,22,23},{24..., dimensions={0} | all-to-all | bytes 2555904 | tf_op jit(solution)/shard_map/all_to_all | solution.py:437
  27.3 0.0 copy-done.2
  27.3 0.0 copy-done
  27.3 0.0 copy-done.1
  27.3 0.0 copy-done.4
  27.3 5.5 %first_forward.1 = (bf16[192,384]{1,0:T(8,128)(2,1)S(1)}, bf16[9,192,384]{2,1,0:T(8,128)(2,1)S(1)}, bf16[8,192,256]{2,1,0:T(8,128)(2,1)S(1)}, bf16[4,384,192]{2,...) custom-call(s32[6]{0:T(128)S(1)} %copy-done.4, ...), custom_call_target="tpu_custom_call" | custom-call | flops 905969664 | bytes 9732120 | tf_op jit(solution)/shard_map/first_forward/pallas_call | solution.py:474
  32.8 1.3 %collective-permute-start = (bf16[192,384]{1,0:T(8,128)(2,1)S(1)}, bf16[192,384]{1,0:T(8,128)(2,1)S(1)}, u32[]{:S(2)}, u32[]{:S(2)}) collective-permute-start(bf16[192,384]{1,0:T(8,128)(2,1)S(1)} %get-tuple-element.22._), channel_id=1, source_target_pairs={{4,8},{5,9},{6,10},{7,11},{0,12},{2,14},{20,24},{21,25},{22,26},{2... | collective-permute-start | bytes 442376 | tf_op jit(solution)/shard_map/ppermute | solution.py:442
  34.1 0.6 near_rows.1
  34.7 1.3 %collective-permute-start.1 = (bf16[96,256]{1,0:T(8,128)(2,1)S(1)}, bf16[96,256]{1,0:T(8,128)(2,1)S(1)}, u32[]{:S(2)}, u32[]{:S(2)}) collective-permute-start(bf16[96,256]{1,0:T(8,128)(2,1)S(1)} %get-tuple-element.27), channel_id=1, source_target_pairs={{4,8},{5,9},{6,10},{7,11},{0,12},{2,14},{20,24},{21,25},{22,26},{2... | collective-permute-start | bytes 147464 | tf_op jit(solution)/shard_map/ppermute | solution.py:442
  36.0 0.8 collective-permute-done.entering
  36.8 0.8 forward.1
  37.5 0.2 collective-permute-done.1.refs_0_
  37.7 1.3 %collective-permute-start.2 = (bf16[192,384]{1,0:T(8,128)(2,1)S(1)}, bf16[192,384]{1,0:T(8,128)(2,1)S(1)}, u32[]{:S(2)}, u32[]{:S(2)}) collective-permute-start(bf16[192,384]{1,0:T(8,128)(2,1)S(1)} %get-tuple-element.33), channel_id=1, source_target_pairs={{8,4},{9,5},{10,6},{11,7},{12,0},{14,2},{24,20},{25,21},{26,22},{2... | collective-permute-start | bytes 442376 | tf_op jit(solution)/shard_map/ppermute | solution.py:442
  39.0 16.8 %collective-permute-done.2.arriving = bf16[192,384]{1,0:T(8,128)(2,1)S(1)} collective-permute-done((bf16[192,384]{1,0:T(8,128)(2,1)S(1)}, bf16[192,384]{1,0:T(8,128)(2,1)S(1)}, u32[]{:S(2)}, u32[]{:S(2)}) %collective-permute-start.2) | collective-permute-done | bytes 147488 | tf_op jit(solution)/shard_map/ppermute | solution.py:442
  55.8 5.0 %backward.1 = (bf16[192,384]{1,0:T(8,128)(2,1)}, bf16[8,192,384]{2,1,0:T(8,128)(2,1)S(1)}) custom-call(bf16[192,384]{1,0:T(8,128)(2,1)S(1)} %collective-permute-done.2.arriving, bf16[9,192,384]{2,1,0:T(8,128)(2,1)S(1)} %get-tuple-element.26.waves, bf16[8,208,384]{2,1,0:T(8,128)(2,1)S(1)} %all_to_all.10.blocks.refs_1_, ...), custom_call_target="tpu_custom_call" | custom-call | flops 905969664 | bytes 7815168 | tf_op jit(solution)/shard_map/backward/pallas_call | solution.py:474
  60.8 0.0 copy-start.3
  60.8 21.6 %all_to_all.11.grads_ref = bf16[8,192,384]{2,1,0:T(8,128)(2,1)S(1)} all-to-all(bf16[8,192,384]{2,1,0:T(8,128)(2,1)S(1)} %get-tuple-element.38), channel_id=1, replica_groups={{0,1,2,3,4,5,6,7},{8,9,10,11,12,13,14,15},{16,17,18,19,20,21,22,23},{24..., dimensions={0} | all-to-all | bytes 2359296 | tf_op jit(solution)/shard_map/all_to_all | solution.py:437
  82.4 0.0 copy-done.3
  82.4 3.2 %sum_windows.1 = f32[1,2,384,384]{3,2,1,0:T(8,128)} custom-call(s32[2,6]{1,0:T(2,128)S(1)} %bitcast.2, bf16[8,192,384]{2,1,0:T(8,128)(2,1)S(1)} %all_to_all.11.grads_ref), custom_call_target="tpu_custom_call" | custom-call | tf_op jit(solution)/shard_map/sum_windows/pallas_call | solution.py:544
  (1 shorter events, 0.0 us)
Async XLA Ops:
  0.7 26.6 %copy-start.2 = (f32[2,192,192]{2,1,0:T(8,128)S(1)}, f32[2,192,192]{2,1,0:T(8,128)}, u32[]{:S(2)}) copy-start(f32[2,192,192]{2,1,0:T(8,128)} %constant.2.clone.dft) | copy-start | bytes 884740
  4.6 22.7 %copy-start = (bf16[4,2,192,192]{3,2,1,0:T(8,128)(2,1)S(1)}, bf16[4,2,192,192]{3,2,1,0:T(8,128)(2,1)}, u32[]{:S(2)}) copy-start(bf16[4,2,192,192]{3,2,1,0:T(8,128)(2,1)} %refs_3_.1) | copy-start | bytes 1769476
  4.6 22.7 %copy-start.1 = (bf16[8,2,192,192]{3,2,1,0:T(8,128)(2,1)S(1)}, bf16[8,2,192,192]{3,2,1,0:T(8,128)(2,1)}, u32[]{:S(2)}) copy-start(bf16[8,2,192,192]{3,2,1,0:T(8,128)(2,1)} %probes.1) | copy-start | bytes 3538948
  4.6 22.7 %copy-start.4 = (s32[6]{0:T(128)S(1)}, s32[6]{0:T(128)}, u32[]{:S(2)}) copy-start(s32[6]{0:T(128)} %group_ref.1) | copy-start | bytes 76
  32.8 4.0 %collective-permute-start = (bf16[192,384]{1,0:T(8,128)(2,1)S(1)}, bf16[192,384]{1,0:T(8,128)(2,1)S(1)}, u32[]{:S(2)}, u32[]{:S(2)}) collective-permute-start(bf16[192,384]{1,0:T(8,128)(2,1)S(1)} %get-tuple-element.22._), channel_id=1, source_target_pairs={{4,8},{5,9},{6,10},{7,11},{0,12},{2,14},{20,24},{21,25},{22,26},{2... | collective-permute-start | bytes 442376 | tf_op jit(solution)/shard_map/ppermute | solution.py:442
  34.7 3.0 %collective-permute-start.1 = (bf16[96,256]{1,0:T(8,128)(2,1)S(1)}, bf16[96,256]{1,0:T(8,128)(2,1)S(1)}, u32[]{:S(2)}, u32[]{:S(2)}) collective-permute-start(bf16[96,256]{1,0:T(8,128)(2,1)S(1)} %get-tuple-element.27), channel_id=1, source_target_pairs={{4,8},{5,9},{6,10},{7,11},{0,12},{2,14},{20,24},{21,25},{22,26},{2... | collective-permute-start | bytes 147464 | tf_op jit(solution)/shard_map/ppermute | solution.py:442
  37.7 18.1 %collective-permute-start.2 = (bf16[192,384]{1,0:T(8,128)(2,1)S(1)}, bf16[192,384]{1,0:T(8,128)(2,1)S(1)}, u32[]{:S(2)}, u32[]{:S(2)}) collective-permute-start(bf16[192,384]{1,0:T(8,128)(2,1)S(1)} %get-tuple-element.33), channel_id=1, source_target_pairs={{8,4},{9,5},{10,6},{11,7},{12,0},{14,2},{24,20},{25,21},{26,22},{2... | collective-permute-start | bytes 442376 | tf_op jit(solution)/shard_map/ppermute | solution.py:442
  60.8 21.6 %copy-start.3 = (s32[6,2]{0,1:T(2,128)S(1)}, s32[6,2]{0,1:T(2,128)}, u32[]{:S(2)}) copy-start(s32[6,2]{0,1:T(2,128)} %param.13) | copy-start | bytes 148

commit v20 on v16

--- a/solution.py
+++ b/solution.py
@@ -296,9 +296,10 @@
     near[...] = observed[...].astype(BF16)
 
 
-def first_kernel(group_ref, probes, blocks, props, dft, leaving, waves, tails, lb, rf, rb, left, right, right_conj, probe, indices, sem):
+def first_kernel(group_ref, probes, blocks, props, dft, leaving, waves, tails, lb, rf, rb, left, right, right_conj, indices, probe, sem):
     size = blocks.shape[0]
     slot, group = place_in(size)
+    read_indices(blocks, indices, props.shape[0])
 
     @pl.when(group == 0)
     def _():
@@ -309,7 +310,6 @@
         copy = pltpu.make_async_copy(probes.at[which], probe, sem)
         copy.start()
         forward_tables(props, rf)
-        read_indices(blocks, indices, props.shape[0])
         copy.wait()
         waves[0] = packed(probe[0].astype(F32), probe[1].astype(F32)).astype(BF16)
         forward_steps(blocks, None, waves, indices, props, rf)
@@ -324,13 +324,12 @@
 
 
 def forward_kernel(stage):
-    def kernel(entering, blocks, tails, props, rf, waves_in, leaving, waves, first_tails, indices):
+    def kernel(indices, entering, blocks, tails, props, rf, waves_in, leaving, waves, first_tails):
         size = blocks.shape[0]
         _, group = place_in(size)
 
         @pl.when(group == stage)
         def _():
-            read_indices(blocks, indices, props.shape[0])
             waves[0] = entering[...]
             forward_steps(blocks, tails, waves, indices, props, rf)
             leaving[...] = waves[size]
@@ -347,15 +346,14 @@
 
 
 def middle_kernel(groups):
-    def kernel(waves, *refs):
+    def kernel(indices, waves, *refs):
         earlier, refs = refs[: groups - 1], refs[groups - 1 :]
-        blocks, tails, props, lb, rb, left, right, right_conj, leaving, grads, lb_out, rb_out, observed, indices = refs
+        blocks, tails, props, lb, rb, left, right, right_conj, leaving, grads, lb_out, rb_out, observed = refs
         size = blocks.shape[0]
         _, group = place_in(size)
 
         @pl.when(group == groups - 1)
         def _():
-            read_indices(blocks, indices, props.shape[0])
             rows = earlier[0].shape[0]
             for n, near in enumerate(earlier):
                 observed[n * rows : (n + 1) * rows, :] = near[...].astype(F32)
@@ -371,12 +369,11 @@
 
 
 def backward_kernel(stage):
-    def kernel(arriving, waves, blocks, tails, lb, rb, grads_in, leaving, grads, indices):
+    def kernel(indices, arriving, waves, blocks, tails, lb, rb, grads_in, leaving, grads):
         _, group = place_in(blocks.shape[0])
 
         @pl.when(group == stage)
         def _():
-            read_indices(blocks, indices, lb.shape[0])
             leaving[...] = backward_steps(blocks, tails, waves, indices, lb, rb, grads, arriving[...])
 
         @pl.when(group != stage)
@@ -469,14 +466,13 @@
     square_table = struct(kinds, 2 * width, 2 * width)
     detector_left = struct(2, 2 * width, width)
     detector_right = struct(2, 2 * width, 2 * width)
-    indices = pltpu.SMEM((size,), jnp.int32)
 
     def call(kernel, name, out_shape, in_specs, scratch_shapes, operands, slices=0):
         return pl.pallas_call(
             kernel,
             out_shape=out_shape,
             in_specs=in_specs,
-            out_specs=[VMEM] * len(out_shape),
+            out_specs=[SMEM if x.dtype == jnp.int32 else VMEM for x in out_shape],
             scratch_shapes=scratch_shapes,
             compiler_params=PARAMS,
             cost_estimate=pl.CostEstimate(
@@ -487,13 +483,13 @@
             name=name,
         )(*operands)
 
-    leaving, waves, tails, lb, rf, rb, *dft = call(
+    leaving, waves, tails, lb, rf, rb, *dft, indices = call(
         first_kernel,
         "first_forward",
         [wave, waves_shape, tails_shape, left_table, square_table, square_table]
-        + [detector_left, detector_right, struct(2 * width, 2 * width)],
+        + [detector_left, detector_right, struct(2 * width, 2 * width), struct(size, kind=jnp.int32)],
         [SMEM, HBM, VMEM, VMEM, VMEM],
-        [pltpu.VMEM(probes.shape[1:], BF16), indices, pltpu.SemaphoreType.DMA],
+        [pltpu.VMEM(probes.shape[1:], BF16), pltpu.SemaphoreType.DMA],
         (probe_group, probes, blocks, propagators, jnp.asarray(dft_constant(width))),
         size,
     )
@@ -505,9 +501,9 @@
             forward_kernel(stage),
             "forward",
             [wave, waves_shape, tails_shape],
-            [VMEM] * 6,
-            [indices],
-            (entering, blocks, tails, propagators, rf, waves),
+            [SMEM] + [VMEM] * 6,
+            [],
+            (indices, entering, blocks, tails, propagators, rf, waves),
             size,
         )
         if stage < groups - 1:
@@ -517,9 +513,9 @@
         middle_kernel(groups),
         "middle",
         [wave, grads_shape, left_table, square_table],
-        [VMEM] * (groups + 8),
-        [pltpu.VMEM((width, 2 * LANES), F32), indices],
-        (waves, *nears, blocks, tails, propagators, lb, rb, *dft),
+        [SMEM] + [VMEM] * (groups + 8),
+        [pltpu.VMEM((width, 2 * LANES), F32)],
+        (indices, waves, *nears, blocks, tails, propagators, lb, rb, *dft),
         size,
     )
 
@@ -529,9 +525,9 @@
             backward_kernel(stage),
             "backward",
             [wave, grads_shape],
-            [VMEM] * 7,
-            [indices],
-            (arriving, waves, blocks, first_tails if stage == 0 else tails, lb, rb, grads),
+            [SMEM] + [VMEM] * 7,
+            [],
+            (indices, arriving, waves, blocks, first_tails if stage == 0 else tails, lb, rb, grads),
             size,
         )
 

time: 86.1 us -> 88.5 us (1.028)
  Pallas kernels: 19 us -> 21.4 us
    pallas_call x5, Pallas kernels: 11.9 us -> 14.3 us  [call(): pl.pallas_call(kernel, out_shape=out_shape, in_specs=in_specs, out_specs=...]
  transfers between devices with their start and end apart: 3 -> 3, of which waited for: 2 -> 2; matrix products, arithmetic and copies ran while one was open for 0% -> 0% of each run, Pallas kernels for 1% -> 2%
where the time goes in v20:
time: 88.5 us; the launch traced here: 88.2 us
  blocking collectives  44.3 us (50%)
  Pallas kernels  21.4 us (24%)
  waiting for transfers between devices  17.7 us (20%)
  starting transfers between devices  3.88 us (4%)
  between operations  0.91 us (1%)
    all_to_all x2, blocking collectives, exchanged(): lax.all_to_all(blocks, 'cuts', 0, 0, axis_index_groups=members, tiled=True)  44.3 us
    ppermute x3, waiting for transfers between devices, handed(): return lax.ppermute(block, 'cuts', route)  17.7 us
    pallas_call x5, Pallas kernels, call(): pl.pallas_call(kernel, out_shape=out_shape, in_specs=in_specs, out_specs=...  14.3 us
    pallas_call x1, Pallas kernels, shards(): pl.pallas_call(window_kernel, out_shape=struct(size, rows, 2 * width), in...  3.93 us
    ppermute x3, starting transfers between devices, handed(): return lax.ppermute(block, 'cuts', route)  3.88 us
    pallas_call x1, Pallas kernels, shards(): pl.pallas_call(gather_kernel, out_shape=jax.ShapeDtypeStruct(objects.shap...  3.17 us
  transfers between devices with their start and end apart: 3, of which 2 were waited for; matrix products, arithmetic and copies ran while one was open for 0% of the time, Pallas kernels for 2%

profile of v20, /device:TPU:0, one launch (start us, length us, event | category | flops | bytes accessed | tf_op | source)
XLA Modules:
  0.0 88.2 jit_solution(7414222430448446960)
XLA Ops:
  0.7 0.0 copy-start.2
  0.7 3.9 %windows.1 = bf16[8,208,384]{2,1,0:T(8,128)(2,1)} custom-call(s32[2,6]{1,0:T(2,128)} %bitcast.1, s32[1]{0:T(128)S(6)} %copy.9.index_ref, bf16[1,2,384,384]{3,2,1,0:T(8,128)(2,1)} %objects_in.1, f32[6,12,192]{2,1,0:T(8,128)} %measured_in.1), custom_call_target="tpu_custom_call" | custom-call | tf_op jit(solution)/shard_map/windows/pallas_call | solution.py:442
  4.6 0.0 copy-start
  4.6 0.0 copy-start.1
  4.6 0.0 copy-start.4
  4.6 22.6 %all_to_all.10.blocks.refs_1_ = bf16[8,208,384]{2,1,0:T(8,128)(2,1)S(1)} all-to-all(bf16[8,208,384]{2,1,0:T(8,128)(2,1)} %windows.1), channel_id=1, replica_groups={{0,1,2,3,4,5,6,7},{8,9,10,11,12,13,14,15},{16,17,18,19,20,21,22,23},{24..., dimensions={0} | all-to-all | bytes 2555904 | tf_op jit(solution)/shard_map/all_to_all | solution.py:435
  27.3 0.0 copy-done.2
  27.3 0.0 copy-done
  27.3 0.0 copy-done.1
  27.3 0.0 copy-done.4
  27.3 6.2 %first_forward.1 = (bf16[192,384]{1,0:T(8,128)(2,1)S(1)}, bf16[9,192,384]{2,1,0:T(8,128)(2,1)S(1)}, bf16[8,192,256]{2,1,0:T(8,128)(2,1)S(1)}, bf16[4,384,192]{2,...) custom-call(s32[6]{0:T(128)S(1)} %copy-done.4, ...), custom_call_target="tpu_custom_call" | custom-call | flops 905969664 | bytes 9732152 | tf_op jit(solution)/shard_map/first_forward/pallas_call | solution.py:471
  33.5 1.3 %collective-permute-start = (bf16[192,384]{1,0:T(8,128)(2,1)S(1)}, bf16[192,384]{1,0:T(8,128)(2,1)S(1)}, u32[]{:S(2)}, u32[]{:S(2)}) collective-permute-start(bf16[192,384]{1,0:T(8,128)(2,1)S(1)} %get-tuple-element.23._), channel_id=1, source_target_pairs={{4,8},{5,9},{6,10},{7,11},{0,12},{2,14},{20,24},{21,25},{22,26},{2... | collective-permute-start | bytes 442376 | tf_op jit(solution)/shard_map/ppermute | solution.py:440
  34.8 1.3 %collective-permute-start.1 = (bf16[96,256]{1,0:T(8,128)(2,1)S(1)}, bf16[96,256]{1,0:T(8,128)(2,1)S(1)}, u32[]{:S(2)}, u32[]{:S(2)}) collective-permute-start(bf16[96,256]{1,0:T(8,128)(2,1)S(1)} %near_rows.1), channel_id=1, source_target_pairs={{4,8},{5,9},{6,10},{7,11},{0,12},{2,14},{20,24},{21,25},{22,26},{2... | collective-permute-start | bytes 147464 | tf_op jit(solution)/shard_map/ppermute | solution.py:440
  36.1 1.4 %collective-permute-done.entering = bf16[192,384]{1,0:T(8,128)(2,1)S(1)} collective-permute-done((bf16[192,384]{1,0:T(8,128)(2,1)S(1)}, bf16[192,384]{1,0:T(8,128)(2,1)S(1)}, u32[]{:S(2)}, u32[]{:S(2)}) %collective-permute-start) | collective-permute-done | bytes 147488 | tf_op jit(solution)/shard_map/ppermute | solution.py:440
  37.5 1.5 %forward.1 = (bf16[192,384]{1,0:T(8,128)(2,1)}, bf16[9,192,384]{2,1,0:T(8,128)(2,1)S(1)}, bf16[8,192,256]{2,1,0:T(8,128)(2,1)S(1)}) custom-call(s32[8]{0:T(128)S(1)} %get-tuple-element.22.indices, bf16[192,384]{1,0:T(8,128)(2,1)S(1)} %collective-permute-done.entering, bf16[8,208,384]{2,1,0:T(8,128)(2,1)S(1)} %all_to_all.10.blocks.refs_1_, ...), custom_call_target="tpu_custom_call" | custom-call | flops 905969664 | bytes 7569440 | tf_op jit(solution)/shard_map/forward/pallas_call | solution.py:471
  39.0 0.0 collective-permute-done.1.refs_0_
  39.0 1.2 %middle.1 = (bf16[192,384]{1,0:T(8,128)(2,1)S(1)}, bf16[8,192,384]{2,1,0:T(8,128)(2,1)S(1)}, bf16[4,384,192]{2,1,0:T(8,128)(2,1)S(1)}, bf16[4,384,384]{2,1,0:T(8,128)(2,1)S(1)}) custom-call(s32[8]{0:T(128)S(1)} %get-tuple-element.22.indices, bf16[9,192,384]{2,1,0:T(8,128)(2,1)S(1)} %get-tuple-element.27.waves, ...), custom_call_target="tpu_custom_call" | custom-call | flops 905969664 | bytes 10076192 | tf_op jit(solution)/shard_map/middle/pallas_call | solution.py:471
  40.2 1.3 %collective-permute-start.2 = (bf16[192,384]{1,0:T(8,128)(2,1)S(1)}, bf16[192,384]{1,0:T(8,128)(2,1)S(1)}, u32[]{:S(2)}, u32[]{:S(2)}) collective-permute-start(bf16[192,384]{1,0:T(8,128)(2,1)S(1)} %get-tuple-element.33), channel_id=1, source_target_pairs={{8,4},{9,5},{10,6},{11,7},{12,0},{14,2},{24,20},{25,21},{26,22},{2... | collective-permute-start | bytes 442376 | tf_op jit(solution)/shard_map/ppermute | solution.py:440
  41.5 16.3 %collective-permute-done.2.arriving = bf16[192,384]{1,0:T(8,128)(2,1)S(1)} collective-permute-done((bf16[192,384]{1,0:T(8,128)(2,1)S(1)}, bf16[192,384]{1,0:T(8,128)(2,1)S(1)}, u32[]{:S(2)}, u32[]{:S(2)}) %collective-permute-start.2) | collective-permute-done | bytes 147488 | tf_op jit(solution)/shard_map/ppermute | solution.py:440
  57.8 5.4 %backward.1 = (bf16[192,384]{1,0:T(8,128)(2,1)}, bf16[8,192,384]{2,1,0:T(8,128)(2,1)S(1)}) custom-call(s32[8]{0:T(128)S(1)} %get-tuple-element.22.indices, bf16[192,384]{1,0:T(8,128)(2,1)S(1)} %collective-permute-done.2.arriving, bf16[9,192,384]{2,1,0:T(8,128)(2,1)S(1)} %get-tuple-element.27.waves, bf16[8,208,384]{2,1,0:T(8,128)(2,1)S(1)} %all_to_all.10.blocks.refs_1_, ...), custom_call_target="tpu_custom_call" | custom-call | flops 905969664 | bytes 7815200 | tf_op jit(solution)/shard_map/backward/pallas_call | solution.py:471
  63.2 0.0 copy-start.3
  63.2 21.6 %all_to_all.11.grads_ref = bf16[8,192,384]{2,1,0:T(8,128)(2,1)S(1)} all-to-all(bf16[8,192,384]{2,1,0:T(8,128)(2,1)S(1)} %get-tuple-element.38), channel_id=1, replica_groups={{0,1,2,3,4,5,6,7},{8,9,10,11,12,13,14,15},{16,17,18,19,20,21,22,23},{24..., dimensions={0} | all-to-all | bytes 2359296 | tf_op jit(solution)/shard_map/all_to_all | solution.py:435
  84.8 0.0 copy-done.3
  84.8 3.2 %sum_windows.1 = f32[1,2,384,384]{3,2,1,0:T(8,128)} custom-call(s32[2,6]{1,0:T(2,128)S(1)} %bitcast.2, bf16[8,192,384]{2,1,0:T(8,128)(2,1)S(1)} %all_to_all.11.grads_ref), custom_call_target="tpu_custom_call" | custom-call | tf_op jit(solution)/shard_map/sum_windows/pallas_call | solution.py:534
  (1 shorter events, 0.0 us)
Async XLA Ops:
  0.7 26.6 %copy-start.2 = (f32[2,192,192]{2,1,0:T(8,128)S(1)}, f32[2,192,192]{2,1,0:T(8,128)}, u32[]{:S(2)}) copy-start(f32[2,192,192]{2,1,0:T(8,128)} %constant.2.clone.dft) | copy-start | bytes 884740
  4.6 22.7 %copy-start = (bf16[4,2,192,192]{3,2,1,0:T(8,128)(2,1)S(1)}, bf16[4,2,192,192]{3,2,1,0:T(8,128)(2,1)}, u32[]{:S(2)}) copy-start(bf16[4,2,192,192]{3,2,1,0:T(8,128)(2,1)} %refs_3_.1) | copy-start | bytes 1769476
  4.6 22.7 %copy-start.1 = (bf16[8,2,192,192]{3,2,1,0:T(8,128)(2,1)S(1)}, bf16[8,2,192,192]{3,2,1,0:T(8,128)(2,1)}, u32[]{:S(2)}) copy-start(bf16[8,2,192,192]{3,2,1,0:T(8,128)(2,1)} %probes.1) | copy-start | bytes 3538948
  4.6 22.7 %copy-start.4 = (s32[6]{0:T(128)S(1)}, s32[6]{0:T(128)}, u32[]{:S(2)}) copy-start(s32[6]{0:T(128)} %group_ref.1) | copy-start | bytes 76
  33.5 4.0 %collective-permute-start = (bf16[192,384]{1,0:T(8,128)(2,1)S(1)}, bf16[192,384]{1,0:T(8,128)(2,1)S(1)}, u32[]{:S(2)}, u32[]{:S(2)}) collective-permute-start(bf16[192,384]{1,0:T(8,128)(2,1)S(1)} %get-tuple-element.23._), channel_id=1, source_target_pairs={{4,8},{5,9},{6,10},{7,11},{0,12},{2,14},{20,24},{21,25},{22,26},{2... | collective-permute-start | bytes 442376 | tf_op jit(solution)/shard_map/ppermute | solution.py:440
  34.8 4.2 %collective-permute-start.1 = (bf16[96,256]{1,0:T(8,128)(2,1)S(1)}, bf16[96,256]{1,0:T(8,128)(2,1)S(1)}, u32[]{:S(2)}, u32[]{:S(2)}) collective-permute-start(bf16[96,256]{1,0:T(8,128)(2,1)S(1)} %near_rows.1), channel_id=1, source_target_pairs={{4,8},{5,9},{6,10},{7,11},{0,12},{2,14},{20,24},{21,25},{22,26},{2... | collective-permute-start | bytes 147464 | tf_op jit(solution)/shard_map/ppermute | solution.py:440
  40.2 17.6 %collective-permute-start.2 = (bf16[192,384]{1,0:T(8,128)(2,1)S(1)}, bf16[192,384]{1,0:T(8,128)(2,1)S(1)}, u32[]{:S(2)}, u32[]{:S(2)}) collective-permute-start(bf16[192,384]{1,0:T(8,128)(2,1)S(1)} %get-tuple-element.33), channel_id=1, source_target_pairs={{8,4},{9,5},{10,6},{11,7},{12,0},{14,2},{24,20},{25,21},{26,22},{2... | collective-permute-start | bytes 442376 | tf_op jit(solution)/shard_map/ppermute | solution.py:440
  63.2 21.6 %copy-start.3 = (s32[6,2]{0,1:T(2,128)S(1)}, s32[6,2]{0,1:T(2,128)}, u32[]{:S(2)}) copy-start(s32[6,2]{0,1:T(2,128)} %param.13) | copy-start | bytes 148

commit v21 on v16

--- a/solution.py
+++ b/solution.py
@@ -296,22 +296,22 @@
     near[...] = observed[...].astype(BF16)
 
 
-def first_kernel(group_ref, probes, blocks, props, dft, leaving, waves, tails, lb, rf, rb, left, right, right_conj, probe, indices, sem):
+def first_kernel(group_in, probes, blocks, props, dft, leaving, waves, tails, lb, rf, rb, left, right, right_conj, group_ref, indices, sem):
     size = blocks.shape[0]
     slot, group = place_in(size)
 
     @pl.when(group == 0)
     def _():
+        copy = pltpu.make_async_copy(group_in, group_ref, sem)
+        copy.start()
+        forward_tables(props, rf)
+        read_indices(blocks, indices, props.shape[0])
+        copy.wait()
         position = 0
         for p, held in enumerate(slots_of(group_ref.shape[0], size)):
             position = jnp.where(slot == held, p, position)
         which = group_ref[position]
-        copy = pltpu.make_async_copy(probes.at[which], probe, sem)
-        copy.start()
-        forward_tables(props, rf)
-        read_indices(blocks, indices, props.shape[0])
-        copy.wait()
-        waves[0] = packed(probe[0].astype(F32), probe[1].astype(F32)).astype(BF16)
+        waves[0] = packed(probes[which, 0].astype(F32), probes[which, 1].astype(F32)).astype(BF16)
         forward_steps(blocks, None, waves, indices, props, rf)
         leaving[...] = waves[size]
 
@@ -399,9 +399,9 @@
         both = jnp.concatenate(
             [jnp.concatenate([x0, xt], axis=1), jnp.concatenate([x1, other], axis=1)], axis=0
         )
-        spread_out.append(dot(both, picker((2 * LANES, extent), offsets_ref[1, p])).astype(BF16))
+        spread_out.append(dot(both, picker((2 * LANES, extent), offsets_ref[1:2, p : p + 1])).astype(BF16))
     rows = jnp.concatenate(
-        [row_picker((extent, width), -offsets_ref[0, p]) for p in range(positions)], axis=1
+        [row_picker((extent, width), -offsets_ref[0:1, p : p + 1]) for p in range(positions)], axis=1
     )
     copies = []
     for c in range(2):
@@ -492,8 +492,8 @@
         "first_forward",
         [wave, waves_shape, tails_shape, left_table, square_table, square_table]
         + [detector_left, detector_right, struct(2 * width, 2 * width)],
-        [SMEM, HBM, VMEM, VMEM, VMEM],
-        [pltpu.VMEM(probes.shape[1:], BF16), indices, pltpu.SemaphoreType.DMA],
+        [HBM, VMEM, VMEM, VMEM, VMEM],
+        [pltpu.SMEM(probe_group.shape, jnp.int32), indices, pltpu.SemaphoreType.DMA],
         (probe_group, probes, blocks, propagators, jnp.asarray(dft_constant(width))),
         size,
     )
@@ -538,7 +538,7 @@
     return pl.pallas_call(
         gather_kernel,
         out_shape=jax.ShapeDtypeStruct(objects.shape, F32),
-        in_specs=[SMEM, VMEM],
+        in_specs=[VMEM, VMEM],
         out_specs=HBM,
         scratch_shapes=[pltpu.VMEM(objects.shape[1:], F32), pltpu.SemaphoreType.DMA((2,))],
         compiler_params=PARAMS,

time: 86.1 us -> 85 us (0.987)
  Pallas kernels: 19 us -> 17.8 us
where the time goes in v21:
time: 85 us; the launch traced here: 84.7 us
  blocking collectives  44.1 us (52%)
  Pallas kernels  17.8 us (21%)
  waiting for transfers between devices  17.7 us (21%)
  starting transfers between devices  4.03 us (5%)
  between operations  0.91 us (1%)
    all_to_all x2, blocking collectives, exchanged(): lax.all_to_all(blocks, 'cuts', 0, 0, axis_index_groups=members, tiled=True)  44.1 us
    ppermute x3, waiting for transfers between devices, handed(): return lax.ppermute(block, 'cuts', route)  17.7 us
    pallas_call x5, Pallas kernels, call(): pl.pallas_call(kernel, out_shape=out_shape, in_specs=in_specs, out_specs=...  11.1 us
    ppermute x3, starting transfers between devices, handed(): return lax.ppermute(block, 'cuts', route)  4.03 us
    pallas_call x1, Pallas kernels, shards(): pl.pallas_call(window_kernel, out_shape=struct(size, rows, 2 * width), in...  3.93 us
    pallas_call x1, Pallas kernels, shards(): pl.pallas_call(gather_kernel, out_shape=jax.ShapeDtypeStruct(objects.shap...  2.77 us
  transfers between devices with their start and end apart: 3, of which 2 were waited for; matrix products, arithmetic and copies ran while one was open for 0% of the time, Pallas kernels for 1%

profile of v21, /device:TPU:0, one launch (start us, length us, event | category | flops | bytes accessed | tf_op | source)
XLA Modules:
  0.0 84.7 jit_solution(3691440904498790071)
XLA Ops:
  0.7 0.0 copy-start.2
  0.7 3.9 %windows.1 = bf16[8,208,384]{2,1,0:T(8,128)(2,1)} custom-call(s32[2,6]{1,0:T(2,128)} %bitcast.1, s32[1]{0:T(128)S(6)} %copy.9.index_ref, bf16[1,2,384,384]{3,2,1,0:T(8,128)(2,1)} %objects_in.1, f32[6,12,192]{2,1,0:T(8,128)} %measured_in.1), custom_call_target="tpu_custom_call" | custom-call | tf_op jit(solution)/shard_map/windows/pallas_call | solution.py:445
  4.6 0.0 copy-start
  4.6 0.0 copy-start.1
  4.6 0.0 copy-start.4
  4.6 22.6 %all_to_all.10.blocks.refs_1_ = bf16[8,208,384]{2,1,0:T(8,128)(2,1)S(1)} all-to-all(bf16[8,208,384]{2,1,0:T(8,128)(2,1)} %windows.1), channel_id=1, replica_groups={{0,1,2,3,4,5,6,7},{8,9,10,11,12,13,14,15},{16,17,18,19,20,21,22,23},{24..., dimensions={0} | all-to-all | bytes 2555904 | tf_op jit(solution)/shard_map/all_to_all | solution.py:438
  27.3 0.0 copy-done.2
  27.3 0.0 copy-done
  27.3 0.0 copy-done.1
  27.3 0.0 copy-done.4
  27.3 4.7 %first_forward.1 = (bf16[192,384]{1,0:T(8,128)(2,1)S(1)}, bf16[9,192,384]{2,1,0:T(8,128)(2,1)S(1)}, bf16[8,192,256]{2,1,0:T(8,128)(2,1)S(1)}, bf16[4,384,192]{2,...) custom-call(s32[6]{0:T(128)S(1)} %copy-done.4, ...), custom_call_target="tpu_custom_call" | custom-call | flops 905969664 | bytes 9732120 | tf_op jit(solution)/shard_map/first_forward/pallas_call | solution.py:475
  32.0 1.4 %collective-permute-start = (bf16[192,384]{1,0:T(8,128)(2,1)S(1)}, bf16[192,384]{1,0:T(8,128)(2,1)S(1)}, u32[]{:S(2)}, u32[]{:S(2)}) collective-permute-start(bf16[192,384]{1,0:T(8,128)(2,1)S(1)} %get-tuple-element.21._), channel_id=1, source_target_pairs={{4,8},{5,9},{6,10},{7,11},{0,12},{2,14},{20,24},{21,25},{22,26},{2... | collective-permute-start | bytes 442376 | tf_op jit(solution)/shard_map/ppermute | solution.py:443
  33.5 1.3 %collective-permute-start.1 = (bf16[96,256]{1,0:T(8,128)(2,1)S(1)}, bf16[96,256]{1,0:T(8,128)(2,1)S(1)}, u32[]{:S(2)}, u32[]{:S(2)}) collective-permute-start(bf16[96,256]{1,0:T(8,128)(2,1)S(1)} %near_rows.1), channel_id=1, source_target_pairs={{4,8},{5,9},{6,10},{7,11},{0,12},{2,14},{20,24},{21,25},{22,26},{2... | collective-permute-start | bytes 147464 | tf_op jit(solution)/shard_map/ppermute | solution.py:443
  34.8 1.4 %collective-permute-done.entering = bf16[192,384]{1,0:T(8,128)(2,1)S(1)} collective-permute-done((bf16[192,384]{1,0:T(8,128)(2,1)S(1)}, bf16[192,384]{1,0:T(8,128)(2,1)S(1)}, u32[]{:S(2)}, u32[]{:S(2)}) %collective-permute-start) | collective-permute-done | bytes 147488 | tf_op jit(solution)/shard_map/ppermute | solution.py:443
  36.2 1.0 %forward.1 = (bf16[192,384]{1,0:T(8,128)(2,1)}, bf16[9,192,384]{2,1,0:T(8,128)(2,1)S(1)}, bf16[8,192,256]{2,1,0:T(8,128)(2,1)S(1)}) custom-call(bf16[192,384]{1,0:T(8,128)(2,1)S(1)} %collective-permute-done.entering, bf16[8,208,384]{2,1,0:T(8,128)(2,1)S(1)} %all_to_all.10.blocks.refs_1_, bf16[8,192,256]{2,1,0:T(8,128)(2,1)S(1)} %get-tuple-element.22.tails.refs_2_, ...), custom_call_target="tpu_custom_call" | custom-call | flops 905969664 | bytes 7569408 | tf_op jit(solution)/shard_map/forward/pallas_call | solution.py:475
  37.1 0.0 collective-permute-done.1.refs_0_
  37.1 0.4 middle.1
  37.6 1.3 %collective-permute-start.2 = (bf16[192,384]{1,0:T(8,128)(2,1)S(1)}, bf16[192,384]{1,0:T(8,128)(2,1)S(1)}, u32[]{:S(2)}, u32[]{:S(2)}) collective-permute-start(bf16[192,384]{1,0:T(8,128)(2,1)S(1)} %get-tuple-element.31), channel_id=1, source_target_pairs={{8,4},{9,5},{10,6},{11,7},{12,0},{14,2},{24,20},{25,21},{26,22},{2... | collective-permute-start | bytes 442376 | tf_op jit(solution)/shard_map/ppermute | solution.py:443
  38.9 16.4 %collective-permute-done.2.arriving = bf16[192,384]{1,0:T(8,128)(2,1)S(1)} collective-permute-done((bf16[192,384]{1,0:T(8,128)(2,1)S(1)}, bf16[192,384]{1,0:T(8,128)(2,1)S(1)}, u32[]{:S(2)}, u32[]{:S(2)}) %collective-permute-start.2) | collective-permute-done | bytes 147488 | tf_op jit(solution)/shard_map/ppermute | solution.py:443
  55.3 5.0 %backward.1 = (bf16[192,384]{1,0:T(8,128)(2,1)}, bf16[8,192,384]{2,1,0:T(8,128)(2,1)S(1)}) custom-call(bf16[192,384]{1,0:T(8,128)(2,1)S(1)} %collective-permute-done.2.arriving, bf16[9,192,384]{2,1,0:T(8,128)(2,1)S(1)} %get-tuple-element.25.waves, bf16[8,208,384]{2,1,0:T(8,128)(2,1)S(1)} %all_to_all.10.blocks.refs_1_, ...), custom_call_target="tpu_custom_call" | custom-call | flops 905969664 | bytes 7815168 | tf_op jit(solution)/shard_map/backward/pallas_call | solution.py:475
  60.2 0.0 copy-start.3
  60.2 21.5 %all_to_all.11.grads_ref = bf16[8,192,384]{2,1,0:T(8,128)(2,1)S(1)} all-to-all(bf16[8,192,384]{2,1,0:T(8,128)(2,1)S(1)} %get-tuple-element.36), channel_id=1, replica_groups={{0,1,2,3,4,5,6,7},{8,9,10,11,12,13,14,15},{16,17,18,19,20,21,22,23},{24..., dimensions={0} | all-to-all | bytes 2359296 | tf_op jit(solution)/shard_map/all_to_all | solution.py:438
  81.7 0.0 copy-done.3
  81.7 2.8 %sum_windows.1 = f32[1,2,384,384]{3,2,1,0:T(8,128)} custom-call(s32[2,6]{1,0:T(2,128)S(1)} %bitcast.2, bf16[8,192,384]{2,1,0:T(8,128)(2,1)S(1)} %all_to_all.11.grads_ref), custom_call_target="tpu_custom_call" | custom-call | tf_op jit(solution)/shard_map/sum_windows/pallas_call | solution.py:538
  (1 shorter events, 0.0 us)
Async XLA Ops:
  0.7 26.6 %copy-start.2 = (f32[2,192,192]{2,1,0:T(8,128)S(1)}, f32[2,192,192]{2,1,0:T(8,128)}, u32[]{:S(2)}) copy-start(f32[2,192,192]{2,1,0:T(8,128)} %constant.2.clone.dft) | copy-start | bytes 884740
  4.6 22.7 %copy-start = (bf16[4,2,192,192]{3,2,1,0:T(8,128)(2,1)S(1)}, bf16[4,2,192,192]{3,2,1,0:T(8,128)(2,1)}, u32[]{:S(2)}) copy-start(bf16[4,2,192,192]{3,2,1,0:T(8,128)(2,1)} %refs_3_.1) | copy-start | bytes 1769476
  4.6 22.7 %copy-start.1 = (bf16[8,2,192,192]{3,2,1,0:T(8,128)(2,1)S(1)}, bf16[8,2,192,192]{3,2,1,0:T(8,128)(2,1)}, u32[]{:S(2)}) copy-start(bf16[8,2,192,192]{3,2,1,0:T(8,128)(2,1)} %probes.1) | copy-start | bytes 3538948
  4.6 22.7 %copy-start.4 = (s32[6]{0:T(128)S(1)}, s32[6]{0:T(128)}, u32[]{:S(2)}) copy-start(s32[6]{0:T(128)} %group_in.1) | copy-start | bytes 76
  32.0 4.1 %collective-permute-start = (bf16[192,384]{1,0:T(8,128)(2,1)S(1)}, bf16[192,384]{1,0:T(8,128)(2,1)S(1)}, u32[]{:S(2)}, u32[]{:S(2)}) collective-permute-start(bf16[192,384]{1,0:T(8,128)(2,1)S(1)} %get-tuple-element.21._), channel_id=1, source_target_pairs={{4,8},{5,9},{6,10},{7,11},{0,12},{2,14},{20,24},{21,25},{22,26},{2... | collective-permute-start | bytes 442376 | tf_op jit(solution)/shard_map/ppermute | solution.py:443
  33.5 3.6 %collective-permute-start.1 = (bf16[96,256]{1,0:T(8,128)(2,1)S(1)}, bf16[96,256]{1,0:T(8,128)(2,1)S(1)}, u32[]{:S(2)}, u32[]{:S(2)}) collective-permute-start(bf16[96,256]{1,0:T(8,128)(2,1)S(1)} %near_rows.1), channel_id=1, source_target_pairs={{4,8},{5,9},{6,10},{7,11},{0,12},{2,14},{20,24},{21,25},{22,26},{2... | collective-permute-start | bytes 147464 | tf_op jit(solution)/shard_map/ppermute | solution.py:443
  37.6 17.7 %collective-permute-start.2 = (bf16[192,384]{1,0:T(8,128)(2,1)S(1)}, bf16[192,384]{1,0:T(8,128)(2,1)S(1)}, u32[]{:S(2)}, u32[]{:S(2)}) collective-permute-start(bf16[192,384]{1,0:T(8,128)(2,1)S(1)} %get-tuple-element.31), channel_id=1, source_target_pairs={{8,4},{9,5},{10,6},{11,7},{12,0},{14,2},{24,20},{25,21},{26,22},{2... | collective-permute-start | bytes 442376 | tf_op jit(solution)/shard_map/ppermute | solution.py:443
  60.2 21.5 %copy-start.3 = (s32[6,2]{0,1:T(2,128)S(1)}, s32[6,2]{0,1:T(2,128)}, u32[]{:S(2)}) copy-start(s32[6,2]{0,1:T(2,128)} %param.13) | copy-start | bytes 148

commit v22 on v21

--- a/solution.py
+++ b/solution.py
@@ -148,18 +148,18 @@
     return [slot ^ flip for slot in slots_of(positions, size)]
 
 
-def window_kernel(offsets_in, index_ref, objects_in, measured_in, blocks_out, blocks, offsets_ref, objects, measured, pickers, sems):
+def window_kernel(offsets_in, index_in, objects_in, measured_in, blocks_out, blocks, index_ref, offsets_ref, objects, measured, pickers, sems):
     positions, near_rows, width = measured.shape
     extent = objects.shape[-1]
     copies = [
         pltpu.make_async_copy(objects_in.at[0, 0], objects.at[0], sems.at[0]),
         pltpu.make_async_copy(objects_in.at[0, 1], objects.at[1], sems.at[1]),
         pltpu.make_async_copy(measured_in, measured, sems.at[2]),
+        pltpu.make_async_copy(index_in, index_ref, sems.at[4 + positions]),
         pltpu.make_async_copy(offsets_in, offsets_ref, sems.at[3]),
     ]
     for copy in reversed(copies):
         copy.start()
-    tag = jnp.full((ROWS, LANES), index_ref[0], jnp.int32).astype(F32)
     size = blocks_out.shape[0]
     _, group = place_in(size)
     flip = lax.rem(group, 2) * (size // 2)
@@ -169,6 +169,7 @@
             pickers[p, c] = picker((extent, 2 * LANES), offsets_ref[1, p], c == 1)
     for copy in copies:
         copy.wait()
+    tag = jnp.full((ROWS, LANES), index_ref[0], jnp.int32).astype(F32)
     sending = []
     for p, slot in enumerate(slots_of(positions, size)):
         start = offsets_ref[0, p]
@@ -445,15 +446,16 @@
     blocks = pl.pallas_call(
         window_kernel,
         out_shape=struct(size, rows, 2 * width),
-        in_specs=[HBM, SMEM, HBM, HBM],
+        in_specs=[HBM, HBM, HBM, HBM],
         out_specs=HBM,
         scratch_shapes=[
             pltpu.VMEM((size, rows, 2 * width), BF16),
+            pltpu.SMEM(prop_index.shape, jnp.int32),
             pltpu.SMEM(offsets.shape[::-1], jnp.int32),
             pltpu.VMEM(objects.shape[1:], BF16),
             pltpu.VMEM(measured.shape, F32),
             pltpu.VMEM((len(slots), 2, objects.shape[-1], 2 * LANES), BF16),
-            pltpu.SemaphoreType.DMA((4 + len(slots),)),
+            pltpu.SemaphoreType.DMA((5 + len(slots),)),
         ],
         compiler_params=ALONE,
         name="windows",

time: 85 us -> 85 us (level)
  no operation moved by 1% of the time
where the time goes in v22:
time: 85 us; the launch traced here: 84.7 us
  blocking collectives  44.1 us (52%)
  Pallas kernels  17.9 us (21%)
  waiting for transfers between devices  17.7 us (21%)
  starting transfers between devices  4.04 us (5%)
  between operations  0.91 us (1%)
    all_to_all x2, blocking collectives, exchanged(): lax.all_to_all(blocks, 'cuts', 0, 0, axis_index_groups=members, tiled=True)  44.1 us
    ppermute x3, waiting for transfers between devices, handed(): return lax.ppermute(block, 'cuts', route)  17.7 us
    pallas_call x5, Pallas kernels, call(): pl.pallas_call(kernel, out_shape=out_shape, in_specs=in_specs, out_specs=...  11.1 us
    ppermute x3, starting transfers between devices, handed(): return lax.ppermute(block, 'cuts', route)  4.04 us
    pallas_call x1, Pallas kernels, shards(): pl.pallas_call(window_kernel, out_shape=struct(size, rows, 2 * width), in...  3.93 us
    pallas_call x1, Pallas kernels, shards(): pl.pallas_call(gather_kernel, out_shape=jax.ShapeDtypeStruct(objects.shap...  2.77 us
  transfers between devices with their start and end apart: 3, of which 2 were waited for; matrix products, arithmetic and copies ran while one was open for 0% of the time, Pallas kernels for 1%

profile of v22, /device:TPU:0, one launch (start us, length us, event | category | flops | bytes accessed | tf_op | source)
XLA Modules:
  0.0 84.7 jit_solution(2531825865241078765)
XLA Ops:
  0.7 0.0 copy-start.2
  0.7 3.9 %windows.1 = bf16[8,208,384]{2,1,0:T(8,128)(2,1)} custom-call(s32[2,6]{1,0:T(2,128)} %bitcast.1, s32[1]{0:T(128)S(6)} %copy.9.index_in, bf16[1,2,384,384]{3,2,1,0:T(8,128)(2,1)} %objects_in.1, f32[6,12,192]{2,1,0:T(8,128)} %measured_in.1), custom_call_target="tpu_custom_call" | custom-call | tf_op jit(solution)/shard_map/windows/pallas_call | solution.py:446
  4.6 0.0 copy-start
  4.6 0.0 copy-start.1
  4.6 0.0 copy-start.4
  4.6 22.6 %all_to_all.10.blocks.refs_1_ = bf16[8,208,384]{2,1,0:T(8,128)(2,1)S(1)} all-to-all(bf16[8,208,384]{2,1,0:T(8,128)(2,1)} %windows.1), channel_id=1, replica_groups={{0,1,2,3,4,5,6,7},{8,9,10,11,12,13,14,15},{16,17,18,19,20,21,22,23},{24..., dimensions={0} | all-to-all | bytes 2555904 | tf_op jit(solution)/shard_map/all_to_all | solution.py:439
  27.3 0.0 copy-done.2
  27.3 0.0 copy-done
  27.3 0.0 copy-done.1
  27.3 0.0 copy-done.4
  27.3 4.7 %first_forward.1 = (bf16[192,384]{1,0:T(8,128)(2,1)S(1)}, bf16[9,192,384]{2,1,0:T(8,128)(2,1)S(1)}, bf16[8,192,256]{2,1,0:T(8,128)(2,1)S(1)}, bf16[4,384,192]{2,...) custom-call(s32[6]{0:T(128)S(1)} %copy-done.4, ...), custom_call_target="tpu_custom_call" | custom-call | flops 905969664 | bytes 9732120 | tf_op jit(solution)/shard_map/first_forward/pallas_call | solution.py:477
  32.0 1.5 %collective-permute-start = (bf16[192,384]{1,0:T(8,128)(2,1)S(1)}, bf16[192,384]{1,0:T(8,128)(2,1)S(1)}, u32[]{:S(2)}, u32[]{:S(2)}) collective-permute-start(bf16[192,384]{1,0:T(8,128)(2,1)S(1)} %get-tuple-element.21._), channel_id=1, source_target_pairs={{4,8},{5,9},{6,10},{7,11},{0,12},{2,14},{20,24},{21,25},{22,26},{2... | collective-permute-start | bytes 442376 | tf_op jit(solution)/shard_map/ppermute | solution.py:444
  33.5 1.3 %collective-permute-start.1 = (bf16[96,256]{1,0:T(8,128)(2,1)S(1)}, bf16[96,256]{1,0:T(8,128)(2,1)S(1)}, u32[]{:S(2)}, u32[]{:S(2)}) collective-permute-start(bf16[96,256]{1,0:T(8,128)(2,1)S(1)} %near_rows.1), channel_id=1, source_target_pairs={{4,8},{5,9},{6,10},{7,11},{0,12},{2,14},{20,24},{21,25},{22,26},{2... | collective-permute-start | bytes 147464 | tf_op jit(solution)/shard_map/ppermute | solution.py:444
  34.8 1.4 %collective-permute-done.entering = bf16[192,384]{1,0:T(8,128)(2,1)S(1)} collective-permute-done((bf16[192,384]{1,0:T(8,128)(2,1)S(1)}, bf16[192,384]{1,0:T(8,128)(2,1)S(1)}, u32[]{:S(2)}, u32[]{:S(2)}) %collective-permute-start) | collective-permute-done | bytes 147488 | tf_op jit(solution)/shard_map/ppermute | solution.py:444
  36.2 1.0 %forward.1 = (bf16[192,384]{1,0:T(8,128)(2,1)}, bf16[9,192,384]{2,1,0:T(8,128)(2,1)S(1)}, bf16[8,192,256]{2,1,0:T(8,128)(2,1)S(1)}) custom-call(bf16[192,384]{1,0:T(8,128)(2,1)S(1)} %collective-permute-done.entering, bf16[8,208,384]{2,1,0:T(8,128)(2,1)S(1)} %all_to_all.10.blocks.refs_1_, bf16[8,192,256]{2,1,0:T(8,128)(2,1)S(1)} %get-tuple-element.22.tails.refs_2_, ...), custom_call_target="tpu_custom_call" | custom-call | flops 905969664 | bytes 7569408 | tf_op jit(solution)/shard_map/forward/pallas_call | solution.py:477
  37.1 0.0 collective-permute-done.1.refs_0_
  37.2 0.4 middle.1
  37.6 1.3 %collective-permute-start.2 = (bf16[192,384]{1,0:T(8,128)(2,1)S(1)}, bf16[192,384]{1,0:T(8,128)(2,1)S(1)}, u32[]{:S(2)}, u32[]{:S(2)}) collective-permute-start(bf16[192,384]{1,0:T(8,128)(2,1)S(1)} %get-tuple-element.31), channel_id=1, source_target_pairs={{8,4},{9,5},{10,6},{11,7},{12,0},{14,2},{24,20},{25,21},{26,22},{2... | collective-permute-start | bytes 442376 | tf_op jit(solution)/shard_map/ppermute | solution.py:444
  38.9 16.4 %collective-permute-done.2.arriving = bf16[192,384]{1,0:T(8,128)(2,1)S(1)} collective-permute-done((bf16[192,384]{1,0:T(8,128)(2,1)S(1)}, bf16[192,384]{1,0:T(8,128)(2,1)S(1)}, u32[]{:S(2)}, u32[]{:S(2)}) %collective-permute-start.2) | collective-permute-done | bytes 147488 | tf_op jit(solution)/shard_map/ppermute | solution.py:444
  55.3 5.0 %backward.1 = (bf16[192,384]{1,0:T(8,128)(2,1)}, bf16[8,192,384]{2,1,0:T(8,128)(2,1)S(1)}) custom-call(bf16[192,384]{1,0:T(8,128)(2,1)S(1)} %collective-permute-done.2.arriving, bf16[9,192,384]{2,1,0:T(8,128)(2,1)S(1)} %get-tuple-element.25.waves, bf16[8,208,384]{2,1,0:T(8,128)(2,1)S(1)} %all_to_all.10.blocks.refs_1_, ...), custom_call_target="tpu_custom_call" | custom-call | flops 905969664 | bytes 7815168 | tf_op jit(solution)/shard_map/backward/pallas_call | solution.py:477
  60.3 0.0 copy-start.3
  60.3 21.5 %all_to_all.11.grads_ref = bf16[8,192,384]{2,1,0:T(8,128)(2,1)S(1)} all-to-all(bf16[8,192,384]{2,1,0:T(8,128)(2,1)S(1)} %get-tuple-element.36), channel_id=1, replica_groups={{0,1,2,3,4,5,6,7},{8,9,10,11,12,13,14,15},{16,17,18,19,20,21,22,23},{24..., dimensions={0} | all-to-all | bytes 2359296 | tf_op jit(solution)/shard_map/all_to_all | solution.py:439
  81.7 0.0 copy-done.3
  81.7 2.8 %sum_windows.1 = f32[1,2,384,384]{3,2,1,0:T(8,128)} custom-call(s32[2,6]{1,0:T(2,128)S(1)} %bitcast.2, bf16[8,192,384]{2,1,0:T(8,128)(2,1)S(1)} %all_to_all.11.grads_ref), custom_call_target="tpu_custom_call" | custom-call | tf_op jit(solution)/shard_map/sum_windows/pallas_call | solution.py:540
  (1 shorter events, 0.0 us)
Async XLA Ops:
  0.7 26.6 %copy-start.2 = (f32[2,192,192]{2,1,0:T(8,128)S(1)}, f32[2,192,192]{2,1,0:T(8,128)}, u32[]{:S(2)}) copy-start(f32[2,192,192]{2,1,0:T(8,128)} %constant.2.clone.dft) | copy-start | bytes 884740
  4.6 22.7 %copy-start = (bf16[4,2,192,192]{3,2,1,0:T(8,128)(2,1)S(1)}, bf16[4,2,192,192]{3,2,1,0:T(8,128)(2,1)}, u32[]{:S(2)}) copy-start(bf16[4,2,192,192]{3,2,1,0:T(8,128)(2,1)} %refs_3_.1) | copy-start | bytes 1769476
  4.6 22.7 %copy-start.1 = (bf16[8,2,192,192]{3,2,1,0:T(8,128)(2,1)S(1)}, bf16[8,2,192,192]{3,2,1,0:T(8,128)(2,1)}, u32[]{:S(2)}) copy-start(bf16[8,2,192,192]{3,2,1,0:T(8,128)(2,1)} %probes.1) | copy-start | bytes 3538948
  4.6 22.7 %copy-start.4 = (s32[6]{0:T(128)S(1)}, s32[6]{0:T(128)}, u32[]{:S(2)}) copy-start(s32[6]{0:T(128)} %group_in.1) | copy-start | bytes 76
  32.0 4.1 %collective-permute-start = (bf16[192,384]{1,0:T(8,128)(2,1)S(1)}, bf16[192,384]{1,0:T(8,128)(2,1)S(1)}, u32[]{:S(2)}, u32[]{:S(2)}) collective-permute-start(bf16[192,384]{1,0:T(8,128)(2,1)S(1)} %get-tuple-element.21._), channel_id=1, source_target_pairs={{4,8},{5,9},{6,10},{7,11},{0,12},{2,14},{20,24},{21,25},{22,26},{2... | collective-permute-start | bytes 442376 | tf_op jit(solution)/shard_map/ppermute | solution.py:444
  33.5 3.6 %collective-permute-start.1 = (bf16[96,256]{1,0:T(8,128)(2,1)S(1)}, bf16[96,256]{1,0:T(8,128)(2,1)S(1)}, u32[]{:S(2)}, u32[]{:S(2)}) collective-permute-start(bf16[96,256]{1,0:T(8,128)(2,1)S(1)} %near_rows.1), channel_id=1, source_target_pairs={{4,8},{5,9},{6,10},{7,11},{0,12},{2,14},{20,24},{21,25},{22,26},{2... | collective-permute-start | bytes 147464 | tf_op jit(solution)/shard_map/ppermute | solution.py:444
  37.6 17.7 %collective-permute-start.2 = (bf16[192,384]{1,0:T(8,128)(2,1)S(1)}, bf16[192,384]{1,0:T(8,128)(2,1)S(1)}, u32[]{:S(2)}, u32[]{:S(2)}) collective-permute-start(bf16[192,384]{1,0:T(8,128)(2,1)S(1)} %get-tuple-element.31), channel_id=1, source_target_pairs={{8,4},{9,5},{10,6},{11,7},{12,0},{14,2},{24,20},{25,21},{26,22},{2... | collective-permute-start | bytes 442376 | tf_op jit(solution)/shard_map/ppermute | solution.py:444
  60.3 21.5 %copy-start.3 = (s32[6,2]{0,1:T(2,128)S(1)}, s32[6,2]{0,1:T(2,128)}, u32[]{:S(2)}) copy-start(s32[6,2]{0,1:T(2,128)} %param.13) | copy-start | bytes 148
